TPU v7x, 32 devices: a whole 2x2x4 slice. The times are simulated.
32 devices in a mesh: wide: 8 (over y, x, core), narrow: 4 (over z).
Axes of the slice: x: 2, y: 2, z: 4, core: 2. Of those that a mesh axis runs over, the one named last changes fastest.
Arguments:
- layer_input: bfloat16 [8192, 2048], P(('wide', 'narrow')), may hold values from -6 to 6
- heads_weight: bfloat16 [2048, 6144], P(('wide', 'narrow')), may hold values from -0.125 to 0.125
- heads_bias: bfloat16 [6144], P(('wide', 'narrow')), may hold values from -3 to 3
- merge_weight: bfloat16 [2048, 2048], P(('wide', 'narrow')), may hold values from -2 to 2
- merge_bias: bfloat16 [2048], P(('wide', 'narrow')), may hold values from -5 to 5
- norm_gains: bfloat16 [2, 2048], P(None, ('wide', 'narrow')), may hold values from 0.25 to 1.75
- norm_shifts: bfloat16 [2, 2048], P(None, ('wide', 'narrow')), may hold values from -3 to 3
- expand_weight: bfloat16 [2048, 2, 5504], P('narrow', None, 'wide'), may hold values from -0.125 to 0.125
- expand_bias: bfloat16 [2, 5504], P(None, ('wide', 'narrow')), may hold values from -3 to 3
- reduce_weight: bfloat16 [5504, 2048], P('wide', 'narrow'), may hold values from -0.625 to 0.625
- reduce_bias: bfloat16 [2048], P('narrow'), may hold values from -5 to 5
- joined: int32 [8], P('wide'), may hold values from 0 to 1, as said below
- prefix: int32 [8, 2], P('wide'), may hold values from 1 to 512
- cotangent: bfloat16 [8192, 2048], P(('wide', 'narrow')), may hold values from -6 to 6
Outputs:
- layer_output: bfloat16 [8192, 2048], P(('wide', 'narrow'))
- input_gradient: float32 [8192, 2048], P(('wide', 'narrow'))
- heads_weight_gradient: float32 [2048, 6144], P(('wide', 'narrow'))
- heads_bias_gradient: float32 [6144], P(('wide', 'narrow'))
- merge_weight_gradient: float32 [2048, 2048], P(('wide', 'narrow'))
- merge_bias_gradient: float32 [2048], P(('wide', 'narrow'))
- gains_gradient: float32 [2, 2048], P(None, ('wide', 'narrow'))
- shifts_gradient: float32 [2, 2048], P(None, ('wide', 'narrow'))
- expand_weight_gradient: float32 [2048, 2, 5504], P('narrow', None, 'wide')
- expand_bias_gradient: float32 [2, 5504], P(None, ('wide', 'narrow'))
- reduce_weight_gradient: float32 [5504, 2048], P('wide', 'narrow')
- reduce_bias_gradient: float32 [2048], P('narrow')
Inputs may be any that keep to these rules, and one draw needn't show every extreme that they name: `joined`: exactly half of the 8 buckets, rounded up, hold one sequence (1); the others hold two sequences of half a bucket each (0).
All inputs are finite; a program needn't handle non-finite values.
Results may differ from a plain program's by a relative error of at most 0.015.
Values may be sent and summed in bfloat16 or wider, within the bound.
A program may use at most 256 MiB of HBM per device.

v0:
```python
import math

import jax
import jax.numpy as jnp
from jax import lax
from jax.sharding import PartitionSpec as P

HEADS = 16
HDIM = 128


residual_scale = 48.0**0.5
norm_eps = 1e-05
masked_value = -1e30


def layout(positions, joined_flag, prefix_pair, bucket_len):
    halfway = bucket_len // 2
    second_seq = (positions >= halfway).astype(jnp.int32) * (1 - joined_flag)
    local_pos = positions - second_seq * halfway
    prefix_len = jnp.where(
        joined_flag == 1,
        prefix_pair[0] + prefix_pair[1],
        jnp.where(second_seq == 1, prefix_pair[1], prefix_pair[0]),
    )
    return (second_seq, local_pos, prefix_len)


def visible(query_pos, key_pos, joined_flag, prefix_pair, bucket_len):
    query_seq, query_local, query_prefix = layout(query_pos, joined_flag, prefix_pair, bucket_len)
    key_seq, key_local, key_prefix = layout(key_pos, joined_flag, prefix_pair, bucket_len)
    same_seq = query_seq[:, None] == key_seq[None, :]
    return same_seq & (
        (key_local[None, :] < key_prefix[None, :]) | (key_local[None, :] <= query_local[:, None])
    )


def rotary_tables(local_pos, head_size):
    halfway = head_size // 2
    inverse = 10000.0 ** (-(2.0 * jnp.arange(halfway).astype(jnp.float32)) / head_size)
    angles = local_pos.astype(jnp.float32)[:, None] * inverse[None, :]
    return (jnp.cos(angles)[:, None, :], jnp.sin(angles)[:, None, :])


def rotate(vectors, cosine, sine_table):
    halfway = vectors.shape[-1] // 2
    first_part, second_part = (vectors[..., :halfway], vectors[..., halfway:])
    return jnp.concatenate(
        [
            first_part * cosine - second_part * sine_table,
            second_part * cosine + first_part * sine_table,
        ],
        axis=-1,
    )


def rotate_back(grads, cosine, sine_table):
    halfway = grads.shape[-1] // 2
    first_part, second_part = (grads[..., :halfway], grads[..., halfway:])
    return jnp.concatenate(
        [
            first_part * cosine + second_part * sine_table,
            second_part * cosine - first_part * sine_table,
        ],
        axis=-1,
    )


def normalize(values, gain, shift):
    centre = jnp.mean(values, axis=-1, keepdims=True)
    centred = values - centre
    variance = jnp.mean(centred * centred, axis=-1, keepdims=True)
    inv_std = lax.rsqrt(variance + norm_eps)
    normed = centred * inv_std
    return (normed * gain + shift, normed, inv_std)


def normalize_back(upstream, normed, inv_std, gain):
    scaled = upstream * gain
    return inv_std * (
        scaled
        - jnp.mean(scaled, axis=-1, keepdims=True)
        - normed * jnp.mean(scaled * normed, axis=-1, keepdims=True)
    )


def collect_params(heads_weight, heads_bias, merge_weight, merge_bias, norm_gains, norm_shifts):
    return (
        lax.all_gather(heads_weight, ("wide", "narrow"), axis=0, tiled=True),
        lax.all_gather(heads_bias, ("wide", "narrow"), axis=0, tiled=True),
        lax.all_gather(merge_weight, ("wide", "narrow"), axis=0, tiled=True),
        lax.all_gather(merge_bias, ("wide", "narrow"), axis=0, tiled=True),
        lax.all_gather(norm_gains, ("wide", "narrow"), axis=1, tiled=True),
        lax.all_gather(norm_shifts, ("wide", "narrow"), axis=1, tiled=True),
    )


def own_blocks(array, dim, wide_count, narrow_count):
    shape = array.shape
    block = shape[dim] // (wide_count * narrow_count)
    split = array.reshape(shape[:dim] + (wide_count, narrow_count, block) + shape[dim + 1 :])
    picked = lax.dynamic_index_in_dim(split, lax.axis_index("narrow"), dim + 1, keepdims=False)
    return picked.reshape(shape[:dim] + (wide_count * block,) + shape[dim + 1 :])


def project_heads(layer_input, heads_full, heads_shift, cosine, sine_table):
    tok_rows = layer_input.shape[0]
    triple = jnp.dot(
        layer_input, heads_full, preferred_element_type=jnp.float32
    ) + heads_shift.astype(jnp.float32)
    triple = triple.reshape(tok_rows, 3, HEADS, HDIM)
    queries = rotate(triple[:, 0], cosine, sine_table).astype(jnp.bfloat16)
    keys_local = (
        rotate(triple[:, 1], cosine, sine_table)
        .astype(jnp.bfloat16)
        .reshape(tok_rows, HEADS * HDIM)
    )
    values_local = triple[:, 2].astype(jnp.bfloat16).reshape(tok_rows, HEADS * HDIM)
    return (queries, keys_local, values_local)


def gather_keys(keys_local, values_local):
    return (
        lax.all_gather(keys_local, "narrow", axis=0, tiled=True),
        lax.all_gather(values_local, "narrow", axis=0, tiled=True),
    )


def grouped(array, group_size):
    row_count = array.shape[0]
    return jnp.moveaxis(array.reshape(row_count, HEADS // group_size, group_size, HDIM), 1, 0)


def ungrouped(array):
    return jnp.moveaxis(array, 0, 1).reshape(array.shape[1], HEADS * HDIM)


def softmax_rows(query_grp, key_grp, key_mask, score_scale):
    scores = (
        jnp.einsum("qgd,kgd->gqk", query_grp, key_grp, preferred_element_type=jnp.float32)
        * score_scale
    )
    scores = jnp.where(key_mask[None], scores, masked_value)
    expo = jnp.exp(scores - jnp.max(scores, axis=-1, keepdims=True))
    return expo / jnp.sum(expo, axis=-1, keepdims=True)


def shards(
    layer_input,
    heads_weight,
    heads_bias,
    merge_weight,
    merge_bias,
    norm_gains,
    norm_shifts,
    expand_weight,
    expand_bias,
    reduce_weight,
    reduce_bias,
    joined,
    prefix,
    cotangent,
):
    tok_rows = layer_input.shape[0]
    model_width = layer_input.shape[1]
    bucket_len = tok_rows * lax.axis_size("narrow")
    group_size = math.gcd(4, HEADS)
    score_scale = HDIM ** (-0.5)
    joined_flag = joined[0]
    prefix_pair = prefix[0]
    positions = lax.axis_index("narrow") * tok_rows + jnp.arange(tok_rows, dtype=jnp.int32)
    all_positions = jnp.arange(bucket_len, dtype=jnp.int32)
    second_seq, local_pos, prefix_len = layout(positions, joined_flag, prefix_pair, bucket_len)
    cosine, sine_table = rotary_tables(local_pos, HDIM)
    key_mask = visible(positions, all_positions, joined_flag, prefix_pair, bucket_len)
    input_float = layer_input.astype(jnp.float32)
    heads_full, heads_shift, merge_full, merge_shift, gains_full, shifts_full = collect_params(
        heads_weight, heads_bias, merge_weight, merge_bias, norm_gains, norm_shifts
    )
    queries, keys_local, values_local = project_heads(
        layer_input, heads_full, heads_shift, cosine, sine_table
    )
    keys_all, values_all = gather_keys(keys_local, values_local)

    def attend_group(items):
        query_grp, key_grp, value_grp = items
        probs_low = softmax_rows(query_grp, key_grp, key_mask, score_scale).astype(jnp.bfloat16)
        return jnp.einsum("gqk,kgd->qgd", probs_low, value_grp, preferred_element_type=jnp.float32)

    mixed_groups = lax.map(
        attend_group,
        (
            grouped(queries, group_size),
            grouped(keys_all.reshape(bucket_len, HEADS, HDIM), group_size),
            grouped(values_all.reshape(bucket_len, HEADS, HDIM), group_size),
        ),
    )
    mixed_low = ungrouped(mixed_groups).astype(jnp.bfloat16)
    attended = jnp.dot(
        mixed_low, merge_full, preferred_element_type=jnp.float32
    ) + merge_shift.astype(jnp.float32)
    gains_float = gains_full.astype(jnp.float32)
    shifts_float = shifts_full.astype(jnp.float32)
    hidden, normed_one, inv_one = normalize(
        residual_scale * input_float + attended, gains_float[0], shifts_float[0]
    )
    hidden_low = hidden.astype(jnp.bfloat16)
    expand_full, expand_shift, reduce_full, reduce_shift = (
        lax.all_gather(expand_weight, "narrow", axis=0, tiled=True),
        lax.all_gather(expand_bias, "narrow", axis=1, tiled=True),
        lax.all_gather(reduce_weight, "narrow", axis=1, tiled=True),
        lax.all_gather(reduce_bias, "narrow", axis=0, tiled=True),
    )
    share = expand_full.shape[2]
    expand_mat = expand_full.reshape(model_width, 2 * share)
    expand_add = expand_shift.reshape(2 * share).astype(jnp.float32)

    def gate_up(piece):
        both = jnp.dot(piece, expand_mat, preferred_element_type=jnp.float32) + expand_add
        return (both[:, :share], both[:, share:])

    gate, upper = gate_up(lax.all_gather(hidden_low, "wide", axis=0, tiled=True))
    active_low = (jax.nn.gelu(gate) * upper).astype(jnp.bfloat16)
    feed = lax.psum_scatter(
        jnp.dot(active_low, reduce_full, preferred_element_type=jnp.float32),
        "wide",
        scatter_dimension=0,
        tiled=True,
    ) + reduce_shift.astype(jnp.float32)
    output_float, normed_two, inv_two = normalize(
        residual_scale * hidden + feed, gains_float[1], shifts_float[1]
    )
    layer_output = output_float.astype(jnp.bfloat16)
    grad_out = cotangent.astype(jnp.float32)
    fresh = lax.optimization_barrier(
        (heads_weight, heads_bias, merge_weight, merge_bias, norm_gains, norm_shifts, grad_out)
    )
    heads_full, heads_shift, merge_full, merge_shift, gains_full, shifts_full = collect_params(
        fresh[0], fresh[1], fresh[2], fresh[3], fresh[4], fresh[5]
    )
    grad_out = fresh[6]
    gains_float = gains_full.astype(jnp.float32)
    queries, keys_local, values_local = project_heads(
        layer_input, heads_full, heads_shift, cosine, sine_table
    )
    keys_all, values_all = gather_keys(keys_local, values_local)
    gain_two_grad = jnp.sum(grad_out * normed_two, axis=0)
    shift_two_grad = jnp.sum(grad_out, axis=0)
    sum_two_grad = normalize_back(grad_out, normed_two, inv_two, gains_float[1])
    feed_grad = sum_two_grad.astype(jnp.bfloat16)
    rows_all, feed_grads_all = (
        lax.all_gather(hidden_low, "wide", axis=0, tiled=True),
        lax.all_gather(feed_grad, "wide", axis=0, tiled=True),
    )
    gate, upper = gate_up(rows_all)
    gelu_value, gelu_pull = jax.vjp(jax.nn.gelu, gate)
    active_again = (gelu_value * upper).astype(jnp.bfloat16)
    active_grad = jnp.einsum(
        "td,fd->tf", feed_grads_all, reduce_full, preferred_element_type=jnp.float32
    )
    gate_grad = gelu_pull(active_grad * upper)[0]
    gate_up_grad = jnp.concatenate([gate_grad, active_grad * gelu_value], axis=1).astype(
        jnp.bfloat16
    )
    reduce_part = jnp.einsum(
        "tf,td->fd", active_again, feed_grads_all, preferred_element_type=jnp.float32
    )
    reduce_bias_part = jnp.sum(feed_grads_all, axis=0, dtype=jnp.float32)
    expand_part = jnp.einsum(
        "td,tf->df", rows_all, gate_up_grad, preferred_element_type=jnp.float32
    ).reshape(model_width, 2, share)
    expand_bias_part = jnp.sum(gate_up_grad, axis=0, dtype=jnp.float32).reshape(2, share)
    expand_weight_gradient, expand_bias_gradient, reduce_weight_gradient, reduce_bias_gradient = (
        lax.psum_scatter(expand_part, "narrow", scatter_dimension=0, tiled=True),
        lax.psum_scatter(expand_bias_part, "narrow", scatter_dimension=1, tiled=True),
        lax.psum_scatter(reduce_part, "narrow", scatter_dimension=1, tiled=True),
        lax.psum_scatter(reduce_bias_part, "narrow", scatter_dimension=0, tiled=True),
    )
    hidden_grad = residual_scale * sum_two_grad + lax.psum_scatter(
        jnp.einsum("te,de->td", gate_up_grad, expand_mat, preferred_element_type=jnp.float32),
        "wide",
        scatter_dimension=0,
        tiled=True,
    )
    gain_one_grad = jnp.sum(hidden_grad * normed_one, axis=0)
    shift_one_grad = jnp.sum(hidden_grad, axis=0)
    sum_one_grad = normalize_back(hidden_grad, normed_one, inv_one, gains_float[0])
    attended_grad = sum_one_grad.astype(jnp.bfloat16)
    mixed_grad = jnp.einsum(
        "te,de->td", attended_grad, merge_full, preferred_element_type=jnp.float32
    ).astype(jnp.bfloat16)

    def attend_back(items):
        query_grp, key_grp, value_grp, upstream_grp = items
        probs = softmax_rows(query_grp, key_grp, key_mask, score_scale)
        probs_low = probs.astype(jnp.bfloat16)
        probs_grad = jnp.einsum(
            "qgd,kgd->gqk", upstream_grp, value_grp, preferred_element_type=jnp.float32
        )
        scores_grad = (
            probs * (probs_grad - jnp.sum(probs * probs_grad, axis=-1, keepdims=True))
        ).astype(jnp.bfloat16)
        query_grads = (
            jnp.einsum("gqk,kgd->qgd", scores_grad, key_grp, preferred_element_type=jnp.float32)
            * score_scale
        )
        key_grads = (
            jnp.einsum("gqk,qgd->kgd", scores_grad, query_grp, preferred_element_type=jnp.float32)
            * score_scale
        )
        value_grads = jnp.einsum(
            "gqk,qgd->kgd", probs_low, upstream_grp, preferred_element_type=jnp.float32
        )
        return (query_grads, key_grads, value_grads)

    query_groups, key_groups, value_groups = lax.map(
        attend_back,
        (
            grouped(queries, group_size),
            grouped(keys_all.reshape(bucket_len, HEADS, HDIM), group_size),
            grouped(values_all.reshape(bucket_len, HEADS, HDIM), group_size),
            grouped(mixed_grad.reshape(tok_rows, HEADS, HDIM), group_size),
        ),
    )
    key_terms = jnp.concatenate([ungrouped(key_groups), ungrouped(value_groups)], axis=1)
    key_value_grads = lax.psum_scatter(key_terms, "narrow", scatter_dimension=0, tiled=True)
    query_back = rotate_back(
        ungrouped(query_groups).reshape(tok_rows, HEADS, HDIM), cosine, sine_table
    )
    key_back = rotate_back(
        key_value_grads[:, :model_width].reshape(tok_rows, HEADS, HDIM), cosine, sine_table
    )
    value_back = key_value_grads[:, model_width:].reshape(tok_rows, HEADS, HDIM)
    triple_grad = (
        jnp.stack([query_back, key_back, value_back], axis=1)
        .reshape(tok_rows, 3 * model_width)
        .astype(jnp.bfloat16)
    )
    input_gradient = residual_scale * sum_one_grad + jnp.einsum(
        "te,de->td", triple_grad, heads_full, preferred_element_type=jnp.float32
    )
    gains_part = jnp.stack([gain_one_grad, gain_two_grad], axis=0)
    shifts_part = jnp.stack([shift_one_grad, shift_two_grad], axis=0)
    wide_count = lax.axis_size("wide")
    narrow_count = lax.axis_size("narrow")
    rows_input, rows_triple, rows_mixed, rows_attended = (
        lax.all_gather(layer_input, "narrow", axis=0, tiled=True),
        lax.all_gather(triple_grad, "narrow", axis=0, tiled=True),
        lax.all_gather(mixed_low, "narrow", axis=0, tiled=True),
        lax.all_gather(attended_grad, "narrow", axis=0, tiled=True),
    )
    stats_bucket = lax.psum(
        jnp.concatenate([gains_part, shifts_part], axis=0).astype(jnp.bfloat16), "narrow"
    ).astype(jnp.float32)
    heads_cols = jnp.einsum(
        "td,te->de",
        own_blocks(rows_input, 1, wide_count, narrow_count),
        rows_triple,
        preferred_element_type=jnp.float32,
    )
    heads_bias_cols = own_blocks(
        jnp.sum(rows_triple, axis=0, dtype=jnp.float32), 0, wide_count, narrow_count
    )
    merge_cols = jnp.einsum(
        "td,te->de",
        own_blocks(rows_mixed, 1, wide_count, narrow_count),
        rows_attended,
        preferred_element_type=jnp.float32,
    )
    merge_bias_cols = own_blocks(
        jnp.sum(rows_attended, axis=0, dtype=jnp.float32), 0, wide_count, narrow_count
    )
    stats_cols = own_blocks(stats_bucket, 1, wide_count, narrow_count)
    (
        heads_weight_gradient,
        heads_bias_gradient,
        merge_weight_gradient,
        merge_bias_gradient,
        stats_summed,
    ) = (
        lax.psum_scatter(heads_cols, "wide", scatter_dimension=0, tiled=True),
        lax.psum_scatter(heads_bias_cols, "wide", scatter_dimension=0, tiled=True),
        lax.psum_scatter(merge_cols, "wide", scatter_dimension=0, tiled=True),
        lax.psum_scatter(merge_bias_cols, "wide", scatter_dimension=0, tiled=True),
        lax.psum_scatter(stats_cols, "wide", scatter_dimension=1, tiled=True),
    )
    gains_gradient = stats_summed[:2]
    shifts_gradient = stats_summed[2:]
    return (
        layer_output,
        input_gradient,
        heads_weight_gradient,
        heads_bias_gradient,
        merge_weight_gradient,
        merge_bias_gradient,
        gains_gradient,
        shifts_gradient,
        expand_weight_gradient,
        expand_bias_gradient,
        reduce_weight_gradient,
        reduce_bias_gradient,
    )


def solution(mesh):
    return jax.shard_map(
        shards,
        mesh=mesh,
        in_specs=(
            P(("wide", "narrow"), None),
            P(("wide", "narrow"), None),
            P(("wide", "narrow")),
            P(("wide", "narrow"), None),
            P(("wide", "narrow")),
            P(None, ("wide", "narrow")),
            P(None, ("wide", "narrow")),
            P("narrow", None, "wide"),
            P(None, ("wide", "narrow")),
            P("wide", "narrow"),
            P("narrow"),
            P("wide"),
            P("wide", None),
            P(("wide", "narrow"), None),
        ),
        out_specs=(
            P(("wide", "narrow"), None),
            P(("wide", "narrow"), None),
            P(("wide", "narrow"), None),
            P(("wide", "narrow")),
            P(("wide", "narrow"), None),
            P(("wide", "narrow")),
            P(None, ("wide", "narrow")),
            P(None, ("wide", "narrow")),
            P("narrow", None, "wide"),
            P(None, ("wide", "narrow")),
            P("wide", "narrow"),
            P("narrow"),
        ),
        check_vma=False,
    )
```

profile of v0, /device:TPU:8, one launch (start us, length us, event | category | flops | bytes accessed | tf_op | source)
XLA Modules:
  0.0 2695.7 jit_solution(1059415338712641476)
XLA Ops:
  11.7 42.6 %all-reduce.9 = (bf16[6144]{0:T(1024)(128)(2,1)S(1)}, bf16[2048]{0:T(1024)(128)(2,1)S(1)}, bf16[6144]{0:T(1024)(128)(2,1)S(1)}) all-reduce(bf16[6144]{0:T(1024)(128)(2,1)S(1)} %dynamic-update-slice, bf16[2048]{0:T(1024)(128)(2,1)S(1)} %dynamic-update-slice.1, ...), channel_id=1, replica_groups=mesh['wide'=8,'narrow'=4] {'wide','narrow'}, use_global_device_ids=true, to_apply=%add | all-reduce | flops 14336 | bytes 57344
  55.3 111.1 %all-gather.38.cloned.1.call-done = bf16[2048,6144]{1,0:T(8,128)(2,1)} async-done(((bf16[64,6144]{1,0:T(8,128)(2,1)}), bf16[2048,6144]{1,0:T(8,128)(2,1)}) %all-gather.38.cloned.1.call-update) | async-done | bytes 25165840 | tf_op jit(solution)/shard_map/all_gather | solution.py:89
  184.6 137.5 %all-gather.22.cloned.1.call-done = bf16[2048,6144]{1,0:T(8,128)(2,1)} async-done(((bf16[64,6144]{1,0:T(8,128)(2,1)}), bf16[2048,6144]{1,0:T(8,128)(2,1)}) %all-gather.22.cloned.1.call-update) | async-done | bytes 25165840 | tf_op jit(solution)/shard_map/all_gather | solution.py:89
  356.0 83.6 %all-gather = bf16[32,64,2]{1,2,0:T(2,128)(2,1)S(1)} all-gather(bf16[1,64,2]{1,2,0:T(2,128)(2,1)S(1)} %bitcast.284), channel_id=1, replica_groups=mesh['wide'=8,'narrow'=4] {'wide','narrow'}, dimensions={0}, use_global_device_ids=true | all-gather | bytes 8448 | tf_op jit(solution)/shard_map/all_gather | solution.py:93
  439.7 80.9 %all-gather.1 = bf16[32,64,2]{1,2,0:T(2,128)(2,1)S(1)} all-gather(bf16[1,64,2]{1,2,0:T(2,128)(2,1)S(1)} %bitcast.287), channel_id=1, replica_groups=mesh['wide'=8,'narrow'=4] {'wide','narrow'}, dimensions={0}, use_global_device_ids=true | all-gather | bytes 8448 | tf_op jit(solution)/shard_map/all_gather | solution.py:94
  554.3 36.9 %all-gather.28.cloned.1.call-done = bf16[2048,2048]{1,0:T(8,128)(2,1)} async-done(((bf16[64,2048]{1,0:T(8,128)(2,1)}), bf16[2048,2048]{1,0:T(8,128)(2,1)}) %all-gather.28.cloned.1.call-update) | async-done | bytes 8388624 | tf_op jit(solution)/shard_map/all_gather | solution.py:91
  608.8 84.2 %all-gather.32.cloned.1.call-done = bf16[2048,2,688]{0,2,1:T(8,128)(2,1)} async-done(((bf16[512,2,688]{0,2,1:T(8,128)(2,1)}), bf16[2048,2,688]{0,2,1:T(8,128)(2,1)}) %all-gather.32.cloned.1.call-update) | async-done | bytes 5636112 | tf_op jit(solution)/shard_map/all_gather | solution.py:209
  693.0 58.0 %all-gather.30.cloned.1.call-done = bf16[2048,2048]{1,0:T(8,128)(2,1)} async-done(((bf16[256,2048]{1,0:T(8,128)(2,1)}), bf16[2048,2048]{1,0:T(8,128)(2,1)}) %all-gather.30.cloned.1.call-update) | async-done | bytes 8388624 | tf_op jit(solution)/shard_map/all_gather | solution.py:222
  833.6 66.3 %all-gather.4 = bf16[32,64,2]{1,2,0:T(2,128)(2,1)S(1)} all-gather(bf16[1,64,2]{1,2,0:T(2,128)(2,1)S(1)} %bitcast.285), channel_id=1, replica_groups=mesh['wide'=8,'narrow'=4] {'wide','narrow'}, dimensions={0}, use_global_device_ids=true | all-gather | bytes 8448 | tf_op jit(solution)/shard_map/all_gather | solution.py:93
  900.1 38.2 %reduce-scatter.12.cloned.1.call-done = f32[256,2048]{1,0:T(8,128)} async-done(((f32[2048,2048]{1,0:T(8,128)}), f32[256,2048]{1,0:T(8,128)}) %reduce-scatter.12.cloned.1.call-update) | async-done | bytes 2097168 | tf_op jit(solution)/shard_map/reduce_scatter | solution.py:224
  945.6 54.5 %all-gather.36.cloned.1.call-done = bf16[2048,2048]{1,0:T(8,128)(2,1)} async-done(((bf16[256,2048]{1,0:T(8,128)(2,1)}), bf16[2048,2048]{1,0:T(8,128)(2,1)}) %all-gather.36.cloned.1.call-update) | async-done | bytes 8388624 | tf_op jit(solution)/shard_map/all_gather | solution.py:253
  1048.0 105.1 %reduce-scatter.14.cloned.1.call-done = f32[256,2048]{1,0:T(8,128)} async-done(((f32[2048,2048]{1,0:T(8,128)}), f32[256,2048]{1,0:T(8,128)}) %reduce-scatter.14.cloned.1.call-update) | async-done | bytes 2097168 | tf_op jit(solution)/shard_map/reduce_scatter | solution.py:279
  1158.7 74.6 %all-gather.42.cloned.1.call-done = bf16[2048,2048]{1,0:T(8,128)(2,1)} async-done(((bf16[64,2048]{1,0:T(8,128)(2,1)}), bf16[2048,2048]{1,0:T(8,128)(2,1)}) %all-gather.42.cloned.1.call-update) | async-done | bytes 8388624 | tf_op jit(solution)/shard_map/all_gather | solution.py:91
  1240.8 70.8 %all-gather.40.cloned.1.call-done = bf16[1024,2048]{0,1:T(8,128)(2,1)} async-done(((bf16[256,2048]{0,1:T(8,128)(2,1)}), bf16[1024,2048]{0,1:T(8,128)(2,1)}) %all-gather.40.cloned.1.call-update) | async-done | bytes 4194320 | tf_op jit(solution)/shard_map/all_gather | solution.py:124
  1311.6 80.2 %all-gather.44.cloned.1.call-done = bf16[1024,2048]{0,1:T(8,128)(2,1)} async-done(((bf16[256,2048]{0,1:T(8,128)(2,1)}), bf16[1024,2048]{0,1:T(8,128)(2,1)}) %all-gather.44.cloned.1.call-update) | async-done | bytes 4194320 | tf_op jit(solution)/shard_map/all_gather | solution.py:125
  1391.8 55.4 %while.29 = (s32[]{:T(128)}, f32[4,256,4,128]{1,3,2,0:T(8,128)}, f32[4,1024,4,128]{1,3,2,0:T(8,128)}, f32[4,1024,4,128]{1,3,2,0:T(8,128)}, bf16[4,1024,4,128]{1,...) while((s32[]{:T(128)}, f32[4,256,4,128]{1,3,2,0:T(8,128)}, ...), condition=%wide.region_18.19_spmd.clone.clone, body=%wide.region_14.18_spmd.clone.sunk.clone | while | flops 1359609856 | bytes 49324156 | solution.py:316
  1461.5 275.8 %reduce-scatter.16.cloned.1.call-done = f32[256,4096]{0,1:T(8,128)} async-done(((f32[1024,4096]{0,1:T(8,128)}), f32[256,4096]{0,1:T(8,128)}) %reduce-scatter.16.cloned.1.call-update) | async-done | bytes 4194320 | tf_op jit(solution)/shard_map/reduce_scatter | solution.py:326
  1823.4 79.0 %all-gather.52.cloned.1.call-done = bf16[1024,2048]{1,0:T(8,128)(2,1)} async-done(((bf16[256,2048]{1,0:T(8,128)(2,1)}), bf16[1024,2048]{1,0:T(8,128)(2,1)}) %all-gather.52.cloned.1.call-update) | async-done | bytes 4194320 | tf_op jit(solution)/shard_map/all_gather | solution.py:350
  1909.4 73.4 %all-gather.46.cloned.1.call-done = bf16[1024,2048]{0,1:T(8,128)(2,1)} async-done(((bf16[256,2048]{0,1:T(8,128)(2,1)}), bf16[1024,2048]{0,1:T(8,128)(2,1)}) %all-gather.46.cloned.1.call-update) | async-done | bytes 4194320 | tf_op jit(solution)/shard_map/all_gather | solution.py:347
  1985.0 215.3 %all-gather.48.cloned.1.call-done = bf16[1024,6144]{0,1:T(8,128)(2,1)} async-done(((bf16[256,6144]{0,1:T(8,128)(2,1)}), bf16[1024,6144]{0,1:T(8,128)(2,1)}) %all-gather.48.cloned.1.call-update) | async-done | bytes 12582928 | tf_op jit(solution)/shard_map/all_gather | solution.py:348
  2293.8 47.5 %reduce-scatter.24.cloned.1.call-done = f32[688,512]{1,0:T(8,128)} async-done(((f32[688,2048]{1,0:T(8,128)}), f32[688,512]{1,0:T(8,128)}) %reduce-scatter.24.cloned.1.call-update) | async-done | bytes 1409040 | tf_op jit(solution)/shard_map/reduce_scatter | solution.py:276
  2341.3 194.2 %reduce-scatter.22.cloned.1.call-done = f32[512,2,688]{0,2,1:T(8,128)} async-done(((f32[2048,2,688]{0,2,1:T(8,128)}), f32[512,2,688]{0,2,1:T(8,128)}) %reduce-scatter.22.cloned.1.call-update) | async-done | bytes 2818064 | tf_op jit(solution)/shard_map/reduce_scatter | solution.py:274
  2535.5 56.3 %reduce-scatter.20.cloned.1.call-done = f32[64,2048]{1,0:T(8,128)} async-done(((f32[512,2048]{1,0:T(8,128)}), f32[64,2048]{1,0:T(8,128)}) %reduce-scatter.20.cloned.1.call-update) | async-done | bytes 524304 | tf_op jit(solution)/shard_map/reduce_scatter | solution.py:383
  2591.8 96.8 %reduce-scatter.18.cloned.1.call-done = f32[64,6144]{1,0:T(8,128)} async-done(((f32[512,6144]{1,0:T(8,128)}), f32[64,6144]{1,0:T(8,128)}) %reduce-scatter.18.cloned.1.call-update) | async-done | bytes 1572880 | tf_op jit(solution)/shard_map/reduce_scatter | solution.py:381
  (294 shorter events, 539.0 us)
Async XLA Ops:
  7.2 159.2 %all-gather.38.cloned.1.call-start = ((), (), s32[]{:S(2)}) async-start(), calls=%async_computation.18 | async-start | bytes 25952256 | tf_op jit(solution)/shard_map/all_gather | solution.py:89
  10.2 312.0 %all-gather.22.cloned.1.call-start = ((), (), s32[]{:S(2)}) async-start(), calls=%async_computation.8 | async-start | bytes 25952256 | tf_op jit(solution)/shard_map/all_gather | solution.py:89
  10.9 517.2 %all-gather.26.cloned.1.call-start = ((), (), s32[]{:S(2)}) async-start(), calls=%async_computation.10 | async-start | bytes 5242880 | tf_op jit(solution)/shard_map/all_gather | solution.py:124
  350.7 177.5 %all-gather.24.cloned.1.call-start = ((), (), s32[]{:S(2)}) async-start(), calls=%async_computation.9 | async-start | bytes 5242880 | tf_op jit(solution)/shard_map/all_gather | solution.py:125
  354.1 237.1 %all-gather.28.cloned.1.call-start = ((), (), s32[]{:S(2)}) async-start(), calls=%async_computation.11 | async-start | bytes 8650752 | tf_op jit(solution)/shard_map/all_gather | solution.py:91
  354.7 338.3 %all-gather.32.cloned.1.call-start = ((), (), s32[]{:S(2)}) async-start(), calls=%async_computation.13 | async-start | bytes 7045120 | tf_op jit(solution)/shard_map/all_gather | solution.py:209
  355.3 395.7 %all-gather.30.cloned.1.call-start = ((), (), s32[]{:S(2)}) async-start(), calls=%async_computation.12 | async-start | bytes 9437184 | tf_op jit(solution)/shard_map/all_gather | solution.py:222
  599.2 209.4 %all-gather.34.cloned.1.call-start = ((), (), s32[]{:S(2)}) async-start(), calls=%async_computation.14 | async-start | bytes 3522560 | tf_op jit(solution)/shard_map/all_gather | solution.py:211
  600.0 338.3 %reduce-scatter.12.cloned.1.call-start = ((), (), s32[]{:S(2)}) async-start(), calls=%async_computation.15 | async-start | bytes 18874368 | tf_op jit(solution)/shard_map/reduce_scatter | solution.py:224
  821.4 178.7 %all-gather.36.cloned.1.call-start = ((), (), s32[]{:S(2)}) async-start(), calls=%async_computation.16 | async-start | bytes 9437184 | tf_op jit(solution)/shard_map/all_gather | solution.py:253
  945.5 207.5 %reduce-scatter.14.cloned.1.call-start = ((), (), s32[]{:S(2)}) async-start(), calls=%async_computation.17 | async-start | bytes 18874368 | tf_op jit(solution)/shard_map/reduce_scatter | solution.py:279
  1037.0 196.3 %all-gather.42.cloned.1.call-start = ((), (), s32[]{:S(2)}) async-start(), calls=%async_computation.20 | async-start | bytes 8650752 | tf_op jit(solution)/shard_map/all_gather | solution.py:91
  1037.6 274.1 %all-gather.40.cloned.1.call-start = ((), (), s32[]{:S(2)}) async-start(), calls=%async_computation.19 | async-start | bytes 5242880 | tf_op jit(solution)/shard_map/all_gather | solution.py:124
  1039.9 351.9 %all-gather.44.cloned.1.call-start = ((), (), s32[]{:S(2)}) async-start(), calls=%async_computation.21 | async-start | bytes 5242880 | tf_op jit(solution)/shard_map/all_gather | solution.py:125
  1042.7 694.6 %reduce-scatter.16.cloned.1.call-start = ((), (), s32[]{:S(2)}) async-start(), calls=%async_computation.22 | async-start | bytes 20971520 | tf_op jit(solution)/shard_map/reduce_scatter | solution.py:326
  1458.8 362.3 %all-gather.50.cloned.1.call-start = ((), (), s32[]{:S(2)}) async-start(), calls=%async_computation.26 | async-start | bytes 5242880 | tf_op jit(solution)/shard_map/all_gather | solution.py:349
  1459.4 443.0 %all-gather.52.cloned.1.call-start = ((), (), s32[]{:S(2)}) async-start(), calls=%async_computation.27 | async-start | bytes 5242880 | tf_op jit(solution)/shard_map/all_gather | solution.py:350
  1460.0 522.7 %all-gather.46.cloned.1.call-start = ((), (), s32[]{:S(2)}) async-start(), calls=%async_computation.23 | async-start | bytes 5242880 | tf_op jit(solution)/shard_map/all_gather | solution.py:347
  1461.4 738.9 %all-gather.48.cloned.1.call-start = ((), (), s32[]{:S(2)}) async-start(), calls=%async_computation.24 | async-start | bytes 15728640 | tf_op jit(solution)/shard_map/all_gather | solution.py:348
  1743.2 500.6 %reduce-scatter.26.cloned.1.call-start = ((), (), s32[]{:S(2)}) async-start(), calls=%async_computation.31 | async-start | bytes 294912
  1769.0 572.3 %reduce-scatter.24.cloned.1.call-start = ((), (), s32[]{:S(2)}) async-start(), calls=%async_computation.30 | async-start | bytes 7045120 | tf_op jit(solution)/shard_map/reduce_scatter | solution.py:276
  1779.2 756.3 %reduce-scatter.22.cloned.1.call-start = ((), (), s32[]{:S(2)}) async-start(), calls=%async_computation.29 | async-start | bytes 14090240 | tf_op jit(solution)/shard_map/reduce_scatter | solution.py:274
  1798.8 793.0 %reduce-scatter.20.cloned.1.call-start = ((), (), s32[]{:S(2)}) async-start(), calls=%async_computation.28 | async-start | bytes 4718592 | tf_op jit(solution)/shard_map/reduce_scatter | solution.py:383
  1909.3 779.3 %reduce-scatter.18.cloned.1.call-start = ((), (), s32[]{:S(2)}) async-start(), calls=%async_computation.25 | async-start | bytes 14155776 | tf_op jit(solution)/shard_map/reduce_scatter | solution.py:381
  (33 other events, 1995.6 us)
Sparse Core Ops, SparseCore 0:
  10.9 155.4 all-gather.37
  169.3 152.8 all-gather.21
  350.8 77.8 all-gather.25
  430.7 79.0 all-gather.23
  512.5 78.6 all-gather.27
  592.7 100.2 all-gather.31
  695.4 55.5 all-gather.29
  752.6 56.0 all-gather.33
  821.5 116.7 reduce-scatter.11
  945.7 54.3 all-gather.35
  1037.1 115.9 reduce-scatter.13
  1155.9 77.3 all-gather.41
  1235.4 76.1 all-gather.39
  1313.0 78.7 all-gather.43
  1459.0 278.2 reduce-scatter.15
  1738.8 82.3 all-gather.49
  1823.2 79.2 all-gather.51
  1904.0 78.7 all-gather.45
  1984.4 215.8 all-gather.47
  2203.5 34.7 reduce-scatter.25
  2241.2 100.1 reduce-scatter.23
  2344.3 191.2 reduce-scatter.21
  2539.5 52.3 reduce-scatter.19
  2596.2 92.4 reduce-scatter.17
where the time goes:
time: 2710 us; the launch traced here: 2700 us
  waiting for transfers between devices  1950 us (72%)
  blocking collectives  358 us (13%)
  matrix products  221 us (8%)
  other arithmetic  89.6 us (3%)
  local copies, waits for them, and re-layouts  55.6 us (2%)
    reduce_scatter x1, waiting for transfers between devices, shards(): lax.psum_scatter(key_terms, 'narrow', scatter_dimension=0, tiled=True)  276 us
    all_gather x2, waiting for transfers between devices, collect_params(): lax.all_gather(heads_weight, ('wide', 'narrow'), axis=0, tiled=True)  249 us
    all_gather x1, waiting for transfers between devices, shards(): lax.all_gather(triple_grad, 'narrow', axis=0, tiled=True)  215 us
    reduce_scatter x1, waiting for transfers between devices, shards(): lax.psum_scatter(expand_part, 'narrow', scatter_dimension=0, tiled=True)  194 us
    all_gather x2, blocking collectives, collect_params(): lax.all_gather(norm_gains, ('wide', 'narrow'), axis=1, tiled=True)  150 us
    all_gather x2, waiting for transfers between devices, collect_params(): lax.all_gather(merge_weight, ('wide', 'narrow'), axis=0, tiled=True)  111 us
    reduce_scatter x1, waiting for transfers between devices, shards(): lax.psum_scatter(jnp.einsum('te,de->td', gate_up_grad, expand_mat, prefer...  105 us
    reduce_scatter x1, waiting for transfers between devices, shards(): lax.psum_scatter(heads_cols, 'wide', scatter_dimension=0, tiled=True)  96.8 us
  transfers between devices with their start and end apart: 24, of which 21 were waited for; matrix products, arithmetic and copies ran while one was open for 7% of the time, Pallas kernels for 0%

commit v1 on v0

v1 whole, which is shorter than its diff:
```python
import jax
import jax.numpy as jnp
from jax import lax
from jax.sharding import PartitionSpec as P

HEADS = 16
HDIM = 128


residual_scale = 48.0**0.5
norm_eps = 1e-05
masked_value = -1e30
both_axes = ("wide", "narrow")


def layout(positions, joined_flag, prefix_pair, bucket_len):
    halfway = bucket_len // 2
    second_seq = (positions >= halfway).astype(jnp.int32) * (1 - joined_flag)
    local_pos = positions - second_seq * halfway
    prefix_len = jnp.where(
        joined_flag == 1,
        prefix_pair[0] + prefix_pair[1],
        jnp.where(second_seq == 1, prefix_pair[1], prefix_pair[0]),
    )
    return (second_seq, local_pos, prefix_len)


def visible(query_pos, key_pos, joined_flag, prefix_pair, bucket_len):
    query_seq, query_local, query_prefix = layout(query_pos, joined_flag, prefix_pair, bucket_len)
    key_seq, key_local, key_prefix = layout(key_pos, joined_flag, prefix_pair, bucket_len)
    same_seq = query_seq[:, None] == key_seq[None, :]
    return same_seq & (
        (key_local[None, :] < key_prefix[None, :]) | (key_local[None, :] <= query_local[:, None])
    )


def rotary_tables(local_pos, head_size):
    halfway = head_size // 2
    inverse = 10000.0 ** (-(2.0 * jnp.arange(halfway).astype(jnp.float32)) / head_size)
    angles = local_pos.astype(jnp.float32)[:, None] * inverse[None, :]
    return (jnp.cos(angles)[:, None, :], jnp.sin(angles)[:, None, :])


def rotate(vectors, cosine, sine_table):
    halfway = vectors.shape[-1] // 2
    first_part, second_part = (vectors[..., :halfway], vectors[..., halfway:])
    return jnp.concatenate(
        [
            first_part * cosine - second_part * sine_table,
            second_part * cosine + first_part * sine_table,
        ],
        axis=-1,
    )


def normalize(values, gain, shift):
    centre = jnp.mean(values, axis=-1, keepdims=True)
    centred = values - centre
    variance = jnp.mean(centred * centred, axis=-1, keepdims=True)
    inv_std = lax.rsqrt(variance + norm_eps)
    normed = centred * inv_std
    return (normed * gain + shift, normed, inv_std)


def normalize_back(upstream, normed, inv_std, gain):
    scaled = upstream * gain
    return inv_std * (
        scaled
        - jnp.mean(scaled, axis=-1, keepdims=True)
        - normed * jnp.mean(scaled * normed, axis=-1, keepdims=True)
    )


def dot(left, right, dims):
    return lax.dot_general(left, right, (dims, ((), ())), preferred_element_type=jnp.float32)


def low(values):
    return values.astype(jnp.bfloat16)


def gather_small(heads_bias, merge_bias, norm_gains, norm_shifts, expand_bias, reduce_bias):
    parts = (heads_bias, merge_bias, norm_gains, norm_shifts, expand_bias, reduce_bias)
    packed = jnp.concatenate([part.reshape(1, -1) for part in parts], axis=1)
    wide_count = lax.axis_size("wide")
    narrow_count = lax.axis_size("narrow")
    count = wide_count * narrow_count
    everyone = lax.all_gather(packed, both_axes, axis=0, tiled=True).astype(jnp.float32)
    pieces = []
    start = 0
    for part in parts:
        pieces.append(everyone[:, start : start + part.size])
        start += part.size

    def pairs(piece):
        return piece.reshape(piece.shape[0], 2, -1).transpose(1, 0, 2).reshape(2, -1)

    own_expand = lax.dynamic_index_in_dim(
        pieces[4].reshape(wide_count, narrow_count, -1), lax.axis_index("wide"), 0, keepdims=False
    )
    reduce_shift = pieces[5].reshape(wide_count, narrow_count, -1)[0].reshape(-1)
    return (
        pieces[0].reshape(-1),
        pieces[1].reshape(-1),
        pairs(pieces[2]),
        pairs(pieces[3]),
        pairs(own_expand),
        reduce_shift,
    )


def shards(
    layer_input,
    heads_weight,
    heads_bias,
    merge_weight,
    merge_bias,
    norm_gains,
    norm_shifts,
    expand_weight,
    expand_bias,
    reduce_weight,
    reduce_bias,
    joined,
    prefix,
    cotangent,
):
    tok_rows, model_width = layer_input.shape
    wide_count = lax.axis_size("wide")
    narrow_count = lax.axis_size("narrow")
    count = wide_count * narrow_count
    bucket_len = tok_rows * narrow_count
    own_heads = HEADS // narrow_count
    own_cols = own_heads * HDIM
    share = expand_weight.shape[2]
    score_scale = HDIM ** (-0.5)
    joined_flag = joined[0]
    prefix_pair = prefix[0]
    narrow_index = lax.axis_index("narrow")
    positions = jnp.arange(bucket_len, dtype=jnp.int32)
    second_seq, local_pos, prefix_len = layout(positions, joined_flag, prefix_pair, bucket_len)
    cosine, sine_table = rotary_tables(local_pos, HDIM)
    key_mask = visible(positions, positions, joined_flag, prefix_pair, bucket_len)

    rows_input = lax.all_gather(layer_input, "narrow", axis=0, tiled=True)
    swapped = lax.all_to_all(
        heads_weight.reshape(-1, 3, narrow_count, own_cols).transpose(2, 0, 1, 3),
        "narrow",
        split_axis=0,
        concat_axis=0,
        tiled=True,
    ).reshape(-1, 3 * own_cols)
    heads_mat = lax.all_gather(swapped, "wide", axis=0, tiled=True)
    heads_shift, merge_shift, gains, shifts, expand_shift, reduce_shift = gather_small(
        heads_bias, merge_bias, norm_gains, norm_shifts, expand_bias, reduce_bias
    )
    merge_full = lax.all_gather(merge_weight, both_axes, axis=0, tiled=True)
    own_shift = lax.dynamic_index_in_dim(
        heads_shift.reshape(3, narrow_count, own_cols), narrow_index, 1, keepdims=False
    ).reshape(-1)
    triple = dot(rows_input, heads_mat, ((1,), (0,))) + own_shift
    triple = triple.reshape(bucket_len, 3, own_heads, HDIM)
    queries = low(rotate(triple[:, 0], cosine, sine_table))
    keys = low(rotate(triple[:, 1], cosine, sine_table))
    values = low(triple[:, 2])
    scores = (
        jnp.einsum("qgd,kgd->gqk", queries, keys, preferred_element_type=jnp.float32) * score_scale
    )
    scores = jnp.where(key_mask[None], scores, masked_value)
    expo = jnp.exp(scores - jnp.max(scores, axis=-1, keepdims=True))
    probs_low = low(expo / jnp.sum(expo, axis=-1, keepdims=True))
    mixed_own = low(
        jnp.einsum("gqk,kgd->qgd", probs_low, values, preferred_element_type=jnp.float32)
    ).reshape(bucket_len, own_cols)
    mixed = lax.all_to_all(mixed_own, "narrow", split_axis=0, concat_axis=1, tiled=True)
    attended = dot(mixed, merge_full, ((1,), (0,))) + merge_shift
    hidden, normed_one, inv_one = normalize(
        residual_scale * layer_input.astype(jnp.float32) + attended, gains[0], shifts[0]
    )
    hidden_low = low(hidden)

    expand_full = lax.all_gather(
        expand_weight.transpose(1, 2, 0), "narrow", axis=2, tiled=True
    ).reshape(2 * share, model_width)
    reduce_full = lax.all_gather(reduce_weight, "narrow", axis=1, tiled=True)
    rows_all = lax.all_gather(hidden_low, "wide", axis=0, tiled=True)
    both = dot(rows_all, expand_full, ((1,), (1,))) + expand_shift.reshape(-1)
    gate, upper = both[:, :share], both[:, share:]
    gelu_value, gelu_pull = jax.vjp(jax.nn.gelu, gate)
    active = low(gelu_value * upper)
    gate_slope = low(gelu_pull(upper)[0])
    gelu_low = low(gelu_value)
    feed = (
        lax.psum_scatter(
            low(dot(active, reduce_full, ((1,), (0,)))), "wide", scatter_dimension=0, tiled=True
        ).astype(jnp.float32)
        + reduce_shift
    )
    output_float, normed_two, inv_two = normalize(
        residual_scale * hidden + feed, gains[1], shifts[1]
    )
    layer_output = low(output_float)

    grad_out = cotangent.astype(jnp.float32)
    gain_two_grad = jnp.sum(grad_out * normed_two, axis=0)
    shift_two_grad = jnp.sum(grad_out, axis=0)
    sum_two_grad = normalize_back(grad_out, normed_two, inv_two, gains[1])
    feed_grad = low(sum_two_grad)
    feed_grads_all = lax.all_gather(feed_grad, "wide", axis=0, tiled=True)
    active_grad = dot(feed_grads_all, reduce_full, ((1,), (1,)))
    gate_up_grad = low(
        jnp.concatenate([active_grad * gate_slope, active_grad * gelu_low], axis=1)
    )
    hidden_part = lax.psum_scatter(
        low(dot(gate_up_grad, expand_full, ((1,), (0,)))),
        "wide",
        scatter_dimension=0,
        tiled=True,
    )
    reduce_part = low(dot(active, feed_grads_all, ((0,), (0,))))
    expand_part = low(dot(gate_up_grad, rows_all, ((0,), (0,)))).reshape(2, share, model_width)
    reduce_weight_gradient = lax.psum_scatter(
        reduce_part, "narrow", scatter_dimension=1, tiled=True
    ).astype(jnp.float32)
    expand_weight_gradient = (
        lax.psum_scatter(expand_part, "narrow", scatter_dimension=2, tiled=True)
        .astype(jnp.float32)
        .transpose(2, 0, 1)
    )
    hidden_grad = residual_scale * sum_two_grad + hidden_part.astype(jnp.float32)
    gain_one_grad = jnp.sum(hidden_grad * normed_one, axis=0)
    shift_one_grad = jnp.sum(hidden_grad, axis=0)
    sum_one_grad = normalize_back(hidden_grad, normed_one, inv_one, gains[0])
    attended_grad = low(sum_one_grad)
    mixed_grad = low(dot(attended_grad, merge_full, ((1,), (1,))))
    upstream = lax.all_to_all(
        mixed_grad, "narrow", split_axis=1, concat_axis=0, tiled=True
    ).reshape(bucket_len, own_heads, HDIM)
    merge_part = low(dot(mixed, attended_grad, ((0,), (0,))))
    merge_weight_gradient = lax.psum_scatter(
        merge_part, both_axes, scatter_dimension=0, tiled=True
    ).astype(jnp.float32)
    probs_grad = jnp.einsum("qgd,kgd->gqk", upstream, values, preferred_element_type=jnp.float32)
    probs = probs_low.astype(jnp.float32)
    scores_grad = low(probs * (probs_grad - jnp.sum(probs * probs_grad, axis=-1, keepdims=True)))
    query_grads = (
        jnp.einsum("gqk,kgd->qgd", scores_grad, keys, preferred_element_type=jnp.float32)
        * score_scale
    )
    key_grads = (
        jnp.einsum("gqk,qgd->kgd", scores_grad, queries, preferred_element_type=jnp.float32)
        * score_scale
    )
    value_grads = jnp.einsum("gqk,qgd->kgd", probs_low, upstream, preferred_element_type=jnp.float32)
    triple_grad = low(
        jnp.stack(
            [
                rotate(query_grads, cosine, -sine_table),
                rotate(key_grads, cosine, -sine_table),
                value_grads,
            ],
            axis=1,
        )
    ).reshape(bucket_len, 3 * own_cols)
    input_part = lax.psum_scatter(
        low(dot(triple_grad, heads_mat, ((1,), (1,)))), "narrow", scatter_dimension=0, tiled=True
    )
    input_gradient = residual_scale * sum_one_grad + input_part.astype(jnp.float32)
    heads_part = lax.psum_scatter(
        low(dot(rows_input, triple_grad, ((0,), (0,)))), "wide", scatter_dimension=0, tiled=True
    )
    heads_weight_gradient = (
        lax.all_to_all(
            heads_part.reshape(narrow_count, -1, 3 * own_cols),
            "narrow",
            split_axis=0,
            concat_axis=0,
            tiled=True,
        )
        .reshape(narrow_count, -1, 3, own_cols)
        .transpose(1, 2, 0, 3)
        .reshape(heads_weight.shape)
        .astype(jnp.float32)
    )

    mine_narrow = (jnp.arange(narrow_count) == narrow_index).astype(jnp.float32)
    mine_wide = (jnp.arange(wide_count) == lax.axis_index("wide")).astype(jnp.float32)
    heads_sums = jnp.sum(triple_grad, axis=0, dtype=jnp.float32).reshape(3, 1, own_cols)
    heads_sums = (heads_sums * mine_narrow[None, :, None]).reshape(count, -1)
    merge_sums = jnp.sum(attended_grad, axis=0, dtype=jnp.float32).reshape(count, -1)
    norm_sums = (
        jnp.stack([gain_one_grad, gain_two_grad, shift_one_grad, shift_two_grad])
        .reshape(4, count, -1)
        .transpose(1, 0, 2)
        .reshape(count, -1)
    )
    expand_sums = jnp.sum(gate_up_grad, axis=0, dtype=jnp.float32)
    expand_sums = (
        expand_sums.reshape(2, narrow_count, -1).transpose(1, 0, 2).reshape(1, narrow_count, -1)
        * mine_wide[:, None, None]
    ).reshape(count, -1)
    reduce_sums = jnp.sum(feed_grad, axis=0, dtype=jnp.float32).reshape(1, narrow_count, -1)
    reduce_sums = jnp.broadcast_to(
        reduce_sums, (wide_count, narrow_count, reduce_sums.shape[2])
    ).reshape(count, -1)
    pieces = (heads_sums, merge_sums, norm_sums, expand_sums, reduce_sums)
    summed = lax.psum_scatter(
        jnp.concatenate(pieces, axis=1), both_axes, scatter_dimension=0, tiled=True
    )[0]
    ends = []
    start = 0
    for piece in pieces:
        ends.append(summed[start : start + piece.shape[1]])
        start += piece.shape[1]
    norm_ends = ends[2].reshape(4, -1)
    return (
        layer_output,
        input_gradient,
        heads_weight_gradient,
        ends[0],
        merge_weight_gradient,
        ends[1],
        norm_ends[:2],
        norm_ends[2:],
        expand_weight_gradient,
        ends[3].reshape(2, -1),
        reduce_weight_gradient,
        ends[4],
    )


def solution(mesh):
    return jax.shard_map(
        shards,
        mesh=mesh,
        in_specs=(
            P(("wide", "narrow"), None),
            P(("wide", "narrow"), None),
            P(("wide", "narrow")),
            P(("wide", "narrow"), None),
            P(("wide", "narrow")),
            P(None, ("wide", "narrow")),
            P(None, ("wide", "narrow")),
            P("narrow", None, "wide"),
            P(None, ("wide", "narrow")),
            P("wide", "narrow"),
            P("narrow"),
            P("wide"),
            P("wide", None),
            P(("wide", "narrow"), None),
        ),
        out_specs=(
            P(("wide", "narrow"), None),
            P(("wide", "narrow"), None),
            P(("wide", "narrow"), None),
            P(("wide", "narrow")),
            P(("wide", "narrow"), None),
            P(("wide", "narrow")),
            P(None, ("wide", "narrow")),
            P(None, ("wide", "narrow")),
            P("narrow", None, "wide"),
            P(None, ("wide", "narrow")),
            P("wide", "narrow"),
            P("narrow"),
        ),
        check_vma=False,
    )
```

time: 2710 us -> 1460 us (0.54)
  waiting for transfers between devices: 1950 us -> 978 us
  blocking collectives: 358 us -> 140 us
  matrix products: 221 us -> 177 us
    all_gather x16 -> x7, waiting for transfers between devices: 1130 us -> 256 us  [the longest x1 91.3 us: shards(): lax.all_gather(expand_weight.transpose(1, 2, 0), 'narrow', axis=2, tiled=...]
    reduce_scatter x6, waiting for transfers between devices: 766 us -> 494 us  [the longest x1 176 us: shards(): lax.psum_scatter(merge_part, both_axes, scatter_dimension=0, tiled=True)]
    all_gather x5 -> x1, blocking collectives: 251 us -> 69.9 us  [gather_small(): lax.all_gather(packed, both_axes, axis=0, tiled=True).astype(jnp.float32)]
    unnamed x25 -> x16, waiting for transfers between devices: 4.31 us -> 131 us
    unnamed x3 -> x0, blocking collectives: 82.7 us -> none
    all_to_all x0 -> x2, blocking collectives: none -> 70.1 us  [the longest x1 41.1 us: shards(): lax.all_to_all(heads_weight.reshape(-1, 3, narrow_count, own_cols).transp...]
    dot_general x41 -> x17, matrix products: 221 us -> 165 us  [the longest x12 144 us: dot(): lax.dot_general(left, right, (dims, ((), ())), preferred_element_type=jnp...]
    all_to_all x0 -> x2, waiting for transfers between devices: none -> 30.7 us  [the longest x1 30.7 us: shards(): lax.all_to_all(mixed_own, 'narrow', split_axis=0, concat_axis=1, tiled=True)]
  transfers between devices with their start and end apart: 24 -> 17, of which waited for: 21 -> 14; matrix products, arithmetic and copies ran while one was open for 7% -> 12% of each run, Pallas kernels for 0% -> 0%
where the time goes in v1:
time: 1460 us; the launch traced here: 1450 us
  waiting for transfers between devices  978 us (67%)
  matrix products  177 us (12%)
  blocking collectives  140 us (10%)
  other arithmetic  65.8 us (5%)
  local copies, waits for them, and re-layouts  62.3 us (4%)
  between operations  16.8 us (1%)
    reduce_scatter x1, waiting for transfers between devices, shards(): lax.psum_scatter(merge_part, both_axes, scatter_dimension=0, tiled=True)  176 us
    dot_general x12, matrix products, dot(): lax.dot_general(left, right, (dims, ((), ())), preferred_element_type=jnp...  144 us
    unnamed x16, waiting for transfers between devices  131 us
    reduce_scatter x1, waiting for transfers between devices, shards(): lax.psum_scatter(expand_part, 'narrow', scatter_dimension=2, tiled=True)  98.1 us
    all_gather x1, waiting for transfers between devices, shards(): lax.all_gather(expand_weight.transpose(1, 2, 0), 'narrow', axis=2, tiled=...  91.3 us
    reduce_scatter x1, waiting for transfers between devices, shards(): lax.psum_scatter(low(dot(active, reduce_full, ((1,), (0,)))), 'wide', sca...  71.9 us
    reduce_scatter x1, waiting for transfers between devices, shards(): lax.psum_scatter(low(dot(gate_up_grad, expand_full, ((1,), (0,)))), 'wide...  71.2 us
    reduce_scatter x1, waiting for transfers between devices, shards(): lax.psum_scatter(low(dot(triple_grad, heads_mat, ((1,), (1,)))), 'narrow'...  70.5 us
  transfers between devices with their start and end apart: 17, of which 14 were waited for; matrix products, arithmetic and copies ran while one was open for 12% of the time, Pallas kernels for 0%

profile of v1, /device:TPU:8, one launch (start us, length us, event | category | flops | bytes accessed | tf_op | source)
XLA Modules:
  0.0 1451.0 jit_solution(11181204851984789237)
XLA Ops:
  10.4 41.1 %all_to_all.45 = bf16[4,64,3,512]{3,1,2,0:T(8,128)(2,1)S(1)} all-to-all(bf16[4,64,3,512]{3,1,2,0:T(8,128)(2,1)S(1)} %copy.130), channel_id=1, replica_groups=mesh['wide'=8,'narrow'=4] {'narrow'}, dimensions={0} | all-to-all | bytes 1572864 | tf_op jit(solution)/shard_map/all_to_all | solution.py:146
  55.8 69.9 %all-gather = bf16[32,1,1368]{2,1,0:T(2,128)(2,1)S(1)} all-gather(bf16[1,1,1368]{2,1,0:T(2,128)(2,1)S(1)} %bitcast.128), channel_id=1, replica_groups=mesh['wide'=8,'narrow'=4] {'wide','narrow'}, dimensions={0}, use_global_device_ids=true | all-gather | bytes 90288 | tf_op jit(solution)/shard_map/all_gather | solution.py:88
  134.3 18.7 %all-gather.11.cloned.1.call-done = bf16[2048,1536]{1,0:T(8,128)(2,1)} async-done(((bf16[256,1536]{1,0:T(8,128)(2,1)}), bf16[2048,1536]{1,0:T(8,128)(2,1)}) %all-gather.11.cloned.1.call-update) | async-done | bytes 6291472 | tf_op jit(solution)/shard_map/all_gather | solution.py:153
  153.0 11.8 convolution_add_fusion.1
  186.0 12.6 fusion.47
  218.9 30.7 %all-to-all-done.1 = bf16[4,256,512]{1,2,0:T(8,128)(2,1)S(1)} async-done(((bf16[4,256,512]{1,2,0:T(8,128)(2,1)}), bf16[4,256,512]{1,2,0:T(8,128)(2,1)S(1)}, u32[]{:S(2)}, u32[]{:S(2)}) %all-to-all-start.1) | async-done | bytes 1048608 | tf_op jit(solution)/shard_map/all_to_all | solution.py:175
  258.9 91.3 %all-gather.17.cloned.1.call-done = bf16[2,688,2048]{2,1,0:T(8,128)(2,1)} async-done(((bf16[2,688,512]{2,1,0:T(8,128)(2,1)}), bf16[2,688,2048]{2,1,0:T(8,128)(2,1)}) %all-gather.17.cloned.1.call-update) | async-done | bytes 5636112 | tf_op jit(solution)/shard_map/all_gather | solution.py:182
  350.2 57.9 %all-gather.15.cloned.1.call-done = bf16[2048,2048]{1,0:T(8,128)(2,1)} async-done(((bf16[256,2048]{1,0:T(8,128)(2,1)}), bf16[2048,2048]{1,0:T(8,128)(2,1)}) %all-gather.15.cloned.1.call-update) | async-done | bytes 8388624 | tf_op jit(solution)/shard_map/all_gather | solution.py:186
  408.1 16.0 %convolution_add_fusion = f32[2048,1376]{0,1:T(8,128)S(1)} fusion(bf16[2048,2048]{1,0:T(8,128)(2,1)} %all-gather.15.cloned.1.call-done, bf16[1376,2048]{1,0:T(8,128)(2,1)} %bitcast.132, f32[1376]{0:T(1024)S(1)} %add.150), kind=kOutput, calls=%fused_computation.10 | convolution fusion | flops 11545542656 | bytes 25302400 | tf_op jit(solution)/shard_map/dot_general | solution.py:75
  431.4 34.2 %all-gather.19.cloned.1.call-done = bf16[688,2048]{1,0:T(8,128)(2,1)} async-done(((bf16[688,512]{1,0:T(8,128)(2,1)}), bf16[688,2048]{1,0:T(8,128)(2,1)}) %all-gather.19.cloned.1.call-update) | async-done | bytes 2818064 | tf_op jit(solution)/shard_map/all_gather | solution.py:185
  477.1 71.9 %reduce-scatter.8.cloned.1.call-done = bf16[256,2048]{1,0:T(8,128)(2,1)} async-done(((bf16[2048,2048]{1,0:T(8,128)(2,1)}), bf16[256,2048]{1,0:T(8,128)(2,1)}) %reduce-scatter.8.cloned.1.call-update) | async-done | bytes 1048592 | tf_op jit(solution)/shard_map/reduce_scatter | solution.py:194
  556.9 54.3 %all-gather.21.cloned.1.call-done = bf16[2048,2048]{1,0:T(8,128)(2,1)} async-done(((bf16[256,2048]{1,0:T(8,128)(2,1)}), bf16[2048,2048]{1,0:T(8,128)(2,1)}) %all-gather.21.cloned.1.call-update) | async-done | bytes 8388624 | tf_op jit(solution)/shard_map/all_gather | solution.py:209
  611.2 16.4 %multiply_convert_fusion.1 = (bf16[2048,688]{0,1:T(8,128)(2,1)S(1)}, bf16[2048,688]{0,1:T(8,128)(2,1)S(1)}) fusion(f32[2048,1376]{0,1:T(8,128)} %copy-done.6, bf16[2048,2048]{1,0:T(8,128)(2,1)} %all-gather.21.cloned.1.call-done, bf16[688,2048]{1,0:T(8,128)(2,1)} %all-gather.19.cloned.1.call-done), kind=kOutput, calls=%fused_computation.33 | convolution fusion | flops 5810814976 | bytes 28114944 | tf_op jit(solution)/shard_map/dot_general | solution.py:75
  630.1 17.8 %convolution_convert_fusion.4 = bf16[2048,2048]{1,0:T(8,128)(2,1)} fusion(bf16[1376,2048]{1,0:T(8,128)(2,1)} %bitcast.133, bf16[2048,688]{0,1:T(8,128)(2,1)S(1)} %get-tuple-element.36, bf16[2048,688]{0,1:T(8,128)(2,1)S(1)} %get-tuple-element.35), kind=kOutput, calls=%fused_computation.20 | convolution fusion | flops 11558191104 | bytes 19660800 | tf_op jit(solution)/shard_map/dot_general | solution.py:75
  648.1 71.2 %reduce-scatter.10.cloned.1.call-done = bf16[256,2048]{1,0:T(8,128)(2,1)} async-done(((bf16[2048,2048]{1,0:T(8,128)(2,1)}), bf16[256,2048]{1,0:T(8,128)(2,1)}) %reduce-scatter.10.cloned.1.call-update) | async-done | bytes 1048592 | tf_op jit(solution)/shard_map/reduce_scatter | solution.py:214
  730.0 29.0 %all_to_all.46 = bf16[256,4,512]{2,0,1:T(8,128)(2,1)S(1)} all-to-all(bf16[256,4,512]{2,0,1:T(8,128)(2,1)S(1)} %bitcast.108), channel_id=1, replica_groups=mesh['wide'=8,'narrow'=4] {'narrow'}, dimensions={1} | all-to-all | bytes 2097152 | tf_op jit(solution)/shard_map/all_to_all | solution.py:236
  770.1 12.3 fusion.2
  823.6 18.6 %convolution_convert_fusion.1 = bf16[1376,2048]{1,0:T(8,128)(2,1)} fusion(bf16[2048,2048]{1,0:T(8,128)(2,1)} %all-gather.15.cloned.1.call-done, bf16[2048,688]{0,1:T(8,128)(2,1)} %copy-done.14, bf16[2048,688]{0,1:T(8,128)(2,1)} %copy-done.13), kind=kOutput, calls=%fused_computation.17 | convolution fusion | flops 11556814848 | bytes 19660800 | tf_op jit(solution)/shard_map/dot_general | solution.py:75
  848.4 11.5 convolution_convert_fusion.5
  881.8 65.1 %reduce-scatter.20.cloned.1.call-done = bf16[688,512]{1,0:T(8,128)(2,1)} async-done(((bf16[688,2048]{1,0:T(8,128)(2,1)}), bf16[688,512]{1,0:T(8,128)(2,1)}) %reduce-scatter.20.cloned.1.call-update) | async-done | bytes 704528 | tf_op jit(solution)/shard_map/reduce_scatter | solution.py:222
  949.3 98.1 %reduce-scatter.18.cloned.1.call-done = bf16[2,688,512]{2,1,0:T(8,128)(2,1)} async-done(((bf16[2,688,2048]{2,1,0:T(8,128)(2,1)}), bf16[2,688,512]{2,1,0:T(8,128)(2,1)}) %reduce-scatter.18.cloned.1.call-update) | async-done | bytes 1409040 | tf_op jit(solution)/shard_map/reduce_scatter | solution.py:226
  1050.7 128.2 %all-reduce.3.cloned.1.call-done = f32[32,1368]{1,0:T(8,128)} async-done(((f32[32,1368]{1,0:T(8,128)}), f32[32,1368]{1,0:T(8,128)}) %all-reduce.3.cloned.1.call-update) | async-done | bytes 175120
  1186.4 70.5 %reduce-scatter.12.cloned.1.call-done = bf16[256,2048]{1,0:T(8,128)(2,1)} async-done(((bf16[1024,2048]{1,0:T(8,128)(2,1)}), bf16[256,2048]{1,0:T(8,128)(2,1)}) %reduce-scatter.12.cloned.1.call-update) | async-done | bytes 1048592 | tf_op jit(solution)/shard_map/reduce_scatter | solution.py:265
  1266.7 175.8 %reduce-scatter.16.cloned.1.call-done = bf16[64,2048]{1,0:T(8,128)(2,1)} async-done(((bf16[2048,2048]{1,0:T(8,128)(2,1)}), bf16[64,2048]{1,0:T(8,128)(2,1)}) %reduce-scatter.16.cloned.1.call-update) | async-done | bytes 262160 | tf_op jit(solution)/shard_map/reduce_scatter | solution.py:240
  (225 shorter events, 209.4 us)
Async XLA Ops:
  7.2 127.1 %all-gather.9.cloned.1.call-start = ((), (), s32[]{:S(2)}) async-start(), calls=%async_computation.11 | async-start | bytes 5242880 | tf_op jit(solution)/shard_map/all_gather | solution.py:145
  7.9 145.1 %all-gather.11.cloned.1.call-start = ((), (), s32[]{:S(2)}) async-start(), calls=%async_computation.12 | async-start | bytes 7077888 | tf_op jit(solution)/shard_map/all_gather | solution.py:153
  52.2 73.6 %copy-start.22 = (s32[1,2]{1,0:T(1,128)S(1)}, s32[1,2]{1,0:T(1,128)}, u32[]{:S(2)}) copy-start(s32[1,2]{1,0:T(1,128)} %param.26) | copy-start | bytes 28
  53.4 196.3 %all-gather.13.cloned.1.call-start = ((), (), s32[]{:S(2)}) async-start(), calls=%async_computation.13 | async-start | bytes 8650752 | tf_op jit(solution)/shard_map/all_gather | solution.py:157
  54.1 296.1 %all-gather.17.cloned.1.call-start = ((), (), s32[]{:S(2)}) async-start(), calls=%async_computation.15 | async-start | bytes 7045120 | tf_op jit(solution)/shard_map/all_gather | solution.py:182
  179.6 27.1 %copy-start.7 = (bf16[1024,1,4,128]{0,3,2,1:T(8,128)(2,1)}, bf16[1024,1,4,128]{0,3,2,1:T(8,128)(2,1)S(1)}, u32[]{:S(2)}) copy-start(bf16[1024,1,4,128]{0,3,2,1:T(8,128)(2,1)S(1)} %copy.167) | copy-start | bytes 3145732
  213.1 36.5 %all-to-all-start.1 = ((bf16[4,256,512]{1,2,0:T(8,128)(2,1)}), bf16[4,256,512]{1,2,0:T(8,128)(2,1)S(1)}, u32[]{:S(2)}, u32[]{:S(2)}) async-start(bf16[4,256,512]{1,2,0:T(8,128)(2,1)} %copy.136), calls=%async_computation.1 | async-start | bytes 2097152 | tf_op jit(solution)/shard_map/all_to_all | solution.py:175
  218.2 189.8 %all-gather.15.cloned.1.call-start = ((), (), s32[]{:S(2)}) async-start(), calls=%async_computation.14 | async-start | bytes 9437184 | tf_op jit(solution)/shard_map/all_gather | solution.py:186
  258.0 207.6 %all-gather.19.cloned.1.call-start = ((), (), s32[]{:S(2)}) async-start(), calls=%async_computation.16 | async-start | bytes 3522560 | tf_op jit(solution)/shard_map/all_gather | solution.py:185
  258.6 290.5 %reduce-scatter.8.cloned.1.call-start = ((), (), s32[]{:S(2)}) async-start(), calls=%async_computation.17 | async-start | bytes 9437184 | tf_op jit(solution)/shard_map/reduce_scatter | solution.py:194
  476.9 134.4 %all-gather.21.cloned.1.call-start = ((), (), s32[]{:S(2)}) async-start(), calls=%async_computation.18 | async-start | bytes 9437184 | tf_op jit(solution)/shard_map/all_gather | solution.py:209
  556.7 162.6 %reduce-scatter.10.cloned.1.call-start = ((), (), s32[]{:S(2)}) async-start(), calls=%async_computation.19 | async-start | bytes 9437184 | tf_op jit(solution)/shard_map/reduce_scatter | solution.py:214
  647.9 226.5 %reduce-scatter.14.cloned.1.call-start = ((), (), s32[]{:S(2)}) async-start(), calls=%async_computation.21 | async-start | bytes 7077888 | tf_op jit(solution)/shard_map/reduce_scatter | solution.py:269
  730.0 30.0 %copy-start.8 = (bf16[1024,1,4,128]{0,3,2,1:T(8,128)(2,1)S(1)}, bf16[1024,1,4,128]{0,3,2,1:T(8,128)(2,1)}, u32[]{:S(2)}) copy-start(bf16[1024,1,4,128]{0,3,2,1:T(8,128)(2,1)} %copy-done.7) | copy-start | bytes 3145732
  759.9 29.9 %slice-start = ((s8[8388608]{0:T(1024)(128)(4,1)}), s8[4194304]{0:T(1024)(128)(4,1)S(1)}, s32[]{:S(2)}) async-start(s8[8388608]{0:T(1024)(128)(4,1)} %bitcast.101), calls=%async_computation.26 | async-start | bytes 8388608
  770.1 12.4 copy-start.17
  770.1 12.4 copy-start.18
  770.1 19.8 %slice-start.1 = ((s8[8388608]{0:T(1024)(128)(4,1)}), s8[4194304]{0:T(1024)(128)(4,1)S(1)}, s32[]{:S(2)}) async-start(s8[8388608]{0:T(1024)(128)(4,1)} %bitcast.101), calls=%async_computation.27 | async-start | bytes 8388608
  813.1 133.9 %reduce-scatter.20.cloned.1.call-start = ((), (), s32[]{:S(2)}) async-start(), calls=%async_computation.24 | async-start | bytes 3522560 | tf_op jit(solution)/shard_map/reduce_scatter | solution.py:222
  823.5 223.9 %reduce-scatter.18.cloned.1.call-start = ((), (), s32[]{:S(2)}) async-start(), calls=%async_computation.23 | async-start | bytes 7045120 | tf_op jit(solution)/shard_map/reduce_scatter | solution.py:226
  842.2 336.7 %all-reduce.3.cloned.1.call-start = ((), (), s32[]{:S(2)}) async-start(), calls=%async_computation.25 | async-start | bytes 360448
  848.4 408.5 %reduce-scatter.12.cloned.1.call-start = ((), (), s32[]{:S(2)}) async-start(), calls=%async_computation.20 | async-start | bytes 5242880 | tf_op jit(solution)/shard_map/reduce_scatter | solution.py:265
  859.9 582.6 %reduce-scatter.16.cloned.1.call-start = ((), (), s32[]{:S(2)}) async-start(), calls=%async_computation.22 | async-start | bytes 8650752 | tf_op jit(solution)/shard_map/reduce_scatter | solution.py:240
  876.7 383.2 %all-to-all-start.3 = ((bf16[4,64,1536]{2,1,0:T(8,128)(2,1)}), bf16[4,64,1536]{2,1,0:T(8,128)(2,1)S(1)}, u32[]{:S(2)}, u32[]{:S(2)}) async-start(bf16[4,64,1536]{2,1,0:T(8,128)(2,1)} %bitcast.27), calls=%async_computation.7 | async-start | bytes 1572864 | tf_op jit(solution)/shard_map/all_to_all | solution.py:273
  (24 other events, 73.5 us)
Sparse Core Ops, SparseCore 0:
  9.6 92.9 all-gather.8
  105.1 47.9 all-gather.10
  156.0 83.9 all-gather.12
  241.4 108.7 all-gather.16
  352.5 55.5 all-gather.14
  409.5 56.0 all-gather.18
  477.0 71.9 reduce-scatter.7
  556.8 54.3 all-gather.20
  648.0 71.2 reduce-scatter.9
  813.2 61.1 reduce-scatter.13
  876.8 70.0 reduce-scatter.19
  949.1 98.2 reduce-scatter.17
  1053.5 125.2 all-reduce.2
  1181.0 75.8 reduce-scatter.11
  1259.1 183.3 reduce-scatter.15

commit v2 on v1

--- a/solution.py
+++ b/solution.py
@@ -1,6 +1,11 @@
+import functools
+import math
+
 import jax
 import jax.numpy as jnp
 from jax import lax
+from jax.experimental import pallas as pl
+from jax.experimental.pallas import tpu as pltpu
 from jax.sharding import PartitionSpec as P
 
 HEADS = 16
@@ -11,6 +16,7 @@
 norm_eps = 1e-05
 masked_value = -1e30
 both_axes = ("wide", "narrow")
+kernel_memory = 60 * 2**20
 
 
 def layout(positions, joined_flag, prefix_pair, bucket_len):
@@ -107,6 +113,539 @@
         pairs(own_expand),
         reduce_shift,
     )
+
+
+def ring_place(wide_count):
+    ring = wide_count // 2
+    mine = lax.axis_index("wide")
+    chip = mine // 2
+    core = mine % 2
+    position = 2 * (chip // 2) + (chip % 2 + chip // 2) % 2
+    return ring, position, core
+
+
+def chip_at(position, ring):
+    position = (position + 2 * ring) % ring
+    return 2 * (position // 2) + (position + position // 2) % 2
+
+
+class PlaneExchange:
+    def __init__(self, wide_count, own, blocks, parts, from_mate, outgoing, incoming, sems):
+        self.ring, self.position, self.core = ring_place(wide_count)
+        self.own, self.blocks, self.parts = own, blocks, parts
+        self.from_mate, self.outgoing, self.incoming = from_mate, outgoing, incoming
+        (
+            self.gather_send,
+            self.gather_recv,
+            self.mate_send,
+            self.mate_recv,
+            self.sum_send,
+            self.sum_recv,
+            self.own_sem,
+        ) = sems
+        self.half = blocks.shape[1] // 2
+        self.far = self.ring // 2
+        self.started = []
+
+    def device(self, offset, mate=False):
+        core = 1 - self.core if mate else self.core
+        return {"wide": 2 * chip_at(self.position + offset, self.ring) + core}
+
+    def slot(self, offset, mate=False):
+        core = 1 - self.core if mate else self.core
+        return 2 * chip_at(self.position + offset, self.ring) + core
+
+    def rows(self, part):
+        return pl.ds(part * self.half, self.half)
+
+    def greet(self):
+        barrier = pltpu.get_barrier_semaphore()
+        for where in (self.device(-1), self.device(1), self.device(0, True)):
+            pl.semaphore_signal(
+                barrier, inc=1, device_id=where, device_id_type=pl.DeviceIdType.MESH
+            )
+        pl.semaphore_wait(barrier, 3)
+
+    def start(self, source, target, send_sem, recv_sem, where):
+        copy = pltpu.make_async_remote_copy(
+            src_ref=source,
+            dst_ref=target,
+            send_sem=send_sem,
+            recv_sem=recv_sem,
+            device_id=where,
+            device_id_type=pl.DeviceIdType.MESH,
+        )
+        copy.start()
+        self.started.append(copy)
+
+    def pass_on(self, lane, slot, part, where, source=None):
+        target = self.blocks.at[slot, self.rows(part)]
+        self.start(
+            target if source is None else source,
+            target,
+            self.gather_send.at[lane, slot, part],
+            self.gather_recv.at[slot, part],
+            where,
+        )
+
+    def arrived(self, slot, part):
+        target = self.blocks.at[slot, self.rows(part)]
+        pltpu.make_async_remote_copy(
+            src_ref=target,
+            dst_ref=target,
+            send_sem=self.gather_send.at[0, slot, part],
+            recv_sem=self.gather_recv.at[slot, part],
+            device_id=self.device(1),
+            device_id_type=pl.DeviceIdType.MESH,
+        ).wait_recv()
+
+    def send_own(self):
+        slot = self.slot(0)
+        keep = pltpu.make_async_copy(self.own, self.blocks.at[slot], self.own_sem)
+        keep.start()
+        first, second = self.own.at[self.rows(0)], self.own.at[self.rows(1)]
+        self.pass_on(0, slot, 0, self.device(1), first)
+        self.pass_on(1, slot, 1, self.device(-1), second)
+        self.pass_on(2, slot, 0, self.device(0, True), first)
+        self.pass_on(2, slot, 1, self.device(0, True), second)
+        self.pass_on(0, slot, 1, self.device(1), second)
+        self.pass_on(1, slot, 0, self.device(-1), first)
+        return keep
+
+    def receive(self, distance):
+        mate = self.device(0, True)
+        left, right = self.slot(-distance), self.slot(distance)
+        if distance == self.far:
+            for part in range(2):
+                self.arrived(left, part)
+                self.pass_on(2, left, part, mate)
+            return
+        further = distance < self.far - 1
+        self.arrived(left, 0)
+        self.pass_on(0, left, 0, self.device(1))
+        self.pass_on(2, left, 0, mate)
+        self.arrived(right, 1)
+        self.pass_on(1, right, 1, self.device(-1))
+        self.pass_on(2, right, 1, mate)
+        self.arrived(left, 1)
+        if further:
+            self.pass_on(0, left, 1, self.device(1))
+        self.pass_on(2, left, 1, mate)
+        self.arrived(right, 0)
+        if further:
+            self.pass_on(1, right, 0, self.device(-1))
+        self.pass_on(2, right, 0, mate)
+
+    def receive_mate(self, offset):
+        for part in range(2):
+            self.arrived(self.slot(offset, True), part)
+
+    def share(self, offset):
+        chip = chip_at(self.position + offset, self.ring)
+        self.start(
+            self.parts.at[self.slot(offset, True)],
+            self.from_mate.at[chip],
+            self.mate_send.at[chip],
+            self.mate_recv.at[chip],
+            self.device(0, True),
+        )
+
+    def shared(self, offset):
+        chip = chip_at(self.position + offset, self.ring)
+        pltpu.make_async_remote_copy(
+            src_ref=self.parts.at[self.slot(offset)],
+            dst_ref=self.from_mate.at[chip],
+            send_sem=self.mate_send.at[chip],
+            recv_sem=self.mate_recv.at[chip],
+            device_id=self.device(0, True),
+            device_id_type=pl.DeviceIdType.MESH,
+        ).wait_recv()
+
+    def chip_sum(self, offset, rows):
+        chip = chip_at(self.position + offset, self.ring)
+        return self.parts[self.slot(offset), rows].astype(jnp.float32) + self.from_mate[
+            chip, rows
+        ].astype(jnp.float32)
+
+    def send_sum(self, way, distance, part):
+        offset = distance if way == 0 else -distance
+        begins = self.far if part == way else self.far - 1
+        target = self.outgoing.at[way, distance - 1, part]
+        if distance < begins:
+            self.sum_arrived(way, distance, part)
+
+        def chunk(i, carry):
+            here = pl.ds(pl.multiple_of(i * 16, 16), 16)
+            there = pl.ds(pl.multiple_of(part * self.half + i * 16, 16), 16)
+            total = self.chip_sum(offset, there)
+            if distance < begins:
+                total += self.incoming[way, distance, part, here].astype(jnp.float32)
+            target[here] = total.astype(jnp.bfloat16)
+            return carry
+
+        lax.fori_loop(0, self.half // 16, chunk, 0)
+        self.start(
+            target,
+            self.incoming.at[way, distance - 1, part],
+            self.sum_send.at[way, distance - 1, part],
+            self.sum_recv.at[way, distance - 1, part],
+            self.device(1 if way == 0 else -1),
+        )
+
+    def sum_arrived(self, way, distance, part):
+        target = self.incoming.at[way, distance, part]
+        pltpu.make_async_remote_copy(
+            src_ref=target,
+            dst_ref=target,
+            send_sem=self.sum_send.at[way, distance, part],
+            recv_sem=self.sum_recv.at[way, distance, part],
+            device_id=self.device(1),
+            device_id_type=pl.DeviceIdType.MESH,
+        ).wait_recv()
+
+    def run(self, compute):
+        keep = self.send_own()
+        keep.wait()
+        self.receive_mate(0)
+        compute(chip_at(self.position, self.ring))
+        self.share(0)
+        for distance in range(1, self.far):
+            self.receive(distance)
+            for offset in (-distance, distance):
+                self.receive_mate(offset)
+                compute(chip_at(self.position + offset, self.ring))
+                self.share(offset)
+            if distance == self.far - 1:
+                self.shared(distance)
+                self.send_sum(0, distance, 1)
+                self.shared(-distance)
+                self.send_sum(1, distance, 0)
+        self.receive(self.far)
+        self.receive_mate(self.far)
+        compute(chip_at(self.position + self.far, self.ring))
+        self.share(self.far)
+        self.shared(self.far)
+        self.send_sum(0, self.far, 0)
+        self.send_sum(1, self.far, 1)
+        for distance in range(self.far - 1, 0, -1):
+            if distance < self.far - 1:
+                self.shared(distance)
+                self.shared(-distance)
+            self.send_sum(0, distance, 0)
+            self.send_sum(1, distance, 1)
+            if distance < self.far - 1:
+                self.send_sum(0, distance, 1)
+                self.send_sum(1, distance, 0)
+
+    def finish(self, result):
+        self.shared(0)
+        for part in range(2):
+            for way in range(2):
+                self.sum_arrived(way, 0, part)
+
+            def chunk(i, carry):
+                here = pl.ds(pl.multiple_of(i * 16, 16), 16)
+                there = pl.ds(pl.multiple_of(part * self.half + i * 16, 16), 16)
+                total = self.chip_sum(0, there)
+                for way in range(2):
+                    total += self.incoming[way, 0, part, here].astype(jnp.float32)
+                result[there] = total
+                return carry
+
+            lax.fori_loop(0, self.half // 16, chunk, 0)
+        for copy in self.started:
+            copy.wait_send()
+
+
+def exchange_scratch(wide_count, rows, width):
+    ring = wide_count // 2
+    far = ring // 2
+    half = rows // 2
+    dma = pltpu.SemaphoreType.DMA
+    return [
+        pltpu.VMEM((wide_count, rows, width), jnp.bfloat16),
+        pltpu.VMEM((wide_count, rows, width), jnp.bfloat16),
+        pltpu.VMEM((ring, rows, width), jnp.bfloat16),
+        pltpu.VMEM((2, far, 2, half, width), jnp.bfloat16),
+        pltpu.VMEM((2, far, 2, half, width), jnp.bfloat16),
+        dma((3, wide_count, 2)),
+        dma((wide_count, 2)),
+        dma((ring,)),
+        dma((ring,)),
+        dma((2, far, 2)),
+        dma((2, far, 2)),
+        dma(()),
+    ]
+
+
+def load_padded(source, target, sem):
+    filled = source.shape[0]
+    copy = pltpu.make_async_copy(source, target.at[pl.ds(0, filled)], sem)
+    copy.start()
+    if filled < target.shape[0]:
+        target[pl.ds(filled, target.shape[0] - filled)] = jnp.zeros(
+            (target.shape[0] - filled, target.shape[1]), target.dtype
+        )
+    return copy
+
+
+def pair_rows(ref, chip):
+    block = ref[pl.ds(2 * chip, 2)]
+    return block.reshape(2 * block.shape[1], block.shape[2])
+
+
+def set_pair(ref, chip, cols, value):
+    rows = ref.shape[1]
+    ref[2 * chip, :, cols] = value[:rows].astype(ref.dtype)
+    ref[2 * chip + 1, :, cols] = value[rows:].astype(ref.dtype)
+
+
+def tiles(count, tile, body):
+    def step(i, carry):
+        body(pl.ds(pl.multiple_of(i * tile, tile), tile))
+        return carry
+
+    lax.fori_loop(0, count // tile, step, 0)
+
+
+def geglu_forward_kernel(
+    wide_count,
+    own,
+    expand,
+    reduce,
+    shift,
+    rows_all,
+    active_out,
+    slope_out,
+    gelu_out,
+    feed,
+    blocks,
+    parts,
+    from_mate,
+    outgoing,
+    incoming,
+    gather_send,
+    gather_recv,
+    mate_send,
+    mate_recv,
+    sum_send,
+    sum_recv,
+    own_sem,
+    expand_mat,
+    reduce_mat,
+    active,
+    slope,
+    gelu,
+    load_sems,
+    keep_sems,
+):
+    sems = (gather_send, gather_recv, mate_send, mate_recv, sum_send, sum_recv, own_sem)
+    plane = PlaneExchange(wide_count, own, blocks, parts, from_mate, outgoing, incoming, sems)
+    loads = [
+        load_padded(expand.at[0], expand_mat.at[0], load_sems.at[0]),
+        load_padded(expand.at[1], expand_mat.at[1], load_sems.at[1]),
+        load_padded(reduce, reduce_mat, load_sems.at[2]),
+    ]
+    plane.greet()
+    kept = []
+    waiting = list(loads)
+
+    def compute(chip):
+        while waiting:
+            waiting.pop().wait()
+
+        def units(cols):
+            rows = pair_rows(blocks, chip)
+            gate = dot(rows, expand_mat[0, cols], ((1,), (1,))) + shift[0:1, cols]
+            upper = dot(rows, expand_mat[1, cols], ((1,), (1,))) + shift[1:2, cols]
+            factor = math.sqrt(2 / math.pi)
+            square = gate * gate
+            bend = jnp.tanh(factor * gate * (1 + 0.044715 * square))
+            value = 0.5 * gate * (1 + bend)
+            pull = 0.5 * (1 + bend) + 0.5 * gate * (1 - bend * bend) * factor * (
+                1 + 3 * 0.044715 * square
+            )
+            set_pair(active, chip, cols, value * upper)
+            set_pair(slope, chip, cols, pull * upper)
+            set_pair(gelu, chip, cols, value)
+
+        tiles(active.shape[2], 256, units)
+
+        def outputs(cols):
+            set_pair(
+                parts, chip, cols, dot(pair_rows(active, chip), reduce_mat[:, cols], ((1,), (0,)))
+            )
+
+        tiles(parts.shape[2], 256, outputs)
+        pair = pl.ds(2 * chip, 2)
+        for index, (source, target) in enumerate(
+            ((active, active_out), (slope, slope_out), (gelu, gelu_out), (blocks, rows_all))
+        ):
+            copy = pltpu.make_async_copy(
+                source.at[pair], target.at[pair], keep_sems.at[chip, index]
+            )
+            copy.start()
+            kept.append(copy)
+
+    plane.run(compute)
+    plane.finish(feed)
+    for copy in kept:
+        copy.wait()
+
+
+def geglu_forward(wide_count, hidden_low, expand_full, reduce_full, shift):
+    rows, width = hidden_low.shape
+    padded = shift.shape[1]
+    anywhere = pl.BlockSpec(memory_space=pl.ANY)
+    vmem = pl.BlockSpec(memory_space=pltpu.VMEM)
+    kept = jax.ShapeDtypeStruct((wide_count, rows, padded), jnp.bfloat16)
+    scratch = exchange_scratch(wide_count, rows, width) + [
+        pltpu.VMEM((2, padded, width), jnp.bfloat16),
+        pltpu.VMEM((padded, width), jnp.bfloat16),
+        pltpu.VMEM((wide_count, rows, padded), jnp.bfloat16),
+        pltpu.VMEM((wide_count, rows, padded), jnp.bfloat16),
+        pltpu.VMEM((wide_count, rows, padded), jnp.bfloat16),
+        pltpu.SemaphoreType.DMA((3,)),
+        pltpu.SemaphoreType.DMA((wide_count // 2, 4)),
+    ]
+    return pl.pallas_call(
+        functools.partial(geglu_forward_kernel, wide_count),
+        out_shape=(
+            jax.ShapeDtypeStruct((wide_count, rows, width), jnp.bfloat16),
+            kept,
+            kept,
+            kept,
+            jax.ShapeDtypeStruct((rows, width), jnp.float32),
+        ),
+        in_specs=[anywhere, anywhere, anywhere, vmem],
+        out_specs=(anywhere, anywhere, anywhere, anywhere, vmem),
+        scratch_shapes=scratch,
+        compiler_params=pltpu.CompilerParams(
+            collective_id=1, has_side_effects=True, vmem_limit_bytes=kernel_memory
+        ),
+        cost_estimate=pl.CostEstimate(
+            flops=6 * wide_count * rows * padded * width, bytes_accessed=200 * 2**20, transcendentals=0
+        ),
+        name="geglu_forward",
+    )(hidden_low, expand_full, reduce_full, shift)
+
+
+def geglu_backward_kernel(
+    wide_count,
+    own,
+    expand,
+    reduce,
+    slope_in,
+    gelu_in,
+    rows_all,
+    unit_grads,
+    hidden_grad,
+    blocks,
+    parts,
+    from_mate,
+    outgoing,
+    incoming,
+    gather_send,
+    gather_recv,
+    mate_send,
+    mate_recv,
+    sum_send,
+    sum_recv,
+    own_sem,
+    expand_mat,
+    reduce_mat,
+    slope,
+    gelu,
+    load_sems,
+    keep_sems,
+):
+    sems = (gather_send, gather_recv, mate_send, mate_recv, sum_send, sum_recv, own_sem)
+    plane = PlaneExchange(wide_count, own, blocks, parts, from_mate, outgoing, incoming, sems)
+    loads = [
+        load_padded(expand.at[0], expand_mat.at[0], load_sems.at[0]),
+        load_padded(expand.at[1], expand_mat.at[1], load_sems.at[1]),
+        load_padded(reduce, reduce_mat, load_sems.at[2]),
+        pltpu.make_async_copy(slope_in, slope, load_sems.at[3]),
+        pltpu.make_async_copy(gelu_in, gelu, load_sems.at[4]),
+    ]
+    for copy in loads[3:]:
+        copy.start()
+    plane.greet()
+    kept = []
+    waiting = list(loads)
+
+    def compute(chip):
+        while waiting:
+            waiting.pop().wait()
+
+        def units(cols):
+            pulled = dot(pair_rows(blocks, chip), reduce_mat[cols], ((1,), (1,)))
+            pair = pl.ds(2 * chip, 2)
+            shape = pulled.shape
+            gate_grad = pulled * slope[pair, :, cols].reshape(shape).astype(jnp.float32)
+            upper_grad = pulled * gelu[pair, :, cols].reshape(shape).astype(jnp.float32)
+            set_pair(slope, chip, cols, gate_grad)
+            set_pair(gelu, chip, cols, upper_grad)
+
+        tiles(slope.shape[2], 256, units)
+
+        def outputs(cols):
+            set_pair(
+                parts,
+                chip,
+                cols,
+                dot(pair_rows(slope, chip), expand_mat[0, :, cols], ((1,), (0,)))
+                + dot(pair_rows(gelu, chip), expand_mat[1, :, cols], ((1,), (0,))),
+            )
+
+        tiles(parts.shape[2], 256, outputs)
+        pair = pl.ds(2 * chip, 2)
+        for index, (source, target) in enumerate(
+            ((slope, unit_grads.at[0]), (gelu, unit_grads.at[1]), (blocks, rows_all))
+        ):
+            copy = pltpu.make_async_copy(
+                source.at[pair], target.at[pair], keep_sems.at[chip, index]
+            )
+            copy.start()
+            kept.append(copy)
+
+    plane.run(compute)
+    plane.finish(hidden_grad)
+    for copy in kept:
+        copy.wait()
+
+
+def geglu_backward(wide_count, feed_grad, expand_full, reduce_full, slope, gelu):
+    rows, width = feed_grad.shape
+    padded = slope.shape[2]
+    anywhere = pl.BlockSpec(memory_space=pl.ANY)
+    vmem = pl.BlockSpec(memory_space=pltpu.VMEM)
+    scratch = exchange_scratch(wide_count, rows, width) + [
+        pltpu.VMEM((2, padded, width), jnp.bfloat16),
+        pltpu.VMEM((padded, width), jnp.bfloat16),
+        pltpu.VMEM((wide_count, rows, padded), jnp.bfloat16),
+        pltpu.VMEM((wide_count, rows, padded), jnp.bfloat16),
+        pltpu.SemaphoreType.DMA((5,)),
+        pltpu.SemaphoreType.DMA((wide_count // 2, 3)),
+    ]
+    return pl.pallas_call(
+        functools.partial(geglu_backward_kernel, wide_count),
+        out_shape=(
+            jax.ShapeDtypeStruct((wide_count, rows, width), jnp.bfloat16),
+            jax.ShapeDtypeStruct((2, wide_count, rows, padded), jnp.bfloat16),
+            jax.ShapeDtypeStruct((rows, width), jnp.float32),
+        ),
+        in_specs=[anywhere] * 5,
+        out_specs=(anywhere, anywhere, vmem),
+        scratch_shapes=scratch,
+        compiler_params=pltpu.CompilerParams(
+            collective_id=2, has_side_effects=True, vmem_limit_bytes=kernel_memory
+        ),
+        cost_estimate=pl.CostEstimate(
+            flops=6 * wide_count * rows * padded * width, bytes_accessed=200 * 2**20, transcendentals=0
+        ),
+        name="geglu_backward",
+    )(feed_grad, expand_full, reduce_full, slope, gelu)
 
 
 def shards(
@@ -179,23 +718,25 @@
     )
     hidden_low = low(hidden)
 
+    tile_rows = -share % 16
+    padded = -(-share // 256) * 256
     expand_full = lax.all_gather(
-        expand_weight.transpose(1, 2, 0), "narrow", axis=2, tiled=True
-    ).reshape(2 * share, model_width)
-    reduce_full = lax.all_gather(reduce_weight, "narrow", axis=1, tiled=True)
-    rows_all = lax.all_gather(hidden_low, "wide", axis=0, tiled=True)
-    both = dot(rows_all, expand_full, ((1,), (1,))) + expand_shift.reshape(-1)
-    gate, upper = both[:, :share], both[:, share:]
-    gelu_value, gelu_pull = jax.vjp(jax.nn.gelu, gate)
-    active = low(gelu_value * upper)
-    gate_slope = low(gelu_pull(upper)[0])
-    gelu_low = low(gelu_value)
-    feed = (
-        lax.psum_scatter(
-            low(dot(active, reduce_full, ((1,), (0,)))), "wide", scatter_dimension=0, tiled=True
-        ).astype(jnp.float32)
-        + reduce_shift
-    )
+        jnp.pad(expand_weight.transpose(1, 2, 0), ((0, 0), (0, tile_rows), (0, 0))),
+        "narrow",
+        axis=2,
+        tiled=True,
+    )
+    reduce_full = lax.all_gather(
+        jnp.pad(reduce_weight, ((0, tile_rows), (0, 0))), "narrow", axis=1, tiled=True
+    )
+    rows_all, active, slope, gelu, feed_sum = geglu_forward(
+        wide_count,
+        hidden_low,
+        expand_full,
+        reduce_full,
+        jnp.pad(expand_shift, ((0, 0), (0, padded - share))),
+    )
+    feed = feed_sum + reduce_shift
     output_float, normed_two, inv_two = normalize(
         residual_scale * hidden + feed, gains[1], shifts[1]
     )
@@ -206,19 +747,15 @@
     shift_two_grad = jnp.sum(grad_out, axis=0)
     sum_two_grad = normalize_back(grad_out, normed_two, inv_two, gains[1])
     feed_grad = low(sum_two_grad)
-    feed_grads_all = lax.all_gather(feed_grad, "wide", axis=0, tiled=True)
-    active_grad = dot(feed_grads_all, reduce_full, ((1,), (1,)))
-    gate_up_grad = low(
-        jnp.concatenate([active_grad * gate_slope, active_grad * gelu_low], axis=1)
-    )
-    hidden_part = lax.psum_scatter(
-        low(dot(gate_up_grad, expand_full, ((1,), (0,)))),
-        "wide",
-        scatter_dimension=0,
-        tiled=True,
-    )
-    reduce_part = low(dot(active, feed_grads_all, ((0,), (0,))))
-    expand_part = low(dot(gate_up_grad, rows_all, ((0,), (0,)))).reshape(2, share, model_width)
+    feed_grads_all, unit_grads, hidden_part = geglu_backward(
+        wide_count, feed_grad, expand_full, reduce_full, slope, gelu
+    )
+    tokens_all = wide_count * tok_rows
+    rows_all = rows_all.reshape(tokens_all, model_width)
+    feed_grads_all = feed_grads_all.reshape(tokens_all, model_width)
+    unit_grads = unit_grads.reshape(2, tokens_all, padded)
+    reduce_part = low(dot(active.reshape(tokens_all, padded), feed_grads_all, ((0,), (0,))))[:share]
+    expand_part = low(dot(unit_grads, rows_all, ((1,), (0,))))[:, :share]
     reduce_weight_gradient = lax.psum_scatter(
         reduce_part, "narrow", scatter_dimension=1, tiled=True
     ).astype(jnp.float32)
@@ -227,7 +764,7 @@
         .astype(jnp.float32)
         .transpose(2, 0, 1)
     )
-    hidden_grad = residual_scale * sum_two_grad + hidden_part.astype(jnp.float32)
+    hidden_grad = residual_scale * sum_two_grad + hidden_part
     gain_one_grad = jnp.sum(hidden_grad * normed_one, axis=0)
     shift_one_grad = jnp.sum(hidden_grad, axis=0)
     sum_one_grad = normalize_back(hidden_grad, normed_one, inv_one, gains[0])
@@ -294,7 +831,7 @@
         .transpose(1, 0, 2)
         .reshape(count, -1)
     )
-    expand_sums = jnp.sum(gate_up_grad, axis=0, dtype=jnp.float32)
+    expand_sums = jnp.sum(unit_grads, axis=1, dtype=jnp.float32)[:, :share]
     expand_sums = (
         expand_sums.reshape(2, narrow_count, -1).transpose(1, 0, 2).reshape(1, narrow_count, -1)
         * mine_wide[:, None, None]

time: 1460 us -> 1320 us (0.904)
  waiting for transfers between devices: 978 us -> 735 us
  Pallas kernels: 0 us -> 171 us
  matrix products: 177 us -> 115 us
    pallas_call x0 -> x2, Pallas kernels: none -> 171 us  [the longest x1 87.5 us: geglu_forward(): pl.pallas_call(functools.partial(geglu_forward_kernel, wide_count), out_s...]
    reduce_scatter x2 -> x0, waiting for transfers between devices: 143 us -> none  [the longest x1 71.9 us: shards(): lax.psum_scatter(low(dot(active, reduce_full, ((1,), (0,)))), 'wide', sca...]
    all_gather x4 -> x2, waiting for transfers between devices: 238 us -> 150 us  [the longest x1 104 us: shards(): lax.all_gather(jnp.pad(expand_weight.transpose(1, 2, 0), ((0, 0), (0, til...]
    dot_general x12 -> x8, matrix products: 144 us -> 81.6 us  [dot(): lax.dot_general(left, right, (dims, ((), ())), preferred_element_type=jnp...]
    reduce_scatter x1, waiting for transfers between devices: 65.1 us -> 49 us  [shards(): lax.psum_scatter(reduce_part, 'narrow', scatter_dimension=1, tiled=True)]
    unnamed x16 -> x12, waiting for transfers between devices: 131 us -> 133 us
  transfers between devices with their start and end apart: 17 -> 13, of which waited for: 14 -> 10; matrix products, arithmetic and copies ran while one was open for 12% -> 12% of each run, Pallas kernels for 0% -> 0%
where the time goes in v2:
time: 1320 us; the launch traced here: 1310 us
  waiting for transfers between devices  735 us (56%)
  Pallas kernels  171 us (13%)
  blocking collectives  138 us (10%)
  matrix products  115 us (9%)
  local copies, waits for them, and re-layouts  62.3 us (5%)
  other arithmetic  60 us (5%)
  between operations  16.7 us (1%)
    reduce_scatter x1, waiting for transfers between devices, shards(): lax.psum_scatter(merge_part, both_axes, scatter_dimension=0, tiled=True)  176 us
    unnamed x12, waiting for transfers between devices  133 us
    all_gather x1, waiting for transfers between devices, shards(): lax.all_gather(jnp.pad(expand_weight.transpose(1, 2, 0), ((0, 0), (0, til...  104 us
    reduce_scatter x1, waiting for transfers between devices, shards(): lax.psum_scatter(expand_part, 'narrow', scatter_dimension=2, tiled=True)  100 us
    pallas_call x1, Pallas kernels, geglu_forward(): pl.pallas_call(functools.partial(geglu_forward_kernel, wide_count), out_s...  87.5 us
    pallas_call x1, Pallas kernels, geglu_backward(): pl.pallas_call(functools.partial(geglu_backward_kernel, wide_count), out_...  83.6 us
    dot_general x8, matrix products, dot(): lax.dot_general(left, right, (dims, ((), ())), preferred_element_type=jnp...  81.6 us
    reduce_scatter x1, waiting for transfers between devices, shards(): lax.psum_scatter(low(dot(triple_grad, heads_mat, ((1,), (1,)))), 'narrow'...  77.2 us
  transfers between devices with their start and end apart: 13, of which 10 were waited for; matrix products, arithmetic and copies ran while one was open for 12% of the time, Pallas kernels for 0%

profile of v2, /device:TPU:8, one launch (start us, length us, event | category | flops | bytes accessed | tf_op | source)
XLA Modules:
  0.0 1310.1 jit_solution(10480202958252725077)
XLA Ops:
  10.4 41.1 %all_to_all.45 = bf16[4,64,3,512]{3,1,2,0:T(8,128)(2,1)S(1)} all-to-all(bf16[4,64,3,512]{3,1,2,0:T(8,128)(2,1)S(1)} %copy.141), channel_id=1, replica_groups=mesh['wide'=8,'narrow'=4] {'narrow'}, dimensions={0} | all-to-all | bytes 1572864 | tf_op jit(solution)/shard_map/all_to_all | solution.py:685
  56.4 69.8 %all-gather = bf16[32,1,1368]{2,1,0:T(2,128)(2,1)S(1)} all-gather(bf16[1,1,1368]{2,1,0:T(2,128)(2,1)S(1)} %bitcast.130), channel_id=1, replica_groups=mesh['wide'=8,'narrow'=4] {'wide','narrow'}, dimensions={0}, use_global_device_ids=true | all-gather | bytes 90288 | tf_op jit(solution)/shard_map/all_gather | solution.py:94
  134.9 18.2 %all-gather.9.cloned.1.call-done = bf16[2048,1536]{1,0:T(8,128)(2,1)} async-done(((bf16[256,1536]{1,0:T(8,128)(2,1)}), bf16[2048,1536]{1,0:T(8,128)(2,1)}) %all-gather.9.cloned.1.call-update) | async-done | bytes 6291472 | tf_op jit(solution)/shard_map/all_gather | solution.py:692
  153.1 11.7 convolution_add_fusion
  164.8 7.7 reshape.414
  185.9 13.0 fusion.43
  198.9 8.3 divide_convert_fusion
  220.6 29.1 %all-to-all-done.1 = bf16[4,256,512]{1,2,0:T(8,128)(2,1)S(1)} async-done(((bf16[4,256,512]{1,2,0:T(8,128)(2,1)}), bf16[4,256,512]{1,2,0:T(8,128)(2,1)S(1)}, u32[]{:S(2)}, u32[]{:S(2)}) %all-to-all-start.1) | async-done | bytes 1048608 | tf_op jit(solution)/shard_map/all_to_all | solution.py:714
  258.0 46.6 %all-gather.15.cloned.1.call-done.reduce = bf16[688,2048]{1,0:T(8,128)(2,1)} async-done(((bf16[688,512]{1,0:T(8,128)(2,1)}), bf16[688,2048]{1,0:T(8,128)(2,1)}) %all-gather.15.cloned.1.call-update) | async-done | bytes 2818064 | tf_op jit(solution)/shard_map/all_gather | solution.py:729
  304.6 103.9 %all-gather.13.cloned.1.call-done.expand = bf16[2,688,2048]{2,1,0:T(8,128)(2,1)} async-done(((bf16[2,688,512]{2,1,0:T(8,128)(2,1)}), bf16[2,688,2048]{2,1,0:T(8,128)(2,1)}) %all-gather.13.cloned.1.call-update) | async-done | bytes 5636112 | tf_op jit(solution)/shard_map/all_gather | solution.py:723
  408.5 87.5 %geglu_forward.1 = (bf16[8,256,2048]{2,1,0:T(8,128)(2,1)}, bf16[8,256,768]{2,1,0:T(8,128)(2,1)}, bf16[8,256,768]{2,1,0:T(8,128)(2,1)}, bf16[8,256,768]{2,1,0:T(8,128)(2,1)}, f32[256,2048]{1,0:T(8,128)}) custom-call(bf16[256,2048]{1,0:T(8,128)(2,1)} %fusion.21.own, bf16[2,688,2048]{2,1,0:T(8,128)(2,1)} %all-gather.13.cloned.1.call-done.expand, ...), custom_call_target="tpu_custom_call" | custom-call | flops 19327352832 | bytes 209715200 | tf_op jit(solution)/shard_map/geglu_forward/pallas_call | solution.py:511
  503.1 83.6 %geglu_backward.1 = (bf16[8,256,2048]{2,1,0:T(8,128)(2,1)}, bf16[2,8,256,768]{3,2,1,0:T(8,128)(2,1)}, f32[256,2048]{1,0:T(8,128)}) custom-call(bf16[256,2048]{1,0:T(8,128)(2,1)} %get-tuple-element.43.own, bf16[2,688,2048]{2,1,0:T(8,128)(2,1)} %all-gather.13.cloned.1.call-done.expand, bf16[688,2048]{1,0:T(8,128)(2,1)} %all-gather.15.cloned.1.call-done.reduce, ...), custom_call_target="tpu_custom_call" | custom-call | flops 19327352832 | bytes 209715200 | tf_op jit(solution)/shard_map/geglu_backward/pallas_call | solution.py:631
  598.5 27.6 %all_to_all.46 = bf16[256,4,512]{2,0,1:T(8,128)(2,1)S(1)} all-to-all(bf16[256,4,512]{2,0,1:T(8,128)(2,1)S(1)} %bitcast.109), channel_id=1, replica_groups=mesh['wide'=8,'narrow'=4] {'narrow'}, dimensions={1} | all-to-all | bytes 2097152 | tf_op jit(solution)/shard_map/all_to_all | solution.py:773
  627.4 10.0 fusion.1
  637.4 12.1 fusion.2
  665.6 11.6 fusion.9
  683.2 11.0 convolution_bitcast_fusion
  697.1 11.1 convolution_convert_fusion.2
  708.2 17.6 %fusion.10 = bf16[2,768,2048]{2,1,0:T(8,128)(2,1)S(1)} fusion(bf16[2,8,256,768]{3,2,1,0:T(8,128)(2,1)} %get-tuple-element.24, bf16[8,256,2048]{2,1,0:T(8,128)(2,1)} %get-tuple-element.25), kind=kOutput, calls=%fused_computation.22 | convolution fusion | flops 12884901888 | bytes 20971520 | tf_op jit(solution)/shard_map/dot_general | solution.py:81
  746.0 130.6 %all-reduce.4.cloned.1.call-done = f32[32,1368]{1,0:T(8,128)} async-done(((f32[32,1368]{1,0:T(8,128)}), f32[32,1368]{1,0:T(8,128)}) %all-reduce.4.cloned.1.call-update) | async-done | bytes 175120
  884.2 49.0 %reduce-scatter.14.cloned.1.call-done = bf16[688,512]{1,0:T(8,128)(2,1)} async-done(((bf16[688,2048]{1,0:T(8,128)(2,1)}), bf16[688,512]{1,0:T(8,128)(2,1)}) %reduce-scatter.14.cloned.1.call-update) | async-done | bytes 704528 | tf_op jit(solution)/shard_map/reduce_scatter | solution.py:759
  935.6 77.2 %reduce-scatter.6.cloned.1.call-done = bf16[256,2048]{1,0:T(8,128)(2,1)} async-done(((bf16[1024,2048]{1,0:T(8,128)(2,1)}), bf16[256,2048]{1,0:T(8,128)(2,1)}) %reduce-scatter.6.cloned.1.call-update) | async-done | bytes 1048592 | tf_op jit(solution)/shard_map/reduce_scatter | solution.py:802
  1015.7 100.1 %reduce-scatter.12.cloned.1.call-done = bf16[2,688,512]{2,1,0:T(8,128)(2,1)} async-done(((bf16[2,688,2048]{2,1,0:T(8,128)(2,1)}), bf16[2,688,512]{2,1,0:T(8,128)(2,1)}) %reduce-scatter.12.cloned.1.call-update) | async-done | bytes 1409040 | tf_op jit(solution)/shard_map/reduce_scatter | solution.py:763
  1126.0 175.6 %reduce-scatter.10.cloned.1.call-done = bf16[64,2048]{1,0:T(8,128)(2,1)} async-done(((bf16[2048,2048]{1,0:T(8,128)(2,1)}), bf16[64,2048]{1,0:T(8,128)(2,1)}) %reduce-scatter.10.cloned.1.call-update) | async-done | bytes 262160 | tf_op jit(solution)/shard_map/reduce_scatter | solution.py:777
  (211 shorter events, 139.1 us)
Async XLA Ops:
  7.2 127.7 %all-gather.7.cloned.1.call-start = ((), (), s32[]{:S(2)}) async-start(), calls=%async_computation.9 | async-start | bytes 5242880 | tf_op jit(solution)/shard_map/all_gather | solution.py:684
  7.9 145.2 %all-gather.9.cloned.1.call-start = ((), (), s32[]{:S(2)}) async-start(), calls=%async_computation.10 | async-start | bytes 7077888 | tf_op jit(solution)/shard_map/all_gather | solution.py:692
  52.3 4.0 copy-start.24
  53.4 73.0 %copy-start.21 = (s32[1,2]{1,0:T(1,128)S(1)}, s32[1,2]{1,0:T(1,128)}, u32[]{:S(2)}) copy-start(s32[1,2]{1,0:T(1,128)} %param.26) | copy-start | bytes 28
  53.4 196.3 %all-gather.11.cloned.1.call-start = ((), (), s32[]{:S(2)}) async-start(), calls=%async_computation.11 | async-start | bytes 8650752 | tf_op jit(solution)/shard_map/all_gather | solution.py:696
  54.1 250.5 %all-gather.15.cloned.1.call-start = ((), (), s32[]{:S(2)}) async-start(), calls=%async_computation.13 | async-start | bytes 3522560 | tf_op jit(solution)/shard_map/all_gather | solution.py:729
  54.7 353.8 %all-gather.13.cloned.1.call-start = ((), (), s32[]{:S(2)}) async-start(), calls=%async_computation.12 | async-start | bytes 7045120 | tf_op jit(solution)/shard_map/all_gather | solution.py:723
  180.8 26.4 %copy-start.7 = (bf16[1024,1,4,128]{0,3,2,1:T(8,128)(2,1)}, bf16[1024,1,4,128]{0,3,2,1:T(8,128)(2,1)S(1)}, u32[]{:S(2)}) copy-start(bf16[1024,1,4,128]{0,3,2,1:T(8,128)(2,1)S(1)} %copy.183) | copy-start | bytes 3145732
  185.9 13.0 copy-start.12
  185.9 13.0 copy-start.14
  213.6 36.1 %all-to-all-start.1 = ((bf16[4,256,512]{1,2,0:T(8,128)(2,1)}), bf16[4,256,512]{1,2,0:T(8,128)(2,1)S(1)}, u32[]{:S(2)}, u32[]{:S(2)}) async-start(bf16[4,256,512]{1,2,0:T(8,128)(2,1)} %copy.147), calls=%async_computation.1 | async-start | bytes 2097152 | tf_op jit(solution)/shard_map/all_to_all | solution.py:714
  218.8 519.8 %reduce-scatter.8.cloned.1.call-start = ((), (), s32[]{:S(2)}) async-start(), calls=%async_computation.15 | async-start | bytes 7077888 | tf_op jit(solution)/shard_map/reduce_scatter | solution.py:806
  249.7 6.5 copy-start.4
  591.9 6.5 copy-start.2
  627.4 29.3 %slice-start = ((s8[8388608]{0:T(1024)(128)(4,1)}), s8[4194304]{0:T(1024)(128)(4,1)S(1)}, s32[]{:S(2)}) async-start(s8[8388608]{0:T(1024)(128)(4,1)} %bitcast.103), calls=%async_computation.20 | async-start | bytes 8388608
  637.4 12.2 copy-start.19
  637.4 12.2 copy-start.20
  637.4 19.4 %slice-start.1 = ((s8[8388608]{0:T(1024)(128)(4,1)}), s8[4194304]{0:T(1024)(128)(4,1)S(1)}, s32[]{:S(2)}) async-start(s8[8388608]{0:T(1024)(128)(4,1)} %bitcast.103), calls=%async_computation.21 | async-start | bytes 8388608
  677.3 199.4 %all-reduce.4.cloned.1.call-start = ((), (), s32[]{:S(2)}) async-start(), calls=%async_computation.19 | async-start | bytes 360448
  683.1 250.2 %reduce-scatter.14.cloned.1.call-start = ((), (), s32[]{:S(2)}) async-start(), calls=%async_computation.18 | async-start | bytes 3522560 | tf_op jit(solution)/shard_map/reduce_scatter | solution.py:759
  696.0 316.9 %reduce-scatter.6.cloned.1.call-start = ((), (), s32[]{:S(2)}) async-start(), calls=%async_computation.14 | async-start | bytes 5242880 | tf_op jit(solution)/shard_map/reduce_scatter | solution.py:802
  708.2 407.6 %reduce-scatter.12.cloned.1.call-start = ((), (), s32[]{:S(2)}) async-start(), calls=%async_computation.17 | async-start | bytes 7045120 | tf_op jit(solution)/shard_map/reduce_scatter | solution.py:763
  728.9 572.7 %reduce-scatter.10.cloned.1.call-start = ((), (), s32[]{:S(2)}) async-start(), calls=%async_computation.16 | async-start | bytes 8650752 | tf_op jit(solution)/shard_map/reduce_scatter | solution.py:777
  740.9 378.2 %all-to-all-start.3 = ((bf16[4,64,1536]{2,1,0:T(8,128)(2,1)}), bf16[4,64,1536]{2,1,0:T(8,128)(2,1)S(1)}, u32[]{:S(2)}, u32[]{:S(2)}) async-start(bf16[4,64,1536]{2,1,0:T(8,128)(2,1)} %bitcast.26), calls=%async_computation.5 | async-start | bytes 1572864 | tf_op jit(solution)/shard_map/all_to_all | solution.py:810
  (19 other events, 54.3 us)
Sparse Core Ops, SparseCore 0:
  9.6 92.9 all-gather.6
  105.0 48.0 all-gather.8
  156.0 83.9 all-gather.10
  241.4 63.1 all-gather.14
  306.1 102.3 all-gather.12
  677.4 61.1 reduce-scatter.7
  745.6 130.9 all-reduce.3
  879.7 53.5 reduce-scatter.13
  935.6 77.2 reduce-scatter.5
  1015.1 100.6 reduce-scatter.11
  1118.2 183.3 reduce-scatter.9

commit v3 on v2

--- a/solution.py
+++ b/solution.py
@@ -130,10 +130,10 @@
 
 
 class PlaneExchange:
-    def __init__(self, wide_count, own, blocks, parts, from_mate, outgoing, incoming, sems):
+    def __init__(self, wide_count, own, blocks, parts, from_mate, incoming, sems):
         self.ring, self.position, self.core = ring_place(wide_count)
         self.own, self.blocks, self.parts = own, blocks, parts
-        self.from_mate, self.outgoing, self.incoming = from_mate, outgoing, incoming
+        self.from_mate, self.incoming = from_mate, incoming
         (
             self.gather_send,
             self.gather_recv,
@@ -143,7 +143,7 @@
             self.sum_recv,
             self.own_sem,
         ) = sems
-        self.half = blocks.shape[1] // 2
+        self.half = parts.shape[1] // 2
         self.far = self.ring // 2
         self.started = []
 
@@ -270,7 +270,7 @@
     def send_sum(self, way, distance, part):
         offset = distance if way == 0 else -distance
         begins = self.far if part == way else self.far - 1
-        target = self.outgoing.at[way, distance - 1, part]
+        slot = self.slot(offset)
         if distance < begins:
             self.sum_arrived(way, distance, part)
 
@@ -280,12 +280,12 @@
             total = self.chip_sum(offset, there)
             if distance < begins:
                 total += self.incoming[way, distance, part, here].astype(jnp.float32)
-            target[here] = total.astype(jnp.bfloat16)
+            self.parts[slot, there] = total.astype(jnp.bfloat16)
             return carry
 
         lax.fori_loop(0, self.half // 16, chunk, 0)
         self.start(
-            target,
+            self.parts.at[slot, self.rows(part)],
             self.incoming.at[way, distance - 1, part],
             self.sum_send.at[way, distance - 1, part],
             self.sum_recv.at[way, distance - 1, part],
@@ -316,17 +316,27 @@
                 compute(chip_at(self.position + offset, self.ring))
                 self.share(offset)
             if distance == self.far - 1:
-                self.shared(distance)
-                self.send_sum(0, distance, 1)
-                self.shared(-distance)
-                self.send_sum(1, distance, 0)
+                self.first_sums()
         self.receive(self.far)
         self.receive_mate(self.far)
         compute(chip_at(self.position + self.far, self.ring))
         self.share(self.far)
+        self.far_sums()
+        self.last_sums()
+
+    def first_sums(self):
+        distance = self.far - 1
+        self.shared(distance)
+        self.send_sum(0, distance, 1)
+        self.shared(-distance)
+        self.send_sum(1, distance, 0)
+
+    def far_sums(self):
         self.shared(self.far)
         self.send_sum(0, self.far, 0)
         self.send_sum(1, self.far, 1)
+
+    def last_sums(self):
         for distance in range(self.far - 1, 0, -1):
             if distance < self.far - 1:
                 self.shared(distance)
@@ -349,33 +359,39 @@
                 total = self.chip_sum(0, there)
                 for way in range(2):
                     total += self.incoming[way, 0, part, here].astype(jnp.float32)
-                result[there] = total
+                result[there] = total.astype(result.dtype)
                 return carry
 
             lax.fori_loop(0, self.half // 16, chunk, 0)
+
+    def drain(self):
         for copy in self.started:
             copy.wait_send()
 
 
-def exchange_scratch(wide_count, rows, width):
+def sum_scratch(wide_count, rows, width):
     ring = wide_count // 2
     far = ring // 2
-    half = rows // 2
     dma = pltpu.SemaphoreType.DMA
     return [
         pltpu.VMEM((wide_count, rows, width), jnp.bfloat16),
-        pltpu.VMEM((wide_count, rows, width), jnp.bfloat16),
         pltpu.VMEM((ring, rows, width), jnp.bfloat16),
-        pltpu.VMEM((2, far, 2, half, width), jnp.bfloat16),
-        pltpu.VMEM((2, far, 2, half, width), jnp.bfloat16),
-        dma((3, wide_count, 2)),
-        dma((wide_count, 2)),
+        pltpu.VMEM((2, far, 2, rows // 2, width), jnp.bfloat16),
         dma((ring,)),
         dma((ring,)),
         dma((2, far, 2)),
         dma((2, far, 2)),
+    ]
+
+
+def exchange_scratch(wide_count, rows, width):
+    dma = pltpu.SemaphoreType.DMA
+    return [
+        pltpu.VMEM((wide_count, rows, width), jnp.bfloat16),
+        dma((3, wide_count, 2)),
+        dma((wide_count, 2)),
         dma(()),
-    ]
+    ] + sum_scratch(wide_count, rows, width)
 
 
 def load_padded(source, target, sem):
@@ -420,17 +436,16 @@
     gelu_out,
     feed,
     blocks,
+    gather_send,
+    gather_recv,
+    own_sem,
     parts,
     from_mate,
-    outgoing,
     incoming,
-    gather_send,
-    gather_recv,
     mate_send,
     mate_recv,
     sum_send,
     sum_recv,
-    own_sem,
     expand_mat,
     reduce_mat,
     active,
@@ -440,7 +455,7 @@
     keep_sems,
 ):
     sems = (gather_send, gather_recv, mate_send, mate_recv, sum_send, sum_recv, own_sem)
-    plane = PlaneExchange(wide_count, own, blocks, parts, from_mate, outgoing, incoming, sems)
+    plane = PlaneExchange(wide_count, own, blocks, parts, from_mate, incoming, sems)
     loads = [
         load_padded(expand.at[0], expand_mat.at[0], load_sems.at[0]),
         load_padded(expand.at[1], expand_mat.at[1], load_sems.at[1]),
@@ -489,6 +504,7 @@
 
     plane.run(compute)
     plane.finish(feed)
+    plane.drain()
     for copy in kept:
         copy.wait()
 
@@ -540,18 +556,18 @@
     rows_all,
     unit_grads,
     hidden_grad,
+    unit_sums,
     blocks,
+    gather_send,
+    gather_recv,
+    own_sem,
     parts,
     from_mate,
-    outgoing,
     incoming,
-    gather_send,
-    gather_recv,
     mate_send,
     mate_recv,
     sum_send,
     sum_recv,
-    own_sem,
     expand_mat,
     reduce_mat,
     slope,
@@ -560,7 +576,7 @@
     keep_sems,
 ):
     sems = (gather_send, gather_recv, mate_send, mate_recv, sum_send, sum_recv, own_sem)
-    plane = PlaneExchange(wide_count, own, blocks, parts, from_mate, outgoing, incoming, sems)
+    plane = PlaneExchange(wide_count, own, blocks, parts, from_mate, incoming, sems)
     loads = [
         load_padded(expand.at[0], expand_mat.at[0], load_sems.at[0]),
         load_padded(expand.at[1], expand_mat.at[1], load_sems.at[1]),
@@ -570,6 +586,7 @@
     ]
     for copy in loads[3:]:
         copy.start()
+    unit_sums[...] = jnp.zeros_like(unit_sums)
     plane.greet()
     kept = []
     waiting = list(loads)
@@ -586,6 +603,8 @@
             upper_grad = pulled * gelu[pair, :, cols].reshape(shape).astype(jnp.float32)
             set_pair(slope, chip, cols, gate_grad)
             set_pair(gelu, chip, cols, upper_grad)
+            unit_sums[0:1, cols] += jnp.sum(gate_grad, axis=0, keepdims=True)
+            unit_sums[1:2, cols] += jnp.sum(upper_grad, axis=0, keepdims=True)
 
         tiles(slope.shape[2], 256, units)
 
@@ -611,6 +630,7 @@
 
     plane.run(compute)
     plane.finish(hidden_grad)
+    plane.drain()
     for copy in kept:
         copy.wait()
 
@@ -634,9 +654,10 @@
             jax.ShapeDtypeStruct((wide_count, rows, width), jnp.bfloat16),
             jax.ShapeDtypeStruct((2, wide_count, rows, padded), jnp.bfloat16),
             jax.ShapeDtypeStruct((rows, width), jnp.float32),
+            jax.ShapeDtypeStruct((2, padded), jnp.float32),
         ),
         in_specs=[anywhere] * 5,
-        out_specs=(anywhere, anywhere, vmem),
+        out_specs=(anywhere, anywhere, vmem, vmem),
         scratch_shapes=scratch,
         compiler_params=pltpu.CompilerParams(
             collective_id=2, has_side_effects=True, vmem_limit_bytes=kernel_memory
@@ -646,6 +667,541 @@
         ),
         name="geglu_backward",
     )(feed_grad, expand_full, reduce_full, slope, gelu)
+
+
+class LineExchange:
+    def __init__(self, narrow_count):
+        self.count = narrow_count
+        self.mine = lax.axis_index("narrow")
+        self.started = []
+
+    def peer(self, offset):
+        return (self.mine + offset) % self.count
+
+    def greet(self, extra=0):
+        barrier = pltpu.get_barrier_semaphore()
+        for offset in range(1, self.count):
+            pl.semaphore_signal(
+                barrier,
+                inc=1,
+                device_id={"narrow": self.peer(offset)},
+                device_id_type=pl.DeviceIdType.MESH,
+            )
+        pl.semaphore_wait(barrier, self.count - 1 + extra)
+
+    def copy(self, source, target, send_sem, recv_sem, where):
+        return pltpu.make_async_remote_copy(
+            src_ref=source,
+            dst_ref=target,
+            send_sem=send_sem,
+            recv_sem=recv_sem,
+            device_id={"narrow": where},
+            device_id_type=pl.DeviceIdType.MESH,
+        )
+
+    def send(self, offset, source, landing, send_sems, recv_sems):
+        peer = self.peer(offset)
+        copy = self.copy(
+            source, landing.at[self.mine], send_sems.at[offset - 1], recv_sems.at[self.mine], peer
+        )
+        copy.start()
+        self.started.append(copy)
+
+    def arrived(self, offset, landing, send_sems, recv_sems):
+        peer = self.peer(offset)
+        self.copy(
+            landing.at[peer], landing.at[peer], send_sems.at[offset - 1], recv_sems.at[peer], peer
+        ).wait_recv()
+
+    def drain(self):
+        for copy in self.started:
+            copy.wait_send()
+
+
+def greet_plane(plane):
+    barrier = pltpu.get_barrier_semaphore()
+    for where in (plane.device(-1), plane.device(1), plane.device(0, True)):
+        pl.semaphore_signal(barrier, inc=1, device_id=where, device_id_type=pl.DeviceIdType.MESH)
+
+
+def rotate_lanes(vectors, cosine, signed_sine):
+    return vectors * cosine + pltpu.roll(vectors, vectors.shape[1] // 2, 1) * signed_sine
+
+
+def attention_backward_kernel(
+    wide_count,
+    narrow_count,
+    attended,
+    merge,
+    mixed,
+    queries,
+    keys,
+    values,
+    probs,
+    cosine,
+    signed_sine,
+    triple,
+    merge_grad,
+    heads_sums,
+    merge_sums,
+    upstream,
+    outbound,
+    probs_held,
+    keys_turned,
+    key_total,
+    value_total,
+    merge_out,
+    merge_in,
+    mixed_send,
+    mixed_recv,
+    merge_send,
+    merge_recv,
+    load_sems,
+    parts,
+    from_mate,
+    incoming,
+    mate_send,
+    mate_recv,
+    sum_send,
+    sum_recv,
+):
+    sems = (None, None, mate_send, mate_recv, sum_send, sum_recv, None)
+    plane = PlaneExchange(wide_count, None, None, parts, from_mate, incoming, sems)
+    line = LineExchange(narrow_count)
+    rows, width = attended.shape
+    own_cols = queries.shape[1]
+    heads = own_cols // HDIM
+    scale = HDIM ** (-0.5)
+
+    def load(head):
+        return pltpu.make_async_copy(
+            probs.at[head], probs_held.at[head % 2], load_sems.at[head % 2]
+        )
+
+    load(0).start()
+    greet_plane(plane)
+    line.greet(3)
+
+    def mixed_part(target, where):
+        part = dot(
+            attended[...],
+            merge[pl.ds(pl.multiple_of(where * own_cols, own_cols), own_cols)],
+            ((1,), (1,)),
+        )
+        target[...] = part.astype(jnp.bfloat16)
+
+    for offset in range(1, narrow_count):
+        place = line.peer(offset)
+        mixed_part(outbound.at[offset - 1], place)
+        line.send(offset, outbound.at[offset - 1], upstream, mixed_send, mixed_recv)
+    mixed_part(upstream.at[line.mine], line.mine)
+
+    block = parts.shape[1]
+
+    def merge_rows(i, carry):
+        cols = pl.ds(pl.multiple_of(i * block, block), block)
+        parts[i] = dot(mixed[:, cols], attended[...], ((0,), (0,))).astype(jnp.bfloat16)
+        return carry
+
+    lax.fori_loop(0, wide_count, merge_rows, 0)
+    for offset in range(plane.ring):
+        plane.share(offset)
+    merge_sums[...] = jnp.sum(attended[...].astype(jnp.float32), axis=0, keepdims=True)
+    plane.first_sums()
+    plane.far_sums()
+    for offset in range(1, narrow_count):
+        line.arrived(offset, upstream, mixed_send, mixed_recv)
+
+    def one_head(head):
+        cols = pl.ds(head * HDIM, HDIM)
+        load(head).wait()
+        if head + 1 < heads:
+            load(head + 1).start()
+        held = probs_held.at[head % 2]
+        keys_turned[...] = keys[:, cols].astype(jnp.float32).T.astype(jnp.bfloat16)
+        key_total[...] = jnp.zeros_like(key_total)
+        value_total[...] = jnp.zeros_like(value_total)
+
+        def chunk(i, carry):
+            here = pl.ds(pl.multiple_of(i * rows, rows), rows)
+            weights_low = held[:, here]
+            up = upstream[i, :, cols]
+            pulled = dot(values[:, cols], up, ((1,), (1,)))
+            weights = weights_low.astype(jnp.float32)
+            scaled = weights * pulled
+            change = (scaled - weights * jnp.sum(scaled, axis=0, keepdims=True)).astype(
+                jnp.bfloat16
+            )
+            key_total[...] += dot(change, queries[here, cols], ((1,), (0,)))
+            value_total[...] += dot(weights_low, up, ((1,), (0,)))
+            query_grad = dot(keys_turned[...], change, ((1,), (0,))).T * scale
+            triple[here, cols] = rotate_lanes(
+                query_grad, cosine[here], signed_sine[here]
+            ).astype(jnp.bfloat16)
+            return carry
+
+        lax.fori_loop(0, narrow_count, chunk, 0)
+
+        def ending(i, carry):
+            here = pl.ds(pl.multiple_of(i * rows, rows), rows)
+            triple[here, pl.ds(own_cols + head * HDIM, HDIM)] = rotate_lanes(
+                key_total[here] * scale, cosine[here], signed_sine[here]
+            ).astype(jnp.bfloat16)
+            triple[here, pl.ds(2 * own_cols + head * HDIM, HDIM)] = value_total[here].astype(
+                jnp.bfloat16
+            )
+            return carry
+
+        lax.fori_loop(0, narrow_count, ending, 0)
+
+    for head in range(heads):
+        one_head(head)
+        if head == heads // 2 - 1:
+            plane.last_sums()
+    total = merge_out.at[...]
+    plane.finish(merge_out)
+    count = merge_grad.shape[0]
+
+    def z_rows(where):
+        return pl.ds(pl.multiple_of(where * count, count), count)
+
+    for offset in range(1, narrow_count):
+        line.send(
+            offset, total.at[z_rows(line.peer(offset))], merge_in, merge_send, merge_recv
+        )
+
+    def column_sums(cols):
+        heads_sums[:, cols] = jnp.sum(
+            triple[:, cols].astype(jnp.float32), axis=0, keepdims=True
+        )
+
+    tiles(3 * own_cols, 256, column_sums)
+    summed = merge_out[z_rows(line.mine)].astype(jnp.float32)
+    for offset in range(1, narrow_count):
+        line.arrived(offset, merge_in, merge_send, merge_recv)
+        summed += merge_in[line.peer(offset)].astype(jnp.float32)
+    merge_grad[...] = summed
+    line.drain()
+    plane.drain()
+
+
+def attention_backward(
+    wide_count,
+    narrow_count,
+    attended_grad,
+    merge_full,
+    mixed,
+    queries,
+    keys,
+    values,
+    probs,
+    cosine,
+    signed_sine,
+):
+    rows, width = attended_grad.shape
+    bucket, own_cols = queries.shape
+    block = width // wide_count
+    count = block // narrow_count
+    anywhere = pl.BlockSpec(memory_space=pl.ANY)
+    vmem = pl.BlockSpec(memory_space=pltpu.VMEM)
+    dma = pltpu.SemaphoreType.DMA
+    return pl.pallas_call(
+        functools.partial(attention_backward_kernel, wide_count, narrow_count),
+        out_shape=(
+            jax.ShapeDtypeStruct((bucket, 3 * own_cols), jnp.bfloat16),
+            jax.ShapeDtypeStruct((count, width), jnp.float32),
+            jax.ShapeDtypeStruct((1, 3 * own_cols), jnp.float32),
+            jax.ShapeDtypeStruct((1, width), jnp.float32),
+        ),
+        in_specs=[vmem] * 6 + [anywhere] + [vmem] * 2,
+        out_specs=(vmem, vmem, vmem, vmem),
+        scratch_shapes=[
+            pltpu.VMEM((narrow_count, rows, own_cols), jnp.bfloat16),
+            pltpu.VMEM((narrow_count - 1, rows, own_cols), jnp.bfloat16),
+            pltpu.VMEM((2, bucket, bucket), jnp.bfloat16),
+            pltpu.VMEM((HDIM, bucket), jnp.bfloat16),
+            pltpu.VMEM((bucket, HDIM), jnp.float32),
+            pltpu.VMEM((bucket, HDIM), jnp.float32),
+            pltpu.VMEM((block, width), jnp.bfloat16),
+            pltpu.VMEM((narrow_count, count, width), jnp.bfloat16),
+            dma((narrow_count - 1,)),
+            dma((narrow_count,)),
+            dma((narrow_count - 1,)),
+            dma((narrow_count,)),
+            dma((2,)),
+        ]
+        + sum_scratch(wide_count, block, width),
+        compiler_params=pltpu.CompilerParams(
+            collective_id=3, has_side_effects=True, vmem_limit_bytes=kernel_memory
+        ),
+        cost_estimate=pl.CostEstimate(
+            flops=60 * 10**9, bytes_accessed=200 * 2**20, transcendentals=0
+        ),
+        name="attention_backward",
+    )(
+        attended_grad, merge_full, mixed, queries, keys, values, probs, cosine, signed_sine
+    )
+
+
+def input_backward_kernel(
+    wide_count,
+    narrow_count,
+    inputs,
+    triple,
+    heads_mat,
+    small,
+    input_part,
+    heads_grad,
+    small_out,
+    line_parts,
+    line_in,
+    heads_out,
+    heads_in,
+    small_wide,
+    small_sum,
+    small_line,
+    line_send,
+    line_recv,
+    heads_send,
+    heads_recv,
+    wide_send,
+    wide_recv,
+    small_send,
+    small_recv,
+    parts,
+    from_mate,
+    incoming,
+    mate_send,
+    mate_recv,
+    sum_send,
+    sum_recv,
+):
+    sems = (None, None, mate_send, mate_recv, sum_send, sum_recv, None)
+    plane = PlaneExchange(wide_count, None, None, parts, from_mate, incoming, sems)
+    line = LineExchange(narrow_count)
+    rows, width = input_part.shape
+    here = line.mine
+    last = narrow_count - 1
+    place = lax.axis_index("wide")
+
+    def wide_peer(offset):
+        return (place + offset) % wide_count
+
+    barrier = pltpu.get_barrier_semaphore()
+    for offset in range(1, wide_count):
+        pl.semaphore_signal(
+            barrier,
+            inc=1,
+            device_id={"wide": wide_peer(offset)},
+            device_id_type=pl.DeviceIdType.MESH,
+        )
+    line.greet(wide_count - 1)
+
+    def small_copy(offset, source, slot):
+        return pltpu.make_async_remote_copy(
+            src_ref=source,
+            dst_ref=small_wide.at[slot],
+            send_sem=wide_send.at[offset - 1],
+            recv_sem=wide_recv.at[slot],
+            device_id={"wide": wide_peer(offset)},
+            device_id_type=pl.DeviceIdType.MESH,
+        )
+
+    small_copies = [
+        small_copy(offset, small.at[wide_peer(offset)], place) for offset in range(1, wide_count)
+    ]
+    for copy in small_copies:
+        copy.start()
+
+    def input_cols(cols):
+        part = dot(triple[...], heads_mat[cols], ((1,), (1,)))
+        for index in range(narrow_count):
+            line_parts[index, :, cols] = part[index * rows : (index + 1) * rows].astype(
+                jnp.bfloat16
+            )
+
+    tiles(width, 256, input_cols)
+
+    def line_copy(way, offset):
+        target = here + offset if way == 0 else here - offset
+        return line.copy(
+            line_parts.at[target],
+            line_in.at[way, offset - 1],
+            line_send.at[way, offset - 1],
+            line_recv.at[way, offset - 1],
+            here + 1 if way == 0 else here - 1,
+        )
+
+    def line_arrived(way, offset):
+        landing = line_in.at[way, offset]
+        line.copy(
+            landing, landing, line_send.at[way, offset], line_recv.at[way, offset], here
+        ).wait_recv()
+
+    def add_line(way, offset, slot):
+        def chunk(i, carry):
+            some = pl.ds(pl.multiple_of(i * 16, 16), 16)
+            line_parts[slot, some] = (
+                line_parts[slot, some].astype(jnp.float32)
+                + line_in[way, offset, some].astype(jnp.float32)
+            ).astype(jnp.bfloat16)
+            return carry
+
+        lax.fori_loop(0, rows // 16, chunk, 0)
+
+    def line_step(offset):
+        for way in range(2):
+            reaches = here + offset <= last if way == 0 else here - offset >= 0
+            follows = here > 0 if way == 0 else here < last
+
+            @pl.when(reaches)
+            def _():
+                if offset < last:
+
+                    @pl.when(follows)
+                    def _():
+                        line_arrived(way, offset)
+                        add_line(way, offset, here + offset if way == 0 else here - offset)
+
+                line_copy(way, offset).start()
+
+    line_step(last)
+
+    block = parts.shape[1]
+
+    def heads_rows(i, carry):
+        cols = pl.ds(pl.multiple_of(i * block, block), block)
+        parts[i] = dot(inputs[:, cols], triple[...], ((0,), (0,))).astype(jnp.bfloat16)
+        return carry
+
+    lax.fori_loop(0, wide_count, heads_rows, 0)
+    for offset in range(plane.ring):
+        plane.share(offset)
+    for offset in range(last - 1, last // 2, -1):
+        line_step(offset)
+    plane.first_sums()
+    plane.far_sums()
+
+    for offset in range(1, wide_count):
+        peer = wide_peer(offset)
+        small_copy(offset, small_wide.at[peer], peer).wait_recv()
+    small_wide[place] = small[place]
+    total = small_wide[0]
+    for index in range(1, wide_count):
+        total += small_wide[index]
+    small_sum[...] = total
+    for offset in range(1, narrow_count):
+        line.send(offset, small_sum.at[line.peer(offset)], small_line, small_send, small_recv)
+
+    plane.last_sums()
+    for offset in range(last // 2, 0, -1):
+        line_step(offset)
+    plane.finish(heads_out)
+    count = heads_grad.shape[0]
+
+    def z_rows(where):
+        return pl.ds(pl.multiple_of(where * count, count), count)
+
+    for offset in range(1, narrow_count):
+        line.send(
+            offset, heads_out.at[z_rows(line.peer(offset))], heads_in, heads_send, heads_recv
+        )
+    heads_in[line.mine] = heads_out[z_rows(line.mine)]
+    small_line[line.mine] = small_sum[line.mine]
+    for offset in range(1, narrow_count):
+        line.arrived(offset, small_line, small_send, small_recv)
+    result = small_line[0]
+    for index in range(1, narrow_count):
+        result += small_line[index]
+    small_out[...] = result
+
+    def own_rows(i, carry):
+        some = pl.ds(pl.multiple_of(i * 16, 16), 16)
+        input_part[some] = line_parts[here, some].astype(jnp.float32)
+        return carry
+
+    lax.fori_loop(0, rows // 16, own_rows, 0)
+    for way in range(2):
+        follows = here > 0 if way == 0 else here < last
+
+        @pl.when(follows)
+        def _():
+            line_arrived(way, 0)
+
+            def chunk(i, carry):
+                some = pl.ds(pl.multiple_of(i * 16, 16), 16)
+                input_part[some] += line_in[way, 0, some].astype(jnp.float32)
+                return carry
+
+            lax.fori_loop(0, rows // 16, chunk, 0)
+
+    for offset in range(1, narrow_count):
+        line.arrived(offset, heads_in, heads_send, heads_recv)
+    own_cols = triple.shape[1] // 3
+    for index in range(narrow_count):
+        for which in range(3):
+            start = (which * narrow_count + index) * own_cols
+            heads_grad[:, start : start + own_cols] = heads_in[
+                index, :, which * own_cols : (which + 1) * own_cols
+            ].astype(jnp.float32)
+    for offset in range(1, narrow_count):
+        for way in range(2):
+            reaches = here + offset <= last if way == 0 else here - offset >= 0
+
+            @pl.when(reaches)
+            def _():
+                line_copy(way, offset).wait_send()
+
+    for copy in small_copies:
+        copy.wait_send()
+    line.drain()
+    plane.drain()
+
+
+def input_backward(wide_count, narrow_count, inputs, triple_grad, heads_mat, small):
+    bucket, width = inputs.shape
+    rows = bucket // narrow_count
+    columns = triple_grad.shape[1]
+    block = width // wide_count
+    count = block // narrow_count
+    vmem = pl.BlockSpec(memory_space=pltpu.VMEM)
+    dma = pltpu.SemaphoreType.DMA
+    lines = small.shape[2]
+    return pl.pallas_call(
+        functools.partial(input_backward_kernel, wide_count, narrow_count),
+        out_shape=(
+            jax.ShapeDtypeStruct((rows, width), jnp.float32),
+            jax.ShapeDtypeStruct((count, narrow_count * columns), jnp.float32),
+            jax.ShapeDtypeStruct((lines, 128), jnp.float32),
+        ),
+        in_specs=[vmem] * 4,
+        out_specs=(vmem, vmem, vmem),
+        scratch_shapes=[
+            pltpu.VMEM((narrow_count, rows, width), jnp.bfloat16),
+            pltpu.VMEM((2, narrow_count - 1, rows, width), jnp.bfloat16),
+            pltpu.VMEM((block, columns), jnp.bfloat16),
+            pltpu.VMEM((narrow_count, count, columns), jnp.bfloat16),
+            pltpu.VMEM((wide_count, narrow_count, lines, 128), jnp.float32),
+            pltpu.VMEM((narrow_count, lines, 128), jnp.float32),
+            pltpu.VMEM((narrow_count, lines, 128), jnp.float32),
+            dma((2, narrow_count - 1)),
+            dma((2, narrow_count - 1)),
+            dma((narrow_count - 1,)),
+            dma((narrow_count,)),
+            dma((wide_count - 1,)),
+            dma((wide_count,)),
+            dma((narrow_count - 1,)),
+            dma((narrow_count,)),
+        ]
+        + sum_scratch(wide_count, block, columns),
+        compiler_params=pltpu.CompilerParams(
+            collective_id=4, has_side_effects=True, vmem_limit_bytes=kernel_memory
+        ),
+        cost_estimate=pl.CostEstimate(
+            flops=80 * 10**9, bytes_accessed=200 * 2**20, transcendentals=0
+        ),
+        name="input_backward",
+    )(inputs, triple_grad, heads_mat, small)
 
 
 def shards(
@@ -703,13 +1259,13 @@
     keys = low(rotate(triple[:, 1], cosine, sine_table))
     values = low(triple[:, 2])
     scores = (
-        jnp.einsum("qgd,kgd->gqk", queries, keys, preferred_element_type=jnp.float32) * score_scale
-    )
-    scores = jnp.where(key_mask[None], scores, masked_value)
-    expo = jnp.exp(scores - jnp.max(scores, axis=-1, keepdims=True))
-    probs_low = low(expo / jnp.sum(expo, axis=-1, keepdims=True))
+        jnp.einsum("kgd,qgd->gkq", keys, queries, preferred_element_type=jnp.float32) * score_scale
+    )
+    scores = jnp.where(key_mask.T[None], scores, masked_value)
+    expo = jnp.exp(scores - jnp.max(scores, axis=1, keepdims=True))
+    probs_low = low(expo / jnp.sum(expo, axis=1, keepdims=True))
     mixed_own = low(
-        jnp.einsum("gqk,kgd->qgd", probs_low, values, preferred_element_type=jnp.float32)
+        jnp.einsum("gkq,kgd->qgd", probs_low, values, preferred_element_type=jnp.float32)
     ).reshape(bucket_len, own_cols)
     mixed = lax.all_to_all(mixed_own, "narrow", split_axis=0, concat_axis=1, tiled=True)
     attended = dot(mixed, merge_full, ((1,), (0,))) + merge_shift
@@ -747,7 +1303,7 @@
     shift_two_grad = jnp.sum(grad_out, axis=0)
     sum_two_grad = normalize_back(grad_out, normed_two, inv_two, gains[1])
     feed_grad = low(sum_two_grad)
-    feed_grads_all, unit_grads, hidden_part = geglu_backward(
+    feed_grads_all, unit_grads, hidden_part, unit_sums = geglu_backward(
         wide_count, feed_grad, expand_full, reduce_full, slope, gelu
     )
     tokens_all = wide_count * tok_rows
@@ -756,6 +1312,9 @@
     unit_grads = unit_grads.reshape(2, tokens_all, padded)
     reduce_part = low(dot(active.reshape(tokens_all, padded), feed_grads_all, ((0,), (0,))))[:share]
     expand_part = low(dot(unit_grads, rows_all, ((1,), (0,))))[:, :share]
+    reduce_part, expand_part, hidden_part = lax.optimization_barrier(
+        (reduce_part, expand_part, hidden_part)
+    )
     reduce_weight_gradient = lax.psum_scatter(
         reduce_part, "narrow", scatter_dimension=1, tiled=True
     ).astype(jnp.float32)
@@ -769,69 +1328,32 @@
     shift_one_grad = jnp.sum(hidden_grad, axis=0)
     sum_one_grad = normalize_back(hidden_grad, normed_one, inv_one, gains[0])
     attended_grad = low(sum_one_grad)
-    mixed_grad = low(dot(attended_grad, merge_full, ((1,), (1,))))
-    upstream = lax.all_to_all(
-        mixed_grad, "narrow", split_axis=1, concat_axis=0, tiled=True
-    ).reshape(bucket_len, own_heads, HDIM)
-    merge_part = low(dot(mixed, attended_grad, ((0,), (0,))))
-    merge_weight_gradient = lax.psum_scatter(
-        merge_part, both_axes, scatter_dimension=0, tiled=True
-    ).astype(jnp.float32)
-    probs_grad = jnp.einsum("qgd,kgd->gqk", upstream, values, preferred_element_type=jnp.float32)
-    probs = probs_low.astype(jnp.float32)
-    scores_grad = low(probs * (probs_grad - jnp.sum(probs * probs_grad, axis=-1, keepdims=True)))
-    query_grads = (
-        jnp.einsum("gqk,kgd->qgd", scores_grad, keys, preferred_element_type=jnp.float32)
-        * score_scale
-    )
-    key_grads = (
-        jnp.einsum("gqk,qgd->kgd", scores_grad, queries, preferred_element_type=jnp.float32)
-        * score_scale
-    )
-    value_grads = jnp.einsum("gqk,qgd->kgd", probs_low, upstream, preferred_element_type=jnp.float32)
-    triple_grad = low(
-        jnp.stack(
-            [
-                rotate(query_grads, cosine, -sine_table),
-                rotate(key_grads, cosine, -sine_table),
-                value_grads,
-            ],
-            axis=1,
-        )
-    ).reshape(bucket_len, 3 * own_cols)
-    input_part = lax.psum_scatter(
-        low(dot(triple_grad, heads_mat, ((1,), (1,)))), "narrow", scatter_dimension=0, tiled=True
-    )
-    input_gradient = residual_scale * sum_one_grad + input_part.astype(jnp.float32)
-    heads_part = lax.psum_scatter(
-        low(dot(rows_input, triple_grad, ((0,), (0,)))), "wide", scatter_dimension=0, tiled=True
-    )
-    heads_weight_gradient = (
-        lax.all_to_all(
-            heads_part.reshape(narrow_count, -1, 3 * own_cols),
-            "narrow",
-            split_axis=0,
-            concat_axis=0,
-            tiled=True,
-        )
-        .reshape(narrow_count, -1, 3, own_cols)
-        .transpose(1, 2, 0, 3)
-        .reshape(heads_weight.shape)
-        .astype(jnp.float32)
+    triple_grad, merge_weight_gradient, heads_sums, merge_sums = attention_backward(
+        wide_count,
+        narrow_count,
+        attended_grad,
+        merge_full,
+        mixed,
+        queries.reshape(bucket_len, own_cols),
+        keys.reshape(bucket_len, own_cols),
+        values.reshape(bucket_len, own_cols),
+        probs_low,
+        jnp.concatenate([cosine[:, 0], cosine[:, 0]], axis=1),
+        jnp.concatenate([sine_table[:, 0], -sine_table[:, 0]], axis=1),
     )
 
     mine_narrow = (jnp.arange(narrow_count) == narrow_index).astype(jnp.float32)
     mine_wide = (jnp.arange(wide_count) == lax.axis_index("wide")).astype(jnp.float32)
-    heads_sums = jnp.sum(triple_grad, axis=0, dtype=jnp.float32).reshape(3, 1, own_cols)
+    heads_sums = heads_sums.reshape(3, 1, own_cols)
     heads_sums = (heads_sums * mine_narrow[None, :, None]).reshape(count, -1)
-    merge_sums = jnp.sum(attended_grad, axis=0, dtype=jnp.float32).reshape(count, -1)
+    merge_sums = merge_sums.reshape(count, -1)
     norm_sums = (
         jnp.stack([gain_one_grad, gain_two_grad, shift_one_grad, shift_two_grad])
         .reshape(4, count, -1)
         .transpose(1, 0, 2)
         .reshape(count, -1)
     )
-    expand_sums = jnp.sum(unit_grads, axis=1, dtype=jnp.float32)[:, :share]
+    expand_sums = unit_sums[:, :share]
     expand_sums = (
         expand_sums.reshape(2, narrow_count, -1).transpose(1, 0, 2).reshape(1, narrow_count, -1)
         * mine_wide[:, None, None]
@@ -841,9 +1363,18 @@
         reduce_sums, (wide_count, narrow_count, reduce_sums.shape[2])
     ).reshape(count, -1)
     pieces = (heads_sums, merge_sums, norm_sums, expand_sums, reduce_sums)
-    summed = lax.psum_scatter(
-        jnp.concatenate(pieces, axis=1), both_axes, scatter_dimension=0, tiled=True
-    )[0]
+    packed = jnp.concatenate(pieces, axis=1)
+    packed = jnp.pad(packed, ((0, 0), (0, -packed.shape[1] % 1024)))
+    input_part, heads_weight_gradient, summed = input_backward(
+        wide_count,
+        narrow_count,
+        rows_input,
+        triple_grad,
+        heads_mat,
+        packed.reshape(wide_count, narrow_count, -1, 128),
+    )
+    input_gradient = residual_scale * sum_one_grad + input_part
+    summed = summed.reshape(-1)
     ends = []
     start = 0
     for piece in pieces:

time: 1320 us -> 933 us (0.71)
  waiting for transfers between devices: 735 us -> 199 us
  Pallas kernels: 171 us -> 431 us
  matrix products: 115 us -> 59.8 us
  blocking collectives: 138 us -> 111 us
    pallas_call x0 -> x2, Pallas kernels: none -> 260 us  [the longest x1 137 us: attention_backward(): pl.pallas_call(functools.partial(attention_backward_kernel, wide_count, n...]
    reduce_scatter x3 -> x0, waiting for transfers between devices: 255 us -> none  [the longest x1 176 us: shards(): lax.psum_scatter(merge_part, both_axes, scatter_dimension=0, tiled=True)]
    unnamed x12 -> x7, waiting for transfers between devices: 133 us -> 2.47 us
    reduce_scatter x1, waiting for transfers between devices: 100 us -> 0.01 us  [shards(): lax.psum_scatter(expand_part, 'narrow', scatter_dimension=2, tiled=True)]
    reduce_scatter x1, waiting for transfers between devices: 49 us -> 0.01 us  [shards(): lax.psum_scatter(reduce_part, 'narrow', scatter_dimension=1, tiled=True)]
    dot_general x8 -> x4, matrix products: 81.6 us -> 45.5 us  [dot(): lax.dot_general(left, right, (dims, ((), ())), preferred_element_type=jnp...]
    all_to_all x1 -> x0, blocking collectives: 27.6 us -> none  [shards(): lax.all_to_all(mixed_grad, 'narrow', split_axis=1, concat_axis=0, tiled=T...]
    dot_general x5 -> x1, matrix products: 20.7 us -> 1.26 us  [shards(): jnp.einsum('gkq,kgd->qgd', probs_low, values, preferred_element_type=jnp....]
  transfers between devices with their start and end apart: 13 -> 8, of which waited for: 10 -> 4; matrix products, arithmetic and copies ran while one was open for 12% -> 12% of each run, Pallas kernels for 0% -> 28%
where the time goes in v3:
time: 933 us; the launch traced here: 929 us
  Pallas kernels  431 us (46%)
  waiting for transfers between devices  199 us (21%)
  blocking collectives  111 us (12%)
  matrix products  59.8 us (6%)
  local copies, waits for them, and re-layouts  53.9 us (6%)
  other arithmetic  52.1 us (6%)
  between operations  16.9 us (2%)
    pallas_call x1, Pallas kernels, attention_backward(): pl.pallas_call(functools.partial(attention_backward_kernel, wide_count, n...  137 us
    pallas_call x1, Pallas kernels, input_backward(): pl.pallas_call(functools.partial(input_backward_kernel, wide_count, narro...  123 us
    all_gather x1, waiting for transfers between devices, shards(): lax.all_gather(jnp.pad(expand_weight.transpose(1, 2, 0), ((0, 0), (0, til...  104 us
    pallas_call x1, Pallas kernels, geglu_forward(): pl.pallas_call(functools.partial(geglu_forward_kernel, wide_count), out_s...  87.5 us
    pallas_call x1, Pallas kernels, geglu_backward(): pl.pallas_call(functools.partial(geglu_backward_kernel, wide_count), out_...  83.7 us
    all_gather x1, blocking collectives, gather_small(): lax.all_gather(packed, both_axes, axis=0, tiled=True).astype(jnp.float32)  69.7 us
    dot_general x4, matrix products, dot(): lax.dot_general(left, right, (dims, ((), ())), preferred_element_type=jnp...  45.5 us
    all_gather x1, waiting for transfers between devices, shards(): lax.all_gather(jnp.pad(reduce_weight, ((0, tile_rows), (0, 0))), 'narrow'...  45.1 us
  transfers between devices with their start and end apart: 8, of which 4 were waited for; matrix products, arithmetic and copies ran while one was open for 12% of the time, Pallas kernels for 28%

profile of v3, /device:TPU:8, one launch (start us, length us, event | category | flops | bytes accessed | tf_op | source)
XLA Modules:
  0.0 929.1 jit_solution(12957738496365357569)
XLA Ops:
  10.4 41.1 %all_to_all.24 = bf16[4,64,3,512]{3,1,2,0:T(8,128)(2,1)S(1)} all-to-all(bf16[4,64,3,512]{3,1,2,0:T(8,128)(2,1)S(1)} %copy.61), channel_id=1, replica_groups=mesh['wide'=8,'narrow'=4] {'narrow'}, dimensions={0} | all-to-all | bytes 1572864 | tf_op jit(solution)/shard_map/all_to_all | solution.py:1241
  57.0 69.7 %all-gather = bf16[32,1,1368]{2,1,0:T(2,128)(2,1)S(1)} all-gather(bf16[1,1,1368]{2,1,0:T(2,128)(2,1)S(1)} %bitcast.95), channel_id=1, replica_groups=mesh['wide'=8,'narrow'=4] {'wide','narrow'}, dimensions={0}, use_global_device_ids=true | all-gather | bytes 90288 | tf_op jit(solution)/shard_map/all_gather | solution.py:94
  134.8 18.3 %all-gather.9.cloned.1.call-done.heads_mat = bf16[2048,1536]{1,0:T(8,128)(2,1)} async-done(((bf16[256,1536]{1,0:T(8,128)(2,1)}), bf16[2048,1536]{1,0:T(8,128)(2,1)}) %all-gather.9.cloned.1.call-update) | async-done | bytes 6291472 | tf_op jit(solution)/shard_map/all_gather | solution.py:1248
  153.1 11.7 %convolution_add_fusion = f32[1024,1536]{1,0:T(8,128)} fusion(bf16[1024,2048]{1,0:T(8,128)(2,1)} %all-gather.7.cloned.1.call-done.inputs, bf16[2048,1536]{1,0:T(8,128)(2,1)} %all-gather.9.cloned.1.call-done.heads_mat, f32[1536]{0:T(1024)S(1)} %add.104), kind=kOutput, calls=%fused_computation.13 | convolution fusion | flops 6444023808 | bytes 16783360 | tf_op jit(solution)/shard_map/dot_general | solution.py:81
  164.8 7.7 reshape.373
  175.4 3.8 fusion.32
  186.0 13.1 %fusion.35 = (f32[4,1024]{1,0:T(4,128)S(1)}, f32[4,1024,1024]{2,1,0:T(8,128)}) fusion(pred[1024,1024]{1,0:T(8,128)(4,1)} %or_and_fusion, bf16[1024,4,64]{2,0,1:T(8,128)(2,1)} %get-tuple-element.74, bf16[1024,4,64]{2,0,1:T(8,128)(2,1)} %get-tuple-element.73, bf16[1024,4,64]{2,0,1:T(8,128)(2,1)S(1)} %get-tuple-element.78, ...), kind=kOutput, calls=%fused_computation.102 | convolution fusion | flops 1094714368 | bytes 19939328 | tf_op jit(solution)/shard_map/sub | solution.py:1265
  199.1 8.5 divide_convert_fusion.probs
  207.6 3.2 copy-done.3
  214.6 5.2 all-to-all-start.1
  221.5 28.9 %all-to-all-done.1 = bf16[4,256,512]{2,1,0:T(8,128)(2,1)S(1)} async-done(((bf16[4,256,512]{2,1,0:T(8,128)(2,1)}), bf16[4,256,512]{2,1,0:T(8,128)(2,1)S(1)}, u32[]{:S(2)}, u32[]{:S(2)}) %all-to-all-start.1) | async-done | bytes 1048608 | tf_op jit(solution)/shard_map/all_to_all | solution.py:1270
  250.5 6.2 fusion.36
  259.5 45.1 %all-gather.15.cloned.1.call-done.reduce = bf16[688,2048]{1,0:T(8,128)(2,1)} async-done(((bf16[688,512]{1,0:T(8,128)(2,1)}), bf16[688,2048]{1,0:T(8,128)(2,1)}) %all-gather.15.cloned.1.call-update) | async-done | bytes 2818064 | tf_op jit(solution)/shard_map/all_gather | solution.py:1285
  304.6 103.9 %all-gather.13.cloned.1.call-done.expand = bf16[2,688,2048]{2,1,0:T(8,128)(2,1)} async-done(((bf16[2,688,512]{2,1,0:T(8,128)(2,1)}), bf16[2,688,2048]{2,1,0:T(8,128)(2,1)}) %all-gather.13.cloned.1.call-update) | async-done | bytes 5636112 | tf_op jit(solution)/shard_map/all_gather | solution.py:1279
  408.5 87.5 %geglu_forward.1 = (bf16[8,256,2048]{2,1,0:T(8,128)(2,1)}, bf16[8,256,768]{2,1,0:T(8,128)(2,1)}, bf16[8,256,768]{2,1,0:T(8,128)(2,1)}, bf16[8,256,768]{2,1,0:T(8,128)(2,1)}, f32[256,2048]{1,0:T(8,128)}) custom-call(bf16[256,2048]{1,0:T(8,128)(2,1)} %fusion.18.own, bf16[2,688,2048]{2,1,0:T(8,128)(2,1)} %all-gather.13.cloned.1.call-done.expand, ...), custom_call_target="tpu_custom_call" | custom-call | flops 19327352832 | bytes 209715200 | tf_op jit(solution)/shard_map/geglu_forward/pallas_call | solution.py:527
  502.8 83.7 %geglu_backward.1 = (bf16[8,256,2048]{2,1,0:T(8,128)(2,1)}, bf16[2,8,256,768]{3,2,1,0:T(8,128)(2,1)}, f32[256,2048]{1,0:T(8,128)}, f32[2,768]{1,0:T(2,128)}) custom-call(bf16[256,2048]{1,0:T(8,128)(2,1)} %get-tuple-element.65.own, bf16[2,688,2048]{2,1,0:T(8,128)(2,1)} %all-gather.13.cloned.1.call-done.expand, ...), custom_call_target="tpu_custom_call" | custom-call | flops 19327352832 | bytes 209715200 | tf_op jit(solution)/shard_map/geglu_backward/pallas_call | solution.py:651
  586.6 17.4 %fusion.7 = bf16[2,768,2048]{2,1,0:T(8,128)(2,1)S(1)} fusion(bf16[2,8,256,768]{3,2,1,0:T(8,128)(2,1)} %get-tuple-element.36, bf16[8,256,2048]{2,1,0:T(8,128)(2,1)} %get-tuple-element.37), kind=kOutput, calls=%fused_computation.12 | convolution fusion | flops 12884901888 | bytes 20971520 | tf_op jit(solution)/shard_map/dot_general | solution.py:81
  607.0 10.1 %convolution_bitcast_fusion = bf16[768,2048]{1,0:T(8,128)(2,1)S(1)} fusion(bf16[8,256,768]{2,1,0:T(8,128)(2,1)} %get-tuple-element.32, bf16[8,256,2048]{2,1,0:T(8,128)(2,1)} %get-tuple-element.35), kind=kOutput, calls=%fused_computation.15 | convolution fusion | flops 6442450944 | bytes 14680064 | tf_op jit(solution)/shard_map/dot_general | solution.py:81
  624.5 3.7 copy_bitcast_fusion.3.queries
  634.7 4.0 fusion.30
  638.7 137.3 %attention_backward.1 = (bf16[1024,1536]{1,0:T(8,128)(2,1)}, f32[64,2048]{1,0:T(8,128)}, f32[1,1536]{1,0:T(1,128)}, f32[1,2048]{1,0:T(1,128)}) custom-call(bf16[256,2048]{1,0:T(8,128)(2,1)} %get-tuple-element.66.attended, bf16[2048,2048]{1,0:T(8,128)(2,1)} %all-gather.11.cloned.1.call-done.merge, bf16[256,2048]{1,0:T(8,128)(2,1)} %bitcast.83, ...), custom_call_target="tpu_custom_call" | custom-call | flops 60000002048 | bytes 209715200 | tf_op jit(solution)/shard_map/attention_backward/pallas_call | solution.py:908
  780.6 123.0 %input_backward.1 = (f32[256,2048]{1,0:T(8,128)}, f32[64,6144]{1,0:T(8,128)}, f32[16,128]{1,0:T(8,128)}) custom-call(bf16[1024,2048]{1,0:T(8,128)(2,1)} %all-gather.7.cloned.1.call-done.inputs, bf16[1024,1536]{1,0:T(8,128)(2,1)} %get-tuple-element.40.triple, bf16[2048,1536]{1,0:T(8,128)(2,1)} %all-gather.9.cloned.1.call-done.heads_mat, ...), custom_call_target="tpu_custom_call" | custom-call | flops 80000000000 | bytes 209715200 | tf_op jit(solution)/shard_map/input_backward/pallas_call | solution.py:1170
  910.8 3.2 multiply_add_fusion
  916.4 3.4 convert_bitcast_fusion
  (178 shorter events, 72.5 us)
Async XLA Ops:
  7.2 127.6 %all-gather.7.cloned.1.call-start = ((), (), s32[]{:S(2)}) async-start(), calls=%async_computation.4 | async-start | bytes 5242880 | tf_op jit(solution)/shard_map/all_gather | solution.py:1240
  7.9 145.2 %all-gather.9.cloned.1.call-start = ((), (), s32[]{:S(2)}) async-start(), calls=%async_computation.5 | async-start | bytes 7077888 | tf_op jit(solution)/shard_map/all_gather | solution.py:1248
  52.2 3.8 copy-start.23
  52.2 3.9 copy-start.24
  52.2 4.0 copy-start.25
  52.2 3.9 copy-start.19
  52.2 4.5 copy-start.21
  52.3 4.6 copy-start.20
  52.3 4.6 copy-start.22
  53.4 197.1 %all-gather.11.cloned.1.call-start = ((), (), s32[]{:S(2)}) async-start(), calls=%async_computation.6 | async-start | bytes 8650752 | tf_op jit(solution)/shard_map/all_gather | solution.py:1252
  54.1 250.5 %all-gather.15.cloned.1.call-start = ((), (), s32[]{:S(2)}) async-start(), calls=%async_computation.8 | async-start | bytes 3522560 | tf_op jit(solution)/shard_map/all_gather | solution.py:1285
  54.7 353.8 %all-gather.13.cloned.1.call-start = ((), (), s32[]{:S(2)}) async-start(), calls=%async_computation.7 | async-start | bytes 7045120 | tf_op jit(solution)/shard_map/all_gather | solution.py:1279
  180.9 26.7 %copy-start.5 = (bf16[1024,1,4,128]{0,3,2,1:T(8,128)(2,1)}, bf16[1024,1,4,128]{0,3,2,1:T(8,128)(2,1)S(1)}, u32[]{:S(2)}) copy-start(bf16[1024,1,4,128]{0,3,2,1:T(8,128)(2,1)S(1)} %copy.80) | copy-start | bytes 3145732
  186.0 13.1 %copy-start.9 = (bf16[1024,4,64]{2,0,1:T(8,128)(2,1)}, bf16[1024,4,64]{2,0,1:T(8,128)(2,1)S(1)}, u32[]{:S(2)}) copy-start(bf16[1024,4,64]{2,0,1:T(8,128)(2,1)S(1)} %get-tuple-element.78) | copy-start | bytes 1572868
  186.0 13.1 %copy-start.11 = (bf16[1024,4,64]{2,0,1:T(8,128)(2,1)}, bf16[1024,4,64]{2,0,1:T(8,128)(2,1)S(1)}, u32[]{:S(2)}) copy-start(bf16[1024,4,64]{2,0,1:T(8,128)(2,1)S(1)} %get-tuple-element.79) | copy-start | bytes 1572868
  214.6 35.9 %copy-start.15 = (bf16[256,2048]{1,0:T(8,128)(2,1)S(1)}, bf16[256,2048]{1,0:T(8,128)(2,1)}, u32[]{:S(2)}) copy-start(bf16[256,2048]{1,0:T(8,128)(2,1)} %param.14) | copy-start | bytes 3145732
  214.6 35.7 %all-to-all-start.1 = ((bf16[4,256,512]{2,1,0:T(8,128)(2,1)}), bf16[4,256,512]{2,1,0:T(8,128)(2,1)S(1)}, u32[]{:S(2)}, u32[]{:S(2)}) async-start(bf16[4,256,512]{2,1,0:T(8,128)(2,1)} %copy.66), calls=%async_computation.1 | async-start | bytes 2097152 | tf_op jit(solution)/shard_map/all_to_all | solution.py:1270
  219.8 694.2 %reduce-scatter.5.cloned.1.call-start = ((), (), s32[]{:S(2)}) async-start(), calls=%async_computation.10 | async-start | bytes 3522560 | tf_op jit(solution)/shard_map/reduce_scatter | solution.py:1318
  250.5 6.3 copy-start.16
  618.9 297.5 %reduce-scatter.3.cloned.1.call-start = ((), (), s32[]{:S(2)}) async-start(), calls=%async_computation.9 | async-start | bytes 7045120 | tf_op jit(solution)/shard_map/reduce_scatter | solution.py:1322
  624.5 3.7 copy-start.12
  624.5 5.2 copy-start.13
  638.7 140.3 %copy-start.18 = (f32[2,768]{1,0:T(2,128)S(1)}, f32[2,768]{1,0:T(2,128)}, u32[]{:S(2)}) copy-start(f32[2,768]{1,0:T(2,128)} %get-tuple-element.43) | copy-start | bytes 18436
  780.6 130.2 %copy-start.6 = (f32[256,2048]{1,0:T(8,128)S(1)}, f32[256,2048]{1,0:T(8,128)}, u32[]{:S(2)}) copy-start(f32[256,2048]{1,0:T(8,128)} %get-tuple-element.67) | copy-start | bytes 6291460
  (10 other events, 22.3 us)
Sparse Core Ops, SparseCore 0:
  9.6 92.9 all-gather.6
  105.0 48.0 all-gather.8
  156.0 83.9 all-gather.10
  241.4 63.1 all-gather.14
  306.0 102.3 all-gather.12
  619.0 76.9 reduce-scatter.4
  698.4 119.9 reduce-scatter.2

commit v4 on v3

--- a/solution.py
+++ b/solution.py
@@ -15,7 +15,6 @@
 residual_scale = 48.0**0.5
 norm_eps = 1e-05
 masked_value = -1e30
-both_axes = ("wide", "narrow")
 kernel_memory = 60 * 2**20
 
 
@@ -31,32 +30,11 @@
     return (second_seq, local_pos, prefix_len)
 
 
-def visible(query_pos, key_pos, joined_flag, prefix_pair, bucket_len):
-    query_seq, query_local, query_prefix = layout(query_pos, joined_flag, prefix_pair, bucket_len)
-    key_seq, key_local, key_prefix = layout(key_pos, joined_flag, prefix_pair, bucket_len)
-    same_seq = query_seq[:, None] == key_seq[None, :]
-    return same_seq & (
-        (key_local[None, :] < key_prefix[None, :]) | (key_local[None, :] <= query_local[:, None])
-    )
-
-
 def rotary_tables(local_pos, head_size):
     halfway = head_size // 2
     inverse = 10000.0 ** (-(2.0 * jnp.arange(halfway).astype(jnp.float32)) / head_size)
     angles = local_pos.astype(jnp.float32)[:, None] * inverse[None, :]
-    return (jnp.cos(angles)[:, None, :], jnp.sin(angles)[:, None, :])
-
-
-def rotate(vectors, cosine, sine_table):
-    halfway = vectors.shape[-1] // 2
-    first_part, second_part = (vectors[..., :halfway], vectors[..., halfway:])
-    return jnp.concatenate(
-        [
-            first_part * cosine - second_part * sine_table,
-            second_part * cosine + first_part * sine_table,
-        ],
-        axis=-1,
-    )
+    return (jnp.cos(angles), jnp.sin(angles))
 
 
 def normalize(values, gain, shift):
@@ -85,33 +63,34 @@
     return values.astype(jnp.bfloat16)
 
 
-def gather_small(heads_bias, merge_bias, norm_gains, norm_shifts, expand_bias, reduce_bias):
-    parts = (heads_bias, merge_bias, norm_gains, norm_shifts, expand_bias, reduce_bias)
-    packed = jnp.concatenate([part.reshape(1, -1) for part in parts], axis=1)
-    wide_count = lax.axis_size("wide")
-    narrow_count = lax.axis_size("narrow")
-    count = wide_count * narrow_count
-    everyone = lax.all_gather(packed, both_axes, axis=0, tiled=True).astype(jnp.float32)
+def pack_small(parts):
+    packed = jnp.concatenate([part.reshape(-1) for part in parts])
+    return jnp.pad(packed, (0, -packed.size % 2048)).reshape(-1, 128)
+
+
+def unpack_small(everyone, parts):
+    wide_count, narrow_count = everyone.shape[:2]
+    everyone = everyone.reshape(wide_count, narrow_count, -1).astype(jnp.float32)
     pieces = []
     start = 0
     for part in parts:
-        pieces.append(everyone[:, start : start + part.size])
+        pieces.append(everyone[:, :, start : start + part.size])
         start += part.size
 
     def pairs(piece):
-        return piece.reshape(piece.shape[0], 2, -1).transpose(1, 0, 2).reshape(2, -1)
+        piece = piece.reshape(-1, 2, piece.shape[-1] // 2)
+        return piece.transpose(1, 0, 2).reshape(2, -1)
 
     own_expand = lax.dynamic_index_in_dim(
-        pieces[4].reshape(wide_count, narrow_count, -1), lax.axis_index("wide"), 0, keepdims=False
-    )
-    reduce_shift = pieces[5].reshape(wide_count, narrow_count, -1)[0].reshape(-1)
+        pieces[4], lax.axis_index("wide"), 0, keepdims=False
+    )
     return (
         pieces[0].reshape(-1),
         pieces[1].reshape(-1),
         pairs(pieces[2]),
         pairs(pieces[3]),
         pairs(own_expand),
-        reduce_shift,
+        pieces[5][0].reshape(-1),
     )
 
 
@@ -201,9 +180,13 @@
 
     def send_own(self):
         slot = self.slot(0)
-        keep = pltpu.make_async_copy(self.own, self.blocks.at[slot], self.own_sem)
-        keep.start()
-        first, second = self.own.at[self.rows(0)], self.own.at[self.rows(1)]
+        keep = None
+        own = self.blocks.at[slot]
+        if self.own is not None:
+            own = self.own
+            keep = pltpu.make_async_copy(own, self.blocks.at[slot], self.own_sem)
+            keep.start()
+        first, second = own.at[self.rows(0)], own.at[self.rows(1)]
         self.pass_on(0, slot, 0, self.device(1), first)
         self.pass_on(1, slot, 1, self.device(-1), second)
         self.pass_on(2, slot, 0, self.device(0, True), first)
@@ -1204,6 +1187,523 @@
     )(inputs, triple_grad, heads_mat, small)
 
 
+def greet_all(wide_count, narrow_count):
+    barrier = pltpu.get_barrier_semaphore()
+    for axis, count in (("wide", wide_count), ("narrow", narrow_count)):
+        place = lax.axis_index(axis)
+        for offset in range(1, count):
+            pl.semaphore_signal(
+                barrier,
+                inc=1,
+                device_id={axis: (place + offset) % count},
+                device_id_type=pl.DeviceIdType.MESH,
+            )
+    pl.semaphore_wait(barrier, wide_count + narrow_count - 2)
+
+
+def gather_kernel(
+    wide_count,
+    narrow_count,
+    own,
+    heads_weight,
+    merge_weight,
+    small,
+    rows_out,
+    heads_out,
+    merge_out,
+    small_out,
+    triple,
+    rows_all,
+    heads_all,
+    merge_all,
+    small_all,
+    rows_send,
+    rows_recv,
+    heads_send,
+    heads_recv,
+    merge_send,
+    merge_recv,
+    small_send,
+    small_recv,
+    wide_send,
+    wide_recv,
+    local_sems,
+    out_sems,
+    heads_ring_send,
+    heads_ring_recv,
+    merge_ring_send,
+    merge_ring_recv,
+):
+    def ring_of(blocks, send, recv):
+        sems = (send, recv, None, None, None, None, None)
+        return PlaneExchange(wide_count, None, blocks, blocks, None, None, sems)
+
+    heads_ring = ring_of(heads_all, heads_ring_send, heads_ring_recv)
+    merge_ring = ring_of(merge_all, merge_ring_send, merge_ring_recv)
+    line = LineExchange(narrow_count)
+    here = line.mine
+    last = narrow_count - 1
+    place = lax.axis_index("wide")
+    slot = heads_ring.slot(0)
+    rows, width = own.shape
+    count = heads_weight.shape[0]
+    columns = heads_all.shape[2]
+    own_cols = columns // 3
+
+    def z_rows(where):
+        return pl.ds(pl.multiple_of(where * count, count), count)
+
+    def head_cols(which, where):
+        start = which * narrow_count * own_cols + where * own_cols
+        return pl.ds(pl.multiple_of(start, own_cols), own_cols)
+
+    def line_rows(way, block):
+        source = rows_all.at[block]
+        return line.copy(
+            source,
+            source,
+            rows_send.at[way, block],
+            rows_recv.at[block],
+            here + 1 if way == 0 else here - 1,
+        )
+
+    def goes(way):
+        return here < last if way == 0 else here > 0
+
+    def has(way, step):
+        return here - step >= 0 if way == 0 else here + step <= last
+
+    def block_of(way, step):
+        return here - step if way == 0 else here + step
+
+    keep_rows = pltpu.make_async_copy(own, rows_all.at[here], local_sems.at[0])
+    keep_rows.start()
+    keeps = [
+        pltpu.make_async_copy(
+            heads_weight.at[:, head_cols(which, here)],
+            heads_all.at[slot, z_rows(here), pl.ds(which * own_cols, own_cols)],
+            local_sems.at[2 + which],
+        )
+        for which in range(3)
+    ]
+    keep_merge = pltpu.make_async_copy(
+        merge_weight, merge_all.at[slot, z_rows(here)], local_sems.at[1]
+    )
+    for copy in keeps + [keep_merge]:
+        copy.start()
+    small_all[place, here] = small[...]
+    greet_all(wide_count, narrow_count)
+
+    def heads_copy(offset, which, where, sender):
+        return line.copy(
+            heads_weight.at[:, head_cols(which, where)],
+            heads_all.at[slot, z_rows(sender), pl.ds(which * own_cols, own_cols)],
+            heads_send.at[offset - 1, which],
+            heads_recv.at[sender, which],
+            where,
+        )
+
+    def merge_copy(offset, where, sender):
+        return line.copy(
+            merge_weight,
+            merge_all.at[slot, z_rows(sender)],
+            merge_send.at[offset - 1],
+            merge_recv.at[sender],
+            where,
+        )
+
+    def small_copy(offset, where, sender):
+        return line.copy(
+            small,
+            small_all.at[place, sender],
+            small_send.at[offset - 1],
+            small_recv.at[sender],
+            where,
+        )
+
+    started = []
+
+    def start(copy):
+        copy.start()
+        started.append(copy)
+
+    for offset in range(1, narrow_count):
+        for which in range(3):
+            start(heads_copy(offset, which, line.peer(offset), here))
+    for offset in range(1, narrow_count):
+        start(small_copy(offset, line.peer(offset), here))
+    keep_rows.wait()
+    for way in range(2):
+
+        @pl.when(goes(way))
+        def _():
+            line_rows(way, here).start()
+
+    for offset in range(1, narrow_count):
+        start(merge_copy(offset, line.peer(offset), here))
+
+    for copy in keeps:
+        copy.wait()
+    for offset in range(1, narrow_count):
+        for which in range(3):
+            heads_copy(offset, which, line.peer(offset), line.peer(offset)).wait_recv()
+    heads_ring.send_own()
+    for offset in range(1, narrow_count):
+        small_copy(offset, line.peer(offset), line.peer(offset)).wait_recv()
+
+    def wide_copy(offset, sender):
+        return pltpu.make_async_remote_copy(
+            src_ref=small_all.at[sender],
+            dst_ref=small_all.at[sender],
+            send_sem=wide_send.at[offset - 1],
+            recv_sem=wide_recv.at[sender],
+            device_id={"wide": (place + offset) % wide_count},
+            device_id_type=pl.DeviceIdType.MESH,
+        )
+
+    for offset in range(1, wide_count):
+        start(wide_copy(offset, place))
+
+    def rows_step(step):
+        for way in range(2):
+
+            @pl.when(has(way, step))
+            def _():
+                line_rows(way, block_of(way, step)).wait_recv()
+
+                @pl.when(goes(way))
+                def _():
+                    line_rows(way, block_of(way, step)).start()
+
+    def project(block):
+        def cols_step(cols):
+            weight = heads_all[:, :, cols].reshape(width, cols.size)
+            triple[pl.ds(pl.multiple_of(block * rows, rows), rows), cols] = dot(
+                rows_all[block], weight, ((1,), (0,))
+            )
+
+        tiles(columns, 256, cols_step)
+
+    def project_step(step):
+        for way in range(2):
+
+            @pl.when(has(way, step))
+            def _():
+                project(block_of(way, step))
+
+    keep_merge.wait()
+    for offset in range(1, narrow_count):
+        merge_copy(offset, line.peer(offset), line.peer(offset)).wait_recv()
+    rows_step(1)
+    merge_ring.send_own()
+
+    def gather(ring, distance):
+        ring.receive(distance)
+        ring.receive_mate(-distance)
+        if distance < ring.far:
+            ring.receive_mate(distance)
+
+    heads_ring.receive_mate(0)
+    for distance in range(1, heads_ring.far + 1):
+        gather(heads_ring, distance)
+    outs = []
+
+    def keep_out(source, target):
+        copy = pltpu.make_async_copy(source, target, out_sems.at[len(outs)])
+        copy.start()
+        outs.append(copy)
+
+    keep_out(heads_all, heads_out)
+    project(here)
+    merge_ring.receive_mate(0)
+    for distance in range(1, merge_ring.far):
+        gather(merge_ring, distance)
+    project_step(1)
+    rows_step(2)
+    gather(merge_ring, merge_ring.far)
+    keep_out(merge_all, merge_out)
+    project_step(2)
+    for step in range(3, narrow_count):
+        rows_step(step)
+        project_step(step)
+    keep_out(rows_all, rows_out)
+    for offset in range(1, wide_count):
+        wide_copy(offset, (place + offset) % wide_count).wait_recv()
+    keep_out(small_all, small_out)
+    for way in range(2):
+        for step in range(narrow_count):
+
+            @pl.when(has(way, step) & goes(way))
+            def _():
+                line_rows(way, block_of(way, step)).wait_send()
+
+    for copy in started:
+        copy.wait_send()
+    heads_ring.drain()
+    merge_ring.drain()
+    for copy in outs:
+        copy.wait()
+
+
+def gather_front(wide_count, narrow_count, layer_input, heads_weight, merge_weight, small):
+    rows, width = layer_input.shape
+    count, all_columns = heads_weight.shape
+    columns = all_columns // narrow_count
+    block = count * narrow_count
+    anywhere = pl.BlockSpec(memory_space=pl.ANY)
+    vmem = pl.BlockSpec(memory_space=pltpu.VMEM)
+    dma = pltpu.SemaphoreType.DMA
+    lines = small.shape[0]
+    shapes = (
+        (narrow_count, rows, width),
+        (wide_count, block, columns),
+        (wide_count, block, width),
+        (wide_count, narrow_count, lines, 128),
+    )
+    far = narrow_count - 1
+    return pl.pallas_call(
+        functools.partial(gather_kernel, wide_count, narrow_count),
+        out_shape=tuple(jax.ShapeDtypeStruct(shape, jnp.bfloat16) for shape in shapes)
+        + (jax.ShapeDtypeStruct((narrow_count * rows, columns), jnp.float32),),
+        in_specs=[anywhere, anywhere, anywhere, vmem],
+        out_specs=(anywhere, anywhere, anywhere, anywhere, vmem),
+        scratch_shapes=[pltpu.VMEM(shape, jnp.bfloat16) for shape in shapes]
+        + [
+            dma((2, narrow_count)),
+            dma((narrow_count,)),
+            dma((far, 3)),
+            dma((narrow_count, 3)),
+            dma((far,)),
+            dma((narrow_count,)),
+            dma((far,)),
+            dma((narrow_count,)),
+            dma((wide_count - 1,)),
+            dma((wide_count,)),
+            dma((5,)),
+            dma((4,)),
+            dma((3, wide_count, 2)),
+            dma((wide_count, 2)),
+            dma((3, wide_count, 2)),
+            dma((wide_count, 2)),
+        ],
+        compiler_params=pltpu.CompilerParams(
+            collective_id=5, has_side_effects=True, vmem_limit_bytes=kernel_memory
+        ),
+        cost_estimate=pl.CostEstimate(
+            flops=80 * 10**9, bytes_accessed=200 * 2**20, transcendentals=0
+        ),
+        name="gather_front",
+    )(layer_input, heads_weight, merge_weight, small)
+
+
+def attention_forward_kernel(
+    narrow_count,
+    triple,
+    heads_shift,
+    cosine,
+    signed_sine,
+    first_query,
+    last_query,
+    own,
+    merge,
+    merge_shift,
+    gain,
+    shift,
+    queries,
+    keys,
+    values,
+    probs,
+    mixed_out,
+    hidden,
+    hidden_low,
+    normed,
+    inv_std,
+    merge_mat,
+    probs_held,
+    values_turned,
+    outbound,
+    mixed,
+    mixed_send,
+    mixed_recv,
+    local_sems,
+):
+    line = LineExchange(narrow_count)
+    bucket, own_cols = queries.shape
+    rows, width = own.shape
+    heads = own_cols // HDIM
+    scale = HDIM ** (-0.5)
+    load_merge = pltpu.make_async_copy(merge, merge_mat, local_sems.at[2])
+    load_merge.start()
+    line.greet()
+
+    def keep(head):
+        return pltpu.make_async_copy(
+            probs_held.at[head % 2], probs.at[head], local_sems.at[head % 2]
+        )
+
+    def mixed_copy(head, offset, where, sender):
+        cols = pl.ds(pl.multiple_of(sender * own_cols + head * HDIM, HDIM), HDIM)
+        return line.copy(
+            outbound.at[where, :, pl.ds(head * HDIM, HDIM)],
+            mixed.at[:, cols],
+            mixed_send.at[offset - 1, head],
+            mixed_recv.at[sender, head],
+            where,
+        )
+
+    started = []
+    for head in range(heads):
+        cols = pl.ds(head * HDIM, HDIM)
+
+        def turn(i, carry):
+            here = pl.ds(pl.multiple_of(i * rows, rows), rows)
+            for which, target in enumerate((queries, keys, values)):
+                wanted = pl.ds(which * own_cols + head * HDIM, HDIM)
+                part = triple[here, wanted] + heads_shift[:, wanted]
+                if which < 2:
+                    part = rotate_lanes(part, cosine[here], -signed_sine[here])
+                else:
+                    values_turned[:, here] = part.T.astype(jnp.bfloat16)
+                target[here, cols] = part.astype(jnp.bfloat16)
+            return carry
+
+        lax.fori_loop(0, narrow_count, turn, 0)
+        if head >= 2:
+            keep(head - 2).wait()
+        held = probs_held.at[head % 2]
+
+        def chunk(i, carry):
+            here = pl.ds(pl.multiple_of(i * rows, rows), rows)
+            scores = dot(keys[:, cols], queries[here, cols], ((1,), (1,))) * scale
+            token = i * rows + lax.broadcasted_iota(jnp.int32, (bucket, rows), 1)
+            seen = (token >= first_query[...]) & (token <= last_query[...])
+            scores = jnp.where(seen, scores, masked_value)
+            expo = jnp.exp(scores - jnp.max(scores, axis=0, keepdims=True))
+            weights = (expo * (1 / jnp.sum(expo, axis=0, keepdims=True))).astype(jnp.bfloat16)
+            held[:, here] = weights
+            mixed_part = dot(values_turned[...], weights, ((1,), (0,)))
+            outbound[i, :, cols] = mixed_part.T.astype(jnp.bfloat16)
+            return carry
+
+        lax.fori_loop(0, narrow_count, chunk, 0)
+        keep(head).start()
+        for offset in range(1, narrow_count):
+            copy = mixed_copy(head, offset, line.peer(offset), line.mine)
+            copy.start()
+            started.append(copy)
+    own_mixed = pltpu.make_async_copy(
+        outbound.at[line.mine],
+        mixed.at[:, pl.ds(pl.multiple_of(line.mine * own_cols, own_cols), own_cols)],
+        local_sems.at[3],
+    )
+    own_mixed.start()
+    own_mixed.wait()
+    load_merge.wait()
+    for offset in range(1, narrow_count):
+        for head in range(heads):
+            mixed_copy(head, offset, line.peer(offset), line.peer(offset)).wait_recv()
+    mixed_out[...] = mixed[...]
+
+    def merge_cols(cols):
+        hidden[:, cols] = (
+            residual_scale * own[:, cols].astype(jnp.float32)
+            + dot(mixed[...], merge_mat[:, cols], ((1,), (0,)))
+            + merge_shift[:, cols]
+        )
+
+    tiles(width, 256, merge_cols)
+
+    def norm_rows(i, carry):
+        some = pl.ds(pl.multiple_of(i * 16, 16), 16)
+        result, centred, inverse = normalize(hidden[some], gain[...], shift[...])
+        hidden[some] = result
+        hidden_low[some] = result.astype(jnp.bfloat16)
+        normed[some] = centred
+        inv_std[some] = inverse
+        return carry
+
+    lax.fori_loop(0, rows // 16, norm_rows, 0)
+    for head in range(max(heads - 2, 0), heads):
+        keep(head).wait()
+    for copy in started:
+        copy.wait_send()
+
+
+def attention_forward(
+    narrow_count,
+    triple,
+    heads_shift,
+    cosine,
+    signed_sine,
+    first_query,
+    last_query,
+    layer_input,
+    merge_full,
+    merge_shift,
+    gain,
+    shift,
+):
+    bucket, columns = triple.shape
+    rows, width = layer_input.shape
+    own_cols = columns // 3
+    heads = own_cols // HDIM
+    anywhere = pl.BlockSpec(memory_space=pl.ANY)
+    vmem = pl.BlockSpec(memory_space=pltpu.VMEM)
+    dma = pltpu.SemaphoreType.DMA
+
+    def low_shape(*shape):
+        return jax.ShapeDtypeStruct(shape, jnp.bfloat16)
+
+    def wide_shape(*shape):
+        return jax.ShapeDtypeStruct(shape, jnp.float32)
+
+    return pl.pallas_call(
+        functools.partial(attention_forward_kernel, narrow_count),
+        out_shape=(
+            low_shape(bucket, own_cols),
+            low_shape(bucket, own_cols),
+            low_shape(bucket, own_cols),
+            low_shape(heads, bucket, bucket),
+            low_shape(rows, width),
+            wide_shape(rows, width),
+            low_shape(rows, width),
+            wide_shape(rows, width),
+            wide_shape(rows, 1),
+        ),
+        in_specs=[vmem] * 7 + [anywhere] + [vmem] * 3,
+        out_specs=(vmem, vmem, vmem, anywhere) + (vmem,) * 5,
+        scratch_shapes=[
+            pltpu.VMEM((width, width), jnp.bfloat16),
+            pltpu.VMEM((2, bucket, bucket), jnp.bfloat16),
+            pltpu.VMEM((HDIM, bucket), jnp.bfloat16),
+            pltpu.VMEM((narrow_count, rows, own_cols), jnp.bfloat16),
+            pltpu.VMEM((rows, width), jnp.bfloat16),
+            dma((narrow_count - 1, heads)),
+            dma((narrow_count, heads)),
+            dma((4,)),
+        ],
+        compiler_params=pltpu.CompilerParams(
+            collective_id=6, has_side_effects=True, vmem_limit_bytes=kernel_memory
+        ),
+        cost_estimate=pl.CostEstimate(
+            flops=60 * 10**9, bytes_accessed=200 * 2**20, transcendentals=0
+        ),
+        name="attention_forward",
+    )(
+        triple,
+        heads_shift,
+        cosine,
+        signed_sine,
+        first_query,
+        last_query,
+        layer_input,
+        merge_full,
+        merge_shift,
+        gain,
+        shift,
+    )
+
+
 def shards(
     layer_input,
     heads_weight,
@@ -1228,51 +1728,56 @@
     own_heads = HEADS // narrow_count
     own_cols = own_heads * HDIM
     share = expand_weight.shape[2]
-    score_scale = HDIM ** (-0.5)
     joined_flag = joined[0]
     prefix_pair = prefix[0]
     narrow_index = lax.axis_index("narrow")
     positions = jnp.arange(bucket_len, dtype=jnp.int32)
     second_seq, local_pos, prefix_len = layout(positions, joined_flag, prefix_pair, bucket_len)
     cosine, sine_table = rotary_tables(local_pos, HDIM)
-    key_mask = visible(positions, positions, joined_flag, prefix_pair, bucket_len)
-
-    rows_input = lax.all_gather(layer_input, "narrow", axis=0, tiled=True)
-    swapped = lax.all_to_all(
-        heads_weight.reshape(-1, 3, narrow_count, own_cols).transpose(2, 0, 1, 3),
-        "narrow",
-        split_axis=0,
-        concat_axis=0,
-        tiled=True,
-    ).reshape(-1, 3 * own_cols)
-    heads_mat = lax.all_gather(swapped, "wide", axis=0, tiled=True)
-    heads_shift, merge_shift, gains, shifts, expand_shift, reduce_shift = gather_small(
-        heads_bias, merge_bias, norm_gains, norm_shifts, expand_bias, reduce_bias
-    )
-    merge_full = lax.all_gather(merge_weight, both_axes, axis=0, tiled=True)
+    first_query = jnp.where(local_pos < prefix_len, positions - local_pos, positions)
+    last_query = jnp.where(
+        (joined_flag == 1) | (second_seq == 1), bucket_len - 1, bucket_len // 2 - 1
+    )
+
+    smalls = (heads_bias, merge_bias, norm_gains, norm_shifts, expand_bias, reduce_bias)
+    rows_input, heads_mat, merge_full, small_all, triple = gather_front(
+        wide_count, narrow_count, layer_input, heads_weight, merge_weight, pack_small(smalls)
+    )
+    rows_input = rows_input.reshape(bucket_len, model_width)
+    heads_mat = heads_mat.reshape(model_width, 3 * own_cols)
+    merge_full = merge_full.reshape(model_width, model_width)
+    heads_shift, merge_shift, gains, shifts, expand_shift, reduce_shift = unpack_small(
+        small_all, smalls
+    )
     own_shift = lax.dynamic_index_in_dim(
         heads_shift.reshape(3, narrow_count, own_cols), narrow_index, 1, keepdims=False
-    ).reshape(-1)
-    triple = dot(rows_input, heads_mat, ((1,), (0,))) + own_shift
-    triple = triple.reshape(bucket_len, 3, own_heads, HDIM)
-    queries = low(rotate(triple[:, 0], cosine, sine_table))
-    keys = low(rotate(triple[:, 1], cosine, sine_table))
-    values = low(triple[:, 2])
-    scores = (
-        jnp.einsum("kgd,qgd->gkq", keys, queries, preferred_element_type=jnp.float32) * score_scale
-    )
-    scores = jnp.where(key_mask.T[None], scores, masked_value)
-    expo = jnp.exp(scores - jnp.max(scores, axis=1, keepdims=True))
-    probs_low = low(expo / jnp.sum(expo, axis=1, keepdims=True))
-    mixed_own = low(
-        jnp.einsum("gkq,kgd->qgd", probs_low, values, preferred_element_type=jnp.float32)
-    ).reshape(bucket_len, own_cols)
-    mixed = lax.all_to_all(mixed_own, "narrow", split_axis=0, concat_axis=1, tiled=True)
-    attended = dot(mixed, merge_full, ((1,), (0,))) + merge_shift
-    hidden, normed_one, inv_one = normalize(
-        residual_scale * layer_input.astype(jnp.float32) + attended, gains[0], shifts[0]
-    )
-    hidden_low = low(hidden)
+    ).reshape(1, -1)
+    cosine_wide = jnp.concatenate([cosine, cosine], axis=1)
+    signed_sine = jnp.concatenate([sine_table, -sine_table], axis=1)
+    (
+        queries,
+        keys,
+        values,
+        probs_low,
+        mixed,
+        hidden,
+        hidden_low,
+        normed_one,
+        inv_one,
+    ) = attention_forward(
+        narrow_count,
+        triple,
+        own_shift,
+        cosine_wide,
+        signed_sine,
+        first_query.reshape(-1, 1),
+        last_query.reshape(-1, 1),
+        layer_input,
+        merge_full,
+        merge_shift.reshape(1, -1),
+        gains[0].reshape(1, -1),
+        shifts[0].reshape(1, -1),
+    )
 
     tile_rows = -share % 16
     padded = -(-share // 256) * 256
@@ -1334,12 +1839,12 @@
         attended_grad,
         merge_full,
         mixed,
-        queries.reshape(bucket_len, own_cols),
-        keys.reshape(bucket_len, own_cols),
-        values.reshape(bucket_len, own_cols),
+        queries,
+        keys,
+        values,
         probs_low,
-        jnp.concatenate([cosine[:, 0], cosine[:, 0]], axis=1),
-        jnp.concatenate([sine_table[:, 0], -sine_table[:, 0]], axis=1),
+        cosine_wide,
+        signed_sine,
     )
 
     mine_narrow = (jnp.arange(narrow_count) == narrow_index).astype(jnp.float32)

time: 933 us -> 851 us (0.912)
  Pallas kernels: 431 us -> 742 us
  waiting for transfers between devices: 199 us -> 1.45 us
  blocking collectives: 111 us -> 0 us
  matrix products: 59.8 us -> 27.5 us
  local copies, waits for them, and re-layouts: 53.9 us -> 26.3 us
  other arithmetic: 52.1 us -> 31.2 us
    pallas_call x0 -> x2, Pallas kernels: none -> 304 us  [the longest x1 253 us: gather_front(): pl.pallas_call(functools.partial(gather_kernel, wide_count, narrow_count)...]
    all_gather x1, waiting for transfers between devices: 104 us -> 0.02 us  [shards(): lax.all_gather(jnp.pad(expand_weight.transpose(1, 2, 0), ((0, 0), (0, til...]
    all_gather x1 -> x0, blocking collectives: 69.7 us -> none  [gather_small(): lax.all_gather(packed, both_axes, axis=0, tiled=True).astype(jnp.float32)]
    all_gather x1, waiting for transfers between devices: 45.1 us -> 0.02 us  [shards(): lax.all_gather(jnp.pad(reduce_weight, ((0, tile_rows), (0, 0))), 'narrow'...]
    all_to_all x1 -> x0, blocking collectives: 41.1 us -> none  [shards(): lax.all_to_all(heads_weight.reshape(-1, 3, narrow_count, own_cols).transp...]
    all_to_all x1 -> x0, waiting for transfers between devices: 28.9 us -> none  [shards(): lax.all_to_all(mixed_own, 'narrow', split_axis=0, concat_axis=1, tiled=True)]
    all_gather x3 -> x0, waiting for transfers between devices: 18.3 us -> none  [the longest x1 18.3 us: shards(): heads_mat = lax.all_gather(swapped, 'wide', axis=0, tiled=True)]
    dot_general x4 -> x2, matrix products: 45.5 us -> 27.5 us  [dot(): lax.dot_general(left, right, (dims, ((), ())), preferred_element_type=jnp...]
  transfers between devices with their start and end apart: 8 -> 4, of which waited for: 4 -> 0; matrix products, arithmetic and copies ran while one was open for 12% -> 5% of each run, Pallas kernels for 28% -> 68%
where the time goes in v4:
time: 851 us; the launch traced here: 845 us
  Pallas kernels  742 us (87%)
  other arithmetic  31.2 us (4%)
  matrix products  27.5 us (3%)
  local copies, waits for them, and re-layouts  26.3 us (3%)
  between operations  16.3 us (2%)
    pallas_call x1, Pallas kernels, gather_front(): pl.pallas_call(functools.partial(gather_kernel, wide_count, narrow_count)...  253 us
    pallas_call x1, Pallas kernels, input_backward(): pl.pallas_call(functools.partial(input_backward_kernel, wide_count, narro...  137 us
    pallas_call x1, Pallas kernels, attention_backward(): pl.pallas_call(functools.partial(attention_backward_kernel, wide_count, n...  130 us
    pallas_call x1, Pallas kernels, geglu_forward(): pl.pallas_call(functools.partial(geglu_forward_kernel, wide_count), out_s...  87.2 us
    pallas_call x1, Pallas kernels, geglu_backward(): pl.pallas_call(functools.partial(geglu_backward_kernel, wide_count), out_...  83.5 us
    pallas_call x1, Pallas kernels, attention_forward(): pl.pallas_call(functools.partial(attention_forward_kernel, narrow_count),...  50.7 us
    dot_general x2, matrix products, dot(): lax.dot_general(left, right, (dims, ((), ())), preferred_element_type=jnp...  27.5 us
  transfers between devices with their start and end apart: 4, of which 0 were waited for; matrix products, arithmetic and copies ran while one was open for 5% of the time, Pallas kernels for 68%

profile of v4, /device:TPU:8, one launch (start us, length us, event | category | flops | bytes accessed | tf_op | source)
XLA Modules:
  0.0 845.2 jit_solution(5495585930100668624)
XLA Ops:
  9.7 253.2 %gather_front.1 = (bf16[4,256,2048]{2,1,0:T(8,128)(2,1)}, bf16[8,256,1536]{2,1,0:T(8,128)(2,1)}, bf16[8,256,2048]{2,1,0:T(8,128)(2,1)}, bf16[8,4,16,128]{3,2,1,0:T(8,128)(2,1)}, f32[1024,1536]{1,0:T(8,128)}) custom-call(bf16[256,2048]{1,0:T(8,128)(2,1)} %own.3, bf16[64,6144]{1,0:T(8,128)(2,1)} %heads_weight.1, bf16[64,2048]{1,0:T(8,128)(2,1)} %merge_weight.1, ...), custom_call_target="tpu_custom_call" | custom-call | flops 80000000000 | bytes 209715200 | tf_op jit(solution)/shard_map/gather_front/pallas_call | solution.py:1464
  270.7 2.3 fusion.12
  273.0 1.9 multiply_sine_fusion
  274.9 1.3 pad_maximum_fusion
  276.2 50.7 %attention_forward.1 = (bf16[1024,512]{1,0:T(8,128)(2,1)}, bf16[1024,512]{1,0:T(8,128)(2,1)}, bf16[1024,512]{1,0:T(8,128)(2,1)}, bf16[4,1024,1024]{2,1,0:T(8,128...) custom-call(f32[1024,1536]{1,0:T(8,128)} %get-tuple-element.45.tripl, ...), custom_call_target="tpu_custom_call" | custom-call | flops 60000002048 | bytes 209715200 | tf_op jit(solution)/shard_map/attention_forward/pallas_call | solution.py:1660
  327.0 87.2 %geglu_forward.1 = (bf16[8,256,2048]{2,1,0:T(8,128)(2,1)}, bf16[8,256,768]{2,1,0:T(8,128)(2,1)}, bf16[8,256,768]{2,1,0:T(8,128)(2,1)}, bf16[8,256,768]{2,1,0:T(8,128)(2,1)}, f32[256,2048]{1,0:T(8,128)}) custom-call(bf16[256,2048]{1,0:T(8,128)(2,1)} %get-tuple-element.49.own, bf16[2,688,2048]{2,1,0:T(8,128)(2,1)} %all-gather.3.cloned.1.call-done.expand, ...), custom_call_target="tpu_custom_call" | custom-call | flops 19327352832 | bytes 209715200 | tf_op jit(solution)/shard_map/geglu_forward/pallas_call | solution.py:510
  414.2 2.6 fusion.19
  419.0 1.7 convert_reduce_fusion.1
  420.7 83.5 %geglu_backward.1 = (bf16[8,256,2048]{2,1,0:T(8,128)(2,1)}, bf16[2,8,256,768]{3,2,1,0:T(8,128)(2,1)}, f32[256,2048]{1,0:T(8,128)}, f32[2,768]{1,0:T(2,128)}) custom-call(bf16[256,2048]{1,0:T(8,128)(2,1)} %get-tuple-element.93.own, bf16[2,688,2048]{2,1,0:T(8,128)(2,1)} %all-gather.3.cloned.1.call-done.expand, ...), custom_call_target="tpu_custom_call" | custom-call | flops 19327352832 | bytes 209715200 | tf_op jit(solution)/shard_map/geglu_backward/pallas_call | solution.py:634
  504.3 17.4 %fusion.2 = bf16[2,768,2048]{2,1,0:T(8,128)(2,1)S(1)} fusion(bf16[2,8,256,768]{3,2,1,0:T(8,128)(2,1)} %get-tuple-element.56, bf16[8,256,2048]{2,1,0:T(8,128)(2,1)} %get-tuple-element.57), kind=kOutput, calls=%fused_computation.4 | convolution fusion | flops 12884901888 | bytes 20971520 | tf_op jit(solution)/shard_map/dot_general | solution.py:59
  521.7 2.9 slice.139
  524.6 10.1 %convolution_bitcast_fusion = bf16[768,2048]{1,0:T(8,128)(2,1)S(1)} fusion(bf16[8,256,768]{2,1,0:T(8,128)(2,1)} %get-tuple-element.52, bf16[8,256,2048]{2,1,0:T(8,128)(2,1)} %get-tuple-element.55), kind=kOutput, calls=%fused_computation.5 | convolution fusion | flops 6442450944 | bytes 14680064 | tf_op jit(solution)/shard_map/dot_general | solution.py:59
  534.7 1.8 slice.140
  537.5 4.6 multiply_reduce_fusion
  542.2 1.6 copy-done
  543.8 3.0 fusion.16.attended
  546.8 130.4 %attention_backward.1 = (bf16[1024,1536]{1,0:T(8,128)(2,1)}, f32[64,2048]{1,0:T(8,128)}, f32[1,1536]{1,0:T(1,128)}, f32[1,2048]{1,0:T(1,128)}) custom-call(bf16[256,2048]{1,0:T(8,128)(2,1)} %fusion.16.attended, bf16[2048,2048]{1,0:T(8,128)(2,1)} %bitcast.61, bf16[256,2048]{1,0:T(8,128)(2,1)} %get-tuple-element.62.mixed, ...), custom_call_target="tpu_custom_call" | custom-call | flops 60000002048 | bytes 209715200 | tf_op jit(solution)/shard_map/attention_backward/pallas_call | solution.py:891
  678.5 1.4 reduce.31
  681.8 137.3 %input_backward.1 = (f32[256,2048]{1,0:T(8,128)}, f32[64,6144]{1,0:T(8,128)}, f32[16,128]{1,0:T(8,128)}) custom-call(bf16[1024,2048]{1,0:T(8,128)(2,1)} %bitcast.63, bf16[1024,1536]{1,0:T(8,128)(2,1)} %get-tuple-element.67.triple, bf16[2048,1536]{1,0:T(8,128)(2,1)} %bitcast.62, f32[8,4,16,128]{3,2,1,0:T(8,128)} %bitcast.47), custom_call_target="tpu_custom_call" | custom-call | flops 80000000000 | bytes 209715200 | tf_op jit(solution)/shard_map/input_backward/pallas_call | solution.py:1153
  819.1 1.3 slice.127
  821.6 1.3 slice.129
  826.4 4.1 multiply_add_fusion
  830.5 2.4 convert_element_type.79
  832.9 3.4 convert_bitcast_fusion
  (113 shorter events, 21.4 us)
Async XLA Ops:
  7.2 1.6 copy-start.11
  7.2 1.7 copy-start.12
  7.2 1.8 copy-start.7
  7.2 1.8 copy-start.8
  7.2 1.8 copy-start.10
  7.2 1.8 copy-start.9
  7.2 319.7 %all-gather.5.cloned.1.call-start = ((), (), s32[]{:S(2)}) async-start(), calls=%async_computation.3 | async-start | bytes 3522560 | tf_op jit(solution)/shard_map/all_gather | solution.py:1790
  8.0 319.0 %all-gather.3.cloned.1.call-start = ((), (), s32[]{:S(2)}) async-start(), calls=%async_computation.2 | async-start | bytes 7045120 | tf_op jit(solution)/shard_map/all_gather | solution.py:1784
  8.7 821.8 %reduce-scatter.5.cloned.1.call-start = ((), (), s32[]{:S(2)}) async-start(), calls=%async_computation.5 | async-start | bytes 3522560 | tf_op jit(solution)/shard_map/reduce_scatter | solution.py:1823
  9.7 257.9 %copy-start.6 = (s32[1,2]{1,0:T(1,128)S(1)}, s32[1,2]{1,0:T(1,128)}, u32[]{:S(2)}) copy-start(s32[1,2]{1,0:T(1,128)} %param.26) | copy-start | bytes 28
  416.8 1.2 copy-start.1
  536.5 0.9 copy-start.4
  536.5 296.4 %reduce-scatter.3.cloned.1.call-start = ((), (), s32[]{:S(2)}) async-start(), calls=%async_computation.4 | async-start | bytes 7045120 | tf_op jit(solution)/shard_map/reduce_scatter | solution.py:1827
  542.1 1.6 copy-start
  546.8 130.7 %copy-start.5 = (f32[2,768]{1,0:T(2,128)S(1)}, f32[2,768]{1,0:T(2,128)}, u32[]{:S(2)}) copy-start(f32[2,768]{1,0:T(2,128)} %get-tuple-element.71) | copy-start | bytes 18436
  832.9 3.4 copy-start.2
  836.3 1.4 copy-start.3
Sparse Core Ops, SparseCore 0:
  9.6 101.6 all-gather.4
  112.9 133.7 all-gather.2
  536.6 75.8 reduce-scatter.4
  614.9 116.1 reduce-scatter.2

commit v5 on v4

--- a/solution.py
+++ b/solution.py
@@ -286,7 +286,8 @@
             device_id_type=pl.DeviceIdType.MESH,
         ).wait_recv()
 
-    def run(self, compute):
+    def run(self, compute, beside=()):
+        beside = list(beside)
         keep = self.send_own()
         keep.wait()
         self.receive_mate(0)
@@ -304,8 +305,14 @@
         self.receive_mate(self.far)
         compute(chip_at(self.position + self.far, self.ring))
         self.share(self.far)
+        for work in beside[: len(beside) // 4]:
+            work()
         self.far_sums()
+        for work in beside[len(beside) // 4 : (5 * len(beside)) // 8]:
+            work()
         self.last_sums()
+        for work in beside[(5 * len(beside)) // 8 :]:
+            work()
 
     def first_sums(self):
         distance = self.far - 1
@@ -536,8 +543,10 @@
     reduce,
     slope_in,
     gelu_in,
-    rows_all,
-    unit_grads,
+    active_in,
+    rows_in,
+    reduce_part,
+    expand_part,
     hidden_grad,
     unit_sums,
     blocks,
@@ -555,6 +564,9 @@
     reduce_mat,
     slope,
     gelu,
+    active,
+    rows_all,
+    staged,
     load_sems,
     keep_sems,
 ):
@@ -567,10 +579,16 @@
         pltpu.make_async_copy(slope_in, slope, load_sems.at[3]),
         pltpu.make_async_copy(gelu_in, gelu, load_sems.at[4]),
     ]
+    late_loads = [
+        pltpu.make_async_copy(active_in, active, load_sems.at[5]),
+        pltpu.make_async_copy(rows_in, rows_all, load_sems.at[6]),
+    ]
     for copy in loads[3:]:
         copy.start()
     unit_sums[...] = jnp.zeros_like(unit_sums)
     plane.greet()
+    for copy in late_loads:
+        copy.start()
     kept = []
     waiting = list(loads)
 
@@ -601,24 +619,54 @@
             )
 
         tiles(parts.shape[2], 256, outputs)
-        pair = pl.ds(2 * chip, 2)
-        for index, (source, target) in enumerate(
-            ((slope, unit_grads.at[0]), (gelu, unit_grads.at[1]), (blocks, rows_all))
-        ):
+
+    def weight_part(left, right, start, target):
+        def work():
+            index = len(kept)
+            if index >= 2:
+                kept[index - 2].wait()
+            tokens = left.shape[0] * left.shape[1]
+            part = dot(
+                left[:, :, start : start + 256].reshape(tokens, 256),
+                right[...].reshape(tokens, right.shape[2]),
+                ((0,), (0,)),
+            )
+            staged[index % 2] = part.astype(jnp.bfloat16)
+            filled = min(256, target.shape[0] - start)
             copy = pltpu.make_async_copy(
-                source.at[pair], target.at[pair], keep_sems.at[chip, index]
+                staged.at[index % 2, pl.ds(0, filled)],
+                target.at[pl.ds(start, filled)],
+                keep_sems.at[index % 2],
             )
             copy.start()
             kept.append(copy)
 
-    plane.run(compute)
+        return work
+
+    works = []
+    for left, right, target in (
+        (active, blocks, reduce_part),
+        (slope, rows_all, expand_part.at[0]),
+        (gelu, rows_all, expand_part.at[1]),
+    ):
+        for start in range(0, target.shape[0], 256):
+            works.append(weight_part(left, right, start, target))
+
+    def load_late():
+        for copy in late_loads:
+            copy.wait()
+
+    works[0] = functools.partial(lambda first: (load_late(), first()), works[0])
+    plane.run(compute, works)
     plane.finish(hidden_grad)
     plane.drain()
-    for copy in kept:
+    for copy in kept[-2:]:
         copy.wait()
 
 
-def geglu_backward(wide_count, feed_grad, expand_full, reduce_full, slope, gelu):
+def geglu_backward(
+    wide_count, feed_grad, expand_full, reduce_full, slope, gelu, active, rows_all
+):
     rows, width = feed_grad.shape
     padded = slope.shape[2]
     anywhere = pl.BlockSpec(memory_space=pl.ANY)
@@ -628,28 +676,31 @@
         pltpu.VMEM((padded, width), jnp.bfloat16),
         pltpu.VMEM((wide_count, rows, padded), jnp.bfloat16),
         pltpu.VMEM((wide_count, rows, padded), jnp.bfloat16),
-        pltpu.SemaphoreType.DMA((5,)),
-        pltpu.SemaphoreType.DMA((wide_count // 2, 3)),
+        pltpu.VMEM((wide_count, rows, padded), jnp.bfloat16),
+        pltpu.VMEM((wide_count, rows, width), jnp.bfloat16),
+        pltpu.VMEM((2, 256, width), jnp.bfloat16),
+        pltpu.SemaphoreType.DMA((7,)),
+        pltpu.SemaphoreType.DMA((2,)),
     ]
     return pl.pallas_call(
         functools.partial(geglu_backward_kernel, wide_count),
         out_shape=(
-            jax.ShapeDtypeStruct((wide_count, rows, width), jnp.bfloat16),
-            jax.ShapeDtypeStruct((2, wide_count, rows, padded), jnp.bfloat16),
+            jax.ShapeDtypeStruct(reduce_full.shape, jnp.bfloat16),
+            jax.ShapeDtypeStruct(expand_full.shape, jnp.bfloat16),
             jax.ShapeDtypeStruct((rows, width), jnp.float32),
             jax.ShapeDtypeStruct((2, padded), jnp.float32),
         ),
-        in_specs=[anywhere] * 5,
+        in_specs=[anywhere] * 7,
         out_specs=(anywhere, anywhere, vmem, vmem),
         scratch_shapes=scratch,
         compiler_params=pltpu.CompilerParams(
             collective_id=2, has_side_effects=True, vmem_limit_bytes=kernel_memory
         ),
         cost_estimate=pl.CostEstimate(
-            flops=6 * wide_count * rows * padded * width, bytes_accessed=200 * 2**20, transcendentals=0
+            flops=12 * wide_count * rows * padded * width, bytes_accessed=200 * 2**20, transcendentals=0
         ),
         name="geglu_backward",
-    )(feed_grad, expand_full, reduce_full, slope, gelu)
+    )(feed_grad, expand_full, reduce_full, slope, gelu, active, rows_all)
 
 
 class LineExchange:
@@ -1391,21 +1442,12 @@
             def _():
                 project(block_of(way, step))
 
-    keep_merge.wait()
-    for offset in range(1, narrow_count):
-        merge_copy(offset, line.peer(offset), line.peer(offset)).wait_recv()
-    rows_step(1)
-    merge_ring.send_own()
-
     def gather(ring, distance):
         ring.receive(distance)
         ring.receive_mate(-distance)
         if distance < ring.far:
             ring.receive_mate(distance)
 
-    heads_ring.receive_mate(0)
-    for distance in range(1, heads_ring.far + 1):
-        gather(heads_ring, distance)
     outs = []
 
     def keep_out(source, target):
@@ -1413,19 +1455,27 @@
         copy.start()
         outs.append(copy)
 
+    rows_step(1)
+    heads_ring.receive_mate(0)
+    for distance in range(1, heads_ring.far):
+        gather(heads_ring, distance)
+    keep_merge.wait()
+    for offset in range(1, narrow_count):
+        merge_copy(offset, line.peer(offset), line.peer(offset)).wait_recv()
+    merge_ring.send_own()
+    gather(heads_ring, heads_ring.far)
     keep_out(heads_all, heads_out)
     project(here)
-    merge_ring.receive_mate(0)
-    for distance in range(1, merge_ring.far):
-        gather(merge_ring, distance)
-    project_step(1)
-    rows_step(2)
+    for step in range(2, narrow_count):
+        rows_step(step)
+        project_step(step - 1)
+        if step == 2:
+            merge_ring.receive_mate(0)
+            for distance in range(1, merge_ring.far):
+                gather(merge_ring, distance)
     gather(merge_ring, merge_ring.far)
     keep_out(merge_all, merge_out)
-    project_step(2)
-    for step in range(3, narrow_count):
-        rows_step(step)
-        project_step(step)
+    project_step(last)
     keep_out(rows_all, rows_out)
     for offset in range(1, wide_count):
         wide_copy(offset, (place + offset) % wide_count).wait_recv()
@@ -1787,6 +1837,7 @@
         axis=2,
         tiled=True,
     )
+    reduce_weight, _ = lax.optimization_barrier((reduce_weight, small_all))
     reduce_full = lax.all_gather(
         jnp.pad(reduce_weight, ((0, tile_rows), (0, 0))), "narrow", axis=1, tiled=True
     )
@@ -1808,23 +1859,14 @@
     shift_two_grad = jnp.sum(grad_out, axis=0)
     sum_two_grad = normalize_back(grad_out, normed_two, inv_two, gains[1])
     feed_grad = low(sum_two_grad)
-    feed_grads_all, unit_grads, hidden_part, unit_sums = geglu_backward(
-        wide_count, feed_grad, expand_full, reduce_full, slope, gelu
-    )
-    tokens_all = wide_count * tok_rows
-    rows_all = rows_all.reshape(tokens_all, model_width)
-    feed_grads_all = feed_grads_all.reshape(tokens_all, model_width)
-    unit_grads = unit_grads.reshape(2, tokens_all, padded)
-    reduce_part = low(dot(active.reshape(tokens_all, padded), feed_grads_all, ((0,), (0,))))[:share]
-    expand_part = low(dot(unit_grads, rows_all, ((1,), (0,))))[:, :share]
-    reduce_part, expand_part, hidden_part = lax.optimization_barrier(
-        (reduce_part, expand_part, hidden_part)
+    reduce_part, expand_part, hidden_part, unit_sums = geglu_backward(
+        wide_count, feed_grad, expand_full, reduce_full, slope, gelu, active, rows_all
     )
     reduce_weight_gradient = lax.psum_scatter(
         reduce_part, "narrow", scatter_dimension=1, tiled=True
-    ).astype(jnp.float32)
+    )[:share].astype(jnp.float32)
     expand_weight_gradient = (
-        lax.psum_scatter(expand_part, "narrow", scatter_dimension=2, tiled=True)
+        lax.psum_scatter(expand_part, "narrow", scatter_dimension=2, tiled=True)[:, :share]
         .astype(jnp.float32)
         .transpose(2, 0, 1)
     )

time: 851 us -> 819 us (0.962)
  Pallas kernels: 742 us -> 644 us
  waiting for transfers between devices: 1.45 us -> 96.2 us
  matrix products: 27.5 us -> 0 us
    pallas_call x1, Pallas kernels: 253 us -> 118 us  [gather_front(): pl.pallas_call(functools.partial(gather_kernel, wide_count, narrow_count)...]
    all_gather x1, waiting for transfers between devices: 0.02 us -> 95.4 us  [shards(): lax.all_gather(jnp.pad(expand_weight.transpose(1, 2, 0), ((0, 0), (0, til...]
    pallas_call x1, Pallas kernels: 50.7 us -> 82.4 us  [attention_forward(): pl.pallas_call(functools.partial(attention_forward_kernel, narrow_count),...]
    dot_general x2 -> x0, matrix products: 27.5 us -> none  [dot(): lax.dot_general(left, right, (dims, ((), ())), preferred_element_type=jnp...]
  transfers between devices with their start and end apart: 4 -> 4, of which waited for: 0 -> 1; matrix products, arithmetic and copies ran while one was open for 5% -> 5% of each run, Pallas kernels for 68% -> 43%
where the time goes in v5:
time: 819 us; the launch traced here: 813 us
  Pallas kernels  644 us (79%)
  waiting for transfers between devices  96.2 us (12%)
  other arithmetic  31.2 us (4%)
  local copies, waits for them, and re-layouts  25.1 us (3%)
  between operations  16.5 us (2%)
    pallas_call x1, Pallas kernels, attention_backward(): pl.pallas_call(functools.partial(attention_backward_kernel, wide_count, n...  134 us
    pallas_call x1, Pallas kernels, input_backward(): pl.pallas_call(functools.partial(input_backward_kernel, wide_count, narro...  134 us
    pallas_call x1, Pallas kernels, gather_front(): pl.pallas_call(functools.partial(gather_kernel, wide_count, narrow_count)...  118 us
    all_gather x1, waiting for transfers between devices, shards(): lax.all_gather(jnp.pad(expand_weight.transpose(1, 2, 0), ((0, 0), (0, til...  95.4 us
    pallas_call x1, Pallas kernels, geglu_forward(): pl.pallas_call(functools.partial(geglu_forward_kernel, wide_count), out_s...  87.7 us
    pallas_call x1, Pallas kernels, geglu_backward(): pl.pallas_call(functools.partial(geglu_backward_kernel, wide_count), out_...  87.6 us
    pallas_call x1, Pallas kernels, attention_forward(): pl.pallas_call(functools.partial(attention_forward_kernel, narrow_count),...  82.4 us
  transfers between devices with their start and end apart: 4, of which 1 were waited for; matrix products, arithmetic and copies ran while one was open for 5% of the time, Pallas kernels for 43%

profile of v5, /device:TPU:8, one launch (start us, length us, event | category | flops | bytes accessed | tf_op | source)
XLA Modules:
  0.0 813.4 jit_solution(8065122177565850766)
XLA Ops:
  9.5 2.1 concatenate.13
  12.2 118.3 %gather_front.1 = (bf16[4,256,2048]{2,1,0:T(8,128)(2,1)}, bf16[8,256,1536]{2,1,0:T(8,128)(2,1)}, bf16[8,256,2048]{2,1,0:T(8,128)(2,1)}, bf16[8,4,16,128]{3,2,1,0:T(8,128)(2,1)}, f32[1024,1536]{1,0:T(8,128)}) custom-call(bf16[256,2048]{1,0:T(8,128)(2,1)} %own.3, bf16[64,6144]{1,0:T(8,128)(2,1)} %heads_weight.1, bf16[64,2048]{1,0:T(8,128)(2,1)} %merge_weight.1, ...), custom_call_target="tpu_custom_call" | custom-call | flops 80000000000 | bytes 209715200 | tf_op jit(solution)/shard_map/gather_front/pallas_call | solution.py:1514
  138.2 2.3 fusion.7
  140.5 1.9 multiply_sine_fusion
  142.4 1.3 pad_maximum_fusion
  143.7 82.4 %attention_forward.1 = (bf16[1024,512]{1,0:T(8,128)(2,1)}, bf16[1024,512]{1,0:T(8,128)(2,1)}, bf16[1024,512]{1,0:T(8,128)(2,1)}, bf16[4,1024,1024]{2,1,0:T(8,128...) custom-call(f32[1024,1536]{1,0:T(8,128)} %get-tuple-element.43.tripl, ...), custom_call_target="tpu_custom_call" | custom-call | flops 60000002048 | bytes 209715200 | tf_op jit(solution)/shard_map/attention_forward/pallas_call | solution.py:1710
  226.1 95.4 %all-gather.3.cloned.1.call-done.expand = bf16[2,688,2048]{2,1,0:T(8,128)(2,1)} async-done(((bf16[2,688,512]{2,1,0:T(8,128)(2,1)}), bf16[2,688,2048]{2,1,0:T(8,128)(2,1)}) %all-gather.3.cloned.1.call-update) | async-done | bytes 5636112 | tf_op jit(solution)/shard_map/all_gather | solution.py:1834
  321.6 87.7 %geglu_forward.1 = (bf16[8,256,2048]{2,1,0:T(8,128)(2,1)}, bf16[8,256,768]{2,1,0:T(8,128)(2,1)}, bf16[8,256,768]{2,1,0:T(8,128)(2,1)}, bf16[8,256,768]{2,1,0:T(8,128)(2,1)}, f32[256,2048]{1,0:T(8,128)}) custom-call(bf16[256,2048]{1,0:T(8,128)(2,1)} %get-tuple-element.47.own, bf16[2,688,2048]{2,1,0:T(8,128)(2,1)} %all-gather.3.cloned.1.call-done.expand, ...), custom_call_target="tpu_custom_call" | custom-call | flops 19327352832 | bytes 209715200 | tf_op jit(solution)/shard_map/geglu_forward/pallas_call | solution.py:517
  409.2 2.6 fusion.14
  414.0 1.7 convert_reduce_fusion.1
  415.8 87.6 %geglu_backward.1 = (bf16[688,2048]{1,0:T(8,128)(2,1)}, bf16[2,688,2048]{2,1,0:T(8,128)(2,1)}, f32[256,2048]{1,0:T(8,128)}, f32[2,768]{1,0:T(2,128)}) custom-call(bf16[256,2048]{1,0:T(8,128)(2,1)} %get-tuple-element.89.own, bf16[2,688,2048]{2,1,0:T(8,128)(2,1)} %all-gather.3.cloned.1.call-done.expand, bf16[688,2048]{1,0:T(8,128)(2,1)} %all-gather.5.cloned.1.call-done.reduce, ...), custom_call_target="tpu_custom_call" | custom-call | flops 38654705664 | bytes 209715200 | tf_op jit(solution)/shard_map/geglu_backward/pallas_call | solution.py:685
  504.4 4.7 multiply_reduce_fusion
  509.1 2.0 copy-done
  511.1 3.0 fusion.11.attended
  514.1 134.3 %attention_backward.1 = (bf16[1024,1536]{1,0:T(8,128)(2,1)}, f32[64,2048]{1,0:T(8,128)}, f32[1,1536]{1,0:T(1,128)}, f32[1,2048]{1,0:T(1,128)}) custom-call(bf16[256,2048]{1,0:T(8,128)(2,1)} %fusion.11.attended, bf16[2048,2048]{1,0:T(8,128)(2,1)} %bitcast.48, bf16[256,2048]{1,0:T(8,128)(2,1)} %get-tuple-element.58.mixed, ...), custom_call_target="tpu_custom_call" | custom-call | flops 60000002048 | bytes 209715200 | tf_op jit(solution)/shard_map/attention_backward/pallas_call | solution.py:942
  649.8 1.4 reduce.31
  653.1 134.0 %input_backward.1 = (f32[256,2048]{1,0:T(8,128)}, f32[64,6144]{1,0:T(8,128)}, f32[16,128]{1,0:T(8,128)}) custom-call(bf16[1024,2048]{1,0:T(8,128)(2,1)} %bitcast.50, bf16[1024,1536]{1,0:T(8,128)(2,1)} %get-tuple-element.63.triple, bf16[2048,1536]{1,0:T(8,128)(2,1)} %bitcast.49, f32[8,4,16,128]{3,2,1,0:T(8,128)} %bitcast.34), custom_call_target="tpu_custom_call" | custom-call | flops 80000000000 | bytes 209715200 | tf_op jit(solution)/shard_map/input_backward/pallas_call | solution.py:1204
  787.1 1.3 slice.117
  788.4 1.2 slice.116
  789.6 1.3 slice.119
  794.4 4.1 multiply_add_fusion
  798.5 2.4 convert_element_type.71
  800.9 3.4 convert_bitcast_fusion
  804.3 1.1 copy.38
  (99 shorter events, 19.3 us)
Async XLA Ops:
  7.2 219.0 %all-gather.5.cloned.1.call-start = ((), (), s32[]{:S(2)}) async-start(), calls=%async_computation.3 | async-start | bytes 3522560 | tf_op jit(solution)/shard_map/all_gather | solution.py:1841
  130.5 1.5 copy-start.4
  130.5 4.6 copy-start.7
  130.5 191.0 %all-gather.3.cloned.1.call-start = ((), (), s32[]{:S(2)}) async-start(), calls=%async_computation.2 | async-start | bytes 7045120 | tf_op jit(solution)/shard_map/all_gather | solution.py:1834
  131.3 667.2 %reduce-scatter.5.cloned.1.call-start = ((), (), s32[]{:S(2)}) async-start(), calls=%async_computation.5 | async-start | bytes 3522560 | tf_op jit(solution)/shard_map/reduce_scatter | solution.py:1865
  411.8 1.2 copy-start.1
  503.4 0.9 copy-start.5
  503.4 297.5 %reduce-scatter.3.cloned.1.call-start = ((), (), s32[]{:S(2)}) async-start(), calls=%async_computation.4 | async-start | bytes 7045120 | tf_op jit(solution)/shard_map/reduce_scatter | solution.py:1869
  509.1 2.0 copy-start
  514.1 134.5 %copy-start.6 = (f32[2,768]{1,0:T(2,128)S(1)}, f32[2,768]{1,0:T(2,128)}, u32[]{:S(2)}) copy-start(f32[2,768]{1,0:T(2,128)} %get-tuple-element.67) | copy-start | bytes 18436
  800.9 3.4 copy-start.2
  804.3 1.4 copy-start.3
Sparse Core Ops, SparseCore 0:
  130.7 85.2 all-gather.4
  217.5 103.9 all-gather.2
  503.5 76.9 reduce-scatter.4
  582.8 117.6 reduce-scatter.2

commit v6 on v4

--- a/solution.py
+++ b/solution.py
@@ -109,7 +109,7 @@
 
 
 class PlaneExchange:
-    def __init__(self, wide_count, own, blocks, parts, from_mate, incoming, sems):
+    def __init__(self, wide_count, own, blocks, parts, from_mate, incoming, sems, cols=None):
         self.ring, self.position, self.core = ring_place(wide_count)
         self.own, self.blocks, self.parts = own, blocks, parts
         self.from_mate, self.incoming = from_mate, incoming
@@ -123,6 +123,7 @@
             self.own_sem,
         ) = sems
         self.half = parts.shape[1] // 2
+        self.cols = slice(None) if cols is None else cols
         self.far = self.ring // 2
         self.started = []
 
@@ -226,8 +227,8 @@
     def share(self, offset):
         chip = chip_at(self.position + offset, self.ring)
         self.start(
-            self.parts.at[self.slot(offset, True)],
-            self.from_mate.at[chip],
+            self.parts.at[self.slot(offset, True), :, self.cols],
+            self.from_mate.at[chip, :, self.cols],
             self.mate_send.at[chip],
             self.mate_recv.at[chip],
             self.device(0, True),
@@ -236,8 +237,8 @@
     def shared(self, offset):
         chip = chip_at(self.position + offset, self.ring)
         pltpu.make_async_remote_copy(
-            src_ref=self.parts.at[self.slot(offset)],
-            dst_ref=self.from_mate.at[chip],
+            src_ref=self.parts.at[self.slot(offset), :, self.cols],
+            dst_ref=self.from_mate.at[chip, :, self.cols],
             send_sem=self.mate_send.at[chip],
             recv_sem=self.mate_recv.at[chip],
             device_id=self.device(0, True),
@@ -246,9 +247,9 @@
 
     def chip_sum(self, offset, rows):
         chip = chip_at(self.position + offset, self.ring)
-        return self.parts[self.slot(offset), rows].astype(jnp.float32) + self.from_mate[
-            chip, rows
-        ].astype(jnp.float32)
+        return self.parts[self.slot(offset), rows, self.cols].astype(
+            jnp.float32
+        ) + self.from_mate[chip, rows, self.cols].astype(jnp.float32)
 
     def send_sum(self, way, distance, part):
         offset = distance if way == 0 else -distance
@@ -262,21 +263,21 @@
             there = pl.ds(pl.multiple_of(part * self.half + i * 16, 16), 16)
             total = self.chip_sum(offset, there)
             if distance < begins:
-                total += self.incoming[way, distance, part, here].astype(jnp.float32)
-            self.parts[slot, there] = total.astype(jnp.bfloat16)
+                total += self.incoming[way, distance, part, here, self.cols].astype(jnp.float32)
+            self.parts[slot, there, self.cols] = total.astype(jnp.bfloat16)
             return carry
 
         lax.fori_loop(0, self.half // 16, chunk, 0)
         self.start(
-            self.parts.at[slot, self.rows(part)],
-            self.incoming.at[way, distance - 1, part],
+            self.parts.at[slot, self.rows(part), self.cols],
+            self.incoming.at[way, distance - 1, part, :, self.cols],
             self.sum_send.at[way, distance - 1, part],
             self.sum_recv.at[way, distance - 1, part],
             self.device(1 if way == 0 else -1),
         )
 
     def sum_arrived(self, way, distance, part):
-        target = self.incoming.at[way, distance, part]
+        target = self.incoming.at[way, distance, part, :, self.cols]
         pltpu.make_async_remote_copy(
             src_ref=target,
             dst_ref=target,
@@ -286,7 +287,7 @@
             device_id_type=pl.DeviceIdType.MESH,
         ).wait_recv()
 
-    def run(self, compute):
+    def run(self, compute, before, between):
         keep = self.send_own()
         keep.wait()
         self.receive_mate(0)
@@ -304,7 +305,43 @@
         self.receive_mate(self.far)
         compute(chip_at(self.position + self.far, self.ring))
         self.share(self.far)
+        before()
         self.far_sums()
+        between()
+        self.last_sums()
+
+    def run_gather(self, compute, between):
+        keep = self.send_own()
+        keep.wait()
+        self.receive_mate(0)
+        compute(chip_at(self.position, self.ring))
+        done = 1
+        for distance in range(1, self.far):
+            self.receive(distance)
+            between(done)
+            done += 1
+            for offset in (-distance, distance):
+                self.receive_mate(offset)
+                compute(chip_at(self.position + offset, self.ring))
+        self.receive(self.far)
+        between(done)
+        done += 1
+        self.receive_mate(self.far)
+        compute(chip_at(self.position + self.far, self.ring))
+        return done
+
+    def run_sums(self, compute):
+        compute(chip_at(self.position + self.far, self.ring))
+        self.share(self.far)
+        for distance in range(self.far - 1, 0, -1):
+            for offset in (-distance, distance):
+                compute(chip_at(self.position + offset, self.ring))
+                self.share(offset)
+            if distance == self.far - 1:
+                self.far_sums()
+                self.first_sums()
+        compute(chip_at(self.position, self.ring))
+        self.share(0)
         self.last_sums()
 
     def first_sums(self):
@@ -341,8 +378,8 @@
                 there = pl.ds(pl.multiple_of(part * self.half + i * 16, 16), 16)
                 total = self.chip_sum(0, there)
                 for way in range(2):
-                    total += self.incoming[way, 0, part, here].astype(jnp.float32)
-                result[there] = total.astype(result.dtype)
+                    total += self.incoming[way, 0, part, here, self.cols].astype(jnp.float32)
+                result[there, self.cols] = total.astype(result.dtype)
                 return carry
 
             lax.fori_loop(0, self.half // 16, chunk, 0)
@@ -399,20 +436,237 @@
     ref[2 * chip + 1, :, cols] = value[rows:].astype(ref.dtype)
 
 
-def tiles(count, tile, body):
+def tiles(count, tile, body, start=0):
     def step(i, carry):
-        body(pl.ds(pl.multiple_of(i * tile, tile), tile))
+        body(pl.ds(pl.multiple_of(start + i * tile, tile), tile))
         return carry
 
     lax.fori_loop(0, count // tile, step, 0)
+
+
+class LineExchange:
+    def __init__(self, narrow_count):
+        self.count = narrow_count
+        self.mine = lax.axis_index("narrow")
+        self.started = []
+
+    def peer(self, offset):
+        return (self.mine + offset) % self.count
+
+    def greet(self, extra=0):
+        barrier = pltpu.get_barrier_semaphore()
+        for offset in range(1, self.count):
+            pl.semaphore_signal(
+                barrier,
+                inc=1,
+                device_id={"narrow": self.peer(offset)},
+                device_id_type=pl.DeviceIdType.MESH,
+            )
+        pl.semaphore_wait(barrier, self.count - 1 + extra)
+
+    def copy(self, source, target, send_sem, recv_sem, where):
+        return pltpu.make_async_remote_copy(
+            src_ref=source,
+            dst_ref=target,
+            send_sem=send_sem,
+            recv_sem=recv_sem,
+            device_id={"narrow": where},
+            device_id_type=pl.DeviceIdType.MESH,
+        )
+
+    def send(self, offset, source, landing, send_sems, recv_sems):
+        peer = self.peer(offset)
+        copy = self.copy(
+            source, landing.at[self.mine], send_sems.at[offset - 1], recv_sems.at[self.mine], peer
+        )
+        copy.start()
+        self.started.append(copy)
+
+    def arrived(self, offset, landing, send_sems, recv_sems):
+        peer = self.peer(offset)
+        self.copy(
+            landing.at[peer], landing.at[peer], send_sems.at[offset - 1], recv_sems.at[peer], peer
+        ).wait_recv()
+
+    def drain(self):
+        for copy in self.started:
+            copy.wait_send()
+
+
+class LineSum:
+    def __init__(self, line, view, landing, send_sems, recv_sems):
+        self.line, self.view, self.landing = line, view, landing
+        self.send_sems, self.recv_sems = send_sems, recv_sems
+        self.last = line.count - 1
+
+    def reaches(self, way, offset):
+        here = self.line.mine
+        return here + offset <= self.last if way == 0 else here - offset >= 0
+
+    def follows(self, way):
+        here = self.line.mine
+        return here > 0 if way == 0 else here < self.last
+
+    def target(self, way, offset):
+        return self.line.mine + offset if way == 0 else self.line.mine - offset
+
+    def copy(self, way, offset):
+        return self.line.copy(
+            self.view(self.target(way, offset)),
+            self.landing.at[way, offset - 1],
+            self.send_sems.at[way, offset - 1],
+            self.recv_sems.at[way, offset - 1],
+            self.line.mine + 1 if way == 0 else self.line.mine - 1,
+        )
+
+    def arrived(self, way, offset):
+        landing = self.landing.at[way, offset]
+        self.line.copy(
+            landing,
+            landing,
+            self.send_sems.at[way, offset],
+            self.recv_sems.at[way, offset],
+            self.line.mine,
+        ).wait_recv()
+
+    def add(self, way, offset):
+        held = self.view(self.target(way, offset))
+
+        def chunk(i, carry):
+            some = pl.ds(pl.multiple_of(i * 16, 16), 16)
+            held[some] = (
+                held[some].astype(jnp.float32)
+                + self.landing[way, offset, some].astype(jnp.float32)
+            ).astype(jnp.bfloat16)
+            return carry
+
+        lax.fori_loop(0, self.landing.shape[2] // 16, chunk, 0)
+
+    def begin(self):
+        for offset in range(self.last, 0, -1):
+            for way in range(2):
+
+                @pl.when(self.reaches(way, offset) & jnp.logical_not(self.follows(way)))
+                def _():
+                    self.copy(way, offset).start()
+
+    def step(self, offset):
+        for way in range(2):
+
+            @pl.when(self.reaches(way, offset) & self.follows(way))
+            def _():
+                self.arrived(way, offset)
+                self.add(way, offset)
+                self.copy(way, offset).start()
+
+    def finish(self, result):
+        held = self.view(self.line.mine)
+        count = self.landing.shape[2] // 16
+
+        def begin(i, carry):
+            some = pl.ds(pl.multiple_of(i * 16, 16), 16)
+            result[some] = held[some].astype(result.dtype)
+            return carry
+
+        lax.fori_loop(0, count, begin, 0)
+        for way in range(2):
+
+            @pl.when(self.follows(way))
+            def _():
+                self.arrived(way, 0)
+
+                def chunk(i, carry):
+                    some = pl.ds(pl.multiple_of(i * 16, 16), 16)
+                    result[some] += self.landing[way, 0, some].astype(result.dtype)
+                    return carry
+
+                lax.fori_loop(0, count, chunk, 0)
+
+    def drain(self):
+        for offset in range(1, self.last + 1):
+            for way in range(2):
+
+                @pl.when(self.reaches(way, offset))
+                def _():
+                    self.copy(way, offset).wait_send()
+
+
+class LineGather:
+    def __init__(self, line, view, send_sems, recv_sems):
+        self.line, self.view = line, view
+        self.send_sems, self.recv_sems = send_sems, recv_sems
+        self.last = line.count - 1
+
+    def copy(self, way, block):
+        target = self.view(block)
+        here = self.line.mine
+        return self.line.copy(
+            target,
+            target,
+            self.send_sems.at[way, block],
+            self.recv_sems.at[block],
+            here + 1 if way == 0 else here - 1,
+        )
+
+    def goes(self, way):
+        return self.line.mine < self.last if way == 0 else self.line.mine > 0
+
+    def has(self, way, step):
+        here = self.line.mine
+        return here - step >= 0 if way == 0 else here + step <= self.last
+
+    def block(self, way, step):
+        return self.line.mine - step if way == 0 else self.line.mine + step
+
+    def send_own(self):
+        for way in range(2):
+
+            @pl.when(self.goes(way))
+            def _():
+                self.copy(way, self.line.mine).start()
+
+    def step(self, step):
+        for way in range(2):
+
+            @pl.when(self.has(way, step))
+            def _():
+                self.copy(way, self.block(way, step)).wait_recv()
+
+                @pl.when(self.goes(way))
+                def _():
+                    self.copy(way, self.block(way, step)).start()
+
+    def each(self, step, body):
+        for way in range(2):
+
+            @pl.when(self.has(way, step))
+            def _():
+                body(self.block(way, step))
+
+    def drain(self):
+        for way in range(2):
+            for step in range(self.last + 1):
+
+                @pl.when(self.has(way, step) & self.goes(way))
+                def _():
+                    self.copy(way, self.block(way, step)).wait_send()
+
+
+def greet_plane(plane):
+    barrier = pltpu.get_barrier_semaphore()
+    for where in (plane.device(-1), plane.device(1), plane.device(0, True)):
+        pl.semaphore_signal(barrier, inc=1, device_id=where, device_id_type=pl.DeviceIdType.MESH)
 
 
 def geglu_forward_kernel(
     wide_count,
+    narrow_count,
     own,
-    expand,
+    gate_expand,
+    upper_expand,
     reduce,
     shift,
+    reduce_out,
     rows_all,
     active_out,
     slope_out,
@@ -436,15 +690,48 @@
     gelu,
     load_sems,
     keep_sems,
+    reduce_send,
+    reduce_recv,
+    late_mate_send,
+    late_mate_recv,
+    late_sum_send,
+    late_sum_recv,
 ):
     sems = (gather_send, gather_recv, mate_send, mate_recv, sum_send, sum_recv, own_sem)
-    plane = PlaneExchange(wide_count, own, blocks, parts, from_mate, incoming, sems)
+    late_sems = (None, None, late_mate_send, late_mate_recv, late_sum_send, late_sum_recv, None)
+    line = LineExchange(narrow_count)
+    filled, cols = reduce.shape
+    width = own.shape[1]
+    upper = (2 * line.mine) // narrow_count
+    late = pl.multiple_of((1 - upper) * (width - cols), cols)
+    early = pl.multiple_of(upper * cols, cols)
+    plane = PlaneExchange(
+        wide_count, own, blocks, parts, from_mate, incoming, sems, pl.ds(early, width - cols)
+    )
+    late_plane = PlaneExchange(
+        wide_count, None, None, parts, from_mate, incoming, late_sems, pl.ds(late, cols)
+    )
     loads = [
-        load_padded(expand.at[0], expand_mat.at[0], load_sems.at[0]),
-        load_padded(expand.at[1], expand_mat.at[1], load_sems.at[1]),
-        load_padded(reduce, reduce_mat, load_sems.at[2]),
+        load_padded(gate_expand, expand_mat.at[0], load_sems.at[0]),
+        load_padded(upper_expand, expand_mat.at[1], load_sems.at[1]),
     ]
-    plane.greet()
+
+    def reduce_cols(block):
+        return reduce_mat.at[
+            pl.ds(0, filled), pl.ds(pl.multiple_of(block * cols, cols), cols)
+        ]
+
+    line_reduce = LineGather(line, reduce_cols, reduce_send, reduce_recv)
+    own_reduce = pltpu.make_async_copy(reduce, reduce_cols(line.mine), load_sems.at[2])
+    own_reduce.start()
+    if filled < reduce_mat.shape[0]:
+        reduce_mat[filled:] = jnp.zeros(
+            (reduce_mat.shape[0] - filled, reduce_mat.shape[1]), reduce_mat.dtype
+        )
+    greet_plane(plane)
+    line.greet(3)
+    own_reduce.wait()
+    line_reduce.send_own()
     kept = []
     waiting = list(loads)
 
@@ -469,12 +756,6 @@
 
         tiles(active.shape[2], 256, units)
 
-        def outputs(cols):
-            set_pair(
-                parts, chip, cols, dot(pair_rows(active, chip), reduce_mat[:, cols], ((1,), (0,)))
-            )
-
-        tiles(parts.shape[2], 256, outputs)
         pair = pl.ds(2 * chip, 2)
         for index, (source, target) in enumerate(
             ((active, active_out), (slope, slope_out), (gelu, gelu_out), (blocks, rows_all))
@@ -485,14 +766,43 @@
             copy.start()
             kept.append(copy)
 
-    plane.run(compute)
+    def compute_sums(start, count):
+        def compute(chip):
+            def outputs(some):
+                part = dot(pair_rows(active, chip), reduce_mat[:, some], ((1,), (0,)))
+                set_pair(parts, chip, some, part)
+
+            tiles(count, 256, outputs, start)
+
+        return compute
+
+    def between(index):
+        if index < narrow_count:
+            line_reduce.step(index)
+
+    done = plane.run_gather(compute, between)
+    for step in range(done, narrow_count - 1):
+        line_reduce.step(step)
+    plane.run_sums(compute_sums(early, width - cols))
+    line_reduce.step(narrow_count - 1)
+    keep_reduce = pltpu.make_async_copy(
+        reduce_mat.at[pl.ds(0, filled)], reduce_out, load_sems.at[3]
+    )
+    keep_reduce.start()
+    late_plane.run_sums(compute_sums(late, cols))
     plane.finish(feed)
+    late_plane.finish(feed)
     plane.drain()
+    late_plane.drain()
+    keep_reduce.wait()
+    line_reduce.drain()
     for copy in kept:
         copy.wait()
 
 
-def geglu_forward(wide_count, hidden_low, expand_full, reduce_full, shift):
+def geglu_forward(
+    wide_count, narrow_count, hidden_low, gate_expand, upper_expand, reduce_weight, shift
+):
     rows, width = hidden_low.shape
     padded = shift.shape[1]
     anywhere = pl.BlockSpec(memory_space=pl.ANY)
@@ -504,20 +814,23 @@
         pltpu.VMEM((wide_count, rows, padded), jnp.bfloat16),
         pltpu.VMEM((wide_count, rows, padded), jnp.bfloat16),
         pltpu.VMEM((wide_count, rows, padded), jnp.bfloat16),
-        pltpu.SemaphoreType.DMA((3,)),
+        pltpu.SemaphoreType.DMA((4,)),
         pltpu.SemaphoreType.DMA((wide_count // 2, 4)),
-    ]
+        pltpu.SemaphoreType.DMA((2, narrow_count)),
+        pltpu.SemaphoreType.DMA((narrow_count,)),
+    ] + sum_scratch(wide_count, rows, width)[3:]
     return pl.pallas_call(
-        functools.partial(geglu_forward_kernel, wide_count),
+        functools.partial(geglu_forward_kernel, wide_count, narrow_count),
         out_shape=(
+            jax.ShapeDtypeStruct((reduce_weight.shape[0], width), jnp.bfloat16),
             jax.ShapeDtypeStruct((wide_count, rows, width), jnp.bfloat16),
             kept,
             kept,
             kept,
             jax.ShapeDtypeStruct((rows, width), jnp.float32),
         ),
-        in_specs=[anywhere, anywhere, anywhere, vmem],
-        out_specs=(anywhere, anywhere, anywhere, anywhere, vmem),
+        in_specs=[anywhere, anywhere, anywhere, anywhere, vmem],
+        out_specs=(anywhere, anywhere, anywhere, anywhere, anywhere, vmem),
         scratch_shapes=scratch,
         compiler_params=pltpu.CompilerParams(
             collective_id=1, has_side_effects=True, vmem_limit_bytes=kernel_memory
@@ -526,18 +839,22 @@
             flops=6 * wide_count * rows * padded * width, bytes_accessed=200 * 2**20, transcendentals=0
         ),
         name="geglu_forward",
-    )(hidden_low, expand_full, reduce_full, shift)
+    )(hidden_low, gate_expand, upper_expand, reduce_weight, shift)
 
 
 def geglu_backward_kernel(
     wide_count,
+    narrow_count,
     own,
-    expand,
+    gate_expand,
+    upper_expand,
     reduce,
     slope_in,
     gelu_in,
-    rows_all,
-    unit_grads,
+    active_in,
+    rows_in,
+    reduce_grad,
+    expand_part,
     hidden_grad,
     unit_sums,
     blocks,
@@ -555,22 +872,44 @@
     reduce_mat,
     slope,
     gelu,
+    active,
+    rows_all,
+    staged,
     load_sems,
     keep_sems,
+    line_in,
+    line_send,
+    line_recv,
 ):
     sems = (gather_send, gather_recv, mate_send, mate_recv, sum_send, sum_recv, own_sem)
     plane = PlaneExchange(wide_count, own, blocks, parts, from_mate, incoming, sems)
     loads = [
-        load_padded(expand.at[0], expand_mat.at[0], load_sems.at[0]),
-        load_padded(expand.at[1], expand_mat.at[1], load_sems.at[1]),
+        load_padded(gate_expand, expand_mat.at[0], load_sems.at[0]),
+        load_padded(upper_expand, expand_mat.at[1], load_sems.at[1]),
         load_padded(reduce, reduce_mat, load_sems.at[2]),
         pltpu.make_async_copy(slope_in, slope, load_sems.at[3]),
         pltpu.make_async_copy(gelu_in, gelu, load_sems.at[4]),
     ]
+    late_loads = [
+        pltpu.make_async_copy(active_in, active, load_sems.at[5]),
+        pltpu.make_async_copy(rows_in, rows_all, load_sems.at[6]),
+    ]
     for copy in loads[3:]:
         copy.start()
     unit_sums[...] = jnp.zeros_like(unit_sums)
-    plane.greet()
+    line = LineExchange(narrow_count)
+    filled, line_cols = line_in.shape[2:]
+
+    def line_part(block):
+        return reduce_mat.at[
+            pl.ds(0, filled), pl.ds(pl.multiple_of(block * line_cols, line_cols), line_cols)
+        ]
+
+    line_sum = LineSum(line, line_part, line_in, line_send, line_recv)
+    greet_plane(plane)
+    line.greet(3)
+    for copy in late_loads:
+        copy.start()
     kept = []
     waiting = list(loads)
 
@@ -601,24 +940,77 @@
             )
 
         tiles(parts.shape[2], 256, outputs)
-        pair = pl.ds(2 * chip, 2)
-        for index, (source, target) in enumerate(
-            ((slope, unit_grads.at[0]), (gelu, unit_grads.at[1]), (blocks, rows_all))
-        ):
+
+    def product(left, right, start):
+        tokens = left.shape[0] * left.shape[1]
+        return dot(
+            left[:, :, start : start + 256].reshape(tokens, 256),
+            right[...].reshape(tokens, right.shape[2]),
+            ((0,), (0,)),
+        ).astype(jnp.bfloat16)
+
+    def reduce_work():
+        for copy in late_loads:
+            copy.wait()
+        for start in range(0, active.shape[2], 256):
+            reduce_mat[start : start + 256] = product(active, blocks, start)
+        line_sum.begin()
+
+    def expand_work(left, start, target):
+        def work():
+            index = len(kept)
+            if index >= 2:
+                kept[index - 2].wait()
+            staged[index % 2] = product(left, rows_all, start)
+            stop = min(256, target.shape[0] - start)
             copy = pltpu.make_async_copy(
-                source.at[pair], target.at[pair], keep_sems.at[chip, index]
+                staged.at[index % 2, pl.ds(0, stop)],
+                target.at[pl.ds(start, stop)],
+                keep_sems.at[index % 2],
             )
             copy.start()
             kept.append(copy)
 
-    plane.run(compute)
+        return work
+
+    works = [
+        expand_work(left, start, target)
+        for left, target in ((slope, expand_part.at[0]), (gelu, expand_part.at[1]))
+        for start in range(0, target.shape[0], 256)
+    ]
+    steps = [
+        functools.partial(line_sum.step, offset) for offset in range(narrow_count - 2, 0, -1)
+    ]
+    middle = len(works) // 2
+    works = [works[:middle], steps[: len(steps) // 2], works[middle:], steps[len(steps) // 2 :]]
+
+    def many(calls):
+        for call in calls:
+            call()
+
+    plane.run(compute, reduce_work, functools.partial(many, works[0] + works[1]))
+    many(works[2])
     plane.finish(hidden_grad)
+    many(works[3])
+    line_sum.finish(reduce_grad)
+    line_sum.drain()
     plane.drain()
-    for copy in kept:
+    for copy in kept[-2:]:
         copy.wait()
 
 
-def geglu_backward(wide_count, feed_grad, expand_full, reduce_full, slope, gelu):
+def geglu_backward(
+    wide_count,
+    narrow_count,
+    feed_grad,
+    gate_expand,
+    upper_expand,
+    reduce_full,
+    slope,
+    gelu,
+    active,
+    rows_all,
+):
     rows, width = feed_grad.shape
     padded = slope.shape[2]
     anywhere = pl.BlockSpec(memory_space=pl.ANY)
@@ -628,83 +1020,38 @@
         pltpu.VMEM((padded, width), jnp.bfloat16),
         pltpu.VMEM((wide_count, rows, padded), jnp.bfloat16),
         pltpu.VMEM((wide_count, rows, padded), jnp.bfloat16),
-        pltpu.SemaphoreType.DMA((5,)),
-        pltpu.SemaphoreType.DMA((wide_count // 2, 3)),
+        pltpu.VMEM((wide_count, rows, padded), jnp.bfloat16),
+        pltpu.VMEM((wide_count, rows, width), jnp.bfloat16),
+        pltpu.VMEM((2, 256, width), jnp.bfloat16),
+        pltpu.SemaphoreType.DMA((7,)),
+        pltpu.SemaphoreType.DMA((2,)),
+        pltpu.VMEM(
+            (2, narrow_count - 1, reduce_full.shape[0], width // narrow_count), jnp.bfloat16
+        ),
+        pltpu.SemaphoreType.DMA((2, narrow_count - 1)),
+        pltpu.SemaphoreType.DMA((2, narrow_count - 1)),
     ]
     return pl.pallas_call(
-        functools.partial(geglu_backward_kernel, wide_count),
+        functools.partial(geglu_backward_kernel, wide_count, narrow_count),
         out_shape=(
-            jax.ShapeDtypeStruct((wide_count, rows, width), jnp.bfloat16),
-            jax.ShapeDtypeStruct((2, wide_count, rows, padded), jnp.bfloat16),
+            jax.ShapeDtypeStruct(
+                (reduce_full.shape[0], width // narrow_count), jnp.float32
+            ),
+            jax.ShapeDtypeStruct((2, *gate_expand.shape), jnp.bfloat16),
             jax.ShapeDtypeStruct((rows, width), jnp.float32),
             jax.ShapeDtypeStruct((2, padded), jnp.float32),
         ),
-        in_specs=[anywhere] * 5,
-        out_specs=(anywhere, anywhere, vmem, vmem),
+        in_specs=[anywhere] * 8,
+        out_specs=(vmem, anywhere, vmem, vmem),
         scratch_shapes=scratch,
         compiler_params=pltpu.CompilerParams(
-            collective_id=2, has_side_effects=True, vmem_limit_bytes=kernel_memory
+            collective_id=2, has_side_effects=True, vmem_limit_bytes=63 * 2**20
         ),
         cost_estimate=pl.CostEstimate(
-            flops=6 * wide_count * rows * padded * width, bytes_accessed=200 * 2**20, transcendentals=0
+            flops=12 * wide_count * rows * padded * width, bytes_accessed=200 * 2**20, transcendentals=0
         ),
         name="geglu_backward",
-    )(feed_grad, expand_full, reduce_full, slope, gelu)
-
-
-class LineExchange:
-    def __init__(self, narrow_count):
-        self.count = narrow_count
-        self.mine = lax.axis_index("narrow")
-        self.started = []
-
-    def peer(self, offset):
-        return (self.mine + offset) % self.count
-
-    def greet(self, extra=0):
-        barrier = pltpu.get_barrier_semaphore()
-        for offset in range(1, self.count):
-            pl.semaphore_signal(
-                barrier,
-                inc=1,
-                device_id={"narrow": self.peer(offset)},
-                device_id_type=pl.DeviceIdType.MESH,
-            )
-        pl.semaphore_wait(barrier, self.count - 1 + extra)
-
-    def copy(self, source, target, send_sem, recv_sem, where):
-        return pltpu.make_async_remote_copy(
-            src_ref=source,
-            dst_ref=target,
-            send_sem=send_sem,
-            recv_sem=recv_sem,
-            device_id={"narrow": where},
-            device_id_type=pl.DeviceIdType.MESH,
-        )
-
-    def send(self, offset, source, landing, send_sems, recv_sems):
-        peer = self.peer(offset)
-        copy = self.copy(
-            source, landing.at[self.mine], send_sems.at[offset - 1], recv_sems.at[self.mine], peer
-        )
-        copy.start()
-        self.started.append(copy)
-
-    def arrived(self, offset, landing, send_sems, recv_sems):
-        peer = self.peer(offset)
-        self.copy(
-            landing.at[peer], landing.at[peer], send_sems.at[offset - 1], recv_sems.at[peer], peer
-        ).wait_recv()
-
-    def drain(self):
-        for copy in self.started:
-            copy.wait_send()
-
-
-def greet_plane(plane):
-    barrier = pltpu.get_barrier_semaphore()
-    for where in (plane.device(-1), plane.device(1), plane.device(0, True)):
-        pl.semaphore_signal(barrier, inc=1, device_id=where, device_id_type=pl.DeviceIdType.MESH)
+    )(feed_grad, gate_expand, upper_expand, reduce_full, slope, gelu, active, rows_all)
 
 
 def rotate_lanes(vectors, cosine, signed_sine):
@@ -1005,50 +1352,8 @@
 
     tiles(width, 256, input_cols)
 
-    def line_copy(way, offset):
-        target = here + offset if way == 0 else here - offset
-        return line.copy(
-            line_parts.at[target],
-            line_in.at[way, offset - 1],
-            line_send.at[way, offset - 1],
-            line_recv.at[way, offset - 1],
-            here + 1 if way == 0 else here - 1,
-        )
-
-    def line_arrived(way, offset):
-        landing = line_in.at[way, offset]
-        line.copy(
-            landing, landing, line_send.at[way, offset], line_recv.at[way, offset], here
-        ).wait_recv()
-
-    def add_line(way, offset, slot):
-        def chunk(i, carry):
-            some = pl.ds(pl.multiple_of(i * 16, 16), 16)
-            line_parts[slot, some] = (
-                line_parts[slot, some].astype(jnp.float32)
-                + line_in[way, offset, some].astype(jnp.float32)
-            ).astype(jnp.bfloat16)
-            return carry
-
-        lax.fori_loop(0, rows // 16, chunk, 0)
-
-    def line_step(offset):
-        for way in range(2):
-            reaches = here + offset <= last if way == 0 else here - offset >= 0
-            follows = here > 0 if way == 0 else here < last
-
-            @pl.when(reaches)
-            def _():
-                if offset < last:
-
-                    @pl.when(follows)
-                    def _():
-                        line_arrived(way, offset)
-                        add_line(way, offset, here + offset if way == 0 else here - offset)
-
-                line_copy(way, offset).start()
-
-    line_step(last)
+    line_sum = LineSum(line, lambda target: line_parts.at[target], line_in, line_send, line_recv)
+    line_sum.begin()
 
     block = parts.shape[1]
 
@@ -1061,7 +1366,7 @@
     for offset in range(plane.ring):
         plane.share(offset)
     for offset in range(last - 1, last // 2, -1):
-        line_step(offset)
+        line_sum.step(offset)
     plane.first_sums()
     plane.far_sums()
 
@@ -1078,7 +1383,7 @@
 
     plane.last_sums()
     for offset in range(last // 2, 0, -1):
-        line_step(offset)
+        line_sum.step(offset)
     plane.finish(heads_out)
     count = heads_grad.shape[0]
 
@@ -1098,26 +1403,7 @@
         result += small_line[index]
     small_out[...] = result
 
-    def own_rows(i, carry):
-        some = pl.ds(pl.multiple_of(i * 16, 16), 16)
-        input_part[some] = line_parts[here, some].astype(jnp.float32)
-        return carry
-
-    lax.fori_loop(0, rows // 16, own_rows, 0)
-    for way in range(2):
-        follows = here > 0 if way == 0 else here < last
-
-        @pl.when(follows)
-        def _():
-            line_arrived(way, 0)
-
-            def chunk(i, carry):
-                some = pl.ds(pl.multiple_of(i * 16, 16), 16)
-                input_part[some] += line_in[way, 0, some].astype(jnp.float32)
-                return carry
-
-            lax.fori_loop(0, rows // 16, chunk, 0)
-
+    line_sum.finish(input_part)
     for offset in range(1, narrow_count):
         line.arrived(offset, heads_in, heads_send, heads_recv)
     own_cols = triple.shape[1] // 3
@@ -1127,14 +1413,7 @@
             heads_grad[:, start : start + own_cols] = heads_in[
                 index, :, which * own_cols : (which + 1) * own_cols
             ].astype(jnp.float32)
-    for offset in range(1, narrow_count):
-        for way in range(2):
-            reaches = here + offset <= last if way == 0 else here - offset >= 0
-
-            @pl.when(reaches)
-            def _():
-                line_copy(way, offset).wait_send()
-
+    line_sum.drain()
     for copy in small_copies:
         copy.wait_send()
     line.drain()
@@ -1257,24 +1536,7 @@
         start = which * narrow_count * own_cols + where * own_cols
         return pl.ds(pl.multiple_of(start, own_cols), own_cols)
 
-    def line_rows(way, block):
-        source = rows_all.at[block]
-        return line.copy(
-            source,
-            source,
-            rows_send.at[way, block],
-            rows_recv.at[block],
-            here + 1 if way == 0 else here - 1,
-        )
-
-    def goes(way):
-        return here < last if way == 0 else here > 0
-
-    def has(way, step):
-        return here - step >= 0 if way == 0 else here + step <= last
-
-    def block_of(way, step):
-        return here - step if way == 0 else here + step
+    line_rows = LineGather(line, lambda block: rows_all.at[block], rows_send, rows_recv)
 
     keep_rows = pltpu.make_async_copy(own, rows_all.at[here], local_sems.at[0])
     keep_rows.start()
@@ -1333,11 +1595,7 @@
     for offset in range(1, narrow_count):
         start(small_copy(offset, line.peer(offset), here))
     keep_rows.wait()
-    for way in range(2):
-
-        @pl.when(goes(way))
-        def _():
-            line_rows(way, here).start()
+    line_rows.send_own()
 
     for offset in range(1, narrow_count):
         start(merge_copy(offset, line.peer(offset), here))
@@ -1364,17 +1622,6 @@
     for offset in range(1, wide_count):
         start(wide_copy(offset, place))
 
-    def rows_step(step):
-        for way in range(2):
-
-            @pl.when(has(way, step))
-            def _():
-                line_rows(way, block_of(way, step)).wait_recv()
-
-                @pl.when(goes(way))
-                def _():
-                    line_rows(way, block_of(way, step)).start()
-
     def project(block):
         def cols_step(cols):
             weight = heads_all[:, :, cols].reshape(width, cols.size)
@@ -1385,17 +1632,7 @@
         tiles(columns, 256, cols_step)
 
     def project_step(step):
-        for way in range(2):
-
-            @pl.when(has(way, step))
-            def _():
-                project(block_of(way, step))
-
-    keep_merge.wait()
-    for offset in range(1, narrow_count):
-        merge_copy(offset, line.peer(offset), line.peer(offset)).wait_recv()
-    rows_step(1)
-    merge_ring.send_own()
+        line_rows.each(step, project)
 
     def gather(ring, distance):
         ring.receive(distance)
@@ -1403,9 +1640,6 @@
         if distance < ring.far:
             ring.receive_mate(distance)
 
-    heads_ring.receive_mate(0)
-    for distance in range(1, heads_ring.far + 1):
-        gather(heads_ring, distance)
     outs = []
 
     def keep_out(source, target):
@@ -1413,30 +1647,32 @@
         copy.start()
         outs.append(copy)
 
+    line_rows.step(1)
+    heads_ring.receive_mate(0)
+    for distance in range(1, heads_ring.far):
+        gather(heads_ring, distance)
+    keep_merge.wait()
+    for offset in range(1, narrow_count):
+        merge_copy(offset, line.peer(offset), line.peer(offset)).wait_recv()
+    merge_ring.send_own()
+    gather(heads_ring, heads_ring.far)
     keep_out(heads_all, heads_out)
     project(here)
-    merge_ring.receive_mate(0)
-    for distance in range(1, merge_ring.far):
-        gather(merge_ring, distance)
-    project_step(1)
-    rows_step(2)
+    for step in range(2, narrow_count):
+        line_rows.step(step)
+        project_step(step - 1)
+        if step == 2:
+            merge_ring.receive_mate(0)
+            for distance in range(1, merge_ring.far):
+                gather(merge_ring, distance)
     gather(merge_ring, merge_ring.far)
     keep_out(merge_all, merge_out)
-    project_step(2)
-    for step in range(3, narrow_count):
-        rows_step(step)
-        project_step(step)
+    project_step(last)
     keep_out(rows_all, rows_out)
     for offset in range(1, wide_count):
         wide_copy(offset, (place + offset) % wide_count).wait_recv()
     keep_out(small_all, small_out)
-    for way in range(2):
-        for step in range(narrow_count):
-
-            @pl.when(has(way, step) & goes(way))
-            def _():
-                line_rows(way, block_of(way, step)).wait_send()
-
+    line_rows.drain()
     for copy in started:
         copy.wait_send()
     heads_ring.drain()
@@ -1781,20 +2017,18 @@
 
     tile_rows = -share % 16
     padded = -(-share // 256) * 256
-    expand_full = lax.all_gather(
-        jnp.pad(expand_weight.transpose(1, 2, 0), ((0, 0), (0, tile_rows), (0, 0))),
-        "narrow",
-        axis=2,
-        tiled=True,
-    )
-    reduce_full = lax.all_gather(
-        jnp.pad(reduce_weight, ((0, tile_rows), (0, 0))), "narrow", axis=1, tiled=True
-    )
-    rows_all, active, slope, gelu, feed_sum = geglu_forward(
+    expand_low = jnp.pad(expand_weight.transpose(1, 2, 0), ((0, 0), (0, tile_rows), (0, 0)))
+    gate_expand = lax.all_gather(expand_low[0], "narrow", axis=1, tiled=True)
+    upper_low, _ = lax.optimization_barrier((expand_low[1], small_all))
+    upper_expand = lax.all_gather(upper_low, "narrow", axis=1, tiled=True)
+    reduce_low = jnp.pad(reduce_weight, ((0, tile_rows), (0, 0)))
+    reduce_full, rows_all, active, slope, gelu, feed_sum = geglu_forward(
         wide_count,
+        narrow_count,
         hidden_low,
-        expand_full,
-        reduce_full,
+        gate_expand,
+        upper_expand,
+        reduce_low,
         jnp.pad(expand_shift, ((0, 0), (0, padded - share))),
     )
     feed = feed_sum + reduce_shift
@@ -1808,23 +2042,20 @@
     shift_two_grad = jnp.sum(grad_out, axis=0)
     sum_two_grad = normalize_back(grad_out, normed_two, inv_two, gains[1])
     feed_grad = low(sum_two_grad)
-    feed_grads_all, unit_grads, hidden_part, unit_sums = geglu_backward(
-        wide_count, feed_grad, expand_full, reduce_full, slope, gelu
-    )
-    tokens_all = wide_count * tok_rows
-    rows_all = rows_all.reshape(tokens_all, model_width)
-    feed_grads_all = feed_grads_all.reshape(tokens_all, model_width)
-    unit_grads = unit_grads.reshape(2, tokens_all, padded)
-    reduce_part = low(dot(active.reshape(tokens_all, padded), feed_grads_all, ((0,), (0,))))[:share]
-    expand_part = low(dot(unit_grads, rows_all, ((1,), (0,))))[:, :share]
-    reduce_part, expand_part, hidden_part = lax.optimization_barrier(
-        (reduce_part, expand_part, hidden_part)
-    )
-    reduce_weight_gradient = lax.psum_scatter(
-        reduce_part, "narrow", scatter_dimension=1, tiled=True
-    ).astype(jnp.float32)
+    reduce_weight_gradient, expand_part, hidden_part, unit_sums = geglu_backward(
+        wide_count,
+        narrow_count,
+        feed_grad,
+        gate_expand,
+        upper_expand,
+        reduce_full,
+        slope,
+        gelu,
+        active,
+        rows_all,
+    )
     expand_weight_gradient = (
-        lax.psum_scatter(expand_part, "narrow", scatter_dimension=2, tiled=True)
+        lax.psum_scatter(expand_part, "narrow", scatter_dimension=2, tiled=True)[:, :share]
         .astype(jnp.float32)
         .transpose(2, 0, 1)
     )
@@ -1897,7 +2128,7 @@
         norm_ends[2:],
         expand_weight_gradient,
         ends[3].reshape(2, -1),
-        reduce_weight_gradient,
+        reduce_weight_gradient[:share],
         ends[4],
     )
 

time: 851 us -> 771 us (0.906)
  Pallas kernels: 742 us -> 696 us
  matrix products: 27.5 us -> 0 us
    pallas_call x1, Pallas kernels: 253 us -> 164 us  [gather_front(): pl.pallas_call(functools.partial(gather_kernel, wide_count, narrow_count)...]
    pallas_call x2, Pallas kernels: 171 us -> 211 us  [the longest x1 118 us: geglu_backward(): pl.pallas_call(functools.partial(geglu_backward_kernel, wide_count, narro...]
    pallas_call x1, Pallas kernels: 50.7 us -> 81.3 us  [attention_forward(): pl.pallas_call(functools.partial(attention_forward_kernel, narrow_count),...]
    pallas_call x1, Pallas kernels: 137 us -> 108 us  [input_backward(): pl.pallas_call(functools.partial(input_backward_kernel, wide_count, narro...]
    dot_general x2 -> x0, matrix products: 27.5 us -> none  [dot(): lax.dot_general(left, right, (dims, ((), ())), preferred_element_type=jnp...]
  transfers between devices with their start and end apart: 4 -> 3, of which waited for: 0 -> 0; matrix products, arithmetic and copies ran while one was open for 5% -> 5% of each run, Pallas kernels for 68% -> 63%
where the time goes in v6:
time: 771 us; the launch traced here: 767 us
  Pallas kernels  696 us (90%)
  other arithmetic  27.5 us (4%)
  local copies, waits for them, and re-layouts  26.1 us (3%)
  between operations  16.4 us (2%)
    pallas_call x1, Pallas kernels, gather_front(): pl.pallas_call(functools.partial(gather_kernel, wide_count, narrow_count)...  164 us
    pallas_call x1, Pallas kernels, attention_backward(): pl.pallas_call(functools.partial(attention_backward_kernel, wide_count, n...  133 us
    pallas_call x1, Pallas kernels, geglu_backward(): pl.pallas_call(functools.partial(geglu_backward_kernel, wide_count, narro...  118 us
    pallas_call x1, Pallas kernels, input_backward(): pl.pallas_call(functools.partial(input_backward_kernel, wide_count, narro...  108 us
    pallas_call x1, Pallas kernels, geglu_forward(): pl.pallas_call(functools.partial(geglu_forward_kernel, wide_count, narrow...  92.6 us
    pallas_call x1, Pallas kernels, attention_forward(): pl.pallas_call(functools.partial(attention_forward_kernel, narrow_count),...  81.3 us
  transfers between devices with their start and end apart: 3, of which 0 were waited for; matrix products, arithmetic and copies ran while one was open for 5% of the time, Pallas kernels for 63%

profile of v6, /device:TPU:8, one launch (start us, length us, event | category | flops | bytes accessed | tf_op | source)
XLA Modules:
  0.0 766.9 jit_solution(12231169723365683448)
XLA Ops:
  7.3 2.5 slice_bitcast_fusion
  10.8 163.7 %gather_front.1 = (bf16[4,256,2048]{2,1,0:T(8,128)(2,1)}, bf16[8,256,1536]{2,1,0:T(8,128)(2,1)}, bf16[8,256,2048]{2,1,0:T(8,128)(2,1)}, bf16[8,4,16,128]{3,2,1,0:T(8,128)(2,1)}, f32[1024,1536]{1,0:T(8,128)}) custom-call(bf16[256,2048]{1,0:T(8,128)(2,1)} %own.3, bf16[64,6144]{1,0:T(8,128)(2,1)} %heads_weight.1, bf16[64,2048]{1,0:T(8,128)(2,1)} %merge_weight.1, ...), custom_call_target="tpu_custom_call" | custom-call | flops 80000000000 | bytes 209715200 | tf_op jit(solution)/shard_map/gather_front/pallas_call | solution.py:1700
  182.2 2.3 fusion.7
  184.5 1.9 multiply_sine_fusion
  187.6 1.3 pad_maximum_fusion
  188.9 81.3 %attention_forward.1 = (bf16[1024,512]{1,0:T(8,128)(2,1)}, bf16[1024,512]{1,0:T(8,128)(2,1)}, bf16[1024,512]{1,0:T(8,128)(2,1)}, bf16[4,1024,1024]{2,1,0:T(8,128...) custom-call(f32[1024,1536]{1,0:T(8,128)} %get-tuple-element.44.tripl, ...), custom_call_target="tpu_custom_call" | custom-call | flops 60000002048 | bytes 209715200 | tf_op jit(solution)/shard_map/attention_forward/pallas_call | solution.py:1896
  271.3 92.6 %geglu_forward.1 = (bf16[688,2048]{1,0:T(8,128)(2,1)}, bf16[8,256,2048]{2,1,0:T(8,128)(2,1)}, bf16[8,256,768]{2,1,0:T(8,128)(2,1)}, bf16[8,256,768]{2,1,0:T(8,12...) custom-call(bf16[256,2048]{1,0:T(8,128)(2,1)} %get-tuple-element.48.own, bf16[688,2048]{1,0:T(8,128)(2,1)} %bitcast.50, ...), custom_call_target="tpu_custom_call" | custom-call | flops 19327352832 | bytes 209715200 | tf_op jit(solution)/shard_map/geglu_forward/pallas_call | solution.py:822
  363.9 2.0 fusion.14
  366.3 1.6 copy-done.5
  368.9 1.8 convert_reduce_fusion.1
  370.7 118.2 %geglu_backward.1 = (f32[688,512]{1,0:T(8,128)}, bf16[2,688,2048]{2,1,0:T(8,128)(2,1)}, f32[256,2048]{1,0:T(8,128)}, f32[2,768]{1,0:T(2,128)}) custom-call(bf16[256,2048]{1,0:T(8,128)(2,1)} %get-tuple-element.91.own, bf16[688,2048]{1,0:T(8,128)(2,1)} %bitcast.51, bf16[688,2048]{1,0:T(8,128)(2,1)} %all-gather.4.cloned.1.call-done.upper_expand, ...), custom_call_target="tpu_custom_call" | custom-call | flops 38654705664 | bytes 209715200 | tf_op jit(solution)/shard_map/geglu_backward/pallas_call | solution.py:1034
  488.9 1.5 copy-done.1
  490.7 4.3 multiply_reduce_fusion
  495.1 1.6 fusion.11.attended
  496.7 132.7 %attention_backward.1 = (bf16[1024,1536]{1,0:T(8,128)(2,1)}, f32[64,2048]{1,0:T(8,128)}, f32[1,1536]{1,0:T(1,128)}, f32[1,2048]{1,0:T(1,128)}) custom-call(bf16[256,2048]{1,0:T(8,128)(2,1)} %fusion.11.attended, bf16[2048,2048]{1,0:T(8,128)(2,1)} %bitcast.53, bf16[256,2048]{1,0:T(8,128)(2,1)} %get-tuple-element.60.mixed, ...), custom_call_target="tpu_custom_call" | custom-call | flops 60000002048 | bytes 209715200 | tf_op jit(solution)/shard_map/attention_backward/pallas_call | solution.py:1238
  630.7 1.4 reduce.32
  634.0 108.1 %input_backward.1 = (f32[256,2048]{1,0:T(8,128)}, f32[64,6144]{1,0:T(8,128)}, f32[16,128]{1,0:T(8,128)}) custom-call(bf16[1024,2048]{1,0:T(8,128)(2,1)} %bitcast.55, bf16[1024,1536]{1,0:T(8,128)(2,1)} %get-tuple-element.65.triple, bf16[2048,1536]{1,0:T(8,128)(2,1)} %bitcast.54, f32[8,4,16,128]{3,2,1,0:T(8,128)} %bitcast.37), custom_call_target="tpu_custom_call" | custom-call | flops 80000000000 | bytes 209715200 | tf_op jit(solution)/shard_map/input_backward/pallas_call | solution.py:1432
  742.0 1.3 slice.127
  743.3 1.2 slice.126
  744.5 1.3 slice.129
  749.3 4.1 multiply_add_fusion
  753.4 3.4 convert_bitcast_fusion
  756.8 1.1 copy.39
  759.0 1.1 copy.41
  (121 shorter events, 18.2 us)
Async XLA Ops:
  7.2 2.7 copy-start.18
  7.2 2.8 copy-start.19
  7.2 2.8 copy-start.14
  7.2 2.9 copy-start.15
  7.2 2.9 copy-start.17
  7.2 2.9 copy-start.16
  7.2 264.0 %all-gather.6.cloned.1.call-start = ((), (), s32[]{:S(2)}) async-start(), calls=%async_computation.3 | async-start | bytes 3522560 | tf_op jit(solution)/shard_map/all_gather | solution.py:2021
  9.8 261.5 %all-gather.4.cloned.1.call-start = ((), (), s32[]{:S(2)}) async-start(), calls=%async_computation.1 | async-start | bytes 3522560 | tf_op jit(solution)/shard_map/all_gather | solution.py:2023
  10.8 165.9 %copy-start.13 = (s32[1,2]{1,0:T(1,128)S(1)}, s32[1,2]{1,0:T(1,128)}, u32[]{:S(2)}) copy-start(s32[1,2]{1,0:T(1,128)} %param.26) | copy-start | bytes 28
  174.6 578.8 %reduce-scatter.2.cloned.1.call-start = ((), (), s32[]{:S(2)}) async-start(), calls=%async_computation.2 | async-start | bytes 7045120 | tf_op jit(solution)/shard_map/reduce_scatter | solution.py:2058
  271.3 92.6 %copy-start.7 = (f32[256,2048]{1,0:T(8,128)S(1)}, f32[256,2048]{1,0:T(8,128)}, u32[]{:S(2)}) copy-start(f32[256,2048]{1,0:T(8,128)} %get-tuple-element.47) | copy-start | bytes 6291460
  365.9 3.0 copy-start
  365.9 2.0 copy-start.5
  488.8 1.6 copy-start.1
  488.8 1.8 copy-start.6
  490.7 4.4 copy-start.2
  495.0 1.7 copy-start.4
  496.7 132.8 %copy-start.11 = (f32[2,768]{1,0:T(2,128)S(1)}, f32[2,768]{1,0:T(2,128)}, u32[]{:S(2)}) copy-start(f32[2,768]{1,0:T(2,128)} %get-tuple-element.69) | copy-start | bytes 18436
  496.7 136.3 %copy-start.12 = (f32[32]{0:T(128)S(1)}, f32[32]{0:T(128)}, u32[]{:S(2)}) copy-start(f32[32]{0:T(128)} %mul.224) | copy-start | bytes 388
  634.0 115.3 %copy-start.3 = (f32[256,2048]{1,0:T(8,128)S(1)}, f32[256,2048]{1,0:T(8,128)}, u32[]{:S(2)}) copy-start(f32[256,2048]{1,0:T(8,128)} %get-tuple-element.58) | copy-start | bytes 6291460
  753.4 3.4 copy-start.8
  756.8 1.4 copy-start.10
  756.8 2.2 copy-start.9
Sparse Core Ops, SparseCore 0:
  10.2 101.6 all-gather.5
  174.7 85.1 all-gather.3
  489.0 143.7 reduce-scatter.1

commit v7 on v6

--- a/solution.py
+++ b/solution.py
@@ -3,6 +3,7 @@
 
 import jax
 import jax.numpy as jnp
+import numpy as np
 from jax import lax
 from jax.experimental import pallas as pl
 from jax.experimental.pallas import tpu as pltpu
@@ -18,23 +19,9 @@
 kernel_memory = 60 * 2**20
 
 
-def layout(positions, joined_flag, prefix_pair, bucket_len):
-    halfway = bucket_len // 2
-    second_seq = (positions >= halfway).astype(jnp.int32) * (1 - joined_flag)
-    local_pos = positions - second_seq * halfway
-    prefix_len = jnp.where(
-        joined_flag == 1,
-        prefix_pair[0] + prefix_pair[1],
-        jnp.where(second_seq == 1, prefix_pair[1], prefix_pair[0]),
-    )
-    return (second_seq, local_pos, prefix_len)
-
-
-def rotary_tables(local_pos, head_size):
-    halfway = head_size // 2
-    inverse = 10000.0 ** (-(2.0 * jnp.arange(halfway).astype(jnp.float32)) / head_size)
-    angles = local_pos.astype(jnp.float32)[:, None] * inverse[None, :]
-    return (jnp.cos(angles), jnp.sin(angles))
+def rotary_speeds(head_size):
+    index = np.arange(head_size) % (head_size // 2)
+    return (10000.0 ** (-2.0 * index / head_size)).astype(np.float32)[None]
 
 
 def normalize(values, gain, shift):
@@ -542,13 +529,12 @@
 
         lax.fori_loop(0, self.landing.shape[2] // 16, chunk, 0)
 
-    def begin(self):
-        for offset in range(self.last, 0, -1):
-            for way in range(2):
-
-                @pl.when(self.reaches(way, offset) & jnp.logical_not(self.follows(way)))
-                def _():
-                    self.copy(way, offset).start()
+    def begin(self, offset):
+        for way in range(2):
+
+            @pl.when(self.reaches(way, offset) & jnp.logical_not(self.follows(way)))
+            def _():
+                self.copy(way, offset).start()
 
     def step(self, offset):
         for way in range(2):
@@ -666,11 +652,20 @@
     upper_expand,
     reduce,
     shift,
+    hidden,
+    cotangent,
+    reduce_shift,
+    gain,
+    norm_shift,
     reduce_out,
     rows_all,
     active_out,
     slope_out,
     gelu_out,
+    layer_output,
+    sum_grad,
+    feed_grad,
+    row_sums,
     feed,
     blocks,
     gather_send,
@@ -792,6 +787,27 @@
     late_plane.run_sums(compute_sums(late, cols))
     plane.finish(feed)
     late_plane.finish(feed)
+
+    row_sums[...] = jnp.zeros_like(row_sums)
+
+    def norm_rows(i, carry):
+        some = pl.ds(pl.multiple_of(i * 16, 16), 16)
+        result, normed, inverse = normalize(
+            residual_scale * hidden[some] + feed[some] + reduce_shift[...],
+            gain[...],
+            norm_shift[...],
+        )
+        layer_output[some] = result.astype(jnp.bfloat16)
+        upstream = cotangent[some].astype(jnp.float32)
+        total = normalize_back(upstream, normed, inverse, gain[...])
+        sum_grad[some] = total
+        feed_grad[some] = total.astype(jnp.bfloat16)
+        row_sums[0:1] += jnp.sum(upstream * normed, axis=0, keepdims=True)
+        row_sums[1:2] += jnp.sum(upstream, axis=0, keepdims=True)
+        row_sums[2:3] += jnp.sum(total, axis=0, keepdims=True)
+        return carry
+
+    lax.fori_loop(0, own.shape[0] // 16, norm_rows, 0)
     plane.drain()
     late_plane.drain()
     keep_reduce.wait()
@@ -801,14 +817,26 @@
 
 
 def geglu_forward(
-    wide_count, narrow_count, hidden_low, gate_expand, upper_expand, reduce_weight, shift
+    wide_count,
+    narrow_count,
+    hidden_low,
+    gate_expand,
+    upper_expand,
+    reduce_weight,
+    shift,
+    hidden,
+    cotangent,
+    reduce_shift,
+    gain,
+    norm_shift,
 ):
     rows, width = hidden_low.shape
     padded = shift.shape[1]
     anywhere = pl.BlockSpec(memory_space=pl.ANY)
     vmem = pl.BlockSpec(memory_space=pltpu.VMEM)
     kept = jax.ShapeDtypeStruct((wide_count, rows, padded), jnp.bfloat16)
-    scratch = exchange_scratch(wide_count, rows, width) + [
+    scratch = [pltpu.VMEM((rows, width), jnp.float32)]
+    scratch += exchange_scratch(wide_count, rows, width) + [
         pltpu.VMEM((2, padded, width), jnp.bfloat16),
         pltpu.VMEM((padded, width), jnp.bfloat16),
         pltpu.VMEM((wide_count, rows, padded), jnp.bfloat16),
@@ -827,10 +855,13 @@
             kept,
             kept,
             kept,
+            jax.ShapeDtypeStruct((rows, width), jnp.bfloat16),
             jax.ShapeDtypeStruct((rows, width), jnp.float32),
+            jax.ShapeDtypeStruct((rows, width), jnp.bfloat16),
+            jax.ShapeDtypeStruct((3, width), jnp.float32),
         ),
-        in_specs=[anywhere, anywhere, anywhere, anywhere, vmem],
-        out_specs=(anywhere, anywhere, anywhere, anywhere, anywhere, vmem),
+        in_specs=[anywhere] * 4 + [vmem] * 6,
+        out_specs=(anywhere,) * 5 + (vmem,) * 4,
         scratch_shapes=scratch,
         compiler_params=pltpu.CompilerParams(
             collective_id=1, has_side_effects=True, vmem_limit_bytes=kernel_memory
@@ -839,7 +870,18 @@
             flops=6 * wide_count * rows * padded * width, bytes_accessed=200 * 2**20, transcendentals=0
         ),
         name="geglu_forward",
-    )(hidden_low, gate_expand, upper_expand, reduce_weight, shift)
+    )(
+        hidden_low,
+        gate_expand,
+        upper_expand,
+        reduce_weight,
+        shift,
+        hidden,
+        cotangent,
+        reduce_shift,
+        gain,
+        norm_shift,
+    )
 
 
 def geglu_backward_kernel(
@@ -954,7 +996,8 @@
             copy.wait()
         for start in range(0, active.shape[2], 256):
             reduce_mat[start : start + 256] = product(active, blocks, start)
-        line_sum.begin()
+        for offset in range(narrow_count - 1, 0, -1):
+            line_sum.begin(offset)
 
     def expand_work(left, start, target):
         def work():
@@ -1061,7 +1104,11 @@
 def attention_backward_kernel(
     wide_count,
     narrow_count,
-    attended,
+    upper_grad,
+    hidden_part,
+    normed,
+    inv_std,
+    gain,
     merge,
     mixed,
     queries,
@@ -1074,6 +1121,9 @@
     merge_grad,
     heads_sums,
     merge_sums,
+    sum_grad,
+    norm_sums,
+    attended,
     upstream,
     outbound,
     probs_held,
@@ -1098,7 +1148,7 @@
     sems = (None, None, mate_send, mate_recv, sum_send, sum_recv, None)
     plane = PlaneExchange(wide_count, None, None, parts, from_mate, incoming, sems)
     line = LineExchange(narrow_count)
-    rows, width = attended.shape
+    rows, width = sum_grad.shape
     own_cols = queries.shape[1]
     heads = own_cols // HDIM
     scale = HDIM ** (-0.5)
@@ -1110,6 +1160,22 @@
 
     load(0).start()
     greet_plane(plane)
+
+    norm_sums[...] = jnp.zeros_like(norm_sums)
+    merge_sums[...] = jnp.zeros_like(merge_sums)
+
+    def norm_rows(i, carry):
+        some = pl.ds(pl.multiple_of(i * 16, 16), 16)
+        hidden_grad = residual_scale * upper_grad[some] + hidden_part[some]
+        norm_sums[0:1] += jnp.sum(hidden_grad * normed[some], axis=0, keepdims=True)
+        norm_sums[1:2] += jnp.sum(hidden_grad, axis=0, keepdims=True)
+        total = normalize_back(hidden_grad, normed[some], inv_std[some], gain[...])
+        sum_grad[some] = total
+        merge_sums[...] += jnp.sum(total, axis=0, keepdims=True)
+        attended[some] = total.astype(jnp.bfloat16)
+        return carry
+
+    lax.fori_loop(0, rows // 16, norm_rows, 0)
     line.greet(3)
 
     def mixed_part(target, where):
@@ -1136,9 +1202,19 @@
     lax.fori_loop(0, wide_count, merge_rows, 0)
     for offset in range(plane.ring):
         plane.share(offset)
-    merge_sums[...] = jnp.sum(attended[...].astype(jnp.float32), axis=0, keepdims=True)
     plane.first_sums()
     plane.far_sums()
+    plane.last_sums()
+    plane.finish(merge_out)
+    count = merge_grad.shape[0]
+
+    def z_rows(where):
+        return pl.ds(pl.multiple_of(where * count, count), count)
+
+    for offset in range(1, narrow_count):
+        line.send(
+            offset, merge_out.at[z_rows(line.peer(offset))], merge_in, merge_send, merge_recv
+        )
     for offset in range(1, narrow_count):
         line.arrived(offset, upstream, mixed_send, mixed_recv)
 
@@ -1186,19 +1262,6 @@
 
     for head in range(heads):
         one_head(head)
-        if head == heads // 2 - 1:
-            plane.last_sums()
-    total = merge_out.at[...]
-    plane.finish(merge_out)
-    count = merge_grad.shape[0]
-
-    def z_rows(where):
-        return pl.ds(pl.multiple_of(where * count, count), count)
-
-    for offset in range(1, narrow_count):
-        line.send(
-            offset, total.at[z_rows(line.peer(offset))], merge_in, merge_send, merge_recv
-        )
 
     def column_sums(cols):
         heads_sums[:, cols] = jnp.sum(
@@ -1218,7 +1281,11 @@
 def attention_backward(
     wide_count,
     narrow_count,
-    attended_grad,
+    upper_grad,
+    hidden_part,
+    normed,
+    inv_std,
+    gain,
     merge_full,
     mixed,
     queries,
@@ -1228,7 +1295,7 @@
     cosine,
     signed_sine,
 ):
-    rows, width = attended_grad.shape
+    rows, width = normed.shape
     bucket, own_cols = queries.shape
     block = width // wide_count
     count = block // narrow_count
@@ -1242,10 +1309,13 @@
             jax.ShapeDtypeStruct((count, width), jnp.float32),
             jax.ShapeDtypeStruct((1, 3 * own_cols), jnp.float32),
             jax.ShapeDtypeStruct((1, width), jnp.float32),
+            jax.ShapeDtypeStruct((rows, width), jnp.float32),
+            jax.ShapeDtypeStruct((2, width), jnp.float32),
         ),
-        in_specs=[vmem] * 6 + [anywhere] + [vmem] * 2,
-        out_specs=(vmem, vmem, vmem, vmem),
+        in_specs=[vmem] * 10 + [anywhere] + [vmem] * 2,
+        out_specs=(vmem,) * 6,
         scratch_shapes=[
+            pltpu.VMEM((rows, width), jnp.bfloat16),
             pltpu.VMEM((narrow_count, rows, own_cols), jnp.bfloat16),
             pltpu.VMEM((narrow_count - 1, rows, own_cols), jnp.bfloat16),
             pltpu.VMEM((2, bucket, bucket), jnp.bfloat16),
@@ -1269,7 +1339,19 @@
         ),
         name="attention_backward",
     )(
-        attended_grad, merge_full, mixed, queries, keys, values, probs, cosine, signed_sine
+        upper_grad,
+        hidden_part,
+        normed,
+        inv_std,
+        gain,
+        merge_full,
+        mixed,
+        queries,
+        keys,
+        values,
+        probs,
+        cosine,
+        signed_sine,
     )
 
 
@@ -1343,17 +1425,26 @@
     for copy in small_copies:
         copy.start()
 
-    def input_cols(cols):
-        part = dot(triple[...], heads_mat[cols], ((1,), (1,)))
-        for index in range(narrow_count):
-            line_parts[index, :, cols] = part[index * rows : (index + 1) * rows].astype(
-                jnp.bfloat16
-            )
-
-    tiles(width, 256, input_cols)
-
     line_sum = LineSum(line, lambda target: line_parts.at[target], line_in, line_send, line_recv)
-    line_sum.begin()
+
+    def input_rows(index):
+        some = pl.ds(pl.multiple_of(index * rows, rows), rows)
+
+        def input_cols(cols):
+            part = dot(triple[some], heads_mat[cols], ((1,), (1,)))
+            line_parts[index, :, cols] = part.astype(jnp.bfloat16)
+
+        tiles(width, 256, input_cols)
+
+    for offset in range(last, 0, -1):
+        for way in range(2):
+
+            @pl.when(line_sum.reaches(way, offset))
+            def _():
+                input_rows(line_sum.target(way, offset))
+
+        line_sum.begin(offset)
+    input_rows(here)
 
     block = parts.shape[1]
 
@@ -1487,14 +1578,20 @@
     heads_weight,
     merge_weight,
     small,
+    buckets,
+    speeds,
     rows_out,
     heads_out,
     merge_out,
     small_out,
     triple,
+    cosine,
+    signed_sine,
+    first_query,
+    last_query,
     rows_all,
     heads_all,
-    merge_all,
+    merge_own,
     small_all,
     rows_send,
     rows_recv,
@@ -1510,15 +1607,9 @@
     out_sems,
     heads_ring_send,
     heads_ring_recv,
-    merge_ring_send,
-    merge_ring_recv,
 ):
-    def ring_of(blocks, send, recv):
-        sems = (send, recv, None, None, None, None, None)
-        return PlaneExchange(wide_count, None, blocks, blocks, None, None, sems)
-
-    heads_ring = ring_of(heads_all, heads_ring_send, heads_ring_recv)
-    merge_ring = ring_of(merge_all, merge_ring_send, merge_ring_recv)
+    ring_sems = (heads_ring_send, heads_ring_recv, None, None, None, None, None)
+    heads_ring = PlaneExchange(wide_count, None, heads_all, heads_all, None, None, ring_sems)
     line = LineExchange(narrow_count)
     here = line.mine
     last = narrow_count - 1
@@ -1549,7 +1640,7 @@
         for which in range(3)
     ]
     keep_merge = pltpu.make_async_copy(
-        merge_weight, merge_all.at[slot, z_rows(here)], local_sems.at[1]
+        merge_weight, merge_own.at[z_rows(here)], local_sems.at[1]
     )
     for copy in keeps + [keep_merge]:
         copy.start()
@@ -1568,7 +1659,7 @@
     def merge_copy(offset, where, sender):
         return line.copy(
             merge_weight,
-            merge_all.at[slot, z_rows(sender)],
+            merge_own.at[z_rows(sender)],
             merge_send.at[offset - 1],
             merge_recv.at[sender],
             where,
@@ -1597,8 +1688,31 @@
     keep_rows.wait()
     line_rows.send_own()
 
-    for offset in range(1, narrow_count):
-        start(merge_copy(offset, line.peer(offset), here))
+    halfway = narrow_count * rows // 2
+    joined = buckets[0]
+
+    def tables(i, carry):
+        some = pl.ds(pl.multiple_of(i * rows, rows), rows)
+        place_in = i * rows + lax.broadcasted_iota(jnp.int32, (rows, 1), 0)
+        second = jnp.where(place_in >= halfway, 1 - joined, 0)
+        local = place_in - second * halfway
+        reach = jnp.where(
+            joined == 1,
+            buckets[1] + buckets[2],
+            jnp.where(second == 1, buckets[2], buckets[1]),
+        )
+        first_query[some] = jnp.where(local < reach, place_in - local, place_in)
+        last_query[some] = jnp.where(
+            (joined == 1) | (second == 1), 2 * halfway - 1, halfway - 1
+        ) + jnp.zeros_like(place_in)
+        angles = local.astype(jnp.float32) * speeds[...]
+        lane = lax.broadcasted_iota(jnp.int32, (rows, HDIM), 1)
+        cosine[some] = jnp.cos(angles)
+        sine = jnp.sin(angles)
+        signed_sine[some] = jnp.where(lane < HDIM // 2, sine, -sine)
+        return carry
+
+    lax.fori_loop(0, narrow_count, tables, 0)
 
     for copy in keeps:
         copy.wait()
@@ -1648,26 +1762,21 @@
         outs.append(copy)
 
     line_rows.step(1)
+    for offset in range(1, narrow_count):
+        start(merge_copy(offset, line.peer(offset), here))
     heads_ring.receive_mate(0)
-    for distance in range(1, heads_ring.far):
+    for distance in range(1, heads_ring.far + 1):
         gather(heads_ring, distance)
-    keep_merge.wait()
-    for offset in range(1, narrow_count):
-        merge_copy(offset, line.peer(offset), line.peer(offset)).wait_recv()
-    merge_ring.send_own()
-    gather(heads_ring, heads_ring.far)
     keep_out(heads_all, heads_out)
     project(here)
     for step in range(2, narrow_count):
         line_rows.step(step)
         project_step(step - 1)
-        if step == 2:
-            merge_ring.receive_mate(0)
-            for distance in range(1, merge_ring.far):
-                gather(merge_ring, distance)
-    gather(merge_ring, merge_ring.far)
-    keep_out(merge_all, merge_out)
     project_step(last)
+    keep_merge.wait()
+    for offset in range(1, narrow_count):
+        merge_copy(offset, line.peer(offset), line.peer(offset)).wait_recv()
+    keep_out(merge_own, merge_out)
     keep_out(rows_all, rows_out)
     for offset in range(1, wide_count):
         wide_copy(offset, (place + offset) % wide_count).wait_recv()
@@ -1676,12 +1785,13 @@
     for copy in started:
         copy.wait_send()
     heads_ring.drain()
-    merge_ring.drain()
     for copy in outs:
         copy.wait()
 
 
-def gather_front(wide_count, narrow_count, layer_input, heads_weight, merge_weight, small):
+def gather_front(
+    wide_count, narrow_count, layer_input, heads_weight, merge_weight, small, buckets, speeds
+):
     rows, width = layer_input.shape
     count, all_columns = heads_weight.shape
     columns = all_columns // narrow_count
@@ -1693,16 +1803,19 @@
     shapes = (
         (narrow_count, rows, width),
         (wide_count, block, columns),
-        (wide_count, block, width),
+        (block, width),
         (wide_count, narrow_count, lines, 128),
     )
     far = narrow_count - 1
+    bucket = narrow_count * rows
+    table = jax.ShapeDtypeStruct((bucket, HDIM), jnp.float32)
+    reach = jax.ShapeDtypeStruct((bucket, 1), jnp.int32)
     return pl.pallas_call(
         functools.partial(gather_kernel, wide_count, narrow_count),
         out_shape=tuple(jax.ShapeDtypeStruct(shape, jnp.bfloat16) for shape in shapes)
-        + (jax.ShapeDtypeStruct((narrow_count * rows, columns), jnp.float32),),
-        in_specs=[anywhere, anywhere, anywhere, vmem],
-        out_specs=(anywhere, anywhere, anywhere, anywhere, vmem),
+        + (jax.ShapeDtypeStruct((bucket, columns), jnp.float32), table, table, reach, reach),
+        in_specs=[anywhere, anywhere, anywhere, vmem, pl.BlockSpec(memory_space=pltpu.SMEM), vmem],
+        out_specs=(anywhere,) * 4 + (vmem,) * 5,
         scratch_shapes=[pltpu.VMEM(shape, jnp.bfloat16) for shape in shapes]
         + [
             dma((2, narrow_count)),
@@ -1719,8 +1832,6 @@
             dma((4,)),
             dma((3, wide_count, 2)),
             dma((wide_count, 2)),
-            dma((3, wide_count, 2)),
-            dma((wide_count, 2)),
         ],
         compiler_params=pltpu.CompilerParams(
             collective_id=5, has_side_effects=True, vmem_limit_bytes=kernel_memory
@@ -1729,10 +1840,11 @@
             flops=80 * 10**9, bytes_accessed=200 * 2**20, transcendentals=0
         ),
         name="gather_front",
-    )(layer_input, heads_weight, merge_weight, small)
+    )(layer_input, heads_weight, merge_weight, small, buckets, speeds)
 
 
 def attention_forward_kernel(
+    wide_count,
     narrow_count,
     triple,
     heads_shift,
@@ -1754,6 +1866,7 @@
     hidden_low,
     normed,
     inv_std,
+    merge_out,
     merge_mat,
     probs_held,
     values_turned,
@@ -1762,15 +1875,21 @@
     mixed_send,
     mixed_recv,
     local_sems,
+    ring_send,
+    ring_recv,
+    own_sem,
 ):
     line = LineExchange(narrow_count)
+    ring_sems = (ring_send, ring_recv, None, None, None, None, own_sem)
+    ring = PlaneExchange(wide_count, merge, merge_mat, merge_mat, None, None, ring_sems)
     bucket, own_cols = queries.shape
     rows, width = own.shape
     heads = own_cols // HDIM
     scale = HDIM ** (-0.5)
-    load_merge = pltpu.make_async_copy(merge, merge_mat, local_sems.at[2])
-    load_merge.start()
-    line.greet()
+    greet_plane(ring)
+    line.greet(3)
+    keep_own = ring.send_own()
+    ring_steps = [functools.partial(ring.receive, step) for step in range(1, ring.far + 1)]
 
     def keep(head):
         return pltpu.make_async_copy(
@@ -1827,6 +1946,8 @@
             copy = mixed_copy(head, offset, line.peer(offset), line.mine)
             copy.start()
             started.append(copy)
+        if ring_steps:
+            ring_steps.pop(0)()
     own_mixed = pltpu.make_async_copy(
         outbound.at[line.mine],
         mixed.at[:, pl.ds(pl.multiple_of(line.mine * own_cols, own_cols), own_cols)],
@@ -1834,7 +1955,13 @@
     )
     own_mixed.start()
     own_mixed.wait()
-    load_merge.wait()
+    keep_own.wait()
+    for step in ring_steps:
+        step()
+    for offset in range(ring.ring):
+        ring.receive_mate(offset)
+    keep_merge = pltpu.make_async_copy(merge_mat, merge_out, local_sems.at[2])
+    keep_merge.start()
     for offset in range(1, narrow_count):
         for head in range(heads):
             mixed_copy(head, offset, line.peer(offset), line.peer(offset)).wait_recv()
@@ -1843,7 +1970,7 @@
     def merge_cols(cols):
         hidden[:, cols] = (
             residual_scale * own[:, cols].astype(jnp.float32)
-            + dot(mixed[...], merge_mat[:, cols], ((1,), (0,)))
+            + dot(mixed[...], merge_mat[:, :, cols].reshape(width, cols.size), ((1,), (0,)))
             + merge_shift[:, cols]
         )
 
@@ -1863,9 +1990,12 @@
         keep(head).wait()
     for copy in started:
         copy.wait_send()
+    ring.drain()
+    keep_merge.wait()
 
 
 def attention_forward(
+    wide_count,
     narrow_count,
     triple,
     heads_shift,
@@ -1874,7 +2004,7 @@
     first_query,
     last_query,
     layer_input,
-    merge_full,
+    merge_block,
     merge_shift,
     gain,
     shift,
@@ -1894,7 +2024,7 @@
         return jax.ShapeDtypeStruct(shape, jnp.float32)
 
     return pl.pallas_call(
-        functools.partial(attention_forward_kernel, narrow_count),
+        functools.partial(attention_forward_kernel, wide_count, narrow_count),
         out_shape=(
             low_shape(bucket, own_cols),
             low_shape(bucket, own_cols),
@@ -1905,11 +2035,12 @@
             low_shape(rows, width),
             wide_shape(rows, width),
             wide_shape(rows, 1),
+            low_shape(wide_count, *merge_block.shape),
         ),
         in_specs=[vmem] * 7 + [anywhere] + [vmem] * 3,
-        out_specs=(vmem, vmem, vmem, anywhere) + (vmem,) * 5,
+        out_specs=(vmem, vmem, vmem, anywhere) + (vmem,) * 5 + (anywhere,),
         scratch_shapes=[
-            pltpu.VMEM((width, width), jnp.bfloat16),
+            pltpu.VMEM((wide_count, *merge_block.shape), jnp.bfloat16),
             pltpu.VMEM((2, bucket, bucket), jnp.bfloat16),
             pltpu.VMEM((HDIM, bucket), jnp.bfloat16),
             pltpu.VMEM((narrow_count, rows, own_cols), jnp.bfloat16),
@@ -1917,6 +2048,9 @@
             dma((narrow_count - 1, heads)),
             dma((narrow_count, heads)),
             dma((4,)),
+            dma((3, wide_count, 2)),
+            dma((wide_count, 2)),
+            dma(()),
         ],
         compiler_params=pltpu.CompilerParams(
             collective_id=6, has_side_effects=True, vmem_limit_bytes=kernel_memory
@@ -1933,7 +2067,7 @@
         first_query,
         last_query,
         layer_input,
-        merge_full,
+        merge_block,
         merge_shift,
         gain,
         shift,
@@ -1964,32 +2098,36 @@
     own_heads = HEADS // narrow_count
     own_cols = own_heads * HDIM
     share = expand_weight.shape[2]
-    joined_flag = joined[0]
-    prefix_pair = prefix[0]
     narrow_index = lax.axis_index("narrow")
-    positions = jnp.arange(bucket_len, dtype=jnp.int32)
-    second_seq, local_pos, prefix_len = layout(positions, joined_flag, prefix_pair, bucket_len)
-    cosine, sine_table = rotary_tables(local_pos, HDIM)
-    first_query = jnp.where(local_pos < prefix_len, positions - local_pos, positions)
-    last_query = jnp.where(
-        (joined_flag == 1) | (second_seq == 1), bucket_len - 1, bucket_len // 2 - 1
-    )
-
     smalls = (heads_bias, merge_bias, norm_gains, norm_shifts, expand_bias, reduce_bias)
-    rows_input, heads_mat, merge_full, small_all, triple = gather_front(
-        wide_count, narrow_count, layer_input, heads_weight, merge_weight, pack_small(smalls)
+    (
+        rows_input,
+        heads_mat,
+        merge_block,
+        small_all,
+        triple,
+        cosine,
+        signed_sine,
+        first_query,
+        last_query,
+    ) = gather_front(
+        wide_count,
+        narrow_count,
+        layer_input,
+        heads_weight,
+        merge_weight,
+        pack_small(smalls),
+        jnp.concatenate([joined, prefix[0]]),
+        jnp.asarray(rotary_speeds(HDIM)),
     )
     rows_input = rows_input.reshape(bucket_len, model_width)
     heads_mat = heads_mat.reshape(model_width, 3 * own_cols)
-    merge_full = merge_full.reshape(model_width, model_width)
     heads_shift, merge_shift, gains, shifts, expand_shift, reduce_shift = unpack_small(
         small_all, smalls
     )
     own_shift = lax.dynamic_index_in_dim(
         heads_shift.reshape(3, narrow_count, own_cols), narrow_index, 1, keepdims=False
     ).reshape(1, -1)
-    cosine_wide = jnp.concatenate([cosine, cosine], axis=1)
-    signed_sine = jnp.concatenate([sine_table, -sine_table], axis=1)
     (
         queries,
         keys,
@@ -2000,16 +2138,18 @@
         hidden_low,
         normed_one,
         inv_one,
+        merge_full,
     ) = attention_forward(
+        wide_count,
         narrow_count,
         triple,
         own_shift,
-        cosine_wide,
+        cosine,
         signed_sine,
-        first_query.reshape(-1, 1),
-        last_query.reshape(-1, 1),
+        first_query,
+        last_query,
         layer_input,
-        merge_full,
+        merge_block,
         merge_shift.reshape(1, -1),
         gains[0].reshape(1, -1),
         shifts[0].reshape(1, -1),
@@ -2022,7 +2162,17 @@
     upper_low, _ = lax.optimization_barrier((expand_low[1], small_all))
     upper_expand = lax.all_gather(upper_low, "narrow", axis=1, tiled=True)
     reduce_low = jnp.pad(reduce_weight, ((0, tile_rows), (0, 0)))
-    reduce_full, rows_all, active, slope, gelu, feed_sum = geglu_forward(
+    (
+        reduce_full,
+        rows_all,
+        active,
+        slope,
+        gelu,
+        layer_output,
+        sum_two_grad,
+        feed_grad,
+        row_sums,
+    ) = geglu_forward(
         wide_count,
         narrow_count,
         hidden_low,
@@ -2030,18 +2180,12 @@
         upper_expand,
         reduce_low,
         jnp.pad(expand_shift, ((0, 0), (0, padded - share))),
+        hidden,
+        cotangent,
+        reduce_shift.reshape(1, -1),
+        gains[1].reshape(1, -1),
+        shifts[1].reshape(1, -1),
     )
-    feed = feed_sum + reduce_shift
-    output_float, normed_two, inv_two = normalize(
-        residual_scale * hidden + feed, gains[1], shifts[1]
-    )
-    layer_output = low(output_float)
-
-    grad_out = cotangent.astype(jnp.float32)
-    gain_two_grad = jnp.sum(grad_out * normed_two, axis=0)
-    shift_two_grad = jnp.sum(grad_out, axis=0)
-    sum_two_grad = normalize_back(grad_out, normed_two, inv_two, gains[1])
-    feed_grad = low(sum_two_grad)
     reduce_weight_gradient, expand_part, hidden_part, unit_sums = geglu_backward(
         wide_count,
         narrow_count,
@@ -2059,22 +2203,28 @@
         .astype(jnp.float32)
         .transpose(2, 0, 1)
     )
-    hidden_grad = residual_scale * sum_two_grad + hidden_part
-    gain_one_grad = jnp.sum(hidden_grad * normed_one, axis=0)
-    shift_one_grad = jnp.sum(hidden_grad, axis=0)
-    sum_one_grad = normalize_back(hidden_grad, normed_one, inv_one, gains[0])
-    attended_grad = low(sum_one_grad)
-    triple_grad, merge_weight_gradient, heads_sums, merge_sums = attention_backward(
+    (
+        triple_grad,
+        merge_weight_gradient,
+        heads_sums,
+        merge_sums,
+        sum_one_grad,
+        norm_one_sums,
+    ) = attention_backward(
         wide_count,
         narrow_count,
-        attended_grad,
-        merge_full,
+        sum_two_grad,
+        hidden_part,
+        normed_one,
+        inv_one,
+        gains[0].reshape(1, -1),
+        merge_full.reshape(model_width, model_width),
         mixed,
         queries,
         keys,
         values,
         probs_low,
-        cosine_wide,
+        cosine,
         signed_sine,
     )
 
@@ -2084,7 +2234,7 @@
     heads_sums = (heads_sums * mine_narrow[None, :, None]).reshape(count, -1)
     merge_sums = merge_sums.reshape(count, -1)
     norm_sums = (
-        jnp.stack([gain_one_grad, gain_two_grad, shift_one_grad, shift_two_grad])
+        jnp.stack([norm_one_sums[0], row_sums[0], norm_one_sums[1], row_sums[1]])
         .reshape(4, count, -1)
         .transpose(1, 0, 2)
         .reshape(count, -1)
@@ -2094,7 +2244,7 @@
         expand_sums.reshape(2, narrow_count, -1).transpose(1, 0, 2).reshape(1, narrow_count, -1)
         * mine_wide[:, None, None]
     ).reshape(count, -1)
-    reduce_sums = jnp.sum(feed_grad, axis=0, dtype=jnp.float32).reshape(1, narrow_count, -1)
+    reduce_sums = row_sums[2].reshape(1, narrow_count, -1)
     reduce_sums = jnp.broadcast_to(
         reduce_sums, (wide_count, narrow_count, reduce_sums.shape[2])
     ).reshape(count, -1)

time: 771 us -> 760 us (0.986)
  Pallas kernels: 696 us -> 647 us
  waiting for transfers between devices: 0.09 us -> 47.3 us
  other arithmetic: 27.5 us -> 9.97 us
    all_gather x1, waiting for transfers between devices: 0.02 us -> 46.6 us  [shards(): gate_expand = lax.all_gather(expand_low[0], 'narrow', axis=1, tiled=True)]
    pallas_call x1, Pallas kernels: 164 us -> 118 us  [gather_front(): pl.pallas_call(functools.partial(gather_kernel, wide_count, narrow_count)...]
    pallas_call x1, Pallas kernels: 133 us -> 118 us  [attention_backward(): pl.pallas_call(functools.partial(attention_backward_kernel, wide_count, n...]
    pallas_call x1, Pallas kernels: 92.6 us -> 107 us  [geglu_forward(): pl.pallas_call(functools.partial(geglu_forward_kernel, wide_count, narrow...]
    pallas_call x1, Pallas kernels: 108 us -> 97 us  [input_backward(): pl.pallas_call(functools.partial(input_backward_kernel, wide_count, narro...]
    reduce_sum x5 -> x0, other arithmetic: 9.42 us -> none  [the longest x1 4.33 us: shards(): gain_one_grad = jnp.sum(hidden_grad * normed_one, axis=0)]
  transfers between devices with their start and end apart: 3 -> 3, of which waited for: 0 -> 1; matrix products, arithmetic and copies ran while one was open for 5% -> 3% of each run, Pallas kernels for 63% -> 40%
where the time goes in v7:
time: 760 us; the launch traced here: 749 us
  Pallas kernels  647 us (85%)
  waiting for transfers between devices  47.3 us (6%)
  local copies, waits for them, and re-layouts  30.1 us (4%)
  between operations  14.9 us (2%)
  other arithmetic  9.97 us (1%)
    pallas_call x1, Pallas kernels, geglu_backward(): pl.pallas_call(functools.partial(geglu_backward_kernel, wide_count, narro...  119 us
    pallas_call x1, Pallas kernels, attention_backward(): pl.pallas_call(functools.partial(attention_backward_kernel, wide_count, n...  118 us
    pallas_call x1, Pallas kernels, gather_front(): pl.pallas_call(functools.partial(gather_kernel, wide_count, narrow_count)...  118 us
    pallas_call x1, Pallas kernels, geglu_forward(): pl.pallas_call(functools.partial(geglu_forward_kernel, wide_count, narrow...  107 us
    pallas_call x1, Pallas kernels, input_backward(): pl.pallas_call(functools.partial(input_backward_kernel, wide_count, narro...  97 us
    pallas_call x1, Pallas kernels, attention_forward(): pl.pallas_call(functools.partial(attention_forward_kernel, wide_count, na...  88.1 us
    all_gather x1, waiting for transfers between devices, shards(): gate_expand = lax.all_gather(expand_low[0], 'narrow', axis=1, tiled=True)  46.6 us
  transfers between devices with their start and end apart: 3, of which 1 were waited for; matrix products, arithmetic and copies ran while one was open for 3% of the time, Pallas kernels for 40%

profile of v7, /device:TPU:8, one launch (start us, length us, event | category | flops | bytes accessed | tf_op | source)
XLA Modules:
  0.0 749.1 jit_solution(13852908755115733479)
XLA Ops:
  7.2 0.8 reshape.124
  9.5 2.1 concatenate.9
  12.8 2.5 slice_bitcast_fusion
  15.9 117.8 %gather_front.1 = (bf16[4,256,2048]{2,1,0:T(8,128)(2,1)}, bf16[8,256,1536]{2,1,0:T(8,128)(2,1)}, bf16[256,2048]{1,0:T(8,128)(2,1)}, bf16[8,4,16,128]{3,2,1,0:T(8...) custom-call(bf16[256,2048]{1,0:T(8,128)(2,1)} %own.3, ...), custom_call_target="tpu_custom_call" | custom-call | flops 80000000000 | bytes 209715200 | tf_op jit(solution)/shard_map/gather_front/pallas_call | solution.py:1813
  134.6 1.0 reshape.142
  142.8 88.1 %attention_forward.1 = (bf16[1024,512]{1,0:T(8,128)(2,1)}, bf16[1024,512]{1,0:T(8,128)(2,1)}, bf16[1024,512]{1,0:T(8,128)(2,1)}, bf16[4,1024,1024]{2,1,0:T(8,128...) custom-call(f32[1024,1536]{1,0:T(8,128)} %get-tuple-element.54.tripl, ...), custom_call_target="tpu_custom_call" | custom-call | flops 60000002048 | bytes 209715200 | tf_op jit(solution)/shard_map/attention_forward/pallas_call | solution.py:2026
  230.9 46.6 %all-gather.6.cloned.1.call-done = bf16[1,688,2048]{2,1,0:T(8,128)(2,1)} async-done(((bf16[1,688,512]{2,1,0:T(8,128)(2,1)}), bf16[1,688,2048]{2,1,0:T(8,128)(2,1)}) %all-gather.6.cloned.1.call-update) | async-done | bytes 2818064 | tf_op jit(solution)/shard_map/all_gather | solution.py:2161
  277.5 106.9 %geglu_forward.1 = (bf16[688,2048]{1,0:T(8,128)(2,1)}, bf16[8,256,2048]{2,1,0:T(8,128)(2,1)}, bf16[8,256,768]{2,1,0:T(8,128)(2,1)}, bf16[8,256,768]{2,1,0:T(8,12...) custom-call(bf16[256,2048]{1,0:T(8,128)(2,1)} %get-tuple-element.61., ...), custom_call_target="tpu_custom_call" | custom-call | flops 19327352832 | bytes 209715200 | tf_op jit(solution)/shard_map/geglu_forward/pallas_call | solution.py:850
  384.4 118.7 %geglu_backward.1 = (f32[688,512]{1,0:T(8,128)}, bf16[2,688,2048]{2,1,0:T(8,128)(2,1)}, f32[256,2048]{1,0:T(8,128)}, f32[2,768]{1,0:T(2,128)}) custom-call(bf16[256,2048]{1,0:T(8,128)(2,1)} %get-tuple-element.66.own, bf16[688,2048]{1,0:T(8,128)(2,1)} %bitcast.46, bf16[688,2048]{1,0:T(8,128)(2,1)} %all-gather.4.cloned.1.call-done.upper_expand, ...), custom_call_target="tpu_custom_call" | custom-call | flops 38654705664 | bytes 209715200 | tf_op jit(solution)/shard_map/geglu_backward/pallas_call | solution.py:1077
  503.2 118.2 %attention_backward.1 = (bf16[1024,1536]{1,0:T(8,128)(2,1)}, f32[64,2048]{1,0:T(8,128)}, f32[1,1536]{1,0:T(1,128)}, f32[1,2048]{1,0:T(1,128)}, f32[256,2048]{1,0:T(8,128)}, /*index=5*/f32[2,2048]{1,0:T(2,128)}) custom-call(f32[256,2048]{1,0:T(8,128)} %get-tuple-element.65.upper_grad, f32[256,2048]{1,0:T(8,128)} %get-tuple-element.72.hidden_part, ...), custom_call_target="tpu_custom_call" | custom-call | flops 60000002048 | bytes 209715200 | tf_op jit(solution)/shard_map/attention_backward/pallas_call | solution.py:1305
  621.5 0.8 fusion.1
  624.0 1.4 reduce.33
  626.7 97.0 %input_backward.1 = (f32[256,2048]{1,0:T(8,128)}, f32[64,6144]{1,0:T(8,128)}, f32[16,128]{1,0:T(8,128)}) custom-call(bf16[1024,2048]{1,0:T(8,128)(2,1)} %bitcast.50, bf16[1024,1536]{1,0:T(8,128)(2,1)} %get-tuple-element.83.triple, bf16[2048,1536]{1,0:T(8,128)(2,1)} %bitcast.49, f32[8,4,16,128]{3,2,1,0:T(8,128)} %bitcast.32), custom_call_target="tpu_custom_call" | custom-call | flops 80000000000 | bytes 209715200 | tf_op jit(solution)/shard_map/input_backward/pallas_call | solution.py:1523
  724.4 1.3 slice.142
  725.8 1.2 slice.139
  727.0 1.3 slice.140
  728.9 0.8 slice_reduce_fusion.5
  731.0 3.2 multiply_add_fusion
  734.2 3.4 convert_bitcast_fusion
  737.6 1.0 copy.43
  738.6 0.8 copy-done.1
  739.4 1.1 copy.44
  740.5 0.8 copy.45
  741.3 1.1 copy.46
  (83 shorter events, 16.4 us)
Async XLA Ops:
  7.2 8.2 %copy-start.9 = (s32[1,2]{1,0:T(1,128)S(1)}, s32[1,2]{1,0:T(1,128)}, u32[]{:S(2)}) copy-start(s32[1,2]{1,0:T(1,128)} %param.27) | copy-start | bytes 28
  7.2 223.7 %all-gather.4.cloned.1.call-start = ((), (), s32[]{:S(2)}) async-start(), calls=%async_computation.1 | async-start | bytes 3522560 | tf_op jit(solution)/shard_map/all_gather | solution.py:2163
  133.8 143.7 %all-gather.6.cloned.1.call-start = ((), (), s32[]{:S(2)}) async-start(), calls=%async_computation.3 | async-start | bytes 3522560 | tf_op jit(solution)/shard_map/all_gather | solution.py:2161
  134.5 599.7 %reduce-scatter.2.cloned.1.call-start = ((), (), s32[]{:S(2)}) async-start(), calls=%async_computation.2 | async-start | bytes 7045120 | tf_op jit(solution)/shard_map/reduce_scatter | solution.py:2202
  503.2 118.3 %copy-start.5 = (f32[3,2048]{1,0:T(4,128)S(1)}, f32[3,2048]{1,0:T(4,128)}, u32[]{:S(2)}) copy-start(f32[3,2048]{1,0:T(4,128)} %get-tuple-element.88) | copy-start | bytes 73732
  503.2 120.1 %copy-start.8 = (f32[4]{0:T(128)S(1)}, f32[4]{0:T(128)}, u32[]{:S(2)}) copy-start(f32[4]{0:T(128)} %compare_convert_fusion.1) | copy-start | bytes 52
  503.2 122.3 %copy-start.6 = (f32[2,768]{1,0:T(2,128)S(1)}, f32[2,768]{1,0:T(2,128)}, u32[]{:S(2)}) copy-start(f32[2,768]{1,0:T(2,128)} %get-tuple-element.89) | copy-start | bytes 18436
  503.2 122.5 %copy-start.7 = (f32[32]{0:T(128)S(1)}, f32[32]{0:T(128)}, u32[]{:S(2)}) copy-start(f32[32]{0:T(128)} %mul.58) | copy-start | bytes 388
  626.7 104.3 %copy-start = (f32[256,2048]{1,0:T(8,128)S(1)}, f32[256,2048]{1,0:T(8,128)}, u32[]{:S(2)}) copy-start(f32[256,2048]{1,0:T(8,128)} %get-tuple-element.81) | copy-start | bytes 6291460
  734.2 3.4 copy-start.3
  737.6 1.8 copy-start.1
  737.6 2.9 copy-start.4
  739.4 1.9 copy-start.2
Sparse Core Ops, SparseCore 0:
  133.9 82.9 all-gather.3
  219.1 58.4 all-gather.5
  503.3 143.5 reduce-scatter.1

commit v8 on v7

--- a/solution.py
+++ b/solution.py
@@ -16,6 +16,7 @@
 residual_scale = 48.0**0.5
 norm_eps = 1e-05
 masked_value = -1e30
+key_tile = 128
 kernel_memory = 60 * 2**20
 
 
@@ -274,7 +275,11 @@
             device_id_type=pl.DeviceIdType.MESH,
         ).wait_recv()
 
-    def run(self, compute, before, between):
+    def run(self, first, second, before, after_far):
+        def compute(chip):
+            first(chip)
+            second(chip)
+
         keep = self.send_own()
         keep.wait()
         self.receive_mate(0)
@@ -290,11 +295,13 @@
                 self.first_sums()
         self.receive(self.far)
         self.receive_mate(self.far)
-        compute(chip_at(self.position + self.far, self.ring))
+        farthest = chip_at(self.position + self.far, self.ring)
+        first(farthest)
+        before()
+        second(farthest)
         self.share(self.far)
-        before()
         self.far_sums()
-        between()
+        after_far()
         self.last_sums()
 
     def run_gather(self, compute, between):
@@ -317,7 +324,7 @@
         compute(chip_at(self.position + self.far, self.ring))
         return done
 
-    def run_sums(self, compute):
+    def start_sums(self, compute):
         compute(chip_at(self.position + self.far, self.ring))
         self.share(self.far)
         for distance in range(self.far - 1, 0, -1):
@@ -329,7 +336,6 @@
                 self.first_sums()
         compute(chip_at(self.position, self.ring))
         self.share(0)
-        self.last_sums()
 
     def first_sums(self):
         distance = self.far - 1
@@ -648,8 +654,7 @@
     wide_count,
     narrow_count,
     own,
-    gate_expand,
-    upper_expand,
+    expand,
     reduce,
     shift,
     hidden,
@@ -707,8 +712,8 @@
         wide_count, None, None, parts, from_mate, incoming, late_sems, pl.ds(late, cols)
     )
     loads = [
-        load_padded(gate_expand, expand_mat.at[0], load_sems.at[0]),
-        load_padded(upper_expand, expand_mat.at[1], load_sems.at[1]),
+        load_padded(expand.at[0], expand_mat.at[0], load_sems.at[0]),
+        load_padded(expand.at[1], expand_mat.at[1], load_sems.at[1]),
     ]
 
     def reduce_cols(block):
@@ -778,13 +783,15 @@
     done = plane.run_gather(compute, between)
     for step in range(done, narrow_count - 1):
         line_reduce.step(step)
-    plane.run_sums(compute_sums(early, width - cols))
+    plane.start_sums(compute_sums(early, width - cols))
     line_reduce.step(narrow_count - 1)
     keep_reduce = pltpu.make_async_copy(
         reduce_mat.at[pl.ds(0, filled)], reduce_out, load_sems.at[3]
     )
     keep_reduce.start()
-    late_plane.run_sums(compute_sums(late, cols))
+    late_plane.start_sums(compute_sums(late, cols))
+    plane.last_sums()
+    late_plane.last_sums()
     plane.finish(feed)
     late_plane.finish(feed)
 
@@ -820,8 +827,7 @@
     wide_count,
     narrow_count,
     hidden_low,
-    gate_expand,
-    upper_expand,
+    expand,
     reduce_weight,
     shift,
     hidden,
@@ -860,7 +866,7 @@
             jax.ShapeDtypeStruct((rows, width), jnp.bfloat16),
             jax.ShapeDtypeStruct((3, width), jnp.float32),
         ),
-        in_specs=[anywhere] * 4 + [vmem] * 6,
+        in_specs=[anywhere] * 3 + [vmem] * 6,
         out_specs=(anywhere,) * 5 + (vmem,) * 4,
         scratch_shapes=scratch,
         compiler_params=pltpu.CompilerParams(
@@ -872,8 +878,7 @@
         name="geglu_forward",
     )(
         hidden_low,
-        gate_expand,
-        upper_expand,
+        expand,
         reduce_weight,
         shift,
         hidden,
@@ -888,8 +893,7 @@
     wide_count,
     narrow_count,
     own,
-    gate_expand,
-    upper_expand,
+    expand,
     reduce,
     slope_in,
     gelu_in,
@@ -926,8 +930,8 @@
     sems = (gather_send, gather_recv, mate_send, mate_recv, sum_send, sum_recv, own_sem)
     plane = PlaneExchange(wide_count, own, blocks, parts, from_mate, incoming, sems)
     loads = [
-        load_padded(gate_expand, expand_mat.at[0], load_sems.at[0]),
-        load_padded(upper_expand, expand_mat.at[1], load_sems.at[1]),
+        load_padded(expand.at[0], expand_mat.at[0], load_sems.at[0]),
+        load_padded(expand.at[1], expand_mat.at[1], load_sems.at[1]),
         load_padded(reduce, reduce_mat, load_sems.at[2]),
         pltpu.make_async_copy(slope_in, slope, load_sems.at[3]),
         pltpu.make_async_copy(gelu_in, gelu, load_sems.at[4]),
@@ -972,6 +976,7 @@
 
         tiles(slope.shape[2], 256, units)
 
+    def compute_sums(chip):
         def outputs(cols):
             set_pair(
                 parts,
@@ -994,10 +999,30 @@
     def reduce_work():
         for copy in late_loads:
             copy.wait()
-        for start in range(0, active.shape[2], 256):
-            reduce_mat[start : start + 256] = product(active, blocks, start)
+
+        def reduce_cols(index):
+            cols = pl.ds(pl.multiple_of(index * line_cols, line_cols), line_cols)
+
+            def units(some):
+                tokens = active.shape[0] * active.shape[1]
+                part = dot(
+                    active[:, :, some].reshape(tokens, some.size),
+                    blocks[:, :, cols].reshape(tokens, line_cols),
+                    ((0,), (0,)),
+                )
+                reduce_mat[some, cols] = part.astype(jnp.bfloat16)
+
+            tiles(active.shape[2], 256, units)
+
         for offset in range(narrow_count - 1, 0, -1):
+            for way in range(2):
+
+                @pl.when(line_sum.reaches(way, offset))
+                def _():
+                    reduce_cols(line_sum.target(way, offset))
+
             line_sum.begin(offset)
+        reduce_cols(line.mine)
 
     def expand_work(left, start, target):
         def work():
@@ -1024,20 +1049,20 @@
     steps = [
         functools.partial(line_sum.step, offset) for offset in range(narrow_count - 2, 0, -1)
     ]
-    middle = len(works) // 2
-    works = [works[:middle], steps[: len(steps) // 2], works[middle:], steps[len(steps) // 2 :]]
+    third = len(works) // 3
+    middle = (len(steps) + 1) // 2
 
     def many(calls):
         for call in calls:
             call()
 
-    plane.run(compute, reduce_work, functools.partial(many, works[0] + works[1]))
-    many(works[2])
+    beside = functools.partial(many, steps[:middle] + works[:third])
+    plane.run(compute, compute_sums, reduce_work, beside)
+    many(works[third : 2 * third] + steps[middle:] + works[2 * third :])
     plane.finish(hidden_grad)
-    many(works[3])
+    plane.drain()
     line_sum.finish(reduce_grad)
     line_sum.drain()
-    plane.drain()
     for copy in kept[-2:]:
         copy.wait()
 
@@ -1046,8 +1071,7 @@
     wide_count,
     narrow_count,
     feed_grad,
-    gate_expand,
-    upper_expand,
+    expand,
     reduce_full,
     slope,
     gelu,
@@ -1080,11 +1104,11 @@
             jax.ShapeDtypeStruct(
                 (reduce_full.shape[0], width // narrow_count), jnp.float32
             ),
-            jax.ShapeDtypeStruct((2, *gate_expand.shape), jnp.bfloat16),
+            jax.ShapeDtypeStruct(expand.shape, jnp.bfloat16),
             jax.ShapeDtypeStruct((rows, width), jnp.float32),
             jax.ShapeDtypeStruct((2, padded), jnp.float32),
         ),
-        in_specs=[anywhere] * 8,
+        in_specs=[anywhere] * 7,
         out_specs=(vmem, anywhere, vmem, vmem),
         scratch_shapes=scratch,
         compiler_params=pltpu.CompilerParams(
@@ -1094,7 +1118,11 @@
             flops=12 * wide_count * rows * padded * width, bytes_accessed=200 * 2**20, transcendentals=0
         ),
         name="geglu_backward",
-    )(feed_grad, gate_expand, upper_expand, reduce_full, slope, gelu, active, rows_all)
+    )(feed_grad, expand, reduce_full, slope, gelu, active, rows_all)
+
+
+def key_slices(bucket):
+    return [slice(start, start + key_tile) for start in range(0, bucket, key_tile)]
 
 
 def rotate_lanes(vectors, cosine, signed_sine):
@@ -1137,6 +1165,8 @@
     merge_send,
     merge_recv,
     load_sems,
+    scaled_held,
+    change_held,
     parts,
     from_mate,
     incoming,
@@ -1151,6 +1181,7 @@
     rows, width = sum_grad.shape
     own_cols = queries.shape[1]
     heads = own_cols // HDIM
+    bucket = queries.shape[0]
     scale = HDIM ** (-0.5)
 
     def load(head):
@@ -1230,17 +1261,23 @@
 
         def chunk(i, carry):
             here = pl.ds(pl.multiple_of(i * rows, rows), rows)
-            weights_low = held[:, here]
             up = upstream[i, :, cols]
-            pulled = dot(values[:, cols], up, ((1,), (1,)))
-            weights = weights_low.astype(jnp.float32)
-            scaled = weights * pulled
-            change = (scaled - weights * jnp.sum(scaled, axis=0, keepdims=True)).astype(
-                jnp.bfloat16
-            )
-            key_total[...] += dot(change, queries[here, cols], ((1,), (0,)))
-            value_total[...] += dot(weights_low, up, ((1,), (0,)))
-            query_grad = dot(keys_turned[...], change, ((1,), (0,))).T * scale
+            query = queries[here, cols]
+            sums = None
+            for some in key_slices(bucket):
+                weights = held[some, here]
+                scaled = weights.astype(jnp.float32) * dot(values[some, cols], up, ((1,), (1,)))
+                scaled_held[some] = scaled
+                part = jnp.sum(scaled.reshape(-1, 8, rows), axis=0)
+                sums = part if sums is None else sums + part
+                value_total[some] += dot(weights, up, ((1,), (0,)))
+            total = jnp.sum(sums, axis=0, keepdims=True)
+            for some in key_slices(bucket):
+                change = scaled_held[some] - held[some, here].astype(jnp.float32) * total
+                change = change.astype(jnp.bfloat16)
+                change_held[some] = change
+                key_total[some] += dot(change, query, ((1,), (0,)))
+            query_grad = dot(keys_turned[...], change_held[...], ((1,), (0,))).T * scale
             triple[here, cols] = rotate_lanes(
                 query_grad, cosine[here], signed_sine[here]
             ).astype(jnp.bfloat16)
@@ -1329,6 +1366,8 @@
             dma((narrow_count - 1,)),
             dma((narrow_count,)),
             dma((2,)),
+            pltpu.VMEM((bucket, rows), jnp.float32),
+            pltpu.VMEM((bucket, rows), jnp.bfloat16),
         ]
         + sum_scratch(wide_count, block, width),
         compiler_params=pltpu.CompilerParams(
@@ -1591,7 +1630,7 @@
     last_query,
     rows_all,
     heads_all,
-    merge_own,
+    merge_all,
     small_all,
     rows_send,
     rows_recv,
@@ -1607,9 +1646,15 @@
     out_sems,
     heads_ring_send,
     heads_ring_recv,
+    merge_ring_send,
+    merge_ring_recv,
 ):
-    ring_sems = (heads_ring_send, heads_ring_recv, None, None, None, None, None)
-    heads_ring = PlaneExchange(wide_count, None, heads_all, heads_all, None, None, ring_sems)
+    def ring_of(blocks, send, recv):
+        sems = (send, recv, None, None, None, None, None)
+        return PlaneExchange(wide_count, None, blocks, blocks, None, None, sems)
+
+    heads_ring = ring_of(heads_all, heads_ring_send, heads_ring_recv)
+    merge_ring = ring_of(merge_all, merge_ring_send, merge_ring_recv)
     line = LineExchange(narrow_count)
     here = line.mine
     last = narrow_count - 1
@@ -1640,7 +1685,7 @@
         for which in range(3)
     ]
     keep_merge = pltpu.make_async_copy(
-        merge_weight, merge_own.at[z_rows(here)], local_sems.at[1]
+        merge_weight, merge_all.at[slot, z_rows(here)], local_sems.at[1]
     )
     for copy in keeps + [keep_merge]:
         copy.start()
@@ -1659,7 +1704,7 @@
     def merge_copy(offset, where, sender):
         return line.copy(
             merge_weight,
-            merge_own.at[z_rows(sender)],
+            merge_all.at[slot, z_rows(sender)],
             merge_send.at[offset - 1],
             merge_recv.at[sender],
             where,
@@ -1771,12 +1816,18 @@
     project(here)
     for step in range(2, narrow_count):
         line_rows.step(step)
+        if step == 2:
+            keep_merge.wait()
+            for offset in range(1, narrow_count):
+                merge_copy(offset, line.peer(offset), line.peer(offset)).wait_recv()
+            merge_ring.send_own()
         project_step(step - 1)
+        if step == 2:
+            merge_ring.receive_mate(0)
+            for distance in range(1, merge_ring.far + 1):
+                gather(merge_ring, distance)
+            keep_out(merge_all, merge_out)
     project_step(last)
-    keep_merge.wait()
-    for offset in range(1, narrow_count):
-        merge_copy(offset, line.peer(offset), line.peer(offset)).wait_recv()
-    keep_out(merge_own, merge_out)
     keep_out(rows_all, rows_out)
     for offset in range(1, wide_count):
         wide_copy(offset, (place + offset) % wide_count).wait_recv()
@@ -1785,6 +1836,7 @@
     for copy in started:
         copy.wait_send()
     heads_ring.drain()
+    merge_ring.drain()
     for copy in outs:
         copy.wait()
 
@@ -1803,7 +1855,7 @@
     shapes = (
         (narrow_count, rows, width),
         (wide_count, block, columns),
-        (block, width),
+        (wide_count, block, width),
         (wide_count, narrow_count, lines, 128),
     )
     far = narrow_count - 1
@@ -1832,6 +1884,8 @@
             dma((4,)),
             dma((3, wide_count, 2)),
             dma((wide_count, 2)),
+            dma((3, wide_count, 2)),
+            dma((wide_count, 2)),
         ],
         compiler_params=pltpu.CompilerParams(
             collective_id=5, has_side_effects=True, vmem_limit_bytes=kernel_memory
@@ -1844,7 +1898,6 @@
 
 
 def attention_forward_kernel(
-    wide_count,
     narrow_count,
     triple,
     heads_shift,
@@ -1866,7 +1919,6 @@
     hidden_low,
     normed,
     inv_std,
-    merge_out,
     merge_mat,
     probs_held,
     values_turned,
@@ -1875,21 +1927,16 @@
     mixed_send,
     mixed_recv,
     local_sems,
-    ring_send,
-    ring_recv,
-    own_sem,
+    scores_held,
 ):
     line = LineExchange(narrow_count)
-    ring_sems = (ring_send, ring_recv, None, None, None, None, own_sem)
-    ring = PlaneExchange(wide_count, merge, merge_mat, merge_mat, None, None, ring_sems)
     bucket, own_cols = queries.shape
     rows, width = own.shape
     heads = own_cols // HDIM
     scale = HDIM ** (-0.5)
-    greet_plane(ring)
-    line.greet(3)
-    keep_own = ring.send_own()
-    ring_steps = [functools.partial(ring.receive, step) for step in range(1, ring.far + 1)]
+    load_merge = pltpu.make_async_copy(merge, merge_mat, local_sems.at[2])
+    load_merge.start()
+    line.greet()
 
     def keep(head):
         return pltpu.make_async_copy(
@@ -1929,14 +1976,26 @@
 
         def chunk(i, carry):
             here = pl.ds(pl.multiple_of(i * rows, rows), rows)
-            scores = dot(keys[:, cols], queries[here, cols], ((1,), (1,))) * scale
-            token = i * rows + lax.broadcasted_iota(jnp.int32, (bucket, rows), 1)
-            seen = (token >= first_query[...]) & (token <= last_query[...])
-            scores = jnp.where(seen, scores, masked_value)
-            expo = jnp.exp(scores - jnp.max(scores, axis=0, keepdims=True))
-            weights = (expo * (1 / jnp.sum(expo, axis=0, keepdims=True))).astype(jnp.bfloat16)
-            held[:, here] = weights
-            mixed_part = dot(values_turned[...], weights, ((1,), (0,)))
+            query = queries[here, cols]
+            token = i * rows + lax.broadcasted_iota(jnp.int32, (key_tile, rows), 1)
+            tops, sums = None, None
+            for some in key_slices(bucket):
+                scores = dot(keys[some, cols], query, ((1,), (1,))) * scale
+                seen = (token >= first_query[some]) & (token <= last_query[some])
+                scores = jnp.where(seen, scores, masked_value)
+                scores_held[some] = scores
+                top = jnp.max(scores.reshape(-1, 8, rows), axis=0)
+                tops = top if tops is None else jnp.maximum(tops, top)
+            top = jnp.max(tops, axis=0, keepdims=True)
+            for some in key_slices(bucket):
+                expo = jnp.exp(scores_held[some] - top)
+                scores_held[some] = expo
+                part = jnp.sum(expo.reshape(-1, 8, rows), axis=0)
+                sums = part if sums is None else sums + part
+            share = 1 / jnp.sum(sums, axis=0, keepdims=True)
+            for some in key_slices(bucket):
+                held[some, here] = (scores_held[some] * share).astype(jnp.bfloat16)
+            mixed_part = dot(values_turned[...], held[:, here], ((1,), (0,)))
             outbound[i, :, cols] = mixed_part.T.astype(jnp.bfloat16)
             return carry
 
@@ -1946,8 +2005,6 @@
             copy = mixed_copy(head, offset, line.peer(offset), line.mine)
             copy.start()
             started.append(copy)
-        if ring_steps:
-            ring_steps.pop(0)()
     own_mixed = pltpu.make_async_copy(
         outbound.at[line.mine],
         mixed.at[:, pl.ds(pl.multiple_of(line.mine * own_cols, own_cols), own_cols)],
@@ -1955,13 +2012,7 @@
     )
     own_mixed.start()
     own_mixed.wait()
-    keep_own.wait()
-    for step in ring_steps:
-        step()
-    for offset in range(ring.ring):
-        ring.receive_mate(offset)
-    keep_merge = pltpu.make_async_copy(merge_mat, merge_out, local_sems.at[2])
-    keep_merge.start()
+    load_merge.wait()
     for offset in range(1, narrow_count):
         for head in range(heads):
             mixed_copy(head, offset, line.peer(offset), line.peer(offset)).wait_recv()
@@ -1970,7 +2021,7 @@
     def merge_cols(cols):
         hidden[:, cols] = (
             residual_scale * own[:, cols].astype(jnp.float32)
-            + dot(mixed[...], merge_mat[:, :, cols].reshape(width, cols.size), ((1,), (0,)))
+            + dot(mixed[...], merge_mat[:, cols], ((1,), (0,)))
             + merge_shift[:, cols]
         )
 
@@ -1990,12 +2041,9 @@
         keep(head).wait()
     for copy in started:
         copy.wait_send()
-    ring.drain()
-    keep_merge.wait()
 
 
 def attention_forward(
-    wide_count,
     narrow_count,
     triple,
     heads_shift,
@@ -2004,7 +2052,7 @@
     first_query,
     last_query,
     layer_input,
-    merge_block,
+    merge_full,
     merge_shift,
     gain,
     shift,
@@ -2024,7 +2072,7 @@
         return jax.ShapeDtypeStruct(shape, jnp.float32)
 
     return pl.pallas_call(
-        functools.partial(attention_forward_kernel, wide_count, narrow_count),
+        functools.partial(attention_forward_kernel, narrow_count),
         out_shape=(
             low_shape(bucket, own_cols),
             low_shape(bucket, own_cols),
@@ -2035,12 +2083,11 @@
             low_shape(rows, width),
             wide_shape(rows, width),
             wide_shape(rows, 1),
-            low_shape(wide_count, *merge_block.shape),
         ),
         in_specs=[vmem] * 7 + [anywhere] + [vmem] * 3,
-        out_specs=(vmem, vmem, vmem, anywhere) + (vmem,) * 5 + (anywhere,),
+        out_specs=(vmem, vmem, vmem, anywhere) + (vmem,) * 5,
         scratch_shapes=[
-            pltpu.VMEM((wide_count, *merge_block.shape), jnp.bfloat16),
+            pltpu.VMEM((width, width), jnp.bfloat16),
             pltpu.VMEM((2, bucket, bucket), jnp.bfloat16),
             pltpu.VMEM((HDIM, bucket), jnp.bfloat16),
             pltpu.VMEM((narrow_count, rows, own_cols), jnp.bfloat16),
@@ -2048,9 +2095,7 @@
             dma((narrow_count - 1, heads)),
             dma((narrow_count, heads)),
             dma((4,)),
-            dma((3, wide_count, 2)),
-            dma((wide_count, 2)),
-            dma(()),
+            pltpu.VMEM((bucket, rows), jnp.float32),
         ],
         compiler_params=pltpu.CompilerParams(
             collective_id=6, has_side_effects=True, vmem_limit_bytes=kernel_memory
@@ -2067,7 +2112,7 @@
         first_query,
         last_query,
         layer_input,
-        merge_block,
+        merge_full,
         merge_shift,
         gain,
         shift,
@@ -2103,7 +2148,7 @@
     (
         rows_input,
         heads_mat,
-        merge_block,
+        merge_full,
         small_all,
         triple,
         cosine,
@@ -2121,6 +2166,7 @@
         jnp.asarray(rotary_speeds(HDIM)),
     )
     rows_input = rows_input.reshape(bucket_len, model_width)
+    merge_full = merge_full.reshape(model_width, model_width)
     heads_mat = heads_mat.reshape(model_width, 3 * own_cols)
     heads_shift, merge_shift, gains, shifts, expand_shift, reduce_shift = unpack_small(
         small_all, smalls
@@ -2138,9 +2184,7 @@
         hidden_low,
         normed_one,
         inv_one,
-        merge_full,
     ) = attention_forward(
-        wide_count,
         narrow_count,
         triple,
         own_shift,
@@ -2149,7 +2193,7 @@
         first_query,
         last_query,
         layer_input,
-        merge_block,
+        merge_full,
         merge_shift.reshape(1, -1),
         gains[0].reshape(1, -1),
         shifts[0].reshape(1, -1),
@@ -2158,9 +2202,7 @@
     tile_rows = -share % 16
     padded = -(-share // 256) * 256
     expand_low = jnp.pad(expand_weight.transpose(1, 2, 0), ((0, 0), (0, tile_rows), (0, 0)))
-    gate_expand = lax.all_gather(expand_low[0], "narrow", axis=1, tiled=True)
-    upper_low, _ = lax.optimization_barrier((expand_low[1], small_all))
-    upper_expand = lax.all_gather(upper_low, "narrow", axis=1, tiled=True)
+    expand_full = lax.all_gather(expand_low, "narrow", axis=2, tiled=True)
     reduce_low = jnp.pad(reduce_weight, ((0, tile_rows), (0, 0)))
     (
         reduce_full,
@@ -2176,8 +2218,7 @@
         wide_count,
         narrow_count,
         hidden_low,
-        gate_expand,
-        upper_expand,
+        expand_full,
         reduce_low,
         jnp.pad(expand_shift, ((0, 0), (0, padded - share))),
         hidden,
@@ -2190,8 +2231,7 @@
         wide_count,
         narrow_count,
         feed_grad,
-        gate_expand,
-        upper_expand,
+        expand_full,
         reduce_full,
         slope,
         gelu,
@@ -2218,7 +2258,7 @@
         normed_one,
         inv_one,
         gains[0].reshape(1, -1),
-        merge_full.reshape(model_width, model_width),
+        merge_full,
         mixed,
         queries,
         keys,

time: 760 us -> 778 us (1.024)
  Pallas kernels: 647 us -> 715 us
  waiting for transfers between devices: 47.3 us -> 0.72 us
    pallas_call x1, Pallas kernels: 118 us -> 227 us  [gather_front(): pl.pallas_call(functools.partial(gather_kernel, wide_count, narrow_count)...]
    all_gather x2 -> x1, waiting for transfers between devices: 46.6 us -> 0.02 us  [shards(): expand_full = lax.all_gather(expand_low, 'narrow', axis=2, tiled=True)]
    pallas_call x1, Pallas kernels: 88.1 us -> 46.9 us  [attention_forward(): pl.pallas_call(functools.partial(attention_forward_kernel, narrow_count),...]
  transfers between devices with their start and end apart: 3 -> 2, of which waited for: 1 -> 0; matrix products, arithmetic and copies ran while one was open for 3% -> 4% of each run, Pallas kernels for 40% -> 64%
where the time goes in v8:
time: 778 us; the launch traced here: 769 us
  Pallas kernels  715 us (92%)
  local copies, waits for them, and re-layouts  27.6 us (4%)
  between operations  15.3 us (2%)
  other arithmetic  10.6 us (1%)
    pallas_call x1, Pallas kernels, gather_front(): pl.pallas_call(functools.partial(gather_kernel, wide_count, narrow_count)...  227 us
    pallas_call x1, Pallas kernels, attention_backward(): pl.pallas_call(functools.partial(attention_backward_kernel, wide_count, n...  119 us
    pallas_call x1, Pallas kernels, geglu_backward(): pl.pallas_call(functools.partial(geglu_backward_kernel, wide_count, narro...  116 us
    pallas_call x1, Pallas kernels, geglu_forward(): pl.pallas_call(functools.partial(geglu_forward_kernel, wide_count, narrow...  103 us
    pallas_call x1, Pallas kernels, input_backward(): pl.pallas_call(functools.partial(input_backward_kernel, wide_count, narro...  103 us
    pallas_call x1, Pallas kernels, attention_forward(): pl.pallas_call(functools.partial(attention_forward_kernel, narrow_count),...  46.9 us
  transfers between devices with their start and end apart: 2, of which 0 were waited for; matrix products, arithmetic and copies ran while one was open for 4% of the time, Pallas kernels for 64%

profile of v8, /device:TPU:8, one launch (start us, length us, event | category | flops | bytes accessed | tf_op | source)
XLA Modules:
  0.0 769.1 jit_solution(18127862984357211533)
XLA Ops:
  8.0 0.8 reshape.124
  10.2 2.1 concatenate.9
  13.6 1.2 pad_add_fusion.buckets
  14.8 226.9 %gather_front.1 = (bf16[4,256,2048]{2,1,0:T(8,128)(2,1)}, bf16[8,256,1536]{2,1,0:T(8,128)(2,1)}, bf16[8,256,2048]{2,1,0:T(8,128)(2,1)}, bf16[8,4,16,128]{3,2,1,0...) custom-call(bf16[256,2048]{1,0:T(8,128)(2,1)} %own.3, ...), custom_call_target="tpu_custom_call" | custom-call | flops 80000000000 | bytes 209715200 | tf_op jit(solution)/shard_map/gather_front/pallas_call | solution.py:1865
  241.7 1.0 reshape.142
  249.9 46.9 %attention_forward.1 = (bf16[1024,512]{1,0:T(8,128)(2,1)}, bf16[1024,512]{1,0:T(8,128)(2,1)}, bf16[1024,512]{1,0:T(8,128)(2,1)}, bf16[4,1024,1024]{2,1,0:T(8,128...) custom-call(f32[1024,1536]{1,0:T(8,128)} %get-tuple-element.52.tripl, ...), custom_call_target="tpu_custom_call" | custom-call | flops 60000002048 | bytes 209715200 | tf_op jit(solution)/shard_map/attention_forward/pallas_call | solution.py:2074
  296.9 102.7 %geglu_forward.1 = (bf16[688,2048]{1,0:T(8,128)(2,1)}, bf16[8,256,2048]{2,1,0:T(8,128)(2,1)}, bf16[8,256,768]{2,1,0:T(8,128)(2,1)}, bf16[8,256,768]{2,1,0:T(8,12...) custom-call(bf16[256,2048]{1,0:T(8,128)(2,1)} %get-tuple-element.59., ...), custom_call_target="tpu_custom_call" | custom-call | flops 19327352832 | bytes 209715200 | tf_op jit(solution)/shard_map/geglu_forward/pallas_call | solution.py:856
  399.6 116.4 %geglu_backward.1 = (f32[688,512]{1,0:T(8,128)}, bf16[2,688,2048]{2,1,0:T(8,128)(2,1)}, f32[256,2048]{1,0:T(8,128)}, f32[2,768]{1,0:T(2,128)}) custom-call(bf16[256,2048]{1,0:T(8,128)(2,1)} %get-tuple-element.63.own, bf16[2,688,2048]{2,1,0:T(8,128)(2,1)} %all-gather.2.cloned.1.call-done.expand, bf16[688,2048]{1,0:T(8,128)(2,1)} %get-tuple-element.64.reduce, ...), custom_call_target="tpu_custom_call" | custom-call | flops 38654705664 | bytes 209715200 | tf_op jit(solution)/shard_map/geglu_backward/pallas_call | solution.py:1101
  516.0 119.2 %attention_backward.1 = (bf16[1024,1536]{1,0:T(8,128)(2,1)}, f32[64,2048]{1,0:T(8,128)}, f32[1,1536]{1,0:T(1,128)}, f32[1,2048]{1,0:T(1,128)}, f32[256,2048]{1,0:T(8,128)}, /*index=5*/f32[2,2048]{1,0:T(2,128)}) custom-call(f32[256,2048]{1,0:T(8,128)} %get-tuple-element.62.upper_grad, f32[256,2048]{1,0:T(8,128)} %get-tuple-element.69.hidden_part, ...), custom_call_target="tpu_custom_call" | custom-call | flops 60000002048 | bytes 209715200 | tf_op jit(solution)/shard_map/attention_backward/pallas_call | solution.py:1342
  635.3 0.8 fusion.1
  637.8 1.4 reduce.33
  639.8 0.8 copy.35
  640.5 102.7 %input_backward.1 = (f32[256,2048]{1,0:T(8,128)}, f32[64,6144]{1,0:T(8,128)}, f32[16,128]{1,0:T(8,128)}) custom-call(bf16[1024,2048]{1,0:T(8,128)(2,1)} %bitcast.46, bf16[1024,1536]{1,0:T(8,128)(2,1)} %get-tuple-element.79.triple, bf16[2048,1536]{1,0:T(8,128)(2,1)} %bitcast.45, f32[8,4,16,128]{3,2,1,0:T(8,128)} %bitcast.29), custom_call_target="tpu_custom_call" | custom-call | flops 80000000000 | bytes 209715200 | tf_op jit(solution)/shard_map/input_backward/pallas_call | solution.py:1562
  743.9 1.3 slice.132
  745.3 1.2 slice.129
  746.5 1.3 slice.130
  748.4 0.8 slice_reduce_fusion.5
  750.5 3.2 multiply_add_fusion
  753.7 3.4 convert_bitcast_fusion
  757.1 1.0 copy.43
  758.0 0.8 copy-done.1
  758.9 1.1 copy.44
  760.0 0.8 copy.45
  760.8 1.1 copy.46
  (77 shorter events, 15.0 us)
Async XLA Ops:
  7.2 289.7 %all-gather.2.cloned.1.call-start = ((), (), s32[]{:S(2)}) async-start(), calls=%async_computation.1 | async-start | bytes 7045120 | tf_op jit(solution)/shard_map/all_gather | solution.py:2205
  7.9 745.8 %reduce-scatter.2.cloned.1.call-start = ((), (), s32[]{:S(2)}) async-start(), calls=%async_computation.2 | async-start | bytes 7045120 | tf_op jit(solution)/shard_map/reduce_scatter | solution.py:2242
  516.0 119.3 %copy-start.5 = (f32[3,2048]{1,0:T(4,128)S(1)}, f32[3,2048]{1,0:T(4,128)}, u32[]{:S(2)}) copy-start(f32[3,2048]{1,0:T(4,128)} %get-tuple-element.84) | copy-start | bytes 73732
  516.0 121.2 %copy-start.8 = (f32[4]{0:T(128)S(1)}, f32[4]{0:T(128)}, u32[]{:S(2)}) copy-start(f32[4]{0:T(128)} %compare_convert_fusion.1) | copy-start | bytes 52
  516.0 123.3 %copy-start.6 = (f32[2,768]{1,0:T(2,128)S(1)}, f32[2,768]{1,0:T(2,128)}, u32[]{:S(2)}) copy-start(f32[2,768]{1,0:T(2,128)} %get-tuple-element.85) | copy-start | bytes 18436
  516.0 123.6 %copy-start.7 = (f32[32]{0:T(128)S(1)}, f32[32]{0:T(128)}, u32[]{:S(2)}) copy-start(f32[32]{0:T(128)} %mul.58) | copy-start | bytes 388
  640.5 109.9 %copy-start = (f32[256,2048]{1,0:T(8,128)S(1)}, f32[256,2048]{1,0:T(8,128)}, u32[]{:S(2)}) copy-start(f32[256,2048]{1,0:T(8,128)} %get-tuple-element.77) | copy-start | bytes 6291460
  753.7 3.4 copy-start.3
  757.1 1.8 copy-start.1
  757.1 2.9 copy-start.4
  758.9 1.9 copy-start.2
Sparse Core Ops, SparseCore 0:
  9.6 166.7 all-gather.1
  516.1 143.7 reduce-scatter.1

commit v9 on v7

--- a/solution.py
+++ b/solution.py
@@ -274,7 +274,11 @@
             device_id_type=pl.DeviceIdType.MESH,
         ).wait_recv()
 
-    def run(self, compute, before, between):
+    def run(self, first, second, before, after_far):
+        def compute(chip):
+            first(chip)
+            second(chip)
+
         keep = self.send_own()
         keep.wait()
         self.receive_mate(0)
@@ -290,11 +294,13 @@
                 self.first_sums()
         self.receive(self.far)
         self.receive_mate(self.far)
-        compute(chip_at(self.position + self.far, self.ring))
+        farthest = chip_at(self.position + self.far, self.ring)
+        first(farthest)
+        before()
+        second(farthest)
         self.share(self.far)
-        before()
         self.far_sums()
-        between()
+        after_far()
         self.last_sums()
 
     def run_gather(self, compute, between):
@@ -317,7 +323,7 @@
         compute(chip_at(self.position + self.far, self.ring))
         return done
 
-    def run_sums(self, compute):
+    def start_sums(self, compute):
         compute(chip_at(self.position + self.far, self.ring))
         self.share(self.far)
         for distance in range(self.far - 1, 0, -1):
@@ -329,7 +335,6 @@
                 self.first_sums()
         compute(chip_at(self.position, self.ring))
         self.share(0)
-        self.last_sums()
 
     def first_sums(self):
         distance = self.far - 1
@@ -648,8 +653,7 @@
     wide_count,
     narrow_count,
     own,
-    gate_expand,
-    upper_expand,
+    expand,
     reduce,
     shift,
     hidden,
@@ -707,8 +711,8 @@
         wide_count, None, None, parts, from_mate, incoming, late_sems, pl.ds(late, cols)
     )
     loads = [
-        load_padded(gate_expand, expand_mat.at[0], load_sems.at[0]),
-        load_padded(upper_expand, expand_mat.at[1], load_sems.at[1]),
+        load_padded(expand.at[0], expand_mat.at[0], load_sems.at[0]),
+        load_padded(expand.at[1], expand_mat.at[1], load_sems.at[1]),
     ]
 
     def reduce_cols(block):
@@ -778,13 +782,15 @@
     done = plane.run_gather(compute, between)
     for step in range(done, narrow_count - 1):
         line_reduce.step(step)
-    plane.run_sums(compute_sums(early, width - cols))
+    plane.start_sums(compute_sums(early, width - cols))
     line_reduce.step(narrow_count - 1)
     keep_reduce = pltpu.make_async_copy(
         reduce_mat.at[pl.ds(0, filled)], reduce_out, load_sems.at[3]
     )
     keep_reduce.start()
-    late_plane.run_sums(compute_sums(late, cols))
+    late_plane.start_sums(compute_sums(late, cols))
+    plane.last_sums()
+    late_plane.last_sums()
     plane.finish(feed)
     late_plane.finish(feed)
 
@@ -820,8 +826,7 @@
     wide_count,
     narrow_count,
     hidden_low,
-    gate_expand,
-    upper_expand,
+    expand,
     reduce_weight,
     shift,
     hidden,
@@ -860,7 +865,7 @@
             jax.ShapeDtypeStruct((rows, width), jnp.bfloat16),
             jax.ShapeDtypeStruct((3, width), jnp.float32),
         ),
-        in_specs=[anywhere] * 4 + [vmem] * 6,
+        in_specs=[anywhere] * 3 + [vmem] * 6,
         out_specs=(anywhere,) * 5 + (vmem,) * 4,
         scratch_shapes=scratch,
         compiler_params=pltpu.CompilerParams(
@@ -872,8 +877,7 @@
         name="geglu_forward",
     )(
         hidden_low,
-        gate_expand,
-        upper_expand,
+        expand,
         reduce_weight,
         shift,
         hidden,
@@ -888,8 +892,7 @@
     wide_count,
     narrow_count,
     own,
-    gate_expand,
-    upper_expand,
+    expand,
     reduce,
     slope_in,
     gelu_in,
@@ -926,8 +929,8 @@
     sems = (gather_send, gather_recv, mate_send, mate_recv, sum_send, sum_recv, own_sem)
     plane = PlaneExchange(wide_count, own, blocks, parts, from_mate, incoming, sems)
     loads = [
-        load_padded(gate_expand, expand_mat.at[0], load_sems.at[0]),
-        load_padded(upper_expand, expand_mat.at[1], load_sems.at[1]),
+        load_padded(expand.at[0], expand_mat.at[0], load_sems.at[0]),
+        load_padded(expand.at[1], expand_mat.at[1], load_sems.at[1]),
         load_padded(reduce, reduce_mat, load_sems.at[2]),
         pltpu.make_async_copy(slope_in, slope, load_sems.at[3]),
         pltpu.make_async_copy(gelu_in, gelu, load_sems.at[4]),
@@ -972,6 +975,7 @@
 
         tiles(slope.shape[2], 256, units)
 
+    def compute_sums(chip):
         def outputs(cols):
             set_pair(
                 parts,
@@ -994,10 +998,30 @@
     def reduce_work():
         for copy in late_loads:
             copy.wait()
-        for start in range(0, active.shape[2], 256):
-            reduce_mat[start : start + 256] = product(active, blocks, start)
+
+        def reduce_cols(index):
+            cols = pl.ds(pl.multiple_of(index * line_cols, line_cols), line_cols)
+
+            def units(some):
+                tokens = active.shape[0] * active.shape[1]
+                part = dot(
+                    active[:, :, some].reshape(tokens, some.size),
+                    blocks[:, :, cols].reshape(tokens, line_cols),
+                    ((0,), (0,)),
+                )
+                reduce_mat[some, cols] = part.astype(jnp.bfloat16)
+
+            tiles(active.shape[2], 256, units)
+
         for offset in range(narrow_count - 1, 0, -1):
+            for way in range(2):
+
+                @pl.when(line_sum.reaches(way, offset))
+                def _():
+                    reduce_cols(line_sum.target(way, offset))
+
             line_sum.begin(offset)
+        reduce_cols(line.mine)
 
     def expand_work(left, start, target):
         def work():
@@ -1024,20 +1048,20 @@
     steps = [
         functools.partial(line_sum.step, offset) for offset in range(narrow_count - 2, 0, -1)
     ]
-    middle = len(works) // 2
-    works = [works[:middle], steps[: len(steps) // 2], works[middle:], steps[len(steps) // 2 :]]
+    third = len(works) // 3
+    middle = (len(steps) + 1) // 2
 
     def many(calls):
         for call in calls:
             call()
 
-    plane.run(compute, reduce_work, functools.partial(many, works[0] + works[1]))
-    many(works[2])
+    beside = functools.partial(many, steps[:middle] + works[:third])
+    plane.run(compute, compute_sums, reduce_work, beside)
+    many(works[third : 2 * third] + steps[middle:] + works[2 * third :])
     plane.finish(hidden_grad)
-    many(works[3])
+    plane.drain()
     line_sum.finish(reduce_grad)
     line_sum.drain()
-    plane.drain()
     for copy in kept[-2:]:
         copy.wait()
 
@@ -1046,8 +1070,7 @@
     wide_count,
     narrow_count,
     feed_grad,
-    gate_expand,
-    upper_expand,
+    expand,
     reduce_full,
     slope,
     gelu,
@@ -1080,11 +1103,11 @@
             jax.ShapeDtypeStruct(
                 (reduce_full.shape[0], width // narrow_count), jnp.float32
             ),
-            jax.ShapeDtypeStruct((2, *gate_expand.shape), jnp.bfloat16),
+            jax.ShapeDtypeStruct(expand.shape, jnp.bfloat16),
             jax.ShapeDtypeStruct((rows, width), jnp.float32),
             jax.ShapeDtypeStruct((2, padded), jnp.float32),
         ),
-        in_specs=[anywhere] * 8,
+        in_specs=[anywhere] * 7,
         out_specs=(vmem, anywhere, vmem, vmem),
         scratch_shapes=scratch,
         compiler_params=pltpu.CompilerParams(
@@ -1094,7 +1117,7 @@
             flops=12 * wide_count * rows * padded * width, bytes_accessed=200 * 2**20, transcendentals=0
         ),
         name="geglu_backward",
-    )(feed_grad, gate_expand, upper_expand, reduce_full, slope, gelu, active, rows_all)
+    )(feed_grad, expand, reduce_full, slope, gelu, active, rows_all)
 
 
 def rotate_lanes(vectors, cosine, signed_sine):
@@ -2158,9 +2181,8 @@
     tile_rows = -share % 16
     padded = -(-share // 256) * 256
     expand_low = jnp.pad(expand_weight.transpose(1, 2, 0), ((0, 0), (0, tile_rows), (0, 0)))
-    gate_expand = lax.all_gather(expand_low[0], "narrow", axis=1, tiled=True)
-    upper_low, _ = lax.optimization_barrier((expand_low[1], small_all))
-    upper_expand = lax.all_gather(upper_low, "narrow", axis=1, tiled=True)
+    expand_low, _ = lax.optimization_barrier((expand_low, small_all))
+    expand_full = lax.all_gather(expand_low, "narrow", axis=2, tiled=True)
     reduce_low = jnp.pad(reduce_weight, ((0, tile_rows), (0, 0)))
     (
         reduce_full,
@@ -2176,8 +2198,7 @@
         wide_count,
         narrow_count,
         hidden_low,
-        gate_expand,
-        upper_expand,
+        expand_full,
         reduce_low,
         jnp.pad(expand_shift, ((0, 0), (0, padded - share))),
         hidden,
@@ -2190,8 +2211,7 @@
         wide_count,
         narrow_count,
         feed_grad,
-        gate_expand,
-        upper_expand,
+        expand_full,
         reduce_full,
         slope,
         gelu,

time: 760 us -> 743 us (0.978)
  waiting for transfers between devices: 47.3 us -> 24.9 us
  Pallas kernels: 647 us -> 656 us
    all_gather x2 -> x1, waiting for transfers between devices: 46.6 us -> 24.9 us  [shards(): expand_full = lax.all_gather(expand_low, 'narrow', axis=2, tiled=True)]
    pallas_call x1, Pallas kernels: 88.1 us -> 95.9 us  [attention_forward(): pl.pallas_call(functools.partial(attention_forward_kernel, wide_count, na...]
  transfers between devices with their start and end apart: 3 -> 2, of which waited for: 1 -> 1; matrix products, arithmetic and copies ran while one was open for 3% -> 3% of each run, Pallas kernels for 40% -> 43%
where the time goes in v9:
time: 743 us; the launch traced here: 734 us
  Pallas kernels  656 us (88%)
  local copies, waits for them, and re-layouts  27.6 us (4%)
  waiting for transfers between devices  24.9 us (3%)
  between operations  15.3 us (2%)
  other arithmetic  10.6 us (1%)
    pallas_call x1, Pallas kernels, attention_backward(): pl.pallas_call(functools.partial(attention_backward_kernel, wide_count, n...  120 us
    pallas_call x1, Pallas kernels, gather_front(): pl.pallas_call(functools.partial(gather_kernel, wide_count, narrow_count)...  118 us
    pallas_call x1, Pallas kernels, geglu_backward(): pl.pallas_call(functools.partial(geglu_backward_kernel, wide_count, narro...  117 us
    pallas_call x1, Pallas kernels, input_backward(): pl.pallas_call(functools.partial(input_backward_kernel, wide_count, narro...  103 us
    pallas_call x1, Pallas kernels, geglu_forward(): pl.pallas_call(functools.partial(geglu_forward_kernel, wide_count, narrow...  103 us
    pallas_call x1, Pallas kernels, attention_forward(): pl.pallas_call(functools.partial(attention_forward_kernel, wide_count, na...  95.9 us
    all_gather x1, waiting for transfers between devices, shards(): expand_full = lax.all_gather(expand_low, 'narrow', axis=2, tiled=True)  24.9 us
  transfers between devices with their start and end apart: 2, of which 1 were waited for; matrix products, arithmetic and copies ran while one was open for 3% of the time, Pallas kernels for 43%

profile of v9, /device:TPU:8, one launch (start us, length us, event | category | flops | bytes accessed | tf_op | source)
XLA Modules:
  0.0 734.5 jit_solution(4248280847261739502)
XLA Ops:
  7.2 0.8 reshape.124
  9.5 2.1 concatenate.9
  12.8 1.2 pad_add_fusion.buckets
  14.1 117.8 %gather_front.1 = (bf16[4,256,2048]{2,1,0:T(8,128)(2,1)}, bf16[8,256,1536]{2,1,0:T(8,128)(2,1)}, bf16[256,2048]{1,0:T(8,128)(2,1)}, bf16[8,4,16,128]{3,2,1,0:T(8...) custom-call(bf16[256,2048]{1,0:T(8,128)(2,1)} %own.3, ...), custom_call_target="tpu_custom_call" | custom-call | flops 80000000000 | bytes 209715200 | tf_op jit(solution)/shard_map/gather_front/pallas_call | solution.py:1836
  132.0 1.0 reshape.142
  140.2 95.9 %attention_forward.1 = (bf16[1024,512]{1,0:T(8,128)(2,1)}, bf16[1024,512]{1,0:T(8,128)(2,1)}, bf16[1024,512]{1,0:T(8,128)(2,1)}, bf16[4,1024,1024]{2,1,0:T(8,128...) custom-call(f32[1024,1536]{1,0:T(8,128)} %get-tuple-element.54.tripl, ...), custom_call_target="tpu_custom_call" | custom-call | flops 60000002048 | bytes 209715200 | tf_op jit(solution)/shard_map/attention_forward/pallas_call | solution.py:2049
  236.2 24.9 %all-gather.2.cloned.1.call-done.expand = bf16[2,688,2048]{2,1,0:T(8,128)(2,1)} async-done(((bf16[2,688,512]{2,1,0:T(8,128)(2,1)}), bf16[2,688,2048]{2,1,0:T(8,128)(2,1)}) %all-gather.2.cloned.1.call-update) | async-done | bytes 5636112 | tf_op jit(solution)/shard_map/all_gather | solution.py:2185
  261.1 102.8 %geglu_forward.1 = (bf16[688,2048]{1,0:T(8,128)(2,1)}, bf16[8,256,2048]{2,1,0:T(8,128)(2,1)}, bf16[8,256,768]{2,1,0:T(8,128)(2,1)}, bf16[8,256,768]{2,1,0:T(8,12...) custom-call(bf16[256,2048]{1,0:T(8,128)(2,1)} %get-tuple-element.61., ...), custom_call_target="tpu_custom_call" | custom-call | flops 19327352832 | bytes 209715200 | tf_op jit(solution)/shard_map/geglu_forward/pallas_call | solution.py:855
  363.9 116.8 %geglu_backward.1 = (f32[688,512]{1,0:T(8,128)}, bf16[2,688,2048]{2,1,0:T(8,128)(2,1)}, f32[256,2048]{1,0:T(8,128)}, f32[2,768]{1,0:T(2,128)}) custom-call(bf16[256,2048]{1,0:T(8,128)(2,1)} %get-tuple-element.66.own, bf16[2,688,2048]{2,1,0:T(8,128)(2,1)} %all-gather.2.cloned.1.call-done.expand, bf16[688,2048]{1,0:T(8,128)(2,1)} %get-tuple-element.67.reduce, ...), custom_call_target="tpu_custom_call" | custom-call | flops 38654705664 | bytes 209715200 | tf_op jit(solution)/shard_map/geglu_backward/pallas_call | solution.py:1100
  480.7 119.6 %attention_backward.1 = (bf16[1024,1536]{1,0:T(8,128)(2,1)}, f32[64,2048]{1,0:T(8,128)}, f32[1,1536]{1,0:T(1,128)}, f32[1,2048]{1,0:T(1,128)}, f32[256,2048]{1,0:T(8,128)}, /*index=5*/f32[2,2048]{1,0:T(2,128)}) custom-call(f32[256,2048]{1,0:T(8,128)} %get-tuple-element.65.upper_grad, f32[256,2048]{1,0:T(8,128)} %get-tuple-element.72.hidden_part, ...), custom_call_target="tpu_custom_call" | custom-call | flops 60000002048 | bytes 209715200 | tf_op jit(solution)/shard_map/attention_backward/pallas_call | solution.py:1328
  600.4 0.8 fusion.1
  602.9 1.4 reduce.33
  605.6 103.0 %input_backward.1 = (f32[256,2048]{1,0:T(8,128)}, f32[64,6144]{1,0:T(8,128)}, f32[16,128]{1,0:T(8,128)}) custom-call(bf16[1024,2048]{1,0:T(8,128)(2,1)} %bitcast.45, bf16[1024,1536]{1,0:T(8,128)(2,1)} %get-tuple-element.83.triple, bf16[2048,1536]{1,0:T(8,128)(2,1)} %bitcast.44, f32[8,4,16,128]{3,2,1,0:T(8,128)} %bitcast.29), custom_call_target="tpu_custom_call" | custom-call | flops 80000000000 | bytes 209715200 | tf_op jit(solution)/shard_map/input_backward/pallas_call | solution.py:1546
  709.3 1.3 slice.132
  710.6 1.2 slice.129
  711.9 1.3 slice.130
  713.8 0.8 slice_reduce_fusion.5
  715.8 3.2 multiply_add_fusion
  719.1 3.4 convert_bitcast_fusion
  722.5 1.0 copy.43
  723.4 0.8 copy-done.1
  724.2 1.1 copy.44
  725.4 0.8 copy.45
  726.2 1.1 copy.46
  (77 shorter events, 15.1 us)
Async XLA Ops:
  7.2 253.9 %all-gather.2.cloned.1.call-start = ((), (), s32[]{:S(2)}) async-start(), calls=%async_computation.1 | async-start | bytes 7045120 | tf_op jit(solution)/shard_map/all_gather | solution.py:2185
  131.9 587.1 %reduce-scatter.2.cloned.1.call-start = ((), (), s32[]{:S(2)}) async-start(), calls=%async_computation.2 | async-start | bytes 7045120 | tf_op jit(solution)/shard_map/reduce_scatter | solution.py:2222
  480.6 119.7 %copy-start.5 = (f32[3,2048]{1,0:T(4,128)S(1)}, f32[3,2048]{1,0:T(4,128)}, u32[]{:S(2)}) copy-start(f32[3,2048]{1,0:T(4,128)} %get-tuple-element.88) | copy-start | bytes 73732
  480.7 121.5 %copy-start.8 = (f32[4]{0:T(128)S(1)}, f32[4]{0:T(128)}, u32[]{:S(2)}) copy-start(f32[4]{0:T(128)} %compare_convert_fusion.1) | copy-start | bytes 52
  480.7 123.7 %copy-start.6 = (f32[2,768]{1,0:T(2,128)S(1)}, f32[2,768]{1,0:T(2,128)}, u32[]{:S(2)}) copy-start(f32[2,768]{1,0:T(2,128)} %get-tuple-element.89) | copy-start | bytes 18436
  480.7 123.9 %copy-start.7 = (f32[32]{0:T(128)S(1)}, f32[32]{0:T(128)}, u32[]{:S(2)}) copy-start(f32[32]{0:T(128)} %mul.58) | copy-start | bytes 388
  605.6 110.3 %copy-start = (f32[256,2048]{1,0:T(8,128)S(1)}, f32[256,2048]{1,0:T(8,128)}, u32[]{:S(2)}) copy-start(f32[256,2048]{1,0:T(8,128)} %get-tuple-element.81) | copy-start | bytes 6291460
  719.1 3.4 copy-start.3
  722.5 1.8 copy-start.1
  722.5 2.9 copy-start.4
  724.2 1.9 copy-start.2
Sparse Core Ops, SparseCore 0:
  132.1 128.9 all-gather.1
  480.8 143.6 reduce-scatter.1

commit v10 on v9

--- a/solution.py
+++ b/solution.py
@@ -50,23 +50,33 @@
     return values.astype(jnp.bfloat16)
 
 
+def small_rows(part):
+    return part.reshape(-1, part.shape[-1]).shape[0], -(-part.shape[-1] // 128)
+
+
 def pack_small(parts):
-    packed = jnp.concatenate([part.reshape(-1) for part in parts])
-    return jnp.pad(packed, (0, -packed.size % 2048)).reshape(-1, 128)
+    pieces = []
+    for part in parts:
+        first, rows = small_rows(part)
+        part = part.reshape(first, -1)
+        part = jnp.pad(part, ((0, 0), (0, rows * 128 - part.shape[1])))
+        pieces.append(part.reshape(first * rows, 128))
+    packed = jnp.concatenate(pieces, axis=0)
+    return jnp.pad(packed, ((0, -packed.shape[0] % 16), (0, 0)))
 
 
 def unpack_small(everyone, parts):
-    wide_count, narrow_count = everyone.shape[:2]
-    everyone = everyone.reshape(wide_count, narrow_count, -1).astype(jnp.float32)
     pieces = []
     start = 0
     for part in parts:
-        pieces.append(everyone[:, :, start : start + part.size])
-        start += part.size
+        first, rows = small_rows(part)
+        piece = everyone[:, :, start : start + first * rows].astype(jnp.float32)
+        piece = piece.reshape(piece.shape[:2] + (first, rows * 128))
+        pieces.append(piece[..., : part.shape[-1]])
+        start += first * rows
 
     def pairs(piece):
-        piece = piece.reshape(-1, 2, piece.shape[-1] // 2)
-        return piece.transpose(1, 0, 2).reshape(2, -1)
+        return piece.reshape((-1,) + piece.shape[-2:]).transpose(1, 0, 2).reshape(2, -1)
 
     own_expand = lax.dynamic_index_in_dim(
         pieces[4], lax.axis_index("wide"), 0, keepdims=False
@@ -303,26 +313,6 @@
         after_far()
         self.last_sums()
 
-    def run_gather(self, compute, between):
-        keep = self.send_own()
-        keep.wait()
-        self.receive_mate(0)
-        compute(chip_at(self.position, self.ring))
-        done = 1
-        for distance in range(1, self.far):
-            self.receive(distance)
-            between(done)
-            done += 1
-            for offset in (-distance, distance):
-                self.receive_mate(offset)
-                compute(chip_at(self.position + offset, self.ring))
-        self.receive(self.far)
-        between(done)
-        done += 1
-        self.receive_mate(self.far)
-        compute(chip_at(self.position + self.far, self.ring))
-        return done
-
     def start_sums(self, compute):
         compute(chip_at(self.position + self.far, self.ring))
         self.share(self.far)
@@ -652,7 +642,7 @@
 def geglu_forward_kernel(
     wide_count,
     narrow_count,
-    own,
+    rows_all,
     expand,
     reduce,
     shift,
@@ -662,7 +652,6 @@
     gain,
     norm_shift,
     reduce_out,
-    rows_all,
     active_out,
     slope_out,
     gelu_out,
@@ -672,9 +661,6 @@
     row_sums,
     feed,
     blocks,
-    gather_send,
-    gather_recv,
-    own_sem,
     parts,
     from_mate,
     incoming,
@@ -696,16 +682,16 @@
     late_sum_send,
     late_sum_recv,
 ):
-    sems = (gather_send, gather_recv, mate_send, mate_recv, sum_send, sum_recv, own_sem)
+    sems = (None, None, mate_send, mate_recv, sum_send, sum_recv, None)
     late_sems = (None, None, late_mate_send, late_mate_recv, late_sum_send, late_sum_recv, None)
     line = LineExchange(narrow_count)
     filled, cols = reduce.shape
-    width = own.shape[1]
+    width = rows_all.shape[2]
     upper = (2 * line.mine) // narrow_count
     late = pl.multiple_of((1 - upper) * (width - cols), cols)
     early = pl.multiple_of(upper * cols, cols)
     plane = PlaneExchange(
-        wide_count, own, blocks, parts, from_mate, incoming, sems, pl.ds(early, width - cols)
+        wide_count, None, None, parts, from_mate, incoming, sems, pl.ds(early, width - cols)
     )
     late_plane = PlaneExchange(
         wide_count, None, None, parts, from_mate, incoming, late_sems, pl.ds(late, cols)
@@ -713,7 +699,9 @@
     loads = [
         load_padded(expand.at[0], expand_mat.at[0], load_sems.at[0]),
         load_padded(expand.at[1], expand_mat.at[1], load_sems.at[1]),
+        pltpu.make_async_copy(rows_all, blocks, load_sems.at[4]),
     ]
+    loads[2].start()
 
     def reduce_cols(block):
         return reduce_mat.at[
@@ -757,7 +745,7 @@
 
         pair = pl.ds(2 * chip, 2)
         for index, (source, target) in enumerate(
-            ((active, active_out), (slope, slope_out), (gelu, gelu_out), (blocks, rows_all))
+            ((active, active_out), (slope, slope_out), (gelu, gelu_out))
         ):
             copy = pltpu.make_async_copy(
                 source.at[pair], target.at[pair], keep_sems.at[chip, index]
@@ -775,12 +763,17 @@
 
         return compute
 
-    def between(index):
-        if index < narrow_count:
-            line_reduce.step(index)
-
-    done = plane.run_gather(compute, between)
-    for step in range(done, narrow_count - 1):
+    offsets = [0]
+    for distance in range(1, plane.far):
+        offsets += [-distance, distance]
+    offsets.append(plane.far)
+    chips = [chip_at(plane.position + offset, plane.ring) for offset in offsets]
+    each = -(-len(chips) // (narrow_count - 2))
+    for step in range(1, narrow_count - 1):
+        if step == 1:
+            compute(chips.pop(0))
+        for _ in range(min(each, len(chips))):
+            compute(chips.pop(0))
         line_reduce.step(step)
     plane.start_sums(compute_sums(early, width - cols))
     line_reduce.step(narrow_count - 1)
@@ -813,7 +806,7 @@
         row_sums[2:3] += jnp.sum(total, axis=0, keepdims=True)
         return carry
 
-    lax.fori_loop(0, own.shape[0] // 16, norm_rows, 0)
+    lax.fori_loop(0, rows_all.shape[1] // 16, norm_rows, 0)
     plane.drain()
     late_plane.drain()
     keep_reduce.wait()
@@ -825,7 +818,7 @@
 def geglu_forward(
     wide_count,
     narrow_count,
-    hidden_low,
+    rows_all,
     expand,
     reduce_weight,
     shift,
@@ -835,20 +828,21 @@
     gain,
     norm_shift,
 ):
-    rows, width = hidden_low.shape
+    _, rows, width = rows_all.shape
     padded = shift.shape[1]
     anywhere = pl.BlockSpec(memory_space=pl.ANY)
     vmem = pl.BlockSpec(memory_space=pltpu.VMEM)
     kept = jax.ShapeDtypeStruct((wide_count, rows, padded), jnp.bfloat16)
     scratch = [pltpu.VMEM((rows, width), jnp.float32)]
-    scratch += exchange_scratch(wide_count, rows, width) + [
+    scratch.append(pltpu.VMEM((wide_count, rows, width), jnp.bfloat16))
+    scratch += sum_scratch(wide_count, rows, width) + [
         pltpu.VMEM((2, padded, width), jnp.bfloat16),
         pltpu.VMEM((padded, width), jnp.bfloat16),
         pltpu.VMEM((wide_count, rows, padded), jnp.bfloat16),
         pltpu.VMEM((wide_count, rows, padded), jnp.bfloat16),
         pltpu.VMEM((wide_count, rows, padded), jnp.bfloat16),
-        pltpu.SemaphoreType.DMA((4,)),
-        pltpu.SemaphoreType.DMA((wide_count // 2, 4)),
+        pltpu.SemaphoreType.DMA((5,)),
+        pltpu.SemaphoreType.DMA((wide_count // 2, 3)),
         pltpu.SemaphoreType.DMA((2, narrow_count)),
         pltpu.SemaphoreType.DMA((narrow_count,)),
     ] + sum_scratch(wide_count, rows, width)[3:]
@@ -856,7 +850,6 @@
         functools.partial(geglu_forward_kernel, wide_count, narrow_count),
         out_shape=(
             jax.ShapeDtypeStruct((reduce_weight.shape[0], width), jnp.bfloat16),
-            jax.ShapeDtypeStruct((wide_count, rows, width), jnp.bfloat16),
             kept,
             kept,
             kept,
@@ -866,7 +859,7 @@
             jax.ShapeDtypeStruct((3, width), jnp.float32),
         ),
         in_specs=[anywhere] * 3 + [vmem] * 6,
-        out_specs=(anywhere,) * 5 + (vmem,) * 4,
+        out_specs=(anywhere,) * 4 + (vmem,) * 4,
         scratch_shapes=scratch,
         compiler_params=pltpu.CompilerParams(
             collective_id=1, has_side_effects=True, vmem_limit_bytes=kernel_memory
@@ -876,7 +869,7 @@
         ),
         name="geglu_forward",
     )(
-        hidden_low,
+        rows_all,
         expand,
         reduce_weight,
         shift,
@@ -1385,6 +1378,7 @@
     triple,
     heads_mat,
     small,
+    sum_grad,
     input_part,
     heads_grad,
     small_out,
@@ -1518,6 +1512,13 @@
     small_out[...] = result
 
     line_sum.finish(input_part)
+
+    def add_residual(i, carry):
+        some = pl.ds(pl.multiple_of(i * 16, 16), 16)
+        input_part[some] += residual_scale * sum_grad[some]
+        return carry
+
+    lax.fori_loop(0, rows // 16, add_residual, 0)
     for offset in range(1, narrow_count):
         line.arrived(offset, heads_in, heads_send, heads_recv)
     own_cols = triple.shape[1] // 3
@@ -1534,7 +1535,9 @@
     plane.drain()
 
 
-def input_backward(wide_count, narrow_count, inputs, triple_grad, heads_mat, small):
+def input_backward(
+    wide_count, narrow_count, inputs, triple_grad, heads_mat, small, sum_grad
+):
     bucket, width = inputs.shape
     rows = bucket // narrow_count
     columns = triple_grad.shape[1]
@@ -1550,7 +1553,7 @@
             jax.ShapeDtypeStruct((count, narrow_count * columns), jnp.float32),
             jax.ShapeDtypeStruct((lines, 128), jnp.float32),
         ),
-        in_specs=[vmem] * 4,
+        in_specs=[vmem] * 5,
         out_specs=(vmem, vmem, vmem),
         scratch_shapes=[
             pltpu.VMEM((narrow_count, rows, width), jnp.bfloat16),
@@ -1577,7 +1580,7 @@
             flops=80 * 10**9, bytes_accessed=200 * 2**20, transcendentals=0
         ),
         name="input_backward",
-    )(inputs, triple_grad, heads_mat, small)
+    )(inputs, triple_grad, heads_mat, small, sum_grad)
 
 
 def greet_all(wide_count, narrow_count):
@@ -1703,13 +1706,13 @@
         copy.start()
         started.append(copy)
 
+    keep_rows.wait()
+    line_rows.send_own()
     for offset in range(1, narrow_count):
         for which in range(3):
             start(heads_copy(offset, which, line.peer(offset), here))
     for offset in range(1, narrow_count):
         start(small_copy(offset, line.peer(offset), here))
-    keep_rows.wait()
-    line_rows.send_own()
 
     halfway = narrow_count * rows // 2
     joined = buckets[0]
@@ -1737,6 +1740,7 @@
 
     lax.fori_loop(0, narrow_count, tables, 0)
 
+    line_rows.step(1)
     for copy in keeps:
         copy.wait()
     for offset in range(1, narrow_count):
@@ -1784,17 +1788,20 @@
         copy.start()
         outs.append(copy)
 
-    line_rows.step(1)
     for offset in range(1, narrow_count):
         start(merge_copy(offset, line.peer(offset), here))
     heads_ring.receive_mate(0)
-    for distance in range(1, heads_ring.far + 1):
+    for distance in range(1, heads_ring.far):
         gather(heads_ring, distance)
+    if last > 1:
+        line_rows.step(2)
+    gather(heads_ring, heads_ring.far)
     keep_out(heads_all, heads_out)
     project(here)
-    for step in range(2, narrow_count):
+    for step in range(3, narrow_count):
+        project_step(step - 2)
         line_rows.step(step)
-        project_step(step - 1)
+    project_step(last - 1)
     project_step(last)
     keep_merge.wait()
     for offset in range(1, narrow_count):
@@ -1890,6 +1897,7 @@
     normed,
     inv_std,
     merge_out,
+    rows_out,
     merge_mat,
     probs_held,
     values_turned,
@@ -1901,10 +1909,16 @@
     ring_send,
     ring_recv,
     own_sem,
+    rows_all,
+    rows_send,
+    rows_recv,
+    rows_sem,
 ):
     line = LineExchange(narrow_count)
     ring_sems = (ring_send, ring_recv, None, None, None, None, own_sem)
     ring = PlaneExchange(wide_count, merge, merge_mat, merge_mat, None, None, ring_sems)
+    rows_sems = (rows_send, rows_recv, None, None, None, None, rows_sem)
+    rows_ring = PlaneExchange(wide_count, hidden_low, rows_all, rows_all, None, None, rows_sems)
     bucket, own_cols = queries.shape
     rows, width = own.shape
     heads = own_cols // HDIM
@@ -1969,7 +1983,7 @@
             copy = mixed_copy(head, offset, line.peer(offset), line.mine)
             copy.start()
             started.append(copy)
-        if ring_steps:
+        if ring_steps and head >= heads - len(ring_steps):
             ring_steps.pop(0)()
     own_mixed = pltpu.make_async_copy(
         outbound.at[line.mine],
@@ -2009,12 +2023,22 @@
         return carry
 
     lax.fori_loop(0, rows // 16, norm_rows, 0)
+    keep_rows = rows_ring.send_own()
+    for step in range(1, rows_ring.far + 1):
+        rows_ring.receive(step)
+    for offset in range(rows_ring.ring):
+        rows_ring.receive_mate(offset)
+    keep_rows.wait()
+    keep_rows = pltpu.make_async_copy(rows_all, rows_out, rows_sem)
+    keep_rows.start()
     for head in range(max(heads - 2, 0), heads):
         keep(head).wait()
     for copy in started:
         copy.wait_send()
     ring.drain()
+    rows_ring.drain()
     keep_merge.wait()
+    keep_rows.wait()
 
 
 def attention_forward(
@@ -2059,9 +2083,10 @@
             wide_shape(rows, width),
             wide_shape(rows, 1),
             low_shape(wide_count, *merge_block.shape),
+            low_shape(wide_count, rows, width),
         ),
         in_specs=[vmem] * 7 + [anywhere] + [vmem] * 3,
-        out_specs=(vmem, vmem, vmem, anywhere) + (vmem,) * 5 + (anywhere,),
+        out_specs=(vmem, vmem, vmem, anywhere) + (vmem,) * 5 + (anywhere,) * 2,
         scratch_shapes=[
             pltpu.VMEM((wide_count, *merge_block.shape), jnp.bfloat16),
             pltpu.VMEM((2, bucket, bucket), jnp.bfloat16),
@@ -2071,6 +2096,10 @@
             dma((narrow_count - 1, heads)),
             dma((narrow_count, heads)),
             dma((4,)),
+            dma((3, wide_count, 2)),
+            dma((wide_count, 2)),
+            dma(()),
+            pltpu.VMEM((wide_count, rows, width), jnp.bfloat16),
             dma((3, wide_count, 2)),
             dma((wide_count, 2)),
             dma(()),
@@ -2162,6 +2191,7 @@
         normed_one,
         inv_one,
         merge_full,
+        rows_all,
     ) = attention_forward(
         wide_count,
         narrow_count,
@@ -2186,7 +2216,6 @@
     reduce_low = jnp.pad(reduce_weight, ((0, tile_rows), (0, 0)))
     (
         reduce_full,
-        rows_all,
         active,
         slope,
         gelu,
@@ -2197,7 +2226,7 @@
     ) = geglu_forward(
         wide_count,
         narrow_count,
-        hidden_low,
+        rows_all,
         expand_full,
         reduce_low,
         jnp.pad(expand_shift, ((0, 0), (0, padded - share))),
@@ -2271,15 +2300,15 @@
     pieces = (heads_sums, merge_sums, norm_sums, expand_sums, reduce_sums)
     packed = jnp.concatenate(pieces, axis=1)
     packed = jnp.pad(packed, ((0, 0), (0, -packed.shape[1] % 1024)))
-    input_part, heads_weight_gradient, summed = input_backward(
+    input_gradient, heads_weight_gradient, summed = input_backward(
         wide_count,
         narrow_count,
         rows_input,
         triple_grad,
         heads_mat,
         packed.reshape(wide_count, narrow_count, -1, 128),
+        sum_one_grad,
     )
-    input_gradient = residual_scale * sum_one_grad + input_part
     summed = summed.reshape(-1)
     ends = []
     start = 0

time: 743 us -> 715 us (0.962)
  waiting for transfers between devices: 24.9 us -> 0.06 us
    pallas_call x1, Pallas kernels: 95.9 us -> 124 us  [attention_forward(): pl.pallas_call(functools.partial(attention_forward_kernel, wide_count, na...]
    all_gather x1, waiting for transfers between devices: 24.9 us -> 0.02 us  [shards(): expand_full = lax.all_gather(expand_low, 'narrow', axis=2, tiled=True)]
    pallas_call x1, Pallas kernels: 117 us -> 106 us  [geglu_backward(): pl.pallas_call(functools.partial(geglu_backward_kernel, wide_count, narro...]
    pallas_call x1, Pallas kernels: 103 us -> 93.3 us  [geglu_forward(): pl.pallas_call(functools.partial(geglu_forward_kernel, wide_count, narrow...]
  transfers between devices with their start and end apart: 2 -> 2, of which waited for: 1 -> 0; matrix products, arithmetic and copies ran while one was open for 3% -> 3% of each run, Pallas kernels for 43% -> 49%
where the time goes in v10:
time: 715 us; the launch traced here: 711 us
  Pallas kernels  657 us (92%)
  local copies, waits for them, and re-layouts  28.6 us (4%)
  between operations  15.4 us (2%)
  other arithmetic  9.72 us (1%)
    pallas_call x1, Pallas kernels, attention_forward(): pl.pallas_call(functools.partial(attention_forward_kernel, wide_count, na...  124 us
    pallas_call x1, Pallas kernels, attention_backward(): pl.pallas_call(functools.partial(attention_backward_kernel, wide_count, n...  119 us
    pallas_call x1, Pallas kernels, gather_front(): pl.pallas_call(functools.partial(gather_kernel, wide_count, narrow_count)...  111 us
    pallas_call x1, Pallas kernels, geglu_backward(): pl.pallas_call(functools.partial(geglu_backward_kernel, wide_count, narro...  106 us
    pallas_call x1, Pallas kernels, input_backward(): pl.pallas_call(functools.partial(input_backward_kernel, wide_count, narro...  104 us
    pallas_call x1, Pallas kernels, geglu_forward(): pl.pallas_call(functools.partial(geglu_forward_kernel, wide_count, narrow...  93.3 us
  transfers between devices with their start and end apart: 2, of which 0 were waited for; matrix products, arithmetic and copies ran while one was open for 3% of the time, Pallas kernels for 49%

profile of v10, /device:TPU:8, one launch (start us, length us, event | category | flops | bytes accessed | tf_op | source)
XLA Modules:
  0.0 711.2 jit_solution(10393069271261262118)
XLA Ops:
  10.6 0.8 concatenate.9
  12.7 1.2 pad_add_fusion.buckets
  13.9 111.0 %gather_front.1 = (bf16[4,256,2048]{2,1,0:T(8,128)(2,1)}, bf16[8,256,1536]{2,1,0:T(8,128)(2,1)}, bf16[256,2048]{1,0:T(8,128)(2,1)}, bf16[8,4,16,128]{3,2,1,0:T(8...) custom-call(bf16[256,2048]{1,0:T(8,128)(2,1)} %own.3, ...), custom_call_target="tpu_custom_call" | custom-call | flops 80000000000 | bytes 209715200 | tf_op jit(solution)/shard_map/gather_front/pallas_call | solution.py:1843
  125.5 0.9 slice.112
  126.4 0.9 slice.121
  127.3 1.0 fusion
  129.8 0.9 convert_reduce_fusion
  135.3 1.3 slice_convert_fusion.1
  136.6 123.5 %attention_forward.1 = (bf16[1024,512]{1,0:T(8,128)(2,1)}, bf16[1024,512]{1,0:T(8,128)(2,1)}, bf16[1024,512]{1,0:T(8,128)(2,1)}, bf16[4,1024,1024]{2,1,0:T(8,128...) custom-call(f32[1024,1536]{1,0:T(8,128)} %get-tuple-element.53.tripl, ...), custom_call_target="tpu_custom_call" | custom-call | flops 60000002048 | bytes 209715200 | tf_op jit(solution)/shard_map/attention_forward/pallas_call | solution.py:2073
  260.1 93.3 %geglu_forward.1 = (bf16[688,2048]{1,0:T(8,128)(2,1)}, bf16[8,256,768]{2,1,0:T(8,128)(2,1)}, bf16[8,256,768]{2,1,0:T(8,128)(2,1)}, bf16[8,256,768]{2,1,0:T(8,128...) custom-call(bf16[8,256,2048]{2,1,0:T(8,128)(2,1)} %get-tuple-element.60, ...), custom_call_target="tpu_custom_call" | custom-call | flops 19327352832 | bytes 209715200 | tf_op jit(solution)/shard_map/geglu_forward/pallas_call | solution.py:849
  353.4 106.1 %geglu_backward.1 = (f32[688,512]{1,0:T(8,128)}, bf16[2,688,2048]{2,1,0:T(8,128)(2,1)}, f32[256,2048]{1,0:T(8,128)}, f32[2,768]{1,0:T(2,128)}) custom-call(bf16[256,2048]{1,0:T(8,128)(2,1)} %get-tuple-element.66.own, bf16[2,688,2048]{2,1,0:T(8,128)(2,1)} %all-gather.2.cloned.1.call-done.expand, bf16[688,2048]{1,0:T(8,128)(2,1)} %get-tuple-element.67.reduce, ...), custom_call_target="tpu_custom_call" | custom-call | flops 38654705664 | bytes 209715200 | tf_op jit(solution)/shard_map/geglu_backward/pallas_call | solution.py:1093
  459.6 119.4 %attention_backward.1 = (bf16[1024,1536]{1,0:T(8,128)(2,1)}, f32[64,2048]{1,0:T(8,128)}, f32[1,1536]{1,0:T(1,128)}, f32[1,2048]{1,0:T(1,128)}, f32[256,2048]{1,0:T(8,128)}, /*index=5*/f32[2,2048]{1,0:T(2,128)}) custom-call(f32[256,2048]{1,0:T(8,128)} %get-tuple-element.65.upper_grad, f32[256,2048]{1,0:T(8,128)} %get-tuple-element.71.hidden_part, ...), custom_call_target="tpu_custom_call" | custom-call | flops 60000002048 | bytes 209715200 | tf_op jit(solution)/shard_map/attention_backward/pallas_call | solution.py:1321
  579.0 0.8 fusion.3
  581.5 1.4 reduce.23
  584.2 103.5 %input_backward.1 = (f32[256,2048]{1,0:T(8,128)}, f32[64,6144]{1,0:T(8,128)}, f32[16,128]{1,0:T(8,128)}) custom-call(bf16[1024,2048]{1,0:T(8,128)(2,1)} %bitcast.63, bf16[1024,1536]{1,0:T(8,128)(2,1)} %get-tuple-element.80.triple, bf16[2048,1536]{1,0:T(8,128)(2,1)} %bitcast.62, f32[8,4,16,128]{3,2,1,0:T(8,128)} %bitcast.43, ...), custom_call_target="tpu_custom_call" | custom-call | flops 80000000000 | bytes 209715200 | tf_op jit(solution)/shard_map/input_backward/pallas_call | solution.py:1549
  688.6 1.3 slice.152
  689.9 1.2 slice.149
  691.2 1.3 slice.150
  695.1 3.5 convert_bitcast_fusion
  698.6 1.0 copy.51
  699.6 1.3 copy.52
  700.9 1.1 copy.53
  702.0 0.8 copy.54
  702.9 1.1 copy.55
  (83 shorter events, 17.2 us)
Async XLA Ops:
  7.2 253.0 %all-gather.2.cloned.1.call-start = ((), (), s32[]{:S(2)}) async-start(), calls=%async_computation.1 | async-start | bytes 7045120 | tf_op jit(solution)/shard_map/all_gather | solution.py:2215
  125.0 570.2 %reduce-scatter.2.cloned.1.call-start = ((), (), s32[]{:S(2)}) async-start(), calls=%async_computation.2 | async-start | bytes 7045120 | tf_op jit(solution)/shard_map/reduce_scatter | solution.py:2251
  459.6 119.4 %copy-start.5 = (f32[3,2048]{1,0:T(4,128)S(1)}, f32[3,2048]{1,0:T(4,128)}, u32[]{:S(2)}) copy-start(f32[3,2048]{1,0:T(4,128)} %get-tuple-element.85) | copy-start | bytes 73732
  459.6 121.3 %copy-start.8 = (f32[4]{0:T(128)S(1)}, f32[4]{0:T(128)}, u32[]{:S(2)}) copy-start(f32[4]{0:T(128)} %compare_convert_fusion.1) | copy-start | bytes 52
  459.6 123.4 %copy-start.6 = (f32[2,768]{1,0:T(2,128)S(1)}, f32[2,768]{1,0:T(2,128)}, u32[]{:S(2)}) copy-start(f32[2,768]{1,0:T(2,128)} %get-tuple-element.86) | copy-start | bytes 18436
  459.6 123.7 %copy-start.7 = (f32[32]{0:T(128)S(1)}, f32[32]{0:T(128)}, u32[]{:S(2)}) copy-start(f32[32]{0:T(128)} %mul.50) | copy-start | bytes 388
  687.8 10.8 %copy-start.3 = (bf16[256,2048]{1,0:T(8,128)(2,1)S(1)}, bf16[256,2048]{1,0:T(8,128)(2,1)}, u32[]{:S(2)}) copy-start(bf16[256,2048]{1,0:T(8,128)(2,1)} %get-tuple-element.121) | copy-start | bytes 3145732
  695.1 4.4 copy-start
  698.6 2.3 copy-start.1
  699.6 2.5 copy-start.4
  700.9 2.0 copy-start.2
Sparse Core Ops, SparseCore 0:
  125.1 131.2 all-gather.1
  459.7 143.8 reduce-scatter.1

commit v11 on v10

--- a/solution.py
+++ b/solution.py
@@ -1381,7 +1381,13 @@
     sum_grad,
     input_part,
     heads_grad,
-    small_out,
+    heads_bias_grad,
+    merge_bias_grad,
+    gains_grad,
+    shifts_grad,
+    expand_bias_grad,
+    reduce_bias_grad,
+    small_result,
     line_parts,
     line_in,
     heads_out,
@@ -1509,7 +1515,24 @@
     result = small_line[0]
     for index in range(1, narrow_count):
         result += small_line[index]
-    small_out[...] = result
+    small_result[...] = result
+    row = 0
+    for target in (
+        heads_bias_grad,
+        merge_bias_grad,
+        gains_grad,
+        shifts_grad,
+        expand_bias_grad,
+        reduce_bias_grad,
+    ):
+        first, size = target.shape
+        for index in range(first):
+            for start in range(0, size, 128):
+                stop = min(start + 128, size)
+                target[index : index + 1, start:stop] = small_result[
+                    row : row + 1, 0 : stop - start
+                ]
+                row += 1
 
     line_sum.finish(input_part)
 
@@ -1536,7 +1559,7 @@
 
 
 def input_backward(
-    wide_count, narrow_count, inputs, triple_grad, heads_mat, small, sum_grad
+    wide_count, narrow_count, inputs, triple_grad, heads_mat, small, sum_grad, small_shapes
 ):
     bucket, width = inputs.shape
     rows = bucket // narrow_count
@@ -1551,11 +1574,12 @@
         out_shape=(
             jax.ShapeDtypeStruct((rows, width), jnp.float32),
             jax.ShapeDtypeStruct((count, narrow_count * columns), jnp.float32),
-            jax.ShapeDtypeStruct((lines, 128), jnp.float32),
-        ),
+        )
+        + tuple(jax.ShapeDtypeStruct(shape, jnp.float32) for shape in small_shapes),
         in_specs=[vmem] * 5,
-        out_specs=(vmem, vmem, vmem),
+        out_specs=(vmem,) * 8,
         scratch_shapes=[
+            pltpu.VMEM((lines, 128), jnp.float32),
             pltpu.VMEM((narrow_count, rows, width), jnp.bfloat16),
             pltpu.VMEM((2, narrow_count - 1, rows, width), jnp.bfloat16),
             pltpu.VMEM((block, columns), jnp.bfloat16),
@@ -1616,6 +1640,7 @@
     first_query,
     last_query,
     rows_all,
+    triple_all,
     heads_all,
     merge_own,
     small_all,
@@ -1633,6 +1658,7 @@
     out_sems,
     heads_ring_send,
     heads_ring_recv,
+    block_sems,
 ):
     ring_sems = (heads_ring_send, heads_ring_recv, None, None, None, None, None)
     heads_ring = PlaneExchange(wide_count, None, heads_all, heads_all, None, None, ring_sems)
@@ -1763,14 +1789,21 @@
     for offset in range(1, wide_count):
         start(wide_copy(offset, place))
 
+    def leave_rows(block):
+        return pltpu.make_async_copy(rows_all.at[block], rows_out.at[block], block_sems.at[0, block])
+
+    def leave_triple(block):
+        return pltpu.make_async_copy(triple_all.at[block], triple.at[block], block_sems.at[1, block])
+
     def project(block):
+        leave_rows(block).start()
+
         def cols_step(cols):
             weight = heads_all[:, :, cols].reshape(width, cols.size)
-            triple[pl.ds(pl.multiple_of(block * rows, rows), rows), cols] = dot(
-                rows_all[block], weight, ((1,), (0,))
-            )
+            triple_all[block, :, cols] = dot(rows_all[block], weight, ((1,), (0,)))
 
         tiles(columns, 256, cols_step)
+        leave_triple(block).start()
 
     def project_step(step):
         line_rows.each(step, project)
@@ -1798,16 +1831,15 @@
     gather(heads_ring, heads_ring.far)
     keep_out(heads_all, heads_out)
     project(here)
+    project_step(1)
     for step in range(3, narrow_count):
-        project_step(step - 2)
+        project_step(step - 1)
         line_rows.step(step)
-    project_step(last - 1)
     project_step(last)
     keep_merge.wait()
     for offset in range(1, narrow_count):
         merge_copy(offset, line.peer(offset), line.peer(offset)).wait_recv()
     keep_out(merge_own, merge_out)
-    keep_out(rows_all, rows_out)
     for offset in range(1, wide_count):
         wide_copy(offset, (place + offset) % wide_count).wait_recv()
     keep_out(small_all, small_out)
@@ -1817,6 +1849,13 @@
     heads_ring.drain()
     for copy in outs:
         copy.wait()
+
+    def left(block, carry):
+        leave_rows(block).wait()
+        leave_triple(block).wait()
+        return carry
+
+    lax.fori_loop(0, narrow_count, left, 0)
 
 
 def gather_front(
@@ -1843,10 +1882,20 @@
     return pl.pallas_call(
         functools.partial(gather_kernel, wide_count, narrow_count),
         out_shape=tuple(jax.ShapeDtypeStruct(shape, jnp.bfloat16) for shape in shapes)
-        + (jax.ShapeDtypeStruct((bucket, columns), jnp.float32), table, table, reach, reach),
+        + (
+            jax.ShapeDtypeStruct((narrow_count, rows, columns), jnp.float32),
+            table,
+            table,
+            reach,
+            reach,
+        ),
         in_specs=[anywhere, anywhere, anywhere, vmem, pl.BlockSpec(memory_space=pltpu.SMEM), vmem],
-        out_specs=(anywhere,) * 4 + (vmem,) * 5,
-        scratch_shapes=[pltpu.VMEM(shape, jnp.bfloat16) for shape in shapes]
+        out_specs=(anywhere,) * 5 + (vmem,) * 4,
+        scratch_shapes=[
+            pltpu.VMEM(shapes[0], jnp.bfloat16),
+            pltpu.VMEM((narrow_count, rows, columns), jnp.float32),
+        ]
+        + [pltpu.VMEM(shape, jnp.bfloat16) for shape in shapes[1:]]
         + [
             dma((2, narrow_count)),
             dma((narrow_count,)),
@@ -1862,6 +1911,7 @@
             dma((4,)),
             dma((3, wide_count, 2)),
             dma((wide_count, 2)),
+            dma((2, narrow_count)),
         ],
         compiler_params=pltpu.CompilerParams(
             collective_id=5, has_side_effects=True, vmem_limit_bytes=kernel_memory
@@ -2174,9 +2224,8 @@
     )
     rows_input = rows_input.reshape(bucket_len, model_width)
     heads_mat = heads_mat.reshape(model_width, 3 * own_cols)
-    heads_shift, merge_shift, gains, shifts, expand_shift, reduce_shift = unpack_small(
-        small_all, smalls
-    )
+    triple = triple.reshape(bucket_len, 3 * own_cols)
+    heads_shift, merge_shift, gains, shifts = unpack_small(small_all, smalls)[:4]
     own_shift = lax.dynamic_index_in_dim(
         heads_shift.reshape(3, narrow_count, own_cols), narrow_index, 1, keepdims=False
     ).reshape(1, -1)
@@ -2208,6 +2257,8 @@
         shifts[0].reshape(1, -1),
     )
 
+    small_late, hidden = lax.optimization_barrier((small_all, hidden))
+    late_gains, late_shifts, expand_shift, reduce_shift = unpack_small(small_late, smalls)[2:]
     tile_rows = -share % 16
     padded = -(-share // 256) * 256
     expand_low = jnp.pad(expand_weight.transpose(1, 2, 0), ((0, 0), (0, tile_rows), (0, 0)))
@@ -2233,8 +2284,8 @@
         hidden,
         cotangent,
         reduce_shift.reshape(1, -1),
-        gains[1].reshape(1, -1),
-        shifts[1].reshape(1, -1),
+        late_gains[1].reshape(1, -1),
+        late_shifts[1].reshape(1, -1),
     )
     reduce_weight_gradient, expand_part, hidden_part, unit_sums = geglu_backward(
         wide_count,
@@ -2266,7 +2317,7 @@
         hidden_part,
         normed_one,
         inv_one,
-        gains[0].reshape(1, -1),
+        late_gains[0].reshape(1, -1),
         merge_full.reshape(model_width, model_width),
         mixed,
         queries,
@@ -2279,28 +2330,32 @@
 
     mine_narrow = (jnp.arange(narrow_count) == narrow_index).astype(jnp.float32)
     mine_wide = (jnp.arange(wide_count) == lax.axis_index("wide")).astype(jnp.float32)
-    heads_sums = heads_sums.reshape(3, 1, own_cols)
-    heads_sums = (heads_sums * mine_narrow[None, :, None]).reshape(count, -1)
-    merge_sums = merge_sums.reshape(count, -1)
-    norm_sums = (
-        jnp.stack([norm_one_sums[0], row_sums[0], norm_one_sums[1], row_sums[1]])
-        .reshape(4, count, -1)
-        .transpose(1, 0, 2)
-        .reshape(count, -1)
-    )
-    expand_sums = unit_sums[:, :share]
-    expand_sums = (
-        expand_sums.reshape(2, narrow_count, -1).transpose(1, 0, 2).reshape(1, narrow_count, -1)
-        * mine_wide[:, None, None]
-    ).reshape(count, -1)
-    reduce_sums = row_sums[2].reshape(1, narrow_count, -1)
+    heads_sums = (heads_sums.reshape(3, 1, own_cols) * mine_narrow[None, :, None]).reshape(count, 1, -1)
+    norm_sums = jnp.stack([norm_one_sums[0], row_sums[0], norm_one_sums[1], row_sums[1]])
+    norm_sums = norm_sums.reshape(4, count, -1).transpose(1, 0, 2)
+    expand_sums = unit_sums[:, :share].reshape(2, narrow_count, -1).transpose(1, 0, 2)[None]
+    expand_sums = (expand_sums * mine_wide[:, None, None, None]).reshape(count, 2, -1)
+    reduce_sums = row_sums[2].reshape(1, narrow_count, 1, -1)
     reduce_sums = jnp.broadcast_to(
-        reduce_sums, (wide_count, narrow_count, reduce_sums.shape[2])
-    ).reshape(count, -1)
-    pieces = (heads_sums, merge_sums, norm_sums, expand_sums, reduce_sums)
-    packed = jnp.concatenate(pieces, axis=1)
-    packed = jnp.pad(packed, ((0, 0), (0, -packed.shape[1] % 1024)))
-    input_gradient, heads_weight_gradient, summed = input_backward(
+        reduce_sums, (wide_count, narrow_count, 1, reduce_sums.shape[3])
+    ).reshape(count, 1, -1)
+    pieces = (heads_sums, merge_sums.reshape(count, 1, -1), norm_sums, expand_sums, reduce_sums)
+    packed = []
+    for piece in pieces:
+        piece = jnp.pad(piece, ((0, 0), (0, 0), (0, -piece.shape[2] % 128)))
+        packed.append(piece.reshape(count, -1, 128))
+    packed = jnp.concatenate(packed, axis=1)
+    packed = jnp.pad(packed, ((0, 0), (0, -packed.shape[1] % 8), (0, 0)))
+    (
+        input_gradient,
+        heads_weight_gradient,
+        heads_bias_gradient,
+        merge_bias_gradient,
+        gains_gradient,
+        shifts_gradient,
+        expand_bias_gradient,
+        reduce_bias_gradient,
+    ) = input_backward(
         wide_count,
         narrow_count,
         rows_input,
@@ -2308,27 +2363,28 @@
         heads_mat,
         packed.reshape(wide_count, narrow_count, -1, 128),
         sum_one_grad,
+        (
+            (1, heads_bias.size),
+            (1, merge_bias.size),
+            norm_gains.shape,
+            norm_shifts.shape,
+            expand_bias.shape,
+            (1, reduce_bias.size),
+        ),
     )
-    summed = summed.reshape(-1)
-    ends = []
-    start = 0
-    for piece in pieces:
-        ends.append(summed[start : start + piece.shape[1]])
-        start += piece.shape[1]
-    norm_ends = ends[2].reshape(4, -1)
     return (
         layer_output,
         input_gradient,
         heads_weight_gradient,
-        ends[0],
+        heads_bias_gradient[0],
         merge_weight_gradient,
-        ends[1],
-        norm_ends[:2],
-        norm_ends[2:],
+        merge_bias_gradient[0],
+        gains_gradient,
+        shifts_gradient,
         expand_weight_gradient,
-        ends[3].reshape(2, -1),
+        expand_bias_gradient,
         reduce_weight_gradient[:share],
-        ends[4],
+        reduce_bias_gradient[0],
     )
 
 

time: 715 us -> 707 us (0.989)
  transfers between devices with their start and end apart: 2 -> 2, of which waited for: 0 -> 0; matrix products, arithmetic and copies ran while one was open for 3% -> 2% of each run, Pallas kernels for 49% -> 49%
where the time goes in v11:
time: 707 us; the launch traced here: 703 us
  Pallas kernels  654 us (93%)
  local copies, waits for them, and re-layouts  24.6 us (3%)
  between operations  15.5 us (2%)
  other arithmetic  8.54 us (1%)
    pallas_call x1, Pallas kernels, attention_forward(): pl.pallas_call(functools.partial(attention_forward_kernel, wide_count, na...  122 us
    pallas_call x1, Pallas kernels, attention_backward(): pl.pallas_call(functools.partial(attention_backward_kernel, wide_count, n...  119 us
    pallas_call x1, Pallas kernels, gather_front(): pl.pallas_call(functools.partial(gather_kernel, wide_count, narrow_count)...  109 us
    pallas_call x1, Pallas kernels, geglu_backward(): pl.pallas_call(functools.partial(geglu_backward_kernel, wide_count, narro...  105 us
    pallas_call x1, Pallas kernels, input_backward(): pl.pallas_call(functools.partial(input_backward_kernel, wide_count, narro...  104 us
    pallas_call x1, Pallas kernels, geglu_forward(): pl.pallas_call(functools.partial(geglu_forward_kernel, wide_count, narrow...  93.7 us
  transfers between devices with their start and end apart: 2, of which 0 were waited for; matrix products, arithmetic and copies ran while one was open for 2% of the time, Pallas kernels for 49%

profile of v11, /device:TPU:8, one launch (start us, length us, event | category | flops | bytes accessed | tf_op | source)
XLA Modules:
  0.0 703.0 jit_solution(17731980938637864702)
XLA Ops:
  10.5 0.7 pad.51
  11.2 0.8 concatenate.9
  12.7 1.2 pad_add_fusion.buckets
  13.9 109.1 %gather_front.1 = (bf16[4,256,2048]{2,1,0:T(8,128)(2,1)}, bf16[8,256,1536]{2,1,0:T(8,128)(2,1)}, bf16[256,2048]{1,0:T(8,128)(2,1)}, bf16[8,4,16,128]{3,2,1,0:T(8...) custom-call(bf16[256,2048]{1,0:T(8,128)(2,1)} %own.3, ...), custom_call_target="tpu_custom_call" | custom-call | flops 80000000000 | bytes 209715200 | tf_op jit(solution)/shard_map/gather_front/pallas_call | solution.py:1882
  123.5 0.9 slice.110
  125.1 0.9 convert_reduce_fusion
  126.0 0.7 reshape.183.merge_shift
  126.8 1.0 fusion.1
  128.5 0.7 reshape.184.gain
  129.7 122.4 %attention_forward.1 = (bf16[1024,512]{1,0:T(8,128)(2,1)}, bf16[1024,512]{1,0:T(8,128)(2,1)}, bf16[1024,512]{1,0:T(8,128)(2,1)}, bf16[4,1024,1024]{2,1,0:T(8,128...) custom-call(f32[1024,1536]{1,0:T(8,128)} %bitcast.78, ...), custom_call_target="tpu_custom_call" | custom-call | flops 60000002048 | bytes 209715200 | tf_op jit(solution)/shard_map/attention_forward/pallas_call | solution.py:2123
  255.7 93.7 %geglu_forward.1 = (bf16[688,2048]{1,0:T(8,128)(2,1)}, bf16[8,256,768]{2,1,0:T(8,128)(2,1)}, bf16[8,256,768]{2,1,0:T(8,128)(2,1)}, bf16[8,256,768]{2,1,0:T(8,128...) custom-call(bf16[8,256,2048]{2,1,0:T(8,128)(2,1)} %get-tuple-element.67, ...), custom_call_target="tpu_custom_call" | custom-call | flops 19327352832 | bytes 209715200 | tf_op jit(solution)/shard_map/geglu_forward/pallas_call | solution.py:849
  349.4 105.5 %geglu_backward.1 = (f32[688,512]{1,0:T(8,128)}, bf16[2,688,2048]{2,1,0:T(8,128)(2,1)}, f32[256,2048]{1,0:T(8,128)}, f32[2,768]{1,0:T(2,128)}) custom-call(bf16[256,2048]{1,0:T(8,128)(2,1)} %get-tuple-element.75.own, bf16[2,688,2048]{2,1,0:T(8,128)(2,1)} %all-gather.2.cloned.1.call-done.expand, bf16[688,2048]{1,0:T(8,128)(2,1)} %get-tuple-element.76.reduce, ...), custom_call_target="tpu_custom_call" | custom-call | flops 38654705664 | bytes 209715200 | tf_op jit(solution)/shard_map/geglu_backward/pallas_call | solution.py:1093
  454.9 119.5 %attention_backward.1 = (bf16[1024,1536]{1,0:T(8,128)(2,1)}, f32[64,2048]{1,0:T(8,128)}, f32[1,1536]{1,0:T(1,128)}, f32[1,2048]{1,0:T(1,128)}, f32[256,2048]{1,0:T(8,128)}, /*index=5*/f32[2,2048]{1,0:T(2,128)}) custom-call(f32[256,2048]{1,0:T(8,128)} %get-tuple-element.74.upper_grad, f32[256,2048]{1,0:T(8,128)} %get-tuple-element.80.hidden_part, ...), custom_call_target="tpu_custom_call" | custom-call | flops 60000002048 | bytes 209715200 | tf_op jit(solution)/shard_map/attention_backward/pallas_call | solution.py:1321
  575.0 1.4 reduce.15
  576.4 0.7 reduce.3
  577.4 0.8 fusion.3
  579.1 0.7 pad.58
  579.9 103.6 %input_backward.1 = (f32[256,2048]{1,0:T(8,128)}, f32[64,6144]{1,0:T(8,128)}, f32[1,192]{1,0:T(1,128)}, f32[1,64]{1,0:T(1,128)}, f32[2,64]{1,0:T(2,128)}, /*inde...) custom-call(bf16[1024,2048]{1,0:T(8,128)(2,1)} %bitcast.79, bf16[1024,1536]{1,0:T(8,128)(2,1)} %get-tuple-element.89.triple, ...), custom_call_target="tpu_custom_call" | custom-call | flops 80000000000 | bytes 209715200 | tf_op jit(solution)/shard_map/input_backward/pallas_call | solution.py:1572
  683.5 3.5 convert_bitcast_fusion
  687.0 1.0 copy.67
  688.0 1.3 copy.68
  689.3 1.1 copy.69
  691.1 0.8 copy.71
  694.1 1.1 copy.76
  (100 shorter events, 14.6 us)
Async XLA Ops:
  7.2 248.5 %all-gather.2.cloned.1.call-start = ((), (), s32[]{:S(2)}) async-start(), calls=%async_computation.1 | async-start | bytes 7045120 | tf_op jit(solution)/shard_map/all_gather | solution.py:2266
  123.0 560.5 %reduce-scatter.2.cloned.1.call-start = ((), (), s32[]{:S(2)}) async-start(), calls=%async_computation.2 | async-start | bytes 7045120 | tf_op jit(solution)/shard_map/reduce_scatter | solution.py:2302
  129.7 122.4 %copy-start.5 = (bf16[8,4,16,128]{3,2,1,0:T(8,128)(2,1)S(1)}, bf16[8,4,16,128]{3,2,1,0:T(8,128)(2,1)}, u32[]{:S(2)}) copy-start(bf16[8,4,16,128]{3,2,1,0:T(8,128)(2,1)} %get-tuple-element.70) | copy-start | bytes 393220
  454.9 119.5 %copy-start.7 = (f32[2,768]{1,0:T(2,128)S(1)}, f32[2,768]{1,0:T(2,128)}, u32[]{:S(2)}) copy-start(f32[2,768]{1,0:T(2,128)} %get-tuple-element.95) | copy-start | bytes 18436
  454.9 122.5 %copy-start.6 = (f32[3,2048]{1,0:T(4,128)S(1)}, f32[3,2048]{1,0:T(4,128)}, u32[]{:S(2)}) copy-start(f32[3,2048]{1,0:T(4,128)} %get-tuple-element.94) | copy-start | bytes 73732
  454.9 123.6 %copy-start.8 = (f32[32]{0:T(128)S(1)}, f32[32]{0:T(128)}, u32[]{:S(2)}) copy-start(f32[32]{0:T(128)} %mul.53) | copy-start | bytes 388
  683.5 3.5 copy-start.3
  683.5 4.5 copy-start
  687.0 2.3 copy-start.1
  688.0 2.5 copy-start.13
  688.0 3.1 copy-start.4
  689.3 2.5 copy-start.14
  689.3 3.1 copy-start.12
  689.3 3.6 copy-start.11
  689.3 4.2 copy-start.10
  689.3 4.8 copy-start.2
  689.3 5.8 copy-start.9
Sparse Core Ops, SparseCore 0:
  123.1 127.7 all-gather.1
  455.0 144.4 reduce-scatter.1

commit v12 on v11

--- a/solution.py
+++ b/solution.py
@@ -50,45 +50,33 @@
     return values.astype(jnp.bfloat16)
 
 
-def small_rows(part):
-    return part.reshape(-1, part.shape[-1]).shape[0], -(-part.shape[-1] // 128)
-
-
-def pack_small(parts):
+def row_places(shapes):
+    places = []
+    start = 0
+    for first, size in shapes:
+        places.append((start, first, size))
+        start += first * -(-size // 128)
+    return places, start + -start % 8
+
+
+def small_piece(block, place, index):
+    start, _, size = place
+    rows = -(-size // 128)
     pieces = []
-    for part in parts:
-        first, rows = small_rows(part)
-        part = part.reshape(first, -1)
-        part = jnp.pad(part, ((0, 0), (0, rows * 128 - part.shape[1])))
-        pieces.append(part.reshape(first * rows, 128))
-    packed = jnp.concatenate(pieces, axis=0)
-    return jnp.pad(packed, ((0, -packed.shape[0] % 16), (0, 0)))
-
-
-def unpack_small(everyone, parts):
-    pieces = []
-    start = 0
-    for part in parts:
-        first, rows = small_rows(part)
-        piece = everyone[:, :, start : start + first * rows].astype(jnp.float32)
-        piece = piece.reshape(piece.shape[:2] + (first, rows * 128))
-        pieces.append(piece[..., : part.shape[-1]])
-        start += first * rows
-
-    def pairs(piece):
-        return piece.reshape((-1,) + piece.shape[-2:]).transpose(1, 0, 2).reshape(2, -1)
-
-    own_expand = lax.dynamic_index_in_dim(
-        pieces[4], lax.axis_index("wide"), 0, keepdims=False
-    )
-    return (
-        pieces[0].reshape(-1),
-        pieces[1].reshape(-1),
-        pairs(pieces[2]),
-        pairs(pieces[3]),
-        pairs(own_expand),
-        pieces[5][0].reshape(-1),
-    )
+    for row in range(rows):
+        stop = min(size - 128 * row, 128)
+        here = start + index * rows + row
+        pieces.append(block[here : here + 1, 0:stop])
+    return pieces
+
+
+def spread_small(target, small, place, index, row=0):
+    at = 0
+    for wide in range(small.shape[0]):
+        for narrow in range(small.shape[1]):
+            for piece in small_piece(small.at[wide, narrow], place, index):
+                target[row : row + 1, at : at + piece.shape[1]] = piece
+                at += piece.shape[1]
 
 
 def ring_place(wide_count):
@@ -642,15 +630,13 @@
 def geglu_forward_kernel(
     wide_count,
     narrow_count,
+    places,
     rows_all,
     expand,
     reduce,
-    shift,
+    small,
     hidden,
     cotangent,
-    reduce_shift,
-    gain,
-    norm_shift,
     reduce_out,
     active_out,
     slope_out,
@@ -681,6 +667,8 @@
     late_mate_recv,
     late_sum_send,
     late_sum_recv,
+    shift,
+    vectors,
 ):
     sems = (None, None, mate_send, mate_recv, sum_send, sum_recv, None)
     late_sems = (None, None, late_mate_send, late_mate_recv, late_sum_send, late_sum_recv, None)
@@ -717,6 +705,21 @@
         )
     greet_plane(plane)
     line.greet(3)
+    place = lax.axis_index("wide")
+    shift[...] = jnp.zeros_like(shift)
+    for index in range(2):
+        at = 0
+        for block in range(narrow_count):
+            for piece in small_piece(small.at[place, block], places[4], index):
+                shift[index : index + 1, at : at + piece.shape[1]] = piece
+                at += piece.shape[1]
+    at = 0
+    for block in range(narrow_count):
+        for piece in small_piece(small.at[0, block], places[5], 0):
+            vectors[0:1, at : at + piece.shape[1]] = piece
+            at += piece.shape[1]
+    spread_small(vectors, small, places[2], 1, 1)
+    spread_small(vectors, small, places[3], 1, 2)
     own_reduce.wait()
     line_reduce.send_own()
     kept = []
@@ -792,13 +795,13 @@
     def norm_rows(i, carry):
         some = pl.ds(pl.multiple_of(i * 16, 16), 16)
         result, normed, inverse = normalize(
-            residual_scale * hidden[some] + feed[some] + reduce_shift[...],
-            gain[...],
-            norm_shift[...],
+            residual_scale * hidden[some] + feed[some] + vectors[0:1],
+            vectors[1:2],
+            vectors[2:3],
         )
         layer_output[some] = result.astype(jnp.bfloat16)
         upstream = cotangent[some].astype(jnp.float32)
-        total = normalize_back(upstream, normed, inverse, gain[...])
+        total = normalize_back(upstream, normed, inverse, vectors[1:2])
         sum_grad[some] = total
         feed_grad[some] = total.astype(jnp.bfloat16)
         row_sums[0:1] += jnp.sum(upstream * normed, axis=0, keepdims=True)
@@ -806,7 +809,7 @@
         row_sums[2:3] += jnp.sum(total, axis=0, keepdims=True)
         return carry
 
-    lax.fori_loop(0, rows_all.shape[1] // 16, norm_rows, 0)
+    lax.fori_loop(0, rows_all.shape[1] // 16, norm_rows, 0, unroll=2)
     plane.drain()
     late_plane.drain()
     keep_reduce.wait()
@@ -818,18 +821,16 @@
 def geglu_forward(
     wide_count,
     narrow_count,
+    places,
     rows_all,
     expand,
     reduce_weight,
-    shift,
+    small,
     hidden,
     cotangent,
-    reduce_shift,
-    gain,
-    norm_shift,
 ):
     _, rows, width = rows_all.shape
-    padded = shift.shape[1]
+    padded = -(-expand.shape[1] // 256) * 256
     anywhere = pl.BlockSpec(memory_space=pl.ANY)
     vmem = pl.BlockSpec(memory_space=pltpu.VMEM)
     kept = jax.ShapeDtypeStruct((wide_count, rows, padded), jnp.bfloat16)
@@ -846,8 +847,9 @@
         pltpu.SemaphoreType.DMA((2, narrow_count)),
         pltpu.SemaphoreType.DMA((narrow_count,)),
     ] + sum_scratch(wide_count, rows, width)[3:]
+    scratch += [pltpu.VMEM((2, padded), jnp.float32), pltpu.VMEM((3, width), jnp.float32)]
     return pl.pallas_call(
-        functools.partial(geglu_forward_kernel, wide_count, narrow_count),
+        functools.partial(geglu_forward_kernel, wide_count, narrow_count, places),
         out_shape=(
             jax.ShapeDtypeStruct((reduce_weight.shape[0], width), jnp.bfloat16),
             kept,
@@ -858,7 +860,7 @@
             jax.ShapeDtypeStruct((rows, width), jnp.bfloat16),
             jax.ShapeDtypeStruct((3, width), jnp.float32),
         ),
-        in_specs=[anywhere] * 3 + [vmem] * 6,
+        in_specs=[anywhere] * 3 + [vmem] * 3,
         out_specs=(anywhere,) * 4 + (vmem,) * 4,
         scratch_shapes=scratch,
         compiler_params=pltpu.CompilerParams(
@@ -872,12 +874,9 @@
         rows_all,
         expand,
         reduce_weight,
-        shift,
+        small,
         hidden,
         cotangent,
-        reduce_shift,
-        gain,
-        norm_shift,
     )
 
 
@@ -1120,11 +1119,12 @@
 def attention_backward_kernel(
     wide_count,
     narrow_count,
+    places,
     upper_grad,
     hidden_part,
     normed,
     inv_std,
-    gain,
+    small,
     merge,
     mixed,
     queries,
@@ -1139,6 +1139,7 @@
     merge_sums,
     sum_grad,
     norm_sums,
+    gain,
     attended,
     upstream,
     outbound,
@@ -1177,6 +1178,7 @@
     load(0).start()
     greet_plane(plane)
 
+    spread_small(gain, small, places[2], 0)
     norm_sums[...] = jnp.zeros_like(norm_sums)
     merge_sums[...] = jnp.zeros_like(merge_sums)
 
@@ -1191,7 +1193,7 @@
         attended[some] = total.astype(jnp.bfloat16)
         return carry
 
-    lax.fori_loop(0, rows // 16, norm_rows, 0)
+    lax.fori_loop(0, rows // 16, norm_rows, 0, unroll=2)
     line.greet(3)
 
     def mixed_part(target, where):
@@ -1297,11 +1299,12 @@
 def attention_backward(
     wide_count,
     narrow_count,
+    places,
     upper_grad,
     hidden_part,
     normed,
     inv_std,
-    gain,
+    small,
     merge_full,
     mixed,
     queries,
@@ -1319,7 +1322,7 @@
     vmem = pl.BlockSpec(memory_space=pltpu.VMEM)
     dma = pltpu.SemaphoreType.DMA
     return pl.pallas_call(
-        functools.partial(attention_backward_kernel, wide_count, narrow_count),
+        functools.partial(attention_backward_kernel, wide_count, narrow_count, places),
         out_shape=(
             jax.ShapeDtypeStruct((bucket, 3 * own_cols), jnp.bfloat16),
             jax.ShapeDtypeStruct((count, width), jnp.float32),
@@ -1331,6 +1334,7 @@
         in_specs=[vmem] * 10 + [anywhere] + [vmem] * 2,
         out_specs=(vmem,) * 6,
         scratch_shapes=[
+            pltpu.VMEM((1, width), jnp.float32),
             pltpu.VMEM((rows, width), jnp.bfloat16),
             pltpu.VMEM((narrow_count, rows, own_cols), jnp.bfloat16),
             pltpu.VMEM((narrow_count - 1, rows, own_cols), jnp.bfloat16),
@@ -1359,7 +1363,7 @@
         hidden_part,
         normed,
         inv_std,
-        gain,
+        small,
         merge_full,
         mixed,
         queries,
@@ -1627,8 +1631,14 @@
     own,
     heads_weight,
     merge_weight,
-    small,
-    buckets,
+    heads_bias,
+    merge_bias,
+    norm_gains,
+    norm_shifts,
+    expand_bias,
+    reduce_bias,
+    joined_ref,
+    prefix_ref,
     speeds,
     rows_out,
     heads_out,
@@ -1639,6 +1649,7 @@
     signed_sine,
     first_query,
     last_query,
+    small,
     rows_all,
     triple_all,
     heads_all,
@@ -1696,6 +1707,18 @@
     )
     for copy in keeps + [keep_merge]:
         copy.start()
+    smalls = (heads_bias, merge_bias, norm_gains, norm_shifts, expand_bias, reduce_bias)
+    small[...] = jnp.zeros_like(small)
+    row = 0
+    for part in smalls:
+        first, size = part.shape
+        for index in range(first):
+            for begin in range(0, size, 128):
+                stop = min(begin + 128, size)
+                small[row : row + 1, 0 : stop - begin] = part[
+                    index : index + 1, begin:stop
+                ].astype(jnp.float32)
+                row += 1
     small_all[place, here] = small[...]
     greet_all(wide_count, narrow_count)
 
@@ -1741,7 +1764,7 @@
         start(small_copy(offset, line.peer(offset), here))
 
     halfway = narrow_count * rows // 2
-    joined = buckets[0]
+    joined = joined_ref[0]
 
     def tables(i, carry):
         some = pl.ds(pl.multiple_of(i * rows, rows), rows)
@@ -1750,8 +1773,8 @@
         local = place_in - second * halfway
         reach = jnp.where(
             joined == 1,
-            buckets[1] + buckets[2],
-            jnp.where(second == 1, buckets[2], buckets[1]),
+            prefix_ref[0, 0] + prefix_ref[0, 1],
+            jnp.where(second == 1, prefix_ref[0, 1], prefix_ref[0, 0]),
         )
         first_query[some] = jnp.where(local < reach, place_in - local, place_in)
         last_query[some] = jnp.where(
@@ -1859,7 +1882,7 @@
 
 
 def gather_front(
-    wide_count, narrow_count, layer_input, heads_weight, merge_weight, small, buckets, speeds
+    wide_count, narrow_count, layer_input, heads_weight, merge_weight, smalls, joined, prefix, speeds
 ):
     rows, width = layer_input.shape
     count, all_columns = heads_weight.shape
@@ -1868,7 +1891,7 @@
     anywhere = pl.BlockSpec(memory_space=pl.ANY)
     vmem = pl.BlockSpec(memory_space=pltpu.VMEM)
     dma = pltpu.SemaphoreType.DMA
-    lines = small.shape[0]
+    lines = row_places([part.shape for part in smalls])[1]
     shapes = (
         (narrow_count, rows, width),
         (wide_count, block, columns),
@@ -1881,21 +1904,24 @@
     reach = jax.ShapeDtypeStruct((bucket, 1), jnp.int32)
     return pl.pallas_call(
         functools.partial(gather_kernel, wide_count, narrow_count),
-        out_shape=tuple(jax.ShapeDtypeStruct(shape, jnp.bfloat16) for shape in shapes)
+        out_shape=tuple(jax.ShapeDtypeStruct(shape, jnp.bfloat16) for shape in shapes[:3])
         + (
+            jax.ShapeDtypeStruct(shapes[3], jnp.float32),
             jax.ShapeDtypeStruct((narrow_count, rows, columns), jnp.float32),
             table,
             table,
             reach,
             reach,
         ),
-        in_specs=[anywhere, anywhere, anywhere, vmem, pl.BlockSpec(memory_space=pltpu.SMEM), vmem],
+        in_specs=[anywhere] * 3 + [vmem] * 6 + [pl.BlockSpec(memory_space=pltpu.SMEM)] * 2 + [vmem],
         out_specs=(anywhere,) * 5 + (vmem,) * 4,
         scratch_shapes=[
+            pltpu.VMEM((lines, 128), jnp.float32),
             pltpu.VMEM(shapes[0], jnp.bfloat16),
             pltpu.VMEM((narrow_count, rows, columns), jnp.float32),
         ]
-        + [pltpu.VMEM(shape, jnp.bfloat16) for shape in shapes[1:]]
+        + [pltpu.VMEM(shape, jnp.bfloat16) for shape in shapes[1:3]]
+        + [pltpu.VMEM(shapes[3], jnp.float32)]
         + [
             dma((2, narrow_count)),
             dma((narrow_count,)),
@@ -1920,23 +1946,21 @@
             flops=80 * 10**9, bytes_accessed=200 * 2**20, transcendentals=0
         ),
         name="gather_front",
-    )(layer_input, heads_weight, merge_weight, small, buckets, speeds)
+    )(layer_input, heads_weight, merge_weight, *smalls, joined, prefix, speeds)
 
 
 def attention_forward_kernel(
     wide_count,
     narrow_count,
+    places,
     triple,
-    heads_shift,
+    small,
     cosine,
     signed_sine,
     first_query,
     last_query,
     own,
     merge,
-    merge_shift,
-    gain,
-    shift,
     queries,
     keys,
     values,
@@ -1963,6 +1987,8 @@
     rows_send,
     rows_recv,
     rows_sem,
+    heads_full,
+    vectors,
 ):
     line = LineExchange(narrow_count)
     ring_sems = (ring_send, ring_recv, None, None, None, None, own_sem)
@@ -1976,6 +2002,10 @@
     greet_plane(ring)
     line.greet(3)
     keep_own = ring.send_own()
+    spread_small(heads_full, small, places[0], 0)
+    spread_small(vectors, small, places[1], 0, 0)
+    spread_small(vectors, small, places[2], 0, 1)
+    spread_small(vectors, small, places[3], 0, 2)
     ring_steps = [functools.partial(ring.receive, step) for step in range(1, ring.far + 1)]
 
     def keep(head):
@@ -2001,7 +2031,9 @@
             here = pl.ds(pl.multiple_of(i * rows, rows), rows)
             for which, target in enumerate((queries, keys, values)):
                 wanted = pl.ds(which * own_cols + head * HDIM, HDIM)
-                part = triple[here, wanted] + heads_shift[:, wanted]
+                begin = (which * narrow_count + line.mine) * own_cols + head * HDIM
+                bias = heads_full[:, pl.ds(pl.multiple_of(begin, HDIM), HDIM)]
+                part = triple[here, wanted] + bias
                 if which < 2:
                     part = rotate_lanes(part, cosine[here], -signed_sine[here])
                 else:
@@ -2058,21 +2090,21 @@
         hidden[:, cols] = (
             residual_scale * own[:, cols].astype(jnp.float32)
             + dot(mixed[...], merge_mat[:, :, cols].reshape(width, cols.size), ((1,), (0,)))
-            + merge_shift[:, cols]
+            + vectors[0:1, cols]
         )
 
     tiles(width, 256, merge_cols)
 
     def norm_rows(i, carry):
         some = pl.ds(pl.multiple_of(i * 16, 16), 16)
-        result, centred, inverse = normalize(hidden[some], gain[...], shift[...])
+        result, centred, inverse = normalize(hidden[some], vectors[1:2], vectors[2:3])
         hidden[some] = result
         hidden_low[some] = result.astype(jnp.bfloat16)
         normed[some] = centred
         inv_std[some] = inverse
         return carry
 
-    lax.fori_loop(0, rows // 16, norm_rows, 0)
+    lax.fori_loop(0, rows // 16, norm_rows, 0, unroll=2)
     keep_rows = rows_ring.send_own()
     for step in range(1, rows_ring.far + 1):
         rows_ring.receive(step)
@@ -2094,17 +2126,15 @@
 def attention_forward(
     wide_count,
     narrow_count,
+    places,
     triple,
-    heads_shift,
+    small,
     cosine,
     signed_sine,
     first_query,
     last_query,
     layer_input,
     merge_block,
-    merge_shift,
-    gain,
-    shift,
 ):
     bucket, columns = triple.shape
     rows, width = layer_input.shape
@@ -2121,7 +2151,7 @@
         return jax.ShapeDtypeStruct(shape, jnp.float32)
 
     return pl.pallas_call(
-        functools.partial(attention_forward_kernel, wide_count, narrow_count),
+        functools.partial(attention_forward_kernel, wide_count, narrow_count, places),
         out_shape=(
             low_shape(bucket, own_cols),
             low_shape(bucket, own_cols),
@@ -2135,7 +2165,7 @@
             low_shape(wide_count, *merge_block.shape),
             low_shape(wide_count, rows, width),
         ),
-        in_specs=[vmem] * 7 + [anywhere] + [vmem] * 3,
+        in_specs=[vmem] * 7 + [anywhere],
         out_specs=(vmem, vmem, vmem, anywhere) + (vmem,) * 5 + (anywhere,) * 2,
         scratch_shapes=[
             pltpu.VMEM((wide_count, *merge_block.shape), jnp.bfloat16),
@@ -2153,6 +2183,8 @@
             dma((3, wide_count, 2)),
             dma((wide_count, 2)),
             dma(()),
+            pltpu.VMEM((1, 3 * width), jnp.float32),
+            pltpu.VMEM((3, width), jnp.float32),
         ],
         compiler_params=pltpu.CompilerParams(
             collective_id=6, has_side_effects=True, vmem_limit_bytes=kernel_memory
@@ -2163,16 +2195,13 @@
         name="attention_forward",
     )(
         triple,
-        heads_shift,
+        small,
         cosine,
         signed_sine,
         first_query,
         last_query,
         layer_input,
         merge_block,
-        merge_shift,
-        gain,
-        shift,
     )
 
 
@@ -2201,7 +2230,15 @@
     own_cols = own_heads * HDIM
     share = expand_weight.shape[2]
     narrow_index = lax.axis_index("narrow")
-    smalls = (heads_bias, merge_bias, norm_gains, norm_shifts, expand_bias, reduce_bias)
+    smalls = (
+        heads_bias.reshape(1, -1),
+        merge_bias.reshape(1, -1),
+        norm_gains,
+        norm_shifts,
+        expand_bias,
+        reduce_bias.reshape(1, -1),
+    )
+    places = row_places([part.shape for part in smalls])[0]
     (
         rows_input,
         heads_mat,
@@ -2218,17 +2255,14 @@
         layer_input,
         heads_weight,
         merge_weight,
-        pack_small(smalls),
-        jnp.concatenate([joined, prefix[0]]),
+        smalls,
+        joined,
+        prefix,
         jnp.asarray(rotary_speeds(HDIM)),
     )
     rows_input = rows_input.reshape(bucket_len, model_width)
     heads_mat = heads_mat.reshape(model_width, 3 * own_cols)
     triple = triple.reshape(bucket_len, 3 * own_cols)
-    heads_shift, merge_shift, gains, shifts = unpack_small(small_all, smalls)[:4]
-    own_shift = lax.dynamic_index_in_dim(
-        heads_shift.reshape(3, narrow_count, own_cols), narrow_index, 1, keepdims=False
-    ).reshape(1, -1)
     (
         queries,
         keys,
@@ -2244,21 +2278,17 @@
     ) = attention_forward(
         wide_count,
         narrow_count,
+        places,
         triple,
-        own_shift,
+        small_all,
         cosine,
         signed_sine,
         first_query,
         last_query,
         layer_input,
         merge_block,
-        merge_shift.reshape(1, -1),
-        gains[0].reshape(1, -1),
-        shifts[0].reshape(1, -1),
     )
 
-    small_late, hidden = lax.optimization_barrier((small_all, hidden))
-    late_gains, late_shifts, expand_shift, reduce_shift = unpack_small(small_late, smalls)[2:]
     tile_rows = -share % 16
     padded = -(-share // 256) * 256
     expand_low = jnp.pad(expand_weight.transpose(1, 2, 0), ((0, 0), (0, tile_rows), (0, 0)))
@@ -2277,15 +2307,13 @@
     ) = geglu_forward(
         wide_count,
         narrow_count,
+        places,
         rows_all,
         expand_full,
         reduce_low,
-        jnp.pad(expand_shift, ((0, 0), (0, padded - share))),
+        small_all,
         hidden,
         cotangent,
-        reduce_shift.reshape(1, -1),
-        late_gains[1].reshape(1, -1),
-        late_shifts[1].reshape(1, -1),
     )
     reduce_weight_gradient, expand_part, hidden_part, unit_sums = geglu_backward(
         wide_count,
@@ -2313,11 +2341,12 @@
     ) = attention_backward(
         wide_count,
         narrow_count,
+        places,
         sum_two_grad,
         hidden_part,
         normed_one,
         inv_one,
-        late_gains[0].reshape(1, -1),
+        small_all,
         merge_full.reshape(model_width, model_width),
         mixed,
         queries,

time: 707 us -> 699 us (0.989)
  local copies, waits for them, and re-layouts: 24.6 us -> 14.9 us
  transfers between devices with their start and end apart: 2 -> 2, of which waited for: 0 -> 1; matrix products, arithmetic and copies ran while one was open for 2% -> 1% of each run, Pallas kernels for 49% -> 50%
where the time goes in v12:
time: 699 us; the launch traced here: 696 us
  Pallas kernels  655 us (94%)
  between operations  15.4 us (2%)
  local copies, waits for them, and re-layouts  14.9 us (2%)
    pallas_call x1, Pallas kernels, attention_forward(): pl.pallas_call(functools.partial(attention_forward_kernel, wide_count, na...  122 us
    pallas_call x1, Pallas kernels, attention_backward(): pl.pallas_call(functools.partial(attention_backward_kernel, wide_count, n...  120 us
    pallas_call x1, Pallas kernels, gather_front(): pl.pallas_call(functools.partial(gather_kernel, wide_count, narrow_count)...  109 us
    pallas_call x1, Pallas kernels, geglu_backward(): pl.pallas_call(functools.partial(geglu_backward_kernel, wide_count, narro...  108 us
    pallas_call x1, Pallas kernels, input_backward(): pl.pallas_call(functools.partial(input_backward_kernel, wide_count, narro...  104 us
    pallas_call x1, Pallas kernels, geglu_forward(): pl.pallas_call(functools.partial(geglu_forward_kernel, wide_count, narrow...  91.8 us
  transfers between devices with their start and end apart: 2, of which 1 were waited for; matrix products, arithmetic and copies ran while one was open for 1% of the time, Pallas kernels for 50%

profile of v12, /device:TPU:8, one launch (start us, length us, event | category | flops | bytes accessed | tf_op | source)
XLA Modules:
  0.0 695.8 jit_solution(11891010253782593741)
XLA Ops:
  7.2 1.3 reshape.107.reduce_bias
  8.5 1.2 reshape.105.heads_bias
  10.4 109.5 %gather_front.1 = (bf16[4,256,2048]{2,1,0:T(8,128)(2,1)}, bf16[8,256,1536]{2,1,0:T(8,128)(2,1)}, bf16[256,2048]{1,0:T(8,128)(2,1)}, f32[8,4,16,128]{3,2,1,0:T(8,...) custom-call(bf16[256,2048]{1,0:T(8,128)(2,1)} %own.3, ...), custom_call_target="tpu_custom_call" | custom-call | flops 80000000000 | bytes 209715200 | tf_op jit(solution)/shard_map/gather_front/pallas_call | solution.py:1905
  120.5 0.6 mul.53
  121.6 122.3 %attention_forward.1 = (bf16[1024,512]{1,0:T(8,128)(2,1)}, bf16[1024,512]{1,0:T(8,128)(2,1)}, bf16[1024,512]{1,0:T(8,128)(2,1)}, bf16[4,1024,1024]{2,1,0:T(8,128...) custom-call(f32[1024,1536]{1,0:T(8,128)} %bitcast.33, ...), custom_call_target="tpu_custom_call" | custom-call | flops 60000002048 | bytes 209715200 | tf_op jit(solution)/shard_map/attention_forward/pallas_call | solution.py:2153
  243.9 3.9 all-gather.2.cloned.1.call-done.expand
  247.8 91.8 %geglu_forward.1 = (bf16[688,2048]{1,0:T(8,128)(2,1)}, bf16[8,256,768]{2,1,0:T(8,128)(2,1)}, bf16[8,256,768]{2,1,0:T(8,128)(2,1)}, bf16[8,256,768]{2,1,0:T(8,128...) custom-call(bf16[8,256,2048]{2,1,0:T(8,128)(2,1)} %get-tuple-element.65, ...), custom_call_target="tpu_custom_call" | custom-call | flops 19327352832 | bytes 209715200 | tf_op jit(solution)/shard_map/geglu_forward/pallas_call | solution.py:851
  339.6 107.7 %geglu_backward.1 = (f32[688,512]{1,0:T(8,128)}, bf16[2,688,2048]{2,1,0:T(8,128)(2,1)}, f32[256,2048]{1,0:T(8,128)}, f32[2,768]{1,0:T(2,128)}) custom-call(bf16[256,2048]{1,0:T(8,128)(2,1)} %get-tuple-element.71.own, bf16[2,688,2048]{2,1,0:T(8,128)(2,1)} %all-gather.2.cloned.1.call-done.expand, bf16[688,2048]{1,0:T(8,128)(2,1)} %get-tuple-element.72.reduce, ...), custom_call_target="tpu_custom_call" | custom-call | flops 38654705664 | bytes 209715200 | tf_op jit(solution)/shard_map/geglu_backward/pallas_call | solution.py:1092
  447.3 119.7 %attention_backward.1 = (bf16[1024,1536]{1,0:T(8,128)(2,1)}, f32[64,2048]{1,0:T(8,128)}, f32[1,1536]{1,0:T(1,128)}, f32[1,2048]{1,0:T(1,128)}, f32[256,2048]{1,0:T(8,128)}, /*index=5*/f32[2,2048]{1,0:T(2,128)}) custom-call(f32[256,2048]{1,0:T(8,128)} %get-tuple-element.70.upper_grad, f32[256,2048]{1,0:T(8,128)} %get-tuple-element.76.hidden_part, ...), custom_call_target="tpu_custom_call" | custom-call | flops 60000002048 | bytes 209715200 | tf_op jit(solution)/shard_map/attention_backward/pallas_call | solution.py:1324
  567.1 0.8 fusion
  568.1 0.7 reduce.1
  569.6 1.4 reduce.9
  571.8 0.7 pad.24
  572.5 103.7 %input_backward.1 = (f32[256,2048]{1,0:T(8,128)}, f32[64,6144]{1,0:T(8,128)}, f32[1,192]{1,0:T(1,128)}, f32[1,64]{1,0:T(1,128)}, f32[2,64]{1,0:T(2,128)}, /*inde...) custom-call(bf16[1024,2048]{1,0:T(8,128)(2,1)} %bitcast.34, bf16[1024,1536]{1,0:T(8,128)(2,1)} %get-tuple-element.85.triple, ...), custom_call_target="tpu_custom_call" | custom-call | flops 80000000000 | bytes 209715200 | tf_op jit(solution)/shard_map/input_backward/pallas_call | solution.py:1576
  676.3 3.5 convert_bitcast_fusion
  679.8 1.0 copy.47
  680.7 1.3 copy.48
  682.1 1.1 copy.49
  683.3 0.6 copy.50
  683.8 0.8 copy.51
  685.1 0.6 copy.53
  686.3 0.6 copy.55
  686.8 1.1 copy.56
  687.9 0.6 copy.57
  (62 shorter events, 4.1 us)
Async XLA Ops:
  7.2 240.6 %all-gather.2.cloned.1.call-start = ((), (), s32[]{:S(2)}) async-start(), calls=%async_computation.1 | async-start | bytes 7045120 | tf_op jit(solution)/shard_map/all_gather | solution.py:2296
  119.9 556.4 %reduce-scatter.2.cloned.1.call-start = ((), (), s32[]{:S(2)}) async-start(), calls=%async_computation.2 | async-start | bytes 7045120 | tf_op jit(solution)/shard_map/reduce_scatter | solution.py:2330
  447.3 119.8 %copy-start.5 = (f32[3,2048]{1,0:T(4,128)S(1)}, f32[3,2048]{1,0:T(4,128)}, u32[]{:S(2)}) copy-start(f32[3,2048]{1,0:T(4,128)} %get-tuple-element.90) | copy-start | bytes 73732
  447.3 121.5 %copy-start.13 = (f32[4]{0:T(128)S(1)}, f32[4]{0:T(128)}, u32[]{:S(2)}) copy-start(f32[4]{0:T(128)} %compare_convert_fusion.1) | copy-start | bytes 52
  447.3 123.7 %copy-start.6 = (f32[2,768]{1,0:T(2,128)S(1)}, f32[2,768]{1,0:T(2,128)}, u32[]{:S(2)}) copy-start(f32[2,768]{1,0:T(2,128)} %get-tuple-element.91) | copy-start | bytes 18436
  447.3 123.8 %copy-start.7 = (f32[32]{0:T(128)S(1)}, f32[32]{0:T(128)}, u32[]{:S(2)}) copy-start(f32[32]{0:T(128)} %mul.53) | copy-start | bytes 388
  676.3 3.5 copy-start.3
  676.3 4.5 copy-start
  679.8 2.3 copy-start.1
  680.7 2.5 copy-start.12
  680.7 3.1 copy-start.4
  682.1 2.5 copy-start.14
  682.1 3.1 copy-start.11
  682.1 3.6 copy-start.10
  682.1 4.2 copy-start.9
  682.1 4.8 copy-start.2
  682.1 5.8 copy-start.8
Sparse Core Ops, SparseCore 0:
  120.0 127.7 all-gather.1
  447.4 143.7 reduce-scatter.1

commit v13 on v12

--- a/solution.py
+++ b/solution.py
@@ -663,6 +663,10 @@
     keep_sems,
     reduce_send,
     reduce_recv,
+    next_mate_send,
+    next_mate_recv,
+    next_sum_send,
+    next_sum_recv,
     late_mate_send,
     late_mate_recv,
     late_sum_send,
@@ -670,20 +674,35 @@
     shift,
     vectors,
 ):
-    sems = (None, None, mate_send, mate_recv, sum_send, sum_recv, None)
-    late_sems = (None, None, late_mate_send, late_mate_recv, late_sum_send, late_sum_recv, None)
     line = LineExchange(narrow_count)
     filled, cols = reduce.shape
     width = rows_all.shape[2]
     upper = (2 * line.mine) // narrow_count
-    late = pl.multiple_of((1 - upper) * (width - cols), cols)
-    early = pl.multiple_of(upper * cols, cols)
-    plane = PlaneExchange(
-        wide_count, None, None, parts, from_mate, incoming, sems, pl.ds(early, width - cols)
+    half = narrow_count // 2
+    windows = (
+        (half * upper, half, half - 1),
+        (half - upper * (half - 1), half - 1, narrow_count - 2),
+        ((narrow_count - 1) * (1 - upper), 1, narrow_count - 1),
     )
-    late_plane = PlaneExchange(
-        wide_count, None, None, parts, from_mate, incoming, late_sems, pl.ds(late, cols)
+    sems = (
+        (mate_send, mate_recv, sum_send, sum_recv),
+        (next_mate_send, next_mate_recv, next_sum_send, next_sum_recv),
+        (late_mate_send, late_mate_recv, late_sum_send, late_sum_recv),
     )
+    planes = [
+        PlaneExchange(
+            wide_count,
+            None,
+            None,
+            parts,
+            from_mate,
+            incoming,
+            (None, None, *own_sems, None),
+            pl.ds(pl.multiple_of(first * cols, cols), blocks_in * cols),
+        )
+        for (first, blocks_in, _), own_sems in zip(windows, sems)
+    ]
+    plane = planes[0]
     loads = [
         load_padded(expand.at[0], expand_mat.at[0], load_sems.at[0]),
         load_padded(expand.at[1], expand_mat.at[1], load_sems.at[1]),
@@ -771,24 +790,26 @@
         offsets += [-distance, distance]
     offsets.append(plane.far)
     chips = [chip_at(plane.position + offset, plane.ring) for offset in offsets]
-    each = -(-len(chips) // (narrow_count - 2))
-    for step in range(1, narrow_count - 1):
-        if step == 1:
-            compute(chips.pop(0))
-        for _ in range(min(each, len(chips))):
-            compute(chips.pop(0))
-        line_reduce.step(step)
-    plane.start_sums(compute_sums(early, width - cols))
-    line_reduce.step(narrow_count - 1)
+    for index, chip in enumerate(chips):
+        if index == len(chips) - 1:
+            line_reduce.step(1)
+        compute(chip)
+    step = 1
+    for window, (first, blocks_in, needed) in enumerate(windows):
+        while step < needed:
+            step += 1
+            line_reduce.step(step)
+        start = pl.multiple_of(first * cols, cols)
+        planes[window].start_sums(compute_sums(start, blocks_in * cols))
+        if window > 0:
+            planes[window - 1].last_sums()
+    planes[-1].last_sums()
     keep_reduce = pltpu.make_async_copy(
         reduce_mat.at[pl.ds(0, filled)], reduce_out, load_sems.at[3]
     )
     keep_reduce.start()
-    late_plane.start_sums(compute_sums(late, cols))
-    plane.last_sums()
-    late_plane.last_sums()
-    plane.finish(feed)
-    late_plane.finish(feed)
+    for part in planes:
+        part.finish(feed)
 
     row_sums[...] = jnp.zeros_like(row_sums)
 
@@ -810,8 +831,8 @@
         return carry
 
     lax.fori_loop(0, rows_all.shape[1] // 16, norm_rows, 0, unroll=2)
-    plane.drain()
-    late_plane.drain()
+    for part in planes:
+        part.drain()
     keep_reduce.wait()
     line_reduce.drain()
     for copy in kept:
@@ -846,7 +867,7 @@
         pltpu.SemaphoreType.DMA((wide_count // 2, 3)),
         pltpu.SemaphoreType.DMA((2, narrow_count)),
         pltpu.SemaphoreType.DMA((narrow_count,)),
-    ] + sum_scratch(wide_count, rows, width)[3:]
+    ] + 2 * sum_scratch(wide_count, rows, width)[3:]
     scratch += [pltpu.VMEM((2, padded), jnp.float32), pltpu.VMEM((3, width), jnp.float32)]
     return pl.pallas_call(
         functools.partial(geglu_forward_kernel, wide_count, narrow_count, places),

time: 699 us -> 689 us (0.986)
  Pallas kernels: 655 us -> 644 us
    pallas_call x1, Pallas kernels: 91.8 us -> 79.9 us  [geglu_forward(): pl.pallas_call(functools.partial(geglu_forward_kernel, wide_count, narrow...]
where the time goes in v13:
time: 689 us; the launch traced here: 685 us
  Pallas kernels  644 us (93%)
  between operations  15.2 us (2%)
  local copies, waits for them, and re-layouts  14.9 us (2%)
    pallas_call x1, Pallas kernels, attention_forward(): pl.pallas_call(functools.partial(attention_forward_kernel, wide_count, na...  122 us
    pallas_call x1, Pallas kernels, attention_backward(): pl.pallas_call(functools.partial(attention_backward_kernel, wide_count, n...  119 us
    pallas_call x1, Pallas kernels, geglu_backward(): pl.pallas_call(functools.partial(geglu_backward_kernel, wide_count, narro...  110 us
    pallas_call x1, Pallas kernels, gather_front(): pl.pallas_call(functools.partial(gather_kernel, wide_count, narrow_count)...  109 us
    pallas_call x1, Pallas kernels, input_backward(): pl.pallas_call(functools.partial(input_backward_kernel, wide_count, narro...  103 us
    pallas_call x1, Pallas kernels, geglu_forward(): pl.pallas_call(functools.partial(geglu_forward_kernel, wide_count, narrow...  79.9 us
  transfers between devices with their start and end apart: 2, of which 1 were waited for; matrix products, arithmetic and copies ran while one was open for 1% of the time, Pallas kernels for 50%

profile of v13, /device:TPU:8, one launch (start us, length us, event | category | flops | bytes accessed | tf_op | source)
XLA Modules:
  0.0 684.9 jit_solution(5597255361547155542)
XLA Ops:
  7.2 1.3 reshape.107.reduce_bias
  8.5 1.2 reshape.105.heads_bias
  10.4 109.5 %gather_front.1 = (bf16[4,256,2048]{2,1,0:T(8,128)(2,1)}, bf16[8,256,1536]{2,1,0:T(8,128)(2,1)}, bf16[256,2048]{1,0:T(8,128)(2,1)}, f32[8,4,16,128]{3,2,1,0:T(8,...) custom-call(bf16[256,2048]{1,0:T(8,128)(2,1)} %own.3, ...), custom_call_target="tpu_custom_call" | custom-call | flops 80000000000 | bytes 209715200 | tf_op jit(solution)/shard_map/gather_front/pallas_call | solution.py:1926
  120.5 0.6 mul.53
  121.6 122.3 %attention_forward.1 = (bf16[1024,512]{1,0:T(8,128)(2,1)}, bf16[1024,512]{1,0:T(8,128)(2,1)}, bf16[1024,512]{1,0:T(8,128)(2,1)}, bf16[4,1024,1024]{2,1,0:T(8,128...) custom-call(f32[1024,1536]{1,0:T(8,128)} %bitcast.33, ...), custom_call_target="tpu_custom_call" | custom-call | flops 60000002048 | bytes 209715200 | tf_op jit(solution)/shard_map/attention_forward/pallas_call | solution.py:2174
  243.9 3.9 all-gather.2.cloned.1.call-done.expand
  247.8 79.9 %geglu_forward.1 = (bf16[688,2048]{1,0:T(8,128)(2,1)}, bf16[8,256,768]{2,1,0:T(8,128)(2,1)}, bf16[8,256,768]{2,1,0:T(8,128)(2,1)}, bf16[8,256,768]{2,1,0:T(8,128...) custom-call(bf16[8,256,2048]{2,1,0:T(8,128)(2,1)} %get-tuple-element.65, ...), custom_call_target="tpu_custom_call" | custom-call | flops 19327352832 | bytes 209715200 | tf_op jit(solution)/shard_map/geglu_forward/pallas_call | solution.py:872
  327.7 109.7 %geglu_backward.1 = (f32[688,512]{1,0:T(8,128)}, bf16[2,688,2048]{2,1,0:T(8,128)(2,1)}, f32[256,2048]{1,0:T(8,128)}, f32[2,768]{1,0:T(2,128)}) custom-call(bf16[256,2048]{1,0:T(8,128)(2,1)} %get-tuple-element.71.own, bf16[2,688,2048]{2,1,0:T(8,128)(2,1)} %all-gather.2.cloned.1.call-done.expand, bf16[688,2048]{1,0:T(8,128)(2,1)} %get-tuple-element.72.reduce, ...), custom_call_target="tpu_custom_call" | custom-call | flops 38654705664 | bytes 209715200 | tf_op jit(solution)/shard_map/geglu_backward/pallas_call | solution.py:1113
  437.4 119.4 %attention_backward.1 = (bf16[1024,1536]{1,0:T(8,128)(2,1)}, f32[64,2048]{1,0:T(8,128)}, f32[1,1536]{1,0:T(1,128)}, f32[1,2048]{1,0:T(1,128)}, f32[256,2048]{1,0:T(8,128)}, /*index=5*/f32[2,2048]{1,0:T(2,128)}) custom-call(f32[256,2048]{1,0:T(8,128)} %get-tuple-element.70.upper_grad, f32[256,2048]{1,0:T(8,128)} %get-tuple-element.76.hidden_part, ...), custom_call_target="tpu_custom_call" | custom-call | flops 60000002048 | bytes 209715200 | tf_op jit(solution)/shard_map/attention_backward/pallas_call | solution.py:1345
  556.9 0.8 fusion
  557.9 0.7 reduce.1
  559.4 1.4 reduce.9
  561.6 0.7 pad.24
  562.3 103.3 %input_backward.1 = (f32[256,2048]{1,0:T(8,128)}, f32[64,6144]{1,0:T(8,128)}, f32[1,192]{1,0:T(1,128)}, f32[1,64]{1,0:T(1,128)}, f32[2,64]{1,0:T(2,128)}, /*inde...) custom-call(bf16[1024,2048]{1,0:T(8,128)(2,1)} %bitcast.34, bf16[1024,1536]{1,0:T(8,128)(2,1)} %get-tuple-element.85.triple, ...), custom_call_target="tpu_custom_call" | custom-call | flops 80000000000 | bytes 209715200 | tf_op jit(solution)/shard_map/input_backward/pallas_call | solution.py:1597
  665.7 3.5 convert_bitcast_fusion
  669.2 1.0 copy.47
  670.1 1.3 copy.48
  671.5 1.1 copy.49
  672.6 0.6 copy.50
  673.2 0.8 copy.51
  674.5 0.6 copy.53
  675.7 0.6 copy.55
  676.2 1.1 copy.56
  677.3 0.6 copy.57
  (62 shorter events, 4.1 us)
Async XLA Ops:
  7.2 240.6 %all-gather.2.cloned.1.call-start = ((), (), s32[]{:S(2)}) async-start(), calls=%async_computation.1 | async-start | bytes 7045120 | tf_op jit(solution)/shard_map/all_gather | solution.py:2317
  119.9 545.8 %reduce-scatter.2.cloned.1.call-start = ((), (), s32[]{:S(2)}) async-start(), calls=%async_computation.2 | async-start | bytes 7045120 | tf_op jit(solution)/shard_map/reduce_scatter | solution.py:2351
  437.4 119.4 %copy-start.5 = (f32[3,2048]{1,0:T(4,128)S(1)}, f32[3,2048]{1,0:T(4,128)}, u32[]{:S(2)}) copy-start(f32[3,2048]{1,0:T(4,128)} %get-tuple-element.90) | copy-start | bytes 73732
  437.4 121.2 %copy-start.13 = (f32[4]{0:T(128)S(1)}, f32[4]{0:T(128)}, u32[]{:S(2)}) copy-start(f32[4]{0:T(128)} %compare_convert_fusion.1) | copy-start | bytes 52
  437.4 123.4 %copy-start.6 = (f32[2,768]{1,0:T(2,128)S(1)}, f32[2,768]{1,0:T(2,128)}, u32[]{:S(2)}) copy-start(f32[2,768]{1,0:T(2,128)} %get-tuple-element.91) | copy-start | bytes 18436
  437.4 123.5 %copy-start.7 = (f32[32]{0:T(128)S(1)}, f32[32]{0:T(128)}, u32[]{:S(2)}) copy-start(f32[32]{0:T(128)} %mul.53) | copy-start | bytes 388
  665.7 3.5 copy-start.3
  665.7 4.5 copy-start
  669.2 2.3 copy-start.1
  670.1 2.5 copy-start.12
  670.1 3.1 copy-start.4
  671.5 2.5 copy-start.14
  671.5 3.1 copy-start.11
  671.5 3.6 copy-start.10
  671.5 4.2 copy-start.9
  671.5 4.8 copy-start.2
  671.5 5.8 copy-start.8
Sparse Core Ops, SparseCore 0:
  120.0 127.7 all-gather.1
  437.5 143.7 reduce-scatter.1

commit v14 on v13

--- a/solution.py
+++ b/solution.py
@@ -252,7 +252,7 @@
             self.parts[slot, there, self.cols] = total.astype(jnp.bfloat16)
             return carry
 
-        lax.fori_loop(0, self.half // 16, chunk, 0)
+        lax.fori_loop(0, self.half // 16, chunk, 0, unroll=2)
         self.start(
             self.parts.at[slot, self.rows(part), self.cols],
             self.incoming.at[way, distance - 1, part, :, self.cols],
@@ -352,7 +352,7 @@
                 result[there, self.cols] = total.astype(result.dtype)
                 return carry
 
-            lax.fori_loop(0, self.half // 16, chunk, 0)
+            lax.fori_loop(0, self.half // 16, chunk, 0, unroll=2)
 
     def drain(self):
         for copy in self.started:
@@ -510,7 +510,7 @@
             ).astype(jnp.bfloat16)
             return carry
 
-        lax.fori_loop(0, self.landing.shape[2] // 16, chunk, 0)
+        lax.fori_loop(0, self.landing.shape[2] // 16, chunk, 0, unroll=2)
 
     def begin(self, offset):
         for way in range(2):
@@ -537,7 +537,7 @@
             result[some] = held[some].astype(result.dtype)
             return carry
 
-        lax.fori_loop(0, count, begin, 0)
+        lax.fori_loop(0, count, begin, 0, unroll=2)
         for way in range(2):
 
             @pl.when(self.follows(way))
@@ -549,7 +549,7 @@
                     result[some] += self.landing[way, 0, some].astype(result.dtype)
                     return carry
 
-                lax.fori_loop(0, count, chunk, 0)
+                lax.fori_loop(0, count, chunk, 0, unroll=2)
 
     def drain(self):
         for offset in range(1, self.last + 1):
@@ -1566,7 +1566,7 @@
         input_part[some] += residual_scale * sum_grad[some]
         return carry
 
-    lax.fori_loop(0, rows // 16, add_residual, 0)
+    lax.fori_loop(0, rows // 16, add_residual, 0, unroll=2)
     for offset in range(1, narrow_count):
         line.arrived(offset, heads_in, heads_send, heads_recv)
     own_cols = triple.shape[1] // 3

time: 689 us -> 689 us (level)
  no operation moved by 1% of the time
where the time goes in v14:
time: 689 us; the launch traced here: 685 us
  Pallas kernels  644 us (93%)
  between operations  15.2 us (2%)
  local copies, waits for them, and re-layouts  14.9 us (2%)
    pallas_call x1, Pallas kernels, attention_forward(): pl.pallas_call(functools.partial(attention_forward_kernel, wide_count, na...  122 us
    pallas_call x1, Pallas kernels, attention_backward(): pl.pallas_call(functools.partial(attention_backward_kernel, wide_count, n...  119 us
    pallas_call x1, Pallas kernels, geglu_backward(): pl.pallas_call(functools.partial(geglu_backward_kernel, wide_count, narro...  110 us
    pallas_call x1, Pallas kernels, gather_front(): pl.pallas_call(functools.partial(gather_kernel, wide_count, narrow_count)...  109 us
    pallas_call x1, Pallas kernels, input_backward(): pl.pallas_call(functools.partial(input_backward_kernel, wide_count, narro...  104 us
    pallas_call x1, Pallas kernels, geglu_forward(): pl.pallas_call(functools.partial(geglu_forward_kernel, wide_count, narrow...  79.9 us
  transfers between devices with their start and end apart: 2, of which 1 were waited for; matrix products, arithmetic and copies ran while one was open for 1% of the time, Pallas kernels for 50%

profile of v14, /device:TPU:8, one launch (start us, length us, event | category | flops | bytes accessed | tf_op | source)
XLA Modules:
  0.0 685.1 jit_solution(8289365109778480781)
XLA Ops:
  7.2 1.3 reshape.107.reduce_bias
  8.5 1.2 reshape.105.heads_bias
  10.4 109.5 %gather_front.1 = (bf16[4,256,2048]{2,1,0:T(8,128)(2,1)}, bf16[8,256,1536]{2,1,0:T(8,128)(2,1)}, bf16[256,2048]{1,0:T(8,128)(2,1)}, f32[8,4,16,128]{3,2,1,0:T(8,...) custom-call(bf16[256,2048]{1,0:T(8,128)(2,1)} %own.3, ...), custom_call_target="tpu_custom_call" | custom-call | flops 80000000000 | bytes 209715200 | tf_op jit(solution)/shard_map/gather_front/pallas_call | solution.py:1926
  120.5 0.6 mul.53
  121.6 122.3 %attention_forward.1 = (bf16[1024,512]{1,0:T(8,128)(2,1)}, bf16[1024,512]{1,0:T(8,128)(2,1)}, bf16[1024,512]{1,0:T(8,128)(2,1)}, bf16[4,1024,1024]{2,1,0:T(8,128...) custom-call(f32[1024,1536]{1,0:T(8,128)} %bitcast.33, ...), custom_call_target="tpu_custom_call" | custom-call | flops 60000002048 | bytes 209715200 | tf_op jit(solution)/shard_map/attention_forward/pallas_call | solution.py:2174
  243.9 3.9 all-gather.2.cloned.1.call-done.expand
  247.8 79.9 %geglu_forward.1 = (bf16[688,2048]{1,0:T(8,128)(2,1)}, bf16[8,256,768]{2,1,0:T(8,128)(2,1)}, bf16[8,256,768]{2,1,0:T(8,128)(2,1)}, bf16[8,256,768]{2,1,0:T(8,128...) custom-call(bf16[8,256,2048]{2,1,0:T(8,128)(2,1)} %get-tuple-element.65, ...), custom_call_target="tpu_custom_call" | custom-call | flops 19327352832 | bytes 209715200 | tf_op jit(solution)/shard_map/geglu_forward/pallas_call | solution.py:872
  327.6 109.6 %geglu_backward.1 = (f32[688,512]{1,0:T(8,128)}, bf16[2,688,2048]{2,1,0:T(8,128)(2,1)}, f32[256,2048]{1,0:T(8,128)}, f32[2,768]{1,0:T(2,128)}) custom-call(bf16[256,2048]{1,0:T(8,128)(2,1)} %get-tuple-element.71.own, bf16[2,688,2048]{2,1,0:T(8,128)(2,1)} %all-gather.2.cloned.1.call-done.expand, bf16[688,2048]{1,0:T(8,128)(2,1)} %get-tuple-element.72.reduce, ...), custom_call_target="tpu_custom_call" | custom-call | flops 38654705664 | bytes 209715200 | tf_op jit(solution)/shard_map/geglu_backward/pallas_call | solution.py:1113
  437.3 119.3 %attention_backward.1 = (bf16[1024,1536]{1,0:T(8,128)(2,1)}, f32[64,2048]{1,0:T(8,128)}, f32[1,1536]{1,0:T(1,128)}, f32[1,2048]{1,0:T(1,128)}, f32[256,2048]{1,0:T(8,128)}, /*index=5*/f32[2,2048]{1,0:T(2,128)}) custom-call(f32[256,2048]{1,0:T(8,128)} %get-tuple-element.70.upper_grad, f32[256,2048]{1,0:T(8,128)} %get-tuple-element.76.hidden_part, ...), custom_call_target="tpu_custom_call" | custom-call | flops 60000002048 | bytes 209715200 | tf_op jit(solution)/shard_map/attention_backward/pallas_call | solution.py:1345
  556.7 0.8 fusion
  557.7 0.7 reduce.1
  559.2 1.4 reduce.9
  561.5 0.7 pad.24
  562.2 103.6 %input_backward.1 = (f32[256,2048]{1,0:T(8,128)}, f32[64,6144]{1,0:T(8,128)}, f32[1,192]{1,0:T(1,128)}, f32[1,64]{1,0:T(1,128)}, f32[2,64]{1,0:T(2,128)}, /*inde...) custom-call(bf16[1024,2048]{1,0:T(8,128)(2,1)} %bitcast.34, bf16[1024,1536]{1,0:T(8,128)(2,1)} %get-tuple-element.85.triple, ...), custom_call_target="tpu_custom_call" | custom-call | flops 80000000000 | bytes 209715200 | tf_op jit(solution)/shard_map/input_backward/pallas_call | solution.py:1597
  665.9 3.5 convert_bitcast_fusion
  669.3 1.0 copy.47
  670.3 1.3 copy.48
  671.7 1.1 copy.49
  672.8 0.6 copy.50
  673.4 0.8 copy.51
  674.7 0.6 copy.53
  675.8 0.6 copy.55
  676.4 1.1 copy.56
  677.5 0.6 copy.57
  (62 shorter events, 4.1 us)
Async XLA Ops:
  7.2 240.6 %all-gather.2.cloned.1.call-start = ((), (), s32[]{:S(2)}) async-start(), calls=%async_computation.1 | async-start | bytes 7045120 | tf_op jit(solution)/shard_map/all_gather | solution.py:2317
  119.9 546.0 %reduce-scatter.2.cloned.1.call-start = ((), (), s32[]{:S(2)}) async-start(), calls=%async_computation.2 | async-start | bytes 7045120 | tf_op jit(solution)/shard_map/reduce_scatter | solution.py:2351
  437.3 119.4 %copy-start.5 = (f32[3,2048]{1,0:T(4,128)S(1)}, f32[3,2048]{1,0:T(4,128)}, u32[]{:S(2)}) copy-start(f32[3,2048]{1,0:T(4,128)} %get-tuple-element.90) | copy-start | bytes 73732
  437.3 121.2 %copy-start.13 = (f32[4]{0:T(128)S(1)}, f32[4]{0:T(128)}, u32[]{:S(2)}) copy-start(f32[4]{0:T(128)} %compare_convert_fusion.1) | copy-start | bytes 52
  437.3 123.4 %copy-start.6 = (f32[2,768]{1,0:T(2,128)S(1)}, f32[2,768]{1,0:T(2,128)}, u32[]{:S(2)}) copy-start(f32[2,768]{1,0:T(2,128)} %get-tuple-element.91) | copy-start | bytes 18436
  437.3 123.5 %copy-start.7 = (f32[32]{0:T(128)S(1)}, f32[32]{0:T(128)}, u32[]{:S(2)}) copy-start(f32[32]{0:T(128)} %mul.53) | copy-start | bytes 388
  665.8 3.5 copy-start.3
  665.8 4.5 copy-start
  669.3 2.3 copy-start.1
  670.3 2.5 copy-start.12
  670.3 3.1 copy-start.4
  671.6 2.5 copy-start.14
  671.6 3.1 copy-start.11
  671.6 3.6 copy-start.10
  671.6 4.2 copy-start.9
  671.6 4.8 copy-start.2
  671.6 5.8 copy-start.8
Sparse Core Ops, SparseCore 0:
  120.0 127.7 all-gather.1
  437.4 143.7 reduce-scatter.1

commit v15 on v13

--- a/solution.py
+++ b/solution.py
@@ -1865,13 +1865,13 @@
         copy.start()
         outs.append(copy)
 
-    for offset in range(1, narrow_count):
-        start(merge_copy(offset, line.peer(offset), here))
     heads_ring.receive_mate(0)
     for distance in range(1, heads_ring.far):
         gather(heads_ring, distance)
     if last > 1:
         line_rows.step(2)
+    for offset in range(1, narrow_count):
+        start(merge_copy(offset, line.peer(offset), here))
     gather(heads_ring, heads_ring.far)
     keep_out(heads_all, heads_out)
     project(here)

time: 689 us -> 686 us (level)
  no operation moved by 1% of the time
where the time goes in v15:
time: 686 us; the launch traced here: 682 us
  Pallas kernels  641 us (93%)
  between operations  15.2 us (2%)
  local copies, waits for them, and re-layouts  14.9 us (2%)
    pallas_call x1, Pallas kernels, attention_backward(): pl.pallas_call(functools.partial(attention_backward_kernel, wide_count, n...  119 us
    pallas_call x1, Pallas kernels, attention_forward(): pl.pallas_call(functools.partial(attention_forward_kernel, wide_count, na...  118 us
    pallas_call x1, Pallas kernels, gather_front(): pl.pallas_call(functools.partial(gather_kernel, wide_count, narrow_count)...  110 us
    pallas_call x1, Pallas kernels, geglu_backward(): pl.pallas_call(functools.partial(geglu_backward_kernel, wide_count, narro...  110 us
    pallas_call x1, Pallas kernels, input_backward(): pl.pallas_call(functools.partial(input_backward_kernel, wide_count, narro...  103 us
    pallas_call x1, Pallas kernels, geglu_forward(): pl.pallas_call(functools.partial(geglu_forward_kernel, wide_count, narrow...  79.9 us
  transfers between devices with their start and end apart: 2, of which 1 were waited for; matrix products, arithmetic and copies ran while one was open for 1% of the time, Pallas kernels for 50%

profile of v15, /device:TPU:8, one launch (start us, length us, event | category | flops | bytes accessed | tf_op | source)
XLA Modules:
  0.0 682.1 jit_solution(1188322305249683720)
XLA Ops:
  7.2 1.3 reshape.107.reduce_bias
  8.5 1.2 reshape.105.heads_bias
  10.4 110.4 %gather_front.1 = (bf16[4,256,2048]{2,1,0:T(8,128)(2,1)}, bf16[8,256,1536]{2,1,0:T(8,128)(2,1)}, bf16[256,2048]{1,0:T(8,128)(2,1)}, f32[8,4,16,128]{3,2,1,0:T(8,...) custom-call(bf16[256,2048]{1,0:T(8,128)(2,1)} %own.3, ...), custom_call_target="tpu_custom_call" | custom-call | flops 80000000000 | bytes 209715200 | tf_op jit(solution)/shard_map/gather_front/pallas_call | solution.py:1926
  121.4 0.6 mul.53
  122.5 118.1 %attention_forward.1 = (bf16[1024,512]{1,0:T(8,128)(2,1)}, bf16[1024,512]{1,0:T(8,128)(2,1)}, bf16[1024,512]{1,0:T(8,128)(2,1)}, bf16[4,1024,1024]{2,1,0:T(8,128...) custom-call(f32[1024,1536]{1,0:T(8,128)} %bitcast.33, ...), custom_call_target="tpu_custom_call" | custom-call | flops 60000002048 | bytes 209715200 | tf_op jit(solution)/shard_map/attention_forward/pallas_call | solution.py:2174
  240.6 3.9 all-gather.2.cloned.1.call-done.expand
  244.5 79.9 %geglu_forward.1 = (bf16[688,2048]{1,0:T(8,128)(2,1)}, bf16[8,256,768]{2,1,0:T(8,128)(2,1)}, bf16[8,256,768]{2,1,0:T(8,128)(2,1)}, bf16[8,256,768]{2,1,0:T(8,128...) custom-call(bf16[8,256,2048]{2,1,0:T(8,128)(2,1)} %get-tuple-element.65, ...), custom_call_target="tpu_custom_call" | custom-call | flops 19327352832 | bytes 209715200 | tf_op jit(solution)/shard_map/geglu_forward/pallas_call | solution.py:872
  324.4 110.1 %geglu_backward.1 = (f32[688,512]{1,0:T(8,128)}, bf16[2,688,2048]{2,1,0:T(8,128)(2,1)}, f32[256,2048]{1,0:T(8,128)}, f32[2,768]{1,0:T(2,128)}) custom-call(bf16[256,2048]{1,0:T(8,128)(2,1)} %get-tuple-element.71.own, bf16[2,688,2048]{2,1,0:T(8,128)(2,1)} %all-gather.2.cloned.1.call-done.expand, bf16[688,2048]{1,0:T(8,128)(2,1)} %get-tuple-element.72.reduce, ...), custom_call_target="tpu_custom_call" | custom-call | flops 38654705664 | bytes 209715200 | tf_op jit(solution)/shard_map/geglu_backward/pallas_call | solution.py:1113
  434.6 119.4 %attention_backward.1 = (bf16[1024,1536]{1,0:T(8,128)(2,1)}, f32[64,2048]{1,0:T(8,128)}, f32[1,1536]{1,0:T(1,128)}, f32[1,2048]{1,0:T(1,128)}, f32[256,2048]{1,0:T(8,128)}, /*index=5*/f32[2,2048]{1,0:T(2,128)}) custom-call(f32[256,2048]{1,0:T(8,128)} %get-tuple-element.70.upper_grad, f32[256,2048]{1,0:T(8,128)} %get-tuple-element.76.hidden_part, ...), custom_call_target="tpu_custom_call" | custom-call | flops 60000002048 | bytes 209715200 | tf_op jit(solution)/shard_map/attention_backward/pallas_call | solution.py:1345
  554.0 0.8 fusion
  555.0 0.7 reduce.1
  556.5 1.4 reduce.9
  558.7 0.7 pad.24
  559.5 103.3 %input_backward.1 = (f32[256,2048]{1,0:T(8,128)}, f32[64,6144]{1,0:T(8,128)}, f32[1,192]{1,0:T(1,128)}, f32[1,64]{1,0:T(1,128)}, f32[2,64]{1,0:T(2,128)}, /*inde...) custom-call(bf16[1024,2048]{1,0:T(8,128)(2,1)} %bitcast.34, bf16[1024,1536]{1,0:T(8,128)(2,1)} %get-tuple-element.85.triple, ...), custom_call_target="tpu_custom_call" | custom-call | flops 80000000000 | bytes 209715200 | tf_op jit(solution)/shard_map/input_backward/pallas_call | solution.py:1597
  662.9 3.5 convert_bitcast_fusion
  666.3 1.0 copy.47
  667.3 1.3 copy.48
  668.7 1.1 copy.49
  669.8 0.6 copy.50
  670.4 0.8 copy.51
  671.7 0.6 copy.53
  672.8 0.6 copy.55
  673.4 1.1 copy.56
  674.5 0.6 copy.57
  (62 shorter events, 4.1 us)
Async XLA Ops:
  7.2 237.3 %all-gather.2.cloned.1.call-start = ((), (), s32[]{:S(2)}) async-start(), calls=%async_computation.1 | async-start | bytes 7045120 | tf_op jit(solution)/shard_map/all_gather | solution.py:2317
  120.8 542.0 %reduce-scatter.2.cloned.1.call-start = ((), (), s32[]{:S(2)}) async-start(), calls=%async_computation.2 | async-start | bytes 7045120 | tf_op jit(solution)/shard_map/reduce_scatter | solution.py:2351
  434.5 119.4 %copy-start.5 = (f32[3,2048]{1,0:T(4,128)S(1)}, f32[3,2048]{1,0:T(4,128)}, u32[]{:S(2)}) copy-start(f32[3,2048]{1,0:T(4,128)} %get-tuple-element.90) | copy-start | bytes 73732
  434.6 121.2 %copy-start.13 = (f32[4]{0:T(128)S(1)}, f32[4]{0:T(128)}, u32[]{:S(2)}) copy-start(f32[4]{0:T(128)} %compare_convert_fusion.1) | copy-start | bytes 52
  434.6 123.4 %copy-start.6 = (f32[2,768]{1,0:T(2,128)S(1)}, f32[2,768]{1,0:T(2,128)}, u32[]{:S(2)}) copy-start(f32[2,768]{1,0:T(2,128)} %get-tuple-element.91) | copy-start | bytes 18436
  434.6 123.5 %copy-start.7 = (f32[32]{0:T(128)S(1)}, f32[32]{0:T(128)}, u32[]{:S(2)}) copy-start(f32[32]{0:T(128)} %mul.53) | copy-start | bytes 388
  662.8 3.5 copy-start.3
  662.8 4.5 copy-start
  666.3 2.3 copy-start.1
  667.3 2.5 copy-start.12
  667.3 3.1 copy-start.4
  668.6 2.5 copy-start.14
  668.6 3.1 copy-start.11
  668.6 3.6 copy-start.10
  668.6 4.2 copy-start.9
  668.6 4.8 copy-start.2
  668.6 5.8 copy-start.8
Sparse Core Ops, SparseCore 0:
  120.9 123.5 all-gather.1
  434.7 143.7 reduce-scatter.1
